TPU v7x, 32 devices: a whole 2x2x4 slice. The times are simulated.
32 devices in a mesh: space: 8 (over z, y), dp: 4 (over x, core).
Axes of the slice: x: 2, y: 2, z: 4, core: 2. Of those that a mesh axis runs over, the one named last changes fastest.
Arguments:
- features: bfloat16 [4, 32, 8, 8, 512], P('dp', 'space'), may hold values from -6 to 6
- occupancy: int32 [4, 32, 512], P('dp', 'space'), may hold values 0 or 1
- counts: int32 [4, 8], P('dp', 'space'), may hold values from 2 to 4, as said below
- send_units: int32 [4, 8, 5, 12], P('dp', 'space'), may hold values from -1 to 23, as said below
- neighbours: int32 [4, 32, 26], P('dp', 'space'), may hold values from -1 to 59, as said below
- weight: bfloat16 [1728, 64], P('dp'), may hold values from -0.15625 to 0.15625
- conv_bias: bfloat16 [64], P('dp'), may hold values from -3 to 3
- cotangent: bfloat16 [4, 32, 8, 8, 512], P('dp', 'space'), may hold values from -6 to 6
Outputs:
- block_output: bfloat16 [4, 32, 8, 8, 512], P('dp', 'space')
- grad_input: bfloat16 [4, 32, 8, 8, 512], P('dp', 'space')
- grad_weight: float32 [1728, 64], P('dp')
- grad_bias: float32 [64], P('dp')
Inputs may be any that keep to these rules, and one draw needn't show every extreme that they name: `counts`: each volume has a device holding 4 bricks. `send_units`: the entry of device q at j and l is -1 or 6 times a slot below counts of q plus ((j * 12 + l) mod 6); it is -1 where device q + j - 2 does not exist; link 0 is used wherever that device exists. `neighbours`: an entry n >= 0 of a brick on device r names a unit that device r + 2 - n // 12 sends, whose face is the one the entry's offset needs (2d if o_d = 1, 2d+1 if o_d = -1, d the first dimension where o is not 0).
All inputs are finite; a program needn't handle non-finite values. No bound on the sum of `occupancy` on one device may be relied on, other than what follows from the above.
Results may differ from a plain program's by a relative error of at most 0.012.
Values may be sent and summed in bfloat16 or wider, within the bound.
No kernel may reach another device: no remote copies, remote signals or barrier semaphores. Data moves between devices by JAX's collectives and lax.ppermute only.
A program may use at most 64 MiB of HBM per device.

v0:
```python
import jax
import jax.numpy as jnp
from jax import lax
from jax.sharding import PartitionSpec as P


def passed_along(block, axis, distance):
    devices = range(lax.axis_size(axis))
    route = [(i - distance, i) for i in devices if i - distance in devices]
    return lax.ppermute(block, axis, route)


def neighbour_offsets():
    return [
        (first - 1, second - 1, third - 1)
        for first in range(3)
        for second in range(3)
        for third in range(3)
        if (first, second, third) != (1, 1, 1)
    ]


def first_moving(offset):
    for dimension in range(3):
        if offset[dimension] != 0:
            return dimension
    return 0


def face_planes(values):
    brick_edge = values.shape[1]
    planes = [
        values[:, 0],
        values[:, brick_edge - 1],
        values[:, :, 0],
        values[:, :, brick_edge - 1],
        values[:, :, :, 0],
        values[:, :, :, brick_edge - 1],
    ]
    return jnp.stack(planes, axis=1)


def rim_region(face_plane, offset, brick_edge):
    moving = first_moving(offset)
    region = face_plane
    other_dims = [dimension for dimension in range(3) if dimension != moving]
    for position, dimension in enumerate(other_dims):
        if offset[dimension] == -1:
            region = lax.slice_in_dim(region, brick_edge - 1, brick_edge, axis=position + 1)
        elif offset[dimension] == 1:
            region = lax.slice_in_dim(region, 0, 1, axis=position + 1)
    return jnp.expand_dims(region, moving + 1)


def halo_block(values, units, listing):
    brick_edge = values.shape[1]
    unit_total = units.shape[0]
    padded = jnp.pad(values, ((0, 0), (1, 1), (1, 1), (1, 1), (0, 0)))
    for offset_index, offset in enumerate(neighbour_offsets()):
        unit_index = listing[:, offset_index]
        face_plane = jnp.take(units, jnp.clip(unit_index, 0, unit_total - 1), axis=0)
        face_plane = face_plane * (unit_index >= 0).astype(face_plane.dtype)[:, None, None, None]
        region = rim_region(face_plane, offset, brick_edge)
        starts = (
            [0] + [0 if step == -1 else 1 if step == 0 else brick_edge + 1 for step in offset] + [0]
        )
        padded = lax.dynamic_update_slice(padded, region, starts)
    return padded


def share_faces(values, send_list):
    slot_count = values.shape[0]
    brick_edge = values.shape[1]
    channels = values.shape[-1]
    spread = send_list.shape[0]
    link_count = send_list.shape[1]
    reach_span = (spread - 1) // 2
    flattened = face_planes(values).reshape(slot_count * 6, brick_edge, brick_edge * channels)
    picked = jnp.take(flattened, jnp.clip(send_list, 0, slot_count * 6 - 1).reshape(-1), axis=0)
    picked = picked * (send_list.reshape(-1) >= 0).astype(values.dtype)[:, None, None]
    outgoing = picked.reshape(spread, link_count, brick_edge, brick_edge * channels)
    pieces = [None] * spread
    pieces[reach_span] = outgoing[reach_span]
    for column in range(spread):
        if column != reach_span:
            pieces[column] = passed_along(outgoing[column], "space", column - reach_span)
    received = jnp.stack(pieces)
    return received.reshape(spread * link_count, brick_edge, brick_edge, channels)


def windows(padded, brick_edge):
    return [
        padded[
            :,
            first : first + brick_edge,
            second : second + brick_edge,
            third : third + brick_edge,
            :,
        ]
        for first in range(3)
        for second in range(3)
        for third in range(3)
    ]


def gathered_columns(brick_block, brick_edge):
    return jnp.concatenate(
        [window.reshape(-1, window.shape[-1]) for window in windows(brick_block[None], brick_edge)],
        axis=1,
    )


def convolve(padded, kernels, brick_edge):
    stacked_kernel = kernels.reshape(-1, kernels.shape[-1])

    def convolve_per_brick(brick_block):
        return jnp.dot(
            gathered_columns(brick_block, brick_edge),
            stacked_kernel,
            preferred_element_type=jnp.float32,
        )

    result = lax.map(convolve_per_brick, padded)
    return result.reshape(padded.shape[0], brick_edge, brick_edge, brick_edge, -1)


def weight_terms(padded, grads, brick_edge):
    channels = padded.shape[-1]

    def weight_per_brick(running_total, brick_pair):
        brick_block, grad_block = brick_pair
        product = lax.dot_general(
            gathered_columns(brick_block, brick_edge),
            grad_block.reshape(-1, channels),
            (((0,), (0,)), ((), ())),
            preferred_element_type=jnp.float32,
        )
        return (running_total + product, None)

    running_total, unused_out = lax.scan(
        weight_per_brick, jnp.zeros((27 * channels, channels), jnp.float32), (padded, grads)
    )
    return running_total


def body(features, occupancy, counts, send_units, neighbours, weight, conv_bias, cotangent):
    slot_count = features.shape[1]
    brick_edge = features.shape[2]
    channels = features.shape[4] // brick_edge
    shard_shape = features.shape
    grid_shape = (slot_count, brick_edge, brick_edge, brick_edge, channels)
    listing = neighbours[0]
    send_list = send_units[0, 0]
    live_slot = (jnp.arange(slot_count, dtype=jnp.int32) < counts[0, 0]).astype(jnp.int32)
    active = (occupancy[0] * live_slot[:, None]).reshape(
        slot_count, brick_edge, brick_edge, brick_edge, 1
    )
    active_full = active.astype(jnp.float32)
    weight_all, bias_all = (
        lax.all_gather(weight, "dp", axis=0, tiled=True),
        lax.all_gather(conv_bias, "dp", axis=0, tiled=True),
    )
    kernels = weight_all.reshape(27, channels, channels)
    masked = features[0].reshape(grid_shape) * active.astype(jnp.bfloat16)
    padded_input = halo_block(masked, share_faces(masked, send_list), listing)
    pre_activation = convolve(padded_input, kernels, brick_edge) + bias_all.astype(jnp.float32)
    sigmoid_pre = jax.nn.sigmoid(pre_activation)
    block_output = (pre_activation * sigmoid_pre * active_full).astype(jnp.bfloat16)
    grad_pre = (
        cotangent[0].reshape(grid_shape).astype(jnp.float32)
        * sigmoid_pre
        * (1.0 + pre_activation * (1.0 - sigmoid_pre))
        * active_full
    ).astype(jnp.bfloat16)
    padded_grad = halo_block(grad_pre, share_faces(grad_pre, send_list), listing)
    mirrored = jnp.swapaxes(kernels[::-1], 1, 2)
    grad_input = (convolve(padded_grad, mirrored, brick_edge) * active_full).astype(jnp.bfloat16)
    weight_grad = weight_terms(padded_input, grad_pre, brick_edge)
    bias_grad = jnp.sum(grad_pre.astype(jnp.float32).reshape(-1, channels), axis=0)
    weight_total, bias_total = lax.psum((weight_grad, bias_grad), "space")
    weight_share, bias_share = (
        lax.psum_scatter(
            weight_total.astype(jnp.bfloat16), "dp", scatter_dimension=0, tiled=True
        ).astype(jnp.float32),
        lax.psum_scatter(
            bias_total.astype(jnp.bfloat16), "dp", scatter_dimension=0, tiled=True
        ).astype(jnp.float32),
    )
    return (
        block_output.reshape(shard_shape),
        grad_input.reshape(shard_shape),
        weight_share,
        bias_share,
    )


def solution(mesh):
    placed = (
        P("dp", "space", None, None, None),
        P("dp", "space", None),
        P("dp", "space"),
        P("dp", "space", None, None),
        P("dp", "space", None),
        P("dp", None),
        P("dp"),
        P("dp", "space", None, None, None),
    )
    return jax.shard_map(
        body,
        mesh=mesh,
        in_specs=placed,
        out_specs=(
            P("dp", "space", None, None, None),
            P("dp", "space", None, None, None),
            P("dp", None),
            P("dp"),
        ),
        check_vma=False,
    )
```

profile of v0, /device:TPU:0, one launch (start us, length us, event | category | flops | bytes accessed | tf_op | source)
XLA Modules:
  0.0 397.2 jit_solution(14896796416140176311)
XLA Ops:
  16.1 6.1 %collective-permute-start.2 = (bf16[12,8,512]{2,1,0:T(8,128)(2,1)S(1)}, bf16[12,8,512]{2,1,0:T(8,128)(2,1)}, u32[]{:S(2)}, u32[]{:S(2)}) collective-permute-start(bf16[12,8,512]{2,1,0:T(8,128)(2,1)S(1)} %get-tuple-element.301), channel_id=1, source_target_pairs={{0,4},{4,8},{8,12},{12,16},{16,20},{20,24},{24,28},{1,5},{5,9},{9,... | collective-permute-start | bytes 294920 | tf_op jit(solution)/shard_map/ppermute | solution.py:10
  22.2 4.6 %collective-permute-start.3 = (bf16[12,8,512]{2,1,0:T(8,128)(2,1)S(1)}, bf16[12,8,512]{2,1,0:T(8,128)(2,1)}, u32[]{:S(2)}, u32[]{:S(2)}) collective-permute-start(bf16[12,8,512]{2,1,0:T(8,128)(2,1)S(1)} %get-tuple-element.300), channel_id=1, source_target_pairs={{0,8},{4,12},{8,16},{12,20},{16,24},{20,28},{1,9},{5,13},{9,17},{1... | collective-permute-start | bytes 294920 | tf_op jit(solution)/shard_map/ppermute | solution.py:10
  53.3 6.2 %all-gather = bf16[4,432,64]{1,2,0:T(8,128)(2,1)S(1)} all-gather(bf16[1,432,64]{1,2,0:T(8,128)(2,1)S(1)} %bitcast.603), channel_id=1, replica_groups=mesh['space'=8,'dp'=4] {'dp'}, dimensions={0}, use_global_device_ids=true | all-gather | bytes 276480 | tf_op jit(solution)/shard_map/all_gather | solution.py:160
  64.0 7.1 %all-reduce.2 = bf16[64]{0:T(256)(128)(2,1)S(1)} all-reduce(bf16[64]{0:T(256)(128)(2,1)S(1)} %dynamic-update-slice), channel_id=1, replica_groups=mesh['space'=8,'dp'=4] {'dp'}, use_global_device_ids=true, to_apply=%add.2 | all-reduce | flops 64 | bytes 256
  122.5 2.8 dynamic_update_slice.175
  125.3 2.8 dynamic_update_slice.176
  137.1 34.4 %while.31 = (s32[]{:T(128)}, f32[4,512,64]{1,2,0:T(8,128)}, bf16[4,10,10,10,64]{4,3,2,1,0:T(8,128)(2,1)S(1)}, bf16[1728,64]{1,0:T(8,128)(2,1)}, s32[]{:T(128)}, /*index=5*/s32[]{:T(128)}, s32[]{}, s32[]{}) while((s32[]{:T(128)}, f32[4,512,64]{1,2,0:T(8,128)}, bf16[4,10,10,10,64]{4,3,2,1,0:T(8,128)(2,1)S(1)}, bf16[1728,64]{1,0:T(8,128)(2,1)}, ...), condition=%wide.region_1.4_spmd, body=%wide.region_0.0_spmd.sunk | while | flops 113246208 | bytes 9421433 | solution.py:123
  137.1 2.1 constant_dynamic-slice_fusion.85
  139.1 4.2 %concatenate.13 = bf16[512,1728]{1,0:T(8,128)(2,1)S(1)} concatenate(bf16[512,64]{1,0:T(8,128)(2,1)} %bitcast.567, bf16[512,64]{1,0:T(8,128)(2,1)} %bitcast.566, bf16[512,64]{1,0:T(8,128)(2,1)} %bitcast.565, bf16[512,64]{1,0:T(8,128)(2,1)} %bitcast.564, bf16[512,64]{1,0:T(8,128)(2,1)} %bitcast.563, bf16[512,64]{1,0:T(8,128)(2,1)} %bitcast.562, bf16[512,64]{1,0:T(8,128)(2,1)} %bitcast.561, ...), dimensions={1} | concatenate | bytes 3538944 | tf_op jit(solution)/shard_map/while/body/eval_jaxpr/concatenate | solution.py:107
  143.3 2.3 fusion.84
  145.7 2.1 constant_dynamic-slice_fusion.85
  147.7 4.2 %concatenate.13 = bf16[512,1728]{1,0:T(8,128)(2,1)S(1)} concatenate(bf16[512,64]{1,0:T(8,128)(2,1)} %bitcast.567, bf16[512,64]{1,0:T(8,128)(2,1)} %bitcast.566, bf16[512,64]{1,0:T(8,128)(2,1)} %bitcast.565, bf16[512,64]{1,0:T(8,128)(2,1)} %bitcast.564, bf16[512,64]{1,0:T(8,128)(2,1)} %bitcast.563, bf16[512,64]{1,0:T(8,128)(2,1)} %bitcast.562, bf16[512,64]{1,0:T(8,128)(2,1)} %bitcast.561, ...), dimensions={1} | concatenate | bytes 3538944 | tf_op jit(solution)/shard_map/while/body/eval_jaxpr/concatenate | solution.py:107
  151.9 2.3 fusion.84
  156.3 4.2 %concatenate.13 = bf16[512,1728]{1,0:T(8,128)(2,1)S(1)} concatenate(bf16[512,64]{1,0:T(8,128)(2,1)} %bitcast.567, bf16[512,64]{1,0:T(8,128)(2,1)} %bitcast.566, bf16[512,64]{1,0:T(8,128)(2,1)} %bitcast.565, bf16[512,64]{1,0:T(8,128)(2,1)} %bitcast.564, bf16[512,64]{1,0:T(8,128)(2,1)} %bitcast.563, bf16[512,64]{1,0:T(8,128)(2,1)} %bitcast.562, bf16[512,64]{1,0:T(8,128)(2,1)} %bitcast.561, ...), dimensions={1} | concatenate | bytes 3538944 | tf_op jit(solution)/shard_map/while/body/eval_jaxpr/concatenate | solution.py:107
  160.5 2.4 fusion.84
  162.9 2.1 constant_dynamic-slice_fusion.85
  164.9 4.2 %concatenate.13 = bf16[512,1728]{1,0:T(8,128)(2,1)S(1)} concatenate(bf16[512,64]{1,0:T(8,128)(2,1)} %bitcast.567, bf16[512,64]{1,0:T(8,128)(2,1)} %bitcast.566, bf16[512,64]{1,0:T(8,128)(2,1)} %bitcast.565, bf16[512,64]{1,0:T(8,128)(2,1)} %bitcast.564, bf16[512,64]{1,0:T(8,128)(2,1)} %bitcast.563, bf16[512,64]{1,0:T(8,128)(2,1)} %bitcast.562, bf16[512,64]{1,0:T(8,128)(2,1)} %bitcast.561, ...), dimensions={1} | concatenate | bytes 3538944 | tf_op jit(solution)/shard_map/while/body/eval_jaxpr/concatenate | solution.py:107
  169.1 2.4 fusion.84
  172.9 2.1 multiply_convert_fusion
  177.0 2.3 reshape.794
  179.3 44.5 %while.33 = (s32[]{:T(128)}, f32[1728,64]{0,1:T(8,128)}, bf16[4,10,10,10,64]{4,3,2,1,0:T(8,128)(2,1)S(1)}, bf16[4,8,8,8,64]{4,3,2,1,0:T(8,128)(2,1)}, s32[]{:T(128)}, /*index=5*/s32[]{:T(128)}, s32[]{}, s32[]{}) while((s32[]{:T(128)}, f32[1728,64]{0,1:T(8,128)}, bf16[4,10,10,10,64]{4,3,2,1,0:T(8,128)(2,1)S(1)}, ...), condition=%wide.region_5.8_spmd.clone, body=%wide.region_4.7_spmd.clone.sunk | while | flops 113467392 | bytes 9928835 | solution.py:140
  179.3 3.0 constant_dynamic-slice_fusion.87
  182.3 5.3 %concatenate.15 = bf16[512,1728]{1,0:T(8,128)(2,1)} concatenate(bf16[512,64]{1,0:T(8,128)(2,1)} %bitcast.540, bf16[512,64]{1,0:T(8,128)(2,1)} %bitcast.539, bf16[512,64]{1,0:T(8,128)(2,1)} %bitcast.538, bf16[512,64]{1,0:T(8,128)(2,1)} %bitcast.537, bf16[512,64]{1,0:T(8,128)(2,1)} %bitcast.536, bf16[512,64]{1,0:T(8,128)(2,1)} %bitcast.535, bf16[512,64]{1,0:T(8,128)(2,1)} %bitcast.534, ...), dimensions={1} | concatenate | bytes 3538944 | tf_op jit(solution)/shard_map/while/body/eval_jaxpr/concatenate | solution.py:107
  187.6 2.8 convolution_add_fusion.2
  190.4 3.0 constant_dynamic-slice_fusion.87
  193.4 5.3 %concatenate.15 = bf16[512,1728]{1,0:T(8,128)(2,1)} concatenate(bf16[512,64]{1,0:T(8,128)(2,1)} %bitcast.540, bf16[512,64]{1,0:T(8,128)(2,1)} %bitcast.539, bf16[512,64]{1,0:T(8,128)(2,1)} %bitcast.538, bf16[512,64]{1,0:T(8,128)(2,1)} %bitcast.537, bf16[512,64]{1,0:T(8,128)(2,1)} %bitcast.536, bf16[512,64]{1,0:T(8,128)(2,1)} %bitcast.535, bf16[512,64]{1,0:T(8,128)(2,1)} %bitcast.534, ...), dimensions={1} | concatenate | bytes 3538944 | tf_op jit(solution)/shard_map/while/body/eval_jaxpr/concatenate | solution.py:107
  198.7 2.8 convolution_add_fusion.2
  201.5 3.0 constant_dynamic-slice_fusion.87
  204.6 5.3 %concatenate.15 = bf16[512,1728]{1,0:T(8,128)(2,1)} concatenate(bf16[512,64]{1,0:T(8,128)(2,1)} %bitcast.540, bf16[512,64]{1,0:T(8,128)(2,1)} %bitcast.539, bf16[512,64]{1,0:T(8,128)(2,1)} %bitcast.538, bf16[512,64]{1,0:T(8,128)(2,1)} %bitcast.537, bf16[512,64]{1,0:T(8,128)(2,1)} %bitcast.536, bf16[512,64]{1,0:T(8,128)(2,1)} %bitcast.535, bf16[512,64]{1,0:T(8,128)(2,1)} %bitcast.534, ...), dimensions={1} | concatenate | bytes 3538944 | tf_op jit(solution)/shard_map/while/body/eval_jaxpr/concatenate | solution.py:107
  209.8 2.8 convolution_add_fusion.2
  212.7 3.0 constant_dynamic-slice_fusion.87
  215.7 5.3 %concatenate.15 = bf16[512,1728]{1,0:T(8,128)(2,1)} concatenate(bf16[512,64]{1,0:T(8,128)(2,1)} %bitcast.540, bf16[512,64]{1,0:T(8,128)(2,1)} %bitcast.539, bf16[512,64]{1,0:T(8,128)(2,1)} %bitcast.538, bf16[512,64]{1,0:T(8,128)(2,1)} %bitcast.537, bf16[512,64]{1,0:T(8,128)(2,1)} %bitcast.536, bf16[512,64]{1,0:T(8,128)(2,1)} %bitcast.535, bf16[512,64]{1,0:T(8,128)(2,1)} %bitcast.534, ...), dimensions={1} | concatenate | bytes 3538944 | tf_op jit(solution)/shard_map/while/body/eval_jaxpr/concatenate | solution.py:107
  221.0 2.8 convolution_add_fusion.2
  226.5 41.2 %all-reduce.6 = (bf16[1728,64]{0,1:T(8,128)(2,1)S(1)}, bf16[64]{0:T(256)(128)(2,1)S(1)}) all-reduce(f32[1728,64]{0,1:T(8,128)S(1)} %copy-done, f32[64]{0:T(128)S(1)} %convert_reduce_fusion), channel_id=1, replica_groups=mesh['space'=8,'dp'=4] {'space'}, use_global_device_ids=true, to_apply=%region_6.9 | all-reduce | flops 110656 | bytes 663936 | tf_op jit(solution)/shard_map/psum | solution.py:180
  268.7 5.8 %all-reduce.3 = bf16[64]{0:T(256)(128)(2,1)S(1)} all-reduce(bf16[64]{0:T(256)(128)(2,1)S(1)} %get-tuple-element.207), channel_id=3, replica_groups=mesh['space'=8,'dp'=4] {'dp'}, use_global_device_ids=true, to_apply=%region_10.13.clone | all-reduce | flops 64 | bytes 256
  280.9 4.6 %collective-permute-start.6 = (bf16[12,8,512]{2,1,0:T(8,128)(2,1)S(1)}, bf16[12,8,512]{2,1,0:T(8,128)(2,1)S(1)}, u32[]{:S(2)}, u32[]{:S(2)}) collective-permute-start(bf16[12,8,512]{2,1,0:T(8,128)(2,1)S(1)} %get-tuple-element.297), channel_id=1, source_target_pairs={{0,4},{4,8},{8,12},{12,16},{16,20},{20,24},{24,28},{1,5},{5,9},{9,... | collective-permute-start | bytes 294920 | tf_op jit(solution)/shard_map/ppermute | solution.py:10
  285.5 4.6 %collective-permute-start.7 = (bf16[12,8,512]{2,1,0:T(8,128)(2,1)S(1)}, bf16[12,8,512]{2,1,0:T(8,128)(2,1)S(1)}, u32[]{:S(2)}, u32[]{:S(2)}) collective-permute-start(bf16[12,8,512]{2,1,0:T(8,128)(2,1)S(1)} %get-tuple-element.296), channel_id=1, source_target_pairs={{0,8},{4,12},{8,16},{12,20},{16,24},{20,28},{1,9},{5,13},{9,17},{1... | collective-permute-start | bytes 294920 | tf_op jit(solution)/shard_map/ppermute | solution.py:10
  339.5 2.8 dynamic_update_slice.201
  342.3 2.8 dynamic_update_slice.202
  347.3 38.6 %while.32 = (s32[]{:T(128)}, f32[4,512,64]{1,2,0:T(8,128)}, bf16[4,10,10,10,64]{4,3,2,1,0:T(8,128)(2,1)S(1)}, bf16[1728,64]{1,0:T(8,128)(2,1)S(1)}, s32[]{:T(128)}, /*index=5*/s32[]{:T(128)}, s32[]{}, s32[]{}) while((s32[]{:T(128)}, f32[4,512,64]{1,2,0:T(8,128)}, bf16[4,10,10,10,64]{4,3,2,1,0:T(8,128)(2,1)S(1)}, ...), condition=%wide.region_3.6_spmd, body=%wide.region_2.5_spmd.sunk | while | flops 113246208 | bytes 9265785 | solution.py:123
  349.2 5.0 %concatenate.14 = bf16[512,1728]{1,0:T(8,128)(2,1)} concatenate(bf16[512,64]{1,0:T(8,128)(2,1)} %bitcast.594, bf16[512,64]{1,0:T(8,128)(2,1)} %bitcast.593, bf16[512,64]{1,0:T(8,128)(2,1)} %bitcast.592, bf16[512,64]{1,0:T(8,128)(2,1)} %bitcast.591, bf16[512,64]{1,0:T(8,128)(2,1)} %bitcast.590, bf16[512,64]{1,0:T(8,128)(2,1)} %bitcast.589, bf16[512,64]{1,0:T(8,128)(2,1)} %bitcast.588, ...), dimensions={1} | concatenate | bytes 3538944 | tf_op jit(solution)/shard_map/while/body/eval_jaxpr/concatenate | solution.py:107
  354.1 2.8 fusion.87
  358.8 5.0 %concatenate.14 = bf16[512,1728]{1,0:T(8,128)(2,1)} concatenate(bf16[512,64]{1,0:T(8,128)(2,1)} %bitcast.594, bf16[512,64]{1,0:T(8,128)(2,1)} %bitcast.593, bf16[512,64]{1,0:T(8,128)(2,1)} %bitcast.592, bf16[512,64]{1,0:T(8,128)(2,1)} %bitcast.591, bf16[512,64]{1,0:T(8,128)(2,1)} %bitcast.590, bf16[512,64]{1,0:T(8,128)(2,1)} %bitcast.589, bf16[512,64]{1,0:T(8,128)(2,1)} %bitcast.588, ...), dimensions={1} | concatenate | bytes 3538944 | tf_op jit(solution)/shard_map/while/body/eval_jaxpr/concatenate | solution.py:107
  363.8 2.8 fusion.87
  368.5 5.0 %concatenate.14 = bf16[512,1728]{1,0:T(8,128)(2,1)} concatenate(bf16[512,64]{1,0:T(8,128)(2,1)} %bitcast.594, bf16[512,64]{1,0:T(8,128)(2,1)} %bitcast.593, bf16[512,64]{1,0:T(8,128)(2,1)} %bitcast.592, bf16[512,64]{1,0:T(8,128)(2,1)} %bitcast.591, bf16[512,64]{1,0:T(8,128)(2,1)} %bitcast.590, bf16[512,64]{1,0:T(8,128)(2,1)} %bitcast.589, bf16[512,64]{1,0:T(8,128)(2,1)} %bitcast.588, ...), dimensions={1} | concatenate | bytes 3538944 | tf_op jit(solution)/shard_map/while/body/eval_jaxpr/concatenate | solution.py:107
  373.4 2.8 fusion.87
  378.1 5.0 %concatenate.14 = bf16[512,1728]{1,0:T(8,128)(2,1)} concatenate(bf16[512,64]{1,0:T(8,128)(2,1)} %bitcast.594, bf16[512,64]{1,0:T(8,128)(2,1)} %bitcast.593, bf16[512,64]{1,0:T(8,128)(2,1)} %bitcast.592, bf16[512,64]{1,0:T(8,128)(2,1)} %bitcast.591, bf16[512,64]{1,0:T(8,128)(2,1)} %bitcast.590, bf16[512,64]{1,0:T(8,128)(2,1)} %bitcast.589, bf16[512,64]{1,0:T(8,128)(2,1)} %bitcast.588, ...), dimensions={1} | concatenate | bytes 3538944 | tf_op jit(solution)/shard_map/while/body/eval_jaxpr/concatenate | solution.py:107
  383.1 2.8 fusion.87
  (514 shorter events, 175.1 us)
Async XLA Ops:
  7.2 381.5 %reduce-scatter.4.cloned.1.call-start = ((), (), s32[]{:S(2)}) async-start(), calls=%async_computation.1 | async-start | bytes 552960
  10.0 67.5 %copy-start.8 = (f32[4,8,8,8]{3,2,1,0:T(8,128)}, f32[4,8,8,8]{3,2,1,0:T(8,128)S(1)}, u32[]{:S(2)}) copy-start(f32[4,8,8,8]{3,2,1,0:T(8,128)S(1)} %get-tuple-element.305) | copy-start | bytes 24580
  11.2 40.7 %copy-start.10 = (bf16[1,4,8,8,512]{4,3,2,1,0:T(8,128)(2,1)S(1)}, bf16[1,4,8,8,512]{4,3,2,1,0:T(8,128)(2,1)}, u32[]{:S(2)}) copy-start(bf16[1,4,8,8,512]{4,3,2,1,0:T(8,128)(2,1)} %param.25) | copy-start | bytes 786436
  12.6 40.7 %copy-start.7 = (bf16[60,8,512]{2,1,0:T(8,128)(2,1)}, bf16[60,8,512]{2,1,0:T(8,128)(2,1)S(1)}, u32[]{:S(2)}) copy-start(bf16[60,8,512]{2,1,0:T(8,128)(2,1)S(1)} %select_multiply_fusion.1) | copy-start | bytes 1474564
  13.4 39.9 %copy-start.14 = (bf16[432,64]{0,1:T(8,128)(2,1)S(1)}, bf16[432,64]{0,1:T(8,128)(2,1)}, u32[]{:S(2)}) copy-start(bf16[432,64]{0,1:T(8,128)(2,1)} %param.23) | copy-start | bytes 165892
  13.4 68.7 %collective-permute-start = (bf16[12,8,512]{2,1,0:T(8,128)(2,1)}, bf16[12,8,512]{2,1,0:T(8,128)(2,1)}, u32[]{:S(2)}, u32[]{:S(2)}) collective-permute-start(bf16[12,8,512]{2,1,0:T(8,128)(2,1)} %get-tuple-element.303), channel_id=1, source_target_pairs={{8,0},{12,4},{16,8},{20,12},{24,16},{28,20},{9,1},{13,5},{17,9},{2... | collective-permute-start | bytes 294920 | tf_op jit(solution)/shard_map/ppermute | solution.py:10
  14.8 68.2 %collective-permute-start.1 = (bf16[12,8,512]{2,1,0:T(8,128)(2,1)}, bf16[12,8,512]{2,1,0:T(8,128)(2,1)}, u32[]{:S(2)}, u32[]{:S(2)}) collective-permute-start(bf16[12,8,512]{2,1,0:T(8,128)(2,1)} %get-tuple-element.302), channel_id=1, source_target_pairs={{4,0},{8,4},{12,8},{16,12},{20,16},{24,20},{28,24},{5,1},{9,5},{13... | collective-permute-start | bytes 294920 | tf_op jit(solution)/shard_map/ppermute | solution.py:10
  16.1 68.7 %collective-permute-start.2 = (bf16[12,8,512]{2,1,0:T(8,128)(2,1)S(1)}, bf16[12,8,512]{2,1,0:T(8,128)(2,1)}, u32[]{:S(2)}, u32[]{:S(2)}) collective-permute-start(bf16[12,8,512]{2,1,0:T(8,128)(2,1)S(1)} %get-tuple-element.301), channel_id=1, source_target_pairs={{0,4},{4,8},{8,12},{12,16},{16,20},{20,24},{24,28},{1,5},{5,9},{9,... | collective-permute-start | bytes 294920 | tf_op jit(solution)/shard_map/ppermute | solution.py:10
  22.2 63.5 %collective-permute-start.3 = (bf16[12,8,512]{2,1,0:T(8,128)(2,1)S(1)}, bf16[12,8,512]{2,1,0:T(8,128)(2,1)}, u32[]{:S(2)}, u32[]{:S(2)}) collective-permute-start(bf16[12,8,512]{2,1,0:T(8,128)(2,1)S(1)} %get-tuple-element.300), channel_id=1, source_target_pairs={{0,8},{4,12},{8,16},{12,20},{16,24},{20,28},{1,9},{5,13},{9,17},{1... | collective-permute-start | bytes 294920 | tf_op jit(solution)/shard_map/ppermute | solution.py:10
  80.0 18.9 %copy-start.33 = (s32[1024]{0:T(1024)}, s32[1024]{0:T(1024)S(1)}, u32[]{:S(2)}) copy-start(s32[1024]{0:T(1024)S(1)} %get-tuple-element.321) | copy-start | bytes 12292
  80.0 19.7 %copy-start.32 = (s32[1024]{0:T(1024)}, s32[1024]{0:T(1024)S(1)}, u32[]{:S(2)}) copy-start(s32[1024]{0:T(1024)S(1)} %get-tuple-element.320) | copy-start | bytes 12292
  80.1 20.4 %copy-start.35 = (s32[1024]{0:T(1024)}, s32[1024]{0:T(1024)S(1)}, u32[]{:S(2)}) copy-start(s32[1024]{0:T(1024)S(1)} %get-tuple-element.319) | copy-start | bytes 12292
  80.1 21.0 %copy-start.34 = (s32[1024]{0:T(1024)}, s32[1024]{0:T(1024)S(1)}, u32[]{:S(2)}) copy-start(s32[1024]{0:T(1024)S(1)} %get-tuple-element.318) | copy-start | bytes 12292
  80.1 21.5 %copy-start.37 = (s32[1024]{0:T(1024)}, s32[1024]{0:T(1024)S(1)}, u32[]{:S(2)}) copy-start(s32[1024]{0:T(1024)S(1)} %get-tuple-element.317) | copy-start | bytes 12292
  80.1 22.1 %copy-start.36 = (s32[1024]{0:T(1024)}, s32[1024]{0:T(1024)S(1)}, u32[]{:S(2)}) copy-start(s32[1024]{0:T(1024)S(1)} %get-tuple-element.316) | copy-start | bytes 12292
  80.2 23.2 %copy-start.39 = (s32[1024]{0:T(1024)}, s32[1024]{0:T(1024)S(1)}, u32[]{:S(2)}) copy-start(s32[1024]{0:T(1024)S(1)} %get-tuple-element.315) | copy-start | bytes 12292
  80.2 24.4 %copy-start.38 = (s32[1024]{0:T(1024)}, s32[1024]{0:T(1024)S(1)}, u32[]{:S(2)}) copy-start(s32[1024]{0:T(1024)S(1)} %get-tuple-element.314) | copy-start | bytes 12292
  111.5 18.6 %copy-start.40 = (bf16[4]{0:T(256)(128)(2,1)S(1)}, bf16[4]{0:T(256)(128)(2,1)}, u32[]{:S(2)}) copy-start(bf16[4]{0:T(256)(128)(2,1)} %get-tuple-element.147) | copy-start | bytes 28
  111.5 18.6 %copy-start.48 = (pred[4]{0:T(512)(128)(4,1)S(1)}, pred[4]{0:T(512)(128)(4,1)}, u32[]{:S(2)}) copy-start(pred[4]{0:T(512)(128)(4,1)} %get-tuple-element.349) | copy-start | bytes 16
  111.5 18.8 %copy-start.55 = (bf16[4]{0:T(256)(128)(2,1)S(1)}, bf16[4]{0:T(256)(128)(2,1)}, u32[]{:S(2)}) copy-start(bf16[4]{0:T(256)(128)(2,1)} %get-tuple-element.148) | copy-start | bytes 28
  111.5 18.8 %copy-start.61 = (pred[4]{0:T(512)(128)(4,1)S(1)}, pred[4]{0:T(512)(128)(4,1)}, u32[]{:S(2)}) copy-start(pred[4]{0:T(512)(128)(4,1)} %get-tuple-element.348) | copy-start | bytes 16
  111.5 19.6 %copy-start.60 = (bf16[4]{0:T(256)(128)(2,1)S(1)}, bf16[4]{0:T(256)(128)(2,1)}, u32[]{:S(2)}) copy-start(bf16[4]{0:T(256)(128)(2,1)} %get-tuple-element.169) | copy-start | bytes 28
  111.5 19.6 %copy-start.63 = (pred[4]{0:T(512)(128)(4,1)S(1)}, pred[4]{0:T(512)(128)(4,1)}, u32[]{:S(2)}) copy-start(pred[4]{0:T(512)(128)(4,1)} %get-tuple-element.347) | copy-start | bytes 16
  111.5 20.5 %copy-start.59 = (bf16[4]{0:T(256)(128)(2,1)S(1)}, bf16[4]{0:T(256)(128)(2,1)}, u32[]{:S(2)}) copy-start(bf16[4]{0:T(256)(128)(2,1)} %get-tuple-element.170) | copy-start | bytes 28
  111.5 20.5 %copy-start.62 = (pred[4]{0:T(512)(128)(4,1)S(1)}, pred[4]{0:T(512)(128)(4,1)}, u32[]{:S(2)}) copy-start(pred[4]{0:T(512)(128)(4,1)} %get-tuple-element.346) | copy-start | bytes 16
  111.5 21.3 %copy-start.45 = (bf16[4]{0:T(256)(128)(2,1)S(1)}, bf16[4]{0:T(256)(128)(2,1)}, u32[]{:S(2)}) copy-start(bf16[4]{0:T(256)(128)(2,1)} %get-tuple-element.171) | copy-start | bytes 28
  111.6 21.3 %copy-start.53 = (pred[4]{0:T(512)(128)(4,1)S(1)}, pred[4]{0:T(512)(128)(4,1)}, u32[]{:S(2)}) copy-start(pred[4]{0:T(512)(128)(4,1)} %get-tuple-element.345) | copy-start | bytes 16
  111.6 21.5 %copy-start.44 = (bf16[4]{0:T(256)(128)(2,1)S(1)}, bf16[4]{0:T(256)(128)(2,1)}, u32[]{:S(2)}) copy-start(bf16[4]{0:T(256)(128)(2,1)} %get-tuple-element.172) | copy-start | bytes 28
  111.6 21.5 %copy-start.50 = (pred[4]{0:T(512)(128)(4,1)S(1)}, pred[4]{0:T(512)(128)(4,1)}, u32[]{:S(2)}) copy-start(pred[4]{0:T(512)(128)(4,1)} %get-tuple-element.344) | copy-start | bytes 16
  111.6 21.9 %copy-start.43 = (bf16[4]{0:T(256)(128)(2,1)S(1)}, bf16[4]{0:T(256)(128)(2,1)}, u32[]{:S(2)}) copy-start(bf16[4]{0:T(256)(128)(2,1)} %get-tuple-element.173) | copy-start | bytes 28
  111.6 21.9 %copy-start.51 = (pred[4]{0:T(512)(128)(4,1)S(1)}, pred[4]{0:T(512)(128)(4,1)}, u32[]{:S(2)}) copy-start(pred[4]{0:T(512)(128)(4,1)} %get-tuple-element.343) | copy-start | bytes 16
  111.6 22.1 %copy-start.58 = (bf16[4]{0:T(256)(128)(2,1)S(1)}, bf16[4]{0:T(256)(128)(2,1)}, u32[]{:S(2)}) copy-start(bf16[4]{0:T(256)(128)(2,1)} %get-tuple-element.174) | copy-start | bytes 28
  111.6 22.1 %copy-start.64 = (pred[4]{0:T(512)(128)(4,1)S(1)}, pred[4]{0:T(512)(128)(4,1)}, u32[]{:S(2)}) copy-start(pred[4]{0:T(512)(128)(4,1)} %get-tuple-element.342) | copy-start | bytes 16
  111.6 22.9 %copy-start.57 = (bf16[4]{0:T(256)(128)(2,1)S(1)}, bf16[4]{0:T(256)(128)(2,1)}, u32[]{:S(2)}) copy-start(bf16[4]{0:T(256)(128)(2,1)} %get-tuple-element.168) | copy-start | bytes 28
  111.6 22.9 %copy-start.66 = (pred[4]{0:T(512)(128)(4,1)S(1)}, pred[4]{0:T(512)(128)(4,1)}, u32[]{:S(2)}) copy-start(pred[4]{0:T(512)(128)(4,1)} %get-tuple-element.341) | copy-start | bytes 16
  111.6 23.7 %copy-start.54 = (bf16[4]{0:T(256)(128)(2,1)S(1)}, bf16[4]{0:T(256)(128)(2,1)}, u32[]{:S(2)}) copy-start(bf16[4]{0:T(256)(128)(2,1)} %get-tuple-element.130) | copy-start | bytes 28
  111.7 23.7 %copy-start.65 = (pred[4]{0:T(512)(128)(4,1)S(1)}, pred[4]{0:T(512)(128)(4,1)}, u32[]{:S(2)}) copy-start(pred[4]{0:T(512)(128)(4,1)} %get-tuple-element.340) | copy-start | bytes 16
  137.1 35.9 %copy-start.67 = (f32[64]{0:T(128)S(1)}, f32[64]{0:T(128)}, u32[]{:S(2)}) copy-start(f32[64]{0:T(128)} %convert_element_type.451) | copy-start | bytes 772
  223.8 50.6 %copy-start.11 = (bf16[4,6,8,8,64]{4,3,2,1,0:T(8,128)(2,1)S(1)}, bf16[4,6,8,8,64]{4,3,2,1,0:T(8,128)(2,1)}, u32[]{:S(2)}) copy-start(bf16[4,6,8,8,64]{4,3,2,1,0:T(8,128)(2,1)} %slice_dynamic-update-slice_fusion.1) | copy-start | bytes 589828
  225.0 52.0 %copy-start.13 = (bf16[4,8,8,1,64]{4,3,2,1,0:T(2,128)(2,1)S(1)}, bf16[4,8,8,1,64]{4,3,2,1,0:T(2,128)(2,1)}, u32[]{:S(2)}) copy-start(bf16[4,8,8,1,64]{4,3,2,1,0:T(2,128)(2,1)} %get-tuple-element.293) | copy-start | bytes 98308
  225.0 52.1 %copy-start.12 = (bf16[4,8,8,1,64]{4,3,2,1,0:T(2,128)(2,1)S(1)}, bf16[4,8,8,1,64]{4,3,2,1,0:T(2,128)(2,1)}, u32[]{:S(2)}) copy-start(bf16[4,8,8,1,64]{4,3,2,1,0:T(2,128)(2,1)} %get-tuple-element.292) | copy-start | bytes 98308
  278.3 12.3 %collective-permute-start.4 = (bf16[12,8,512]{2,1,0:T(8,128)(2,1)S(1)}, bf16[12,8,512]{2,1,0:T(8,128)(2,1)S(1)}, u32[]{:S(2)}, u32[]{:S(2)}) collective-permute-start(bf16[12,8,512]{2,1,0:T(8,128)(2,1)S(1)} %get-tuple-element.299), channel_id=1, source_target_pairs={{8,0},{12,4},{16,8},{20,12},{24,16},{28,20},{9,1},{13,5},{17,9},{2... | collective-permute-start | bytes 294920 | tf_op jit(solution)/shard_map/ppermute | solution.py:10
  279.6 11.0 %collective-permute-start.5 = (bf16[12,8,512]{2,1,0:T(8,128)(2,1)S(1)}, bf16[12,8,512]{2,1,0:T(8,128)(2,1)S(1)}, u32[]{:S(2)}, u32[]{:S(2)}) collective-permute-start(bf16[12,8,512]{2,1,0:T(8,128)(2,1)S(1)} %get-tuple-element.298), channel_id=1, source_target_pairs={{4,0},{8,4},{12,8},{16,12},{20,16},{24,20},{28,24},{5,1},{9,5},{13... | collective-permute-start | bytes 294920 | tf_op jit(solution)/shard_map/ppermute | solution.py:10
  280.9 9.8 %collective-permute-start.6 = (bf16[12,8,512]{2,1,0:T(8,128)(2,1)S(1)}, bf16[12,8,512]{2,1,0:T(8,128)(2,1)S(1)}, u32[]{:S(2)}, u32[]{:S(2)}) collective-permute-start(bf16[12,8,512]{2,1,0:T(8,128)(2,1)S(1)} %get-tuple-element.297), channel_id=1, source_target_pairs={{0,4},{4,8},{8,12},{12,16},{16,20},{20,24},{24,28},{1,5},{5,9},{9,... | collective-permute-start | bytes 294920 | tf_op jit(solution)/shard_map/ppermute | solution.py:10
  285.5 6.7 %collective-permute-start.7 = (bf16[12,8,512]{2,1,0:T(8,128)(2,1)S(1)}, bf16[12,8,512]{2,1,0:T(8,128)(2,1)S(1)}, u32[]{:S(2)}, u32[]{:S(2)}) collective-permute-start(bf16[12,8,512]{2,1,0:T(8,128)(2,1)S(1)} %get-tuple-element.296), channel_id=1, source_target_pairs={{0,8},{4,12},{8,16},{12,20},{16,24},{20,28},{1,9},{5,13},{9,17},{1... | collective-permute-start | bytes 294920 | tf_op jit(solution)/shard_map/ppermute | solution.py:10
  294.0 23.9 %copy-start.56 = (bf16[4]{0:T(256)(128)(2,1)S(1)}, bf16[4]{0:T(256)(128)(2,1)}, u32[]{:S(2)}) copy-start(bf16[4]{0:T(256)(128)(2,1)} %get-tuple-element.131) | copy-start | bytes 28
  294.0 23.9 %copy-start.70 = (pred[4]{0:T(512)(128)(4,1)S(1)}, pred[4]{0:T(512)(128)(4,1)}, u32[]{:S(2)}) copy-start(pred[4]{0:T(512)(128)(4,1)} %compare_and_fusion.25) | copy-start | bytes 16
  325.6 21.7 %copy-start.1 = (bf16[27,64,64]{2,1,0:T(8,128)(2,1)S(1)}, bf16[27,64,64]{2,1,0:T(8,128)(2,1)}, u32[]{:S(2)}) copy-start(bf16[27,64,64]{2,1,0:T(8,128)(2,1)} %copy.467) | copy-start | bytes 663556
  (61 other events, 383.7 us)
Sparse Core Ops, SparseCore 0:
  268.8 19.8 reduce-scatter.3
where the time goes:
time: 404 us; the launch traced here: 397 us
  local copies, waits for them, and re-layouts  190 us (47%)
  other arithmetic  69.3 us (17%)
  blocking collectives  60.2 us (15%)
  matrix products  32 us (8%)
  starting transfers between devices  25.2 us (6%)
  between operations  18.3 us (5%)
    concatenate x12, local copies, waits for them, and re-layouts, gathered_columns(): jnp.concatenate([window.reshape(-1, window.shape[-1]) for window in windo...  57.6 us
    gather x52, local copies, waits for them, and re-layouts, halo_block(): jnp.take(units, jnp.clip(unit_index, 0, unit_total - 1), axis=0)  48.9 us
    psum x1, blocking collectives, body(): weight_total, bias_total = lax.psum((weight_grad, bias_grad), 'space')  41.2 us
    broadcast_in_dim x52, other arithmetic, rim_region(): return jnp.expand_dims(region, moving + 1)  35.8 us
    slice x12, local copies, waits for them, and re-layouts, windows(): padded[:, first:first + brick_edge, second:second + brick_edge, third:thi...  27.8 us
    ppermute x8, starting transfers between devices, passed_along(): return lax.ppermute(block, axis, route)  25.2 us
    dot_general x8, matrix products, convolve_per_brick(): jnp.dot(gathered_columns(brick_block, brick_edge), stacked_kernel, prefer...  20.7 us
    dynamic_update_slice x52, local copies, waits for them, and re-layouts, halo_block(): padded = lax.dynamic_update_slice(padded, region, starts)  16.5 us
  transfers between devices with their start and end apart: 9, of which 1 were waited for; matrix products, arithmetic and copies ran while one was open for 36% of the time, Pallas kernels for 0%

commit v1 on v0

v1 whole, which is shorter than its diff:
```python
import functools

import jax
import jax.numpy as jnp
from jax import lax
from jax.experimental import pallas as pl
from jax.experimental.pallas import tpu as pltpu
from jax.sharding import PartitionSpec as P

F32 = jnp.float32
BF16 = jnp.bfloat16
LANES = 128
UNIT_ROWS = 32
Z_ROWS = 64
DN_NT = (((1,), (1,)), ((), ()))
DN_NN = (((1,), (0,)), ((), ()))


def vmem():
    return pl.BlockSpec(memory_space=pltpu.VMEM)


def smem():
    return pl.BlockSpec(memory_space=pltpu.SMEM)


def offset_number(ox, oy, oz):
    flat = (ox + 1) * 9 + (oy + 1) * 3 + (oz + 1)
    return flat if flat < 13 else flat - 1


def low_half(shape):
    return lax.broadcasted_iota(jnp.int32, shape, len(shape) - 1) % LANES < 64


def chunk_rows(block):
    return [block[8 * q : 8 * q + 8] for q in range(4)]


def pack_units(values, send, outs):
    slots = values.shape[1] // 64 - 1
    low = low_half((64, LANES))
    for column, out in enumerate(outs):

        def base(link):
            unit = send[column, link]
            slot = jnp.where(unit < 0, slots, (unit * 43) >> 8)
            return pl.multiple_of(slot * 64, 64)

        for half in range(2):
            for face in range(4):
                start = base(half * 6 + face)
                if face < 2:
                    where = pl.ds(start + 56 * face, 8)
                else:
                    where = pl.ds(start + 7 * (face - 2), 8, stride=8)
                packed = jnp.concatenate([values[q, where, :] for q in range(4)], axis=0)
                at = (half * 4 + face) * UNIT_ROWS
                out[at : at + UNIT_ROWS, :] = packed.astype(BF16)
            first = values[0, pl.ds(base(half * 6 + 4), 64), :]
            last = values[3, pl.ds(base(half * 6 + 5), 64), :]
            at = 8 * UNIT_ROWS + half * Z_ROWS
            out[at : at + Z_ROWS, :] = jnp.where(low, first, last).astype(BF16)


def prepare_kernel(
    features, occupancy, counts, send, listing, weight_t, bias,
    masked_out, mask_out, rows_out, shard_out, u0, u1, u2, u3, u4, values,
):
    bricks = features.shape[0]
    live = lax.broadcasted_iota(jnp.int32, (bricks, 512), 0) < counts[0, 0]
    occ = jnp.where(live, occupancy[...], 0).astype(F32)
    row = lax.broadcasted_iota(jnp.int32, (64, 512), 0)
    col = lax.broadcasted_iota(jnp.int32, (64, 512), 1)
    same = (col >> 3) == row
    spread = jnp.concatenate(
        [jnp.where(same, occ[b : b + 1, :], 0.0) for b in range(bricks)], axis=0
    ).astype(BF16)
    z_row = lax.broadcasted_iota(jnp.int32, (512, 512), 0) & 7
    z_col = lax.broadcasted_iota(jnp.int32, (512, 512), 1) >> 6
    expand = jnp.where(z_row == z_col, 1.0, 0.0).astype(BF16)
    mask = jnp.dot(spread, expand, preferred_element_type=F32)
    mask_out[...] = mask.astype(BF16).reshape(mask_out.shape)
    value = features[...].astype(F32).reshape(bricks * 64, 512) * mask
    masked_out[...] = value.astype(BF16).reshape(masked_out.shape)
    for q in range(4):
        values[q, 0 : bricks * 64, :] = value[:, q * LANES : (q + 1) * LANES]
    values[:, bricks * 64 :, :] = jnp.zeros((4, 64, LANES), F32)
    pack_units(values, send, (u0, u1, u2, u3, u4))

    number = listing[...]
    column = (number * 43) >> 9
    link = number - column * 12
    half = (link >= 6).astype(jnp.int32)
    face = link - 6 * half
    base = column * (8 * UNIT_ROWS + 2 * Z_ROWS)
    plain = base + (half * 4 + face) * UNIT_ROWS
    paired = base + 8 * UNIT_ROWS + half * Z_ROWS
    none = 5 * (8 * UNIT_ROWS + 2 * Z_ROWS)
    rows_out[...] = jnp.where(number < 0, none, jnp.where(face < 4, plain, paired))

    shard = weight_t.shape[1]
    width = shard_out.shape[1]
    count = bias.shape[1]
    shard_out[...] = jnp.zeros(shard_out.shape, F32)
    shard_out[:, 0:shard] = weight_t[...].astype(F32)
    shard_out[0:1, shard : shard + count] = bias[...].astype(F32)


def gather_units(table, received):
    at = 0
    for part in received:
        table[at : at + part.shape[0], :] = part[...]
        at += part.shape[0]
    table[at:, :] = jnp.zeros((table.shape[0] - at, LANES), BF16)


def assemble(source, table, rows, windows, sides, walls):
    low8 = low_half((8, LANES))
    sub = lax.broadcasted_iota(jnp.int32, (8, LANES), 0)
    top, bottom = sub == 0, sub == 7

    def put(pair, xp, per_brick):
        for e in range(3):
            stacked = [
                jnp.concatenate([per_brick[0][e][i], per_brick[1][e][i]], axis=0)
                for i in range(5)
            ]
            low16 = low_half((16, LANES))
            before = [stacked[4]] + stacked[:3]
            after = stacked[1:4] + [stacked[4]]
            for q in range(4):
                windows[e, q, pair, xp, :, 0:LANES] = stacked[q].astype(BF16)
                windows[e, q, pair, xp, :, LANES:] = jnp.where(
                    low16, after[q], before[q]
                ).astype(BF16)

    def one_pair(pair, carry):
        def unit(brick, ox, oy, oz):
            return pl.multiple_of(rows[brick, offset_number(ox, oy, oz)], UNIT_ROWS)

        def plane(brick, ox, oy):
            chunks = chunk_rows(table[pl.ds(unit(brick, ox, oy, 0), UNIT_ROWS), :].astype(F32))
            after = table[pl.ds(unit(brick, ox, oy, 1), UNIT_ROWS), :].astype(F32)[0:8]
            before = table[pl.ds(unit(brick, ox, oy, -1), UNIT_ROWS), :].astype(F32)[24:32]
            return chunks + [jnp.where(low8, after, before)]

        for b2 in range(2):
            brick = pair * 2 + b2
            low64 = low_half((64, LANES))
            after = table[pl.ds(unit(brick, 0, 0, 1), Z_ROWS), :].astype(F32)
            before = table[pl.ds(unit(brick, 0, 0, -1), Z_ROWS), :].astype(F32)
            walls[b2] = jnp.where(low64, after, before)
            for side, oy in enumerate((-1, 1)):
                for i, part in enumerate(plane(brick, 0, oy)):
                    sides[b2, side, i] = part

        for ox in (-1, 1):
            per_brick = []
            for b2 in range(2):
                brick = pair * 2 + b2
                centre = plane(brick, ox, 0)
                lower = plane(brick, ox, -1)
                upper = plane(brick, ox, 1)
                per_brick.append(
                    [
                        [
                            pltpu.roll(jnp.where(bottom, l, c), 1, 0)
                            for l, c in zip(lower, centre)
                        ],
                        centre,
                        [
                            pltpu.roll(jnp.where(top, u, c), 7, 0)
                            for u, c in zip(upper, centre)
                        ],
                    ]
                )
            put(pair, 0 if ox < 0 else 9, per_brick)

        def one_x(x, carry):
            per_brick = []
            for b2 in range(2):
                brick = pair * 2 + b2
                block = source[brick, x].astype(F32)
                centre = [block[:, q * LANES : (q + 1) * LANES] for q in range(4)]
                centre.append(walls[b2, pl.ds(pl.multiple_of(x * 8, 8), 8), :])
                lower = [
                    jnp.broadcast_to(sides[b2, 0, i, pl.ds(x, 1), :], (8, LANES))
                    for i in range(5)
                ]
                upper = [
                    jnp.broadcast_to(sides[b2, 1, i, pl.ds(x, 1), :], (8, LANES))
                    for i in range(5)
                ]
                per_brick.append(
                    [
                        [jnp.where(top, l, pltpu.roll(c, 1, 0)) for l, c in zip(lower, centre)],
                        centre,
                        [
                            jnp.where(bottom, u, pltpu.roll(c, 7, 0))
                            for u, c in zip(upper, centre)
                        ],
                    ]
                )
            put(pair, x + 1, per_brick)
            return carry

        return lax.fori_loop(0, 8, one_x, carry)

    lax.fori_loop(0, windows.shape[2], one_pair, 0)


def spread_weights(gathered, flat, shifted, shard):
    for k in range(gathered.shape[0]):
        flat[:, k * shard : (k + 1) * shard] = gathered[k][:, 0:shard].astype(F32)
    total = gathered.shape[0] * shard
    flat[:, total:] = jnp.zeros((64, flat.shape[1] - total), F32)
    shifted[:, :] = pltpu.roll(flat[...], flat.shape[1] - 64, 1)


def taps_pair(flat, shifted, first):
    if first % 2 == 0:
        return flat[:, first * 64 : first * 64 + LANES]
    return shifted[:, (first - 1) * 64 : (first - 1) * 64 + LANES]


def forward_kernel(
    masked, mask, cotangent, gathered, rows, send, r0, r1, r2, r3, r4,
    block_out, grad_out, u0, u1, u2, u3, u4, *rest, shard,
):
    chunk_outs = rest[:-9]
    table, windows, sides, walls, flat, shifted, toeplitz, values, flipped = rest[-9:]
    groups = gathered.shape[0]
    bricks = masked.shape[0]
    pairs = bricks // 2
    gather_units(table, (r0, r1, r2, r3, r4))
    assemble(masked, table, rows, windows, sides, walls)
    spread_weights(gathered, flat, shifted, shard)
    low = low_half((64, LANES))
    for ae in range(9):
        one = taps_pair(flat, shifted, 3 * ae)
        two = jnp.where(low, taps_pair(flat, shifted, 3 * ae + 2), 0.0)
        late = jnp.concatenate([one, two], axis=1)
        toeplitz[ae, 64:128, :] = late.astype(BF16)
        toeplitz[ae, 0:64, :] = pltpu.roll(late, 192, 1).astype(BF16)

    lane = lax.broadcasted_iota(jnp.int32, (1, LANES), 1)
    bias_lane = shard % LANES
    bias_tile = shard - bias_lane
    count = 64 // groups
    bias_row = jnp.zeros((1, LANES), F32)
    for k in range(groups):
        tile = gathered[k][0:16, bias_tile : bias_tile + LANES].astype(F32)[0:8]
        moved = pltpu.roll(tile, (count * k - bias_lane) % LANES, 1)[0:1]
        bias_row += jnp.where((lane >= count * k) & (lane < count * (k + 1)), moved, 0.0)
    bias_row += pltpu.roll(jnp.broadcast_to(bias_row, (8, LANES)), 64, 1)[0:1]

    values[:, bricks * 64 :, :] = jnp.zeros((4, 64, LANES), F32)

    def one_chunk(q, bias_sum):
        total = jnp.zeros((pairs * LANES, LANES), F32)
        for a in range(3):
            for e in range(3):
                window = windows[e, q, :, a : a + 8].reshape(pairs * LANES, 256)
                total += lax.dot_general(
                    window, toeplitz[3 * a + e], DN_NT, preferred_element_type=F32
                )
        pre = (total + bias_row).reshape(pairs, 8, 2, 8, LANES)
        lanes = pl.ds(pl.multiple_of(q * LANES, LANES), LANES)
        for brick in range(bricks):
            p = pre[brick // 2, :, brick % 2]
            active = mask[brick, :, :, lanes].astype(F32)
            sig = jax.nn.sigmoid(p)
            block_out[brick, :, :, lanes] = (p * sig * active).astype(BF16)
            grad = (
                cotangent[brick, :, :, lanes].astype(F32)
                * sig
                * (1.0 + p * (1.0 - sig))
                * active
            ).astype(BF16)
            grad_out[brick, :, :, lanes] = grad
            wide = grad.astype(F32).reshape(64, LANES)
            values[q, brick * 64 : (brick + 1) * 64, :] = wide
            bias_sum += jnp.sum(wide.reshape(8, 8, LANES), axis=0)
        return bias_sum

    bias_sum = lax.fori_loop(0, 4, one_chunk, jnp.zeros((8, LANES), F32))
    pack_units(values, send, (u0, u1, u2, u3, u4))

    for q in range(4):
        for pair in range(pairs):
            by_x = []
            for x in range(8):
                for b2 in range(2):
                    at = (pair * 2 + b2) * 64 + x * 8
                    by_x.append(values[q, at : at + 8, :])
            flipped[q, :, pair * LANES : (pair + 1) * LANES] = jnp.transpose(
                jnp.concatenate(by_x, axis=0)
            ).astype(BF16)
    for ae in range(9):
        a, e = ae // 3, ae % 3
        total = jnp.zeros((LANES, 256), F32)
        for q in range(4):
            window = windows[e, q, :, a : a + 8].reshape(pairs * LANES, 256)
            total += jnp.dot(flipped[q], window, preferred_element_type=F32)
        flat[:, 192 * ae : 192 * ae + 256] = total[64:128] + pltpu.roll(total[0:64], 64, 1)

    width = chunk_outs[0].shape[1]
    bias_all = jnp.sum(bias_sum, axis=0, keepdims=True)
    bias_all = jnp.broadcast_to(bias_all, (8, LANES))
    bias_all = bias_all + pltpu.roll(bias_all, 64, 1)
    bias_all = pltpu.roll(bias_all, bias_lane, 1)
    row8 = lax.broadcasted_iota(jnp.int32, (8, LANES), 0)
    lane8 = lax.broadcasted_iota(jnp.int32, (8, LANES), 1)
    keep = (row8 == 0) & (lane8 >= bias_lane) & (lane8 < bias_lane + 64)
    me = lax.axis_index("dp")
    for k in range(groups):
        part = flat[:, k * shard : (k + 1) * shard]
        shifted[:, 0:shard] = part
        shifted[:, shard:width] = jnp.zeros((64, width - shard), F32)
        tile = shifted[0:8, bias_tile : bias_tile + LANES]
        shifted[0:8, bias_tile : bias_tile + LANES] = jnp.where(keep, bias_all, tile)
        block = shifted[:, 0:width].astype(BF16)
        for m in range(groups):

            @pl.when(me ^ m == k)
            def _(m=m, block=block):
                chunk_outs[m][...] = block


def backward_kernel(
    grad, mask, gathered, rows, r0, r1, r2, r3, r4, out,
    table, windows, sides, walls, flat, shifted, toeplitz, *, shard,
):
    bricks = grad.shape[0]
    pairs = bricks // 2
    gather_units(table, (r0, r1, r2, r3, r4))
    assemble(grad, table, rows, windows, sides, walls)
    spread_weights(gathered, flat, shifted, shard)
    low = low_half((64, LANES))
    for ae in range(9):
        m = 3 * (8 - ae)
        first = taps_pair(flat, shifted, m)
        second = taps_pair(flat, shifted, m + 1)
        third = taps_pair(flat, shifted, m + 2)
        toeplitz[ae, 0:64, :] = second.astype(BF16)
        toeplitz[ae, 64:128, :] = first.astype(BF16)
        toeplitz[ae, 128:192, :] = jnp.where(low, 0.0, pltpu.roll(first, 64, 1)).astype(BF16)
        toeplitz[ae, 192:256, :] = jnp.where(low, third, 0.0).astype(BF16)

    def one_chunk(q, carry):
        total = jnp.zeros((pairs * LANES, LANES), F32)
        for a in range(3):
            for e in range(3):
                window = windows[e, q, :, a : a + 8].reshape(pairs * LANES, 256)
                total += jnp.dot(window, toeplitz[3 * a + e], preferred_element_type=F32)
        total = total.reshape(pairs, 8, 2, 8, LANES)
        lanes = pl.ds(pl.multiple_of(q * LANES, LANES), LANES)
        for brick in range(bricks):
            active = mask[brick, :, :, lanes].astype(F32)
            out[brick, :, :, lanes] = (total[brick // 2, :, brick % 2] * active).astype(BF16)
        return carry

    lax.fori_loop(0, 4, one_chunk, 0)


def finish_kernel(mine, other, weight_out, bias_out):
    shard = weight_out.shape[1]
    count = bias_out.shape[1]
    total = mine[...].astype(F32) + other[...].astype(F32)
    weight_out[...] = total[:, 0:shard]
    bias_lane = shard % LANES
    bias_tile = shard - bias_lane
    tile = total[0:8, bias_tile : bias_tile + LANES]
    me = lax.axis_index("dp")
    moved = pltpu.roll(tile, 2 * LANES - bias_lane - me * count, 1)
    bias_out[...] = moved[0:1, 0:count]


def passed_along(block, axis, distance):
    devices = range(lax.axis_size(axis))
    route = [(i - distance, i) for i in devices if i - distance in devices]
    return lax.ppermute(block, axis, route)


def swapped(block, axis, bit):
    return lax.ppermute(block, axis, [(i, i ^ bit) for i in range(lax.axis_size(axis))])


def exchanged(units):
    reach = len(units) // 2
    return [
        unit if column == reach else passed_along(unit, "space", column - reach)
        for column, unit in enumerate(units)
    ]


def body(features, occupancy, counts, send_units, neighbours, weight, conv_bias, cotangent):
    grid_shape = features.shape[1:]
    bricks = grid_shape[0]
    pairs = bricks // 2
    spread = send_units.shape[2]
    shard = weight.shape[0]
    channels = weight.shape[1]
    groups = lax.axis_size("dp")
    count = conv_bias.shape[0]
    width = -(-(shard + channels) // LANES) * LANES
    unit_rows = 8 * UNIT_ROWS + 2 * Z_ROWS
    units_type = jax.ShapeDtypeStruct((unit_rows, LANES), BF16)
    grid_type = jax.ShapeDtypeStruct(grid_shape, BF16)
    send = send_units[0, 0]
    params = pltpu.CompilerParams(vmem_limit_bytes=48 * 1024 * 1024)

    masked, mask, rows, own_shard, *units = pl.pallas_call(
        prepare_kernel,
        name="prepare",
        out_shape=[
            grid_type,
            grid_type,
            jax.ShapeDtypeStruct(neighbours.shape[1:], jnp.int32),
            jax.ShapeDtypeStruct((channels, width), F32),
        ]
        + [units_type] * spread,
        in_specs=[vmem(), vmem(), smem(), smem(), vmem(), vmem(), vmem()],
        out_specs=[vmem()] * (4 + spread),
        scratch_shapes=[pltpu.VMEM((4, (bricks + 1) * 64, LANES), F32)],
        compiler_params=params,
    )(
        features[0],
        occupancy[0],
        counts,
        send,
        neighbours[0],
        weight.T,
        conv_bias.reshape(1, count),
    )

    received = exchanged(units)
    gathered = lax.all_gather(own_shard.astype(BF16), "dp", axis=0)

    table = pltpu.VMEM((spread * unit_rows + Z_ROWS, LANES), BF16)
    windows = pltpu.VMEM((3, 4, pairs, 10, 16, 256), BF16)
    sides = pltpu.VMEM((2, 2, 5, 8, LANES), F32)
    walls = pltpu.VMEM((2, 64, LANES), F32)
    flat = pltpu.VMEM((channels, 28 * 64), F32)
    block_output, grad, *rest = pl.pallas_call(
        functools.partial(forward_kernel, shard=shard),
        name="forward",
        out_shape=[grid_type, grid_type]
        + [units_type] * spread
        + [jax.ShapeDtypeStruct((channels, width), BF16)] * groups,
        in_specs=[vmem()] * 4 + [smem(), smem()] + [vmem()] * spread,
        out_specs=[vmem()] * (2 + spread + groups),
        scratch_shapes=[
            table,
            windows,
            sides,
            walls,
            flat,
            flat,
            pltpu.VMEM((9, LANES, 256), BF16),
            pltpu.VMEM((4, (bricks + 1) * 64, LANES), F32),
            pltpu.VMEM((4, LANES, pairs * LANES), BF16),
        ],
        compiler_params=params,
    )(masked, mask, cotangent[0], gathered, rows, send, *received)
    grad_units, blocks = rest[:spread], rest[spread:]

    grad_received = exchanged(grad_units)
    shares = [blocks[0]] + [swapped(blocks[m], "dp", m) for m in range(1, groups)]

    grad_input = pl.pallas_call(
        functools.partial(backward_kernel, shard=shard),
        name="backward",
        out_shape=grid_type,
        in_specs=[vmem()] * 3 + [smem()] + [vmem()] * spread,
        out_specs=vmem(),
        scratch_shapes=[
            table,
            windows,
            sides,
            walls,
            flat,
            flat,
            pltpu.VMEM((9, 256, LANES), BF16),
        ],
        compiler_params=params,
    )(grad, mask, gathered, rows, *grad_received)

    total = sum(share.astype(F32) for share in shares).astype(BF16)
    devices = lax.axis_size("space")
    bit = 1
    while 2 * bit < devices:
        total = (total.astype(F32) + swapped(total, "space", bit).astype(F32)).astype(BF16)
        bit *= 2
    weight_share, bias_share = pl.pallas_call(
        finish_kernel,
        name="finish",
        out_shape=[
            jax.ShapeDtypeStruct((channels, shard), F32),
            jax.ShapeDtypeStruct((1, count), F32),
        ],
        in_specs=[vmem()] * 2,
        out_specs=[vmem()] * 2,
        compiler_params=params,
    )(total, swapped(total, "space", bit))
    return (
        block_output[None],
        grad_input[None],
        weight_share.T,
        bias_share.reshape(count),
    )


def solution(mesh):
    placed = (
        P("dp", "space", None, None, None),
        P("dp", "space", None),
        P("dp", "space"),
        P("dp", "space", None, None),
        P("dp", "space", None),
        P("dp", None),
        P("dp"),
        P("dp", "space", None, None, None),
    )
    return jax.shard_map(
        body,
        mesh=mesh,
        in_specs=placed,
        out_specs=(
            P("dp", "space", None, None, None),
            P("dp", "space", None, None, None),
            P("dp", None),
            P("dp"),
        ),
        check_vma=False,
    )
```

time: 404 us -> 62.8 us (0.16); the launches traced: 397 us -> 61.6 us
  local copies, waits for them, and re-layouts: 190 us -> 3.17 us
  other arithmetic: 69.3 us -> 0.09 us
  blocking collectives: 60.2 us -> 6.32 us
  matrix products: 32 us -> 0 us
  between operations: 18.3 us -> 1.43 us
  Pallas kernels: 0 us -> 11.4 us
  starting transfers between devices: 25.2 us -> 31.6 us
  waiting for transfers between devices: 1.55 us -> 7.6 us
    concatenate x12 -> x0, local copies, waits for them, and re-layouts: 57.6 us -> none  [gathered_columns(): jnp.concatenate([window.reshape(-1, window.shape[-1]) for window in windo...]
    gather x54 -> x0, local copies, waits for them, and re-layouts: 50.2 us -> none  [the longest x52 48.9 us: halo_block(): jnp.take(units, jnp.clip(unit_index, 0, unit_total - 1), axis=0)]
    psum x1 -> x0, blocking collectives: 41.2 us -> none  [body(): weight_total, bias_total = lax.psum((weight_grad, bias_grad), 'space')]
    broadcast_in_dim x52 -> x0, other arithmetic: 35.8 us -> none  [rim_region(): return jnp.expand_dims(region, moving + 1)]
    dot_general x12 -> x0, matrix products: 32 us -> none  [the longest x8 20.7 us: convolve_per_brick(): jnp.dot(gathered_columns(brick_block, brick_edge), stacked_kernel, prefer...]
    slice x16 -> x0, local copies, waits for them, and re-layouts: 29.6 us -> none  [the longest x12 27.8 us: windows(): padded[:, first:first + brick_edge, second:second + brick_edge, third:thi...]
    dynamic_update_slice x52 -> x0, local copies, waits for them, and re-layouts: 16.5 us -> none  [halo_block(): padded = lax.dynamic_update_slice(padded, region, starts)]
    select_n x27 -> x0, other arithmetic: 14.4 us -> none  [the longest x26 14.4 us: halo_block(): jnp.take(units, jnp.clip(unit_index, 0, unit_total - 1), axis=0)]
  transfers between devices with their start and end apart: 9 -> 14, of which waited for: 1 -> 4; matrix products, arithmetic and copies ran while one was open for 36% -> 0% of each run, Pallas kernels for 0% -> 6%
where the time goes in v1:
time: 62.8 us; the launch traced here: 61.6 us
  starting transfers between devices  31.6 us (50%)
  Pallas kernels  11.4 us (18%)
  waiting for transfers between devices  7.6 us (12%)
  blocking collectives  6.32 us (10%)
  local copies, waits for them, and re-layouts  3.17 us (5%)
  between operations  1.43 us (2%)
    ppermute x8, starting transfers between devices, passed_along(): return lax.ppermute(block, axis, route)  24.4 us
    ppermute x6, starting transfers between devices, swapped(): lax.ppermute(block, axis, [(i, i ^ bit) for i in range(lax.axis_size(axis...  7.24 us
    ppermute x6, waiting for transfers between devices, swapped(): lax.ppermute(block, axis, [(i, i ^ bit) for i in range(lax.axis_size(axis...  6.73 us
    all_gather x1, blocking collectives, body(): gathered = lax.all_gather(own_shard.astype(BF16), 'dp', axis=0)  6.32 us
    pallas_call x1, Pallas kernels, body(): pl.pallas_call(functools.partial(forward_kernel, shard=shard), name='forw...  5.73 us
    pallas_call x1, Pallas kernels, body(): pl.pallas_call(functools.partial(backward_kernel, shard=shard), name='bac...  3.96 us
    unnamed x13, local copies, waits for them, and re-layouts  3.17 us
  transfers between devices with their start and end apart: 14, of which 4 were waited for; matrix products, arithmetic and copies ran while one was open for 0% of the time, Pallas kernels for 6%

profile of v1, /device:TPU:0, one launch (start us, length us, event | category | flops | bytes accessed | tf_op | source)
XLA Modules:
  0.0 61.6 jit_solution(2869395675875649893)
XLA Ops:
  1.3 0.0 copy-start.3
  1.3 0.7 %copy.14 = s32[1,1,5,12]{3,2,1,0:T(8,128)S(1)} copy(s32[1,1,5,12]{3,1,2,0:T(1,128)} %param.11) | data formatting | bytes 480
  2.0 0.0 copy-start.4
  2.0 0.0 copy-start.5
  2.0 0.0 copy-done.3
  2.0 0.7 %copy-done.4 = s32[1,4,26]{2,1,0:T(4,128)S(1)} copy-done((s32[1,4,26]{2,1,0:T(4,128)S(1)}, s32[1,4,26]{2,1,0:T(4,128)}, u32[]{:S(2)}) %copy-start.4) | copy-done | bytes 440
  2.7 0.0 copy-done.5
  2.7 0.0 copy-start
  2.7 0.9 %copy-done = bf16[1,4,8,8,512]{4,3,2,1,0:T(8,128)(2,1)S(1)} copy-done((bf16[1,4,8,8,512]{4,3,2,1,0:T(8,128)(2,1)S(1)}, bf16[1,4,8,8,512]{4,3,2,1,0:T(8,128)(2,1)}, u32[]{:S(2)}) %copy-start) | copy-done | bytes 262168
  3.6 0.0 copy-start.2
  3.6 0.8 %copy-done.2 = bf16[432,64]{0,1:T(8,128)(2,1)S(1)} copy-done((bf16[432,64]{0,1:T(8,128)(2,1)S(1)}, bf16[432,64]{0,1:T(8,128)(2,1)}, u32[]{:S(2)}) %copy-start.2) | copy-done | bytes 55320
  4.5 1.0 %prepare.1 = (bf16[4,8,8,512]{3,2,1,0:T(8,128)(2,1)S(1)}, bf16[4,8,8,512]{3,2,1,0:T(8,128)(2,1)S(1)}, s32[4,26]{1,0:T(4,128)S(1)}, f32[64,512]{1,0:T(8,128)S(1)}...) custom-call(bf16[4,8,8,512]{3,2,1,0:T(8,128)(2,1)S(1)} %bitcast.16, ...), custom_call_target="tpu_custom_call" | custom-call | tf_op jit(solution)/shard_map/prepare/pallas_call | solution.py:414
  5.5 1.3 %collective-permute-start = (bf16[384,128]{1,0:T(8,128)(2,1)S(1)}, bf16[384,128]{1,0:T(8,128)(2,1)S(1)}, u32[]{:S(2)}, u32[]{:S(2)}) collective-permute-start(bf16[384,128]{1,0:T(8,128)(2,1)S(1)} %get-tuple-element.30), channel_id=1, source_target_pairs={{8,0},{12,4},{16,8},{20,12},{24,16},{28,20},{9,1},{13,5},{17,9},{2... | collective-permute-start | bytes 294920 | tf_op jit(solution)/shard_map/ppermute | solution.py:383
  6.8 1.3 %collective-permute-start.1 = (bf16[384,128]{1,0:T(8,128)(2,1)S(1)}, bf16[384,128]{1,0:T(8,128)(2,1)S(1)}, u32[]{:S(2)}, u32[]{:S(2)}) collective-permute-start(bf16[384,128]{1,0:T(8,128)(2,1)S(1)} %get-tuple-element.31), channel_id=1, source_target_pairs={{4,0},{8,4},{12,8},{16,12},{20,16},{24,20},{28,24},{5,1},{9,5},{13... | collective-permute-start | bytes 294920 | tf_op jit(solution)/shard_map/ppermute | solution.py:383
  8.1 5.5 %collective-permute-start.2 = (bf16[384,128]{1,0:T(8,128)(2,1)S(1)}, bf16[384,128]{1,0:T(8,128)(2,1)S(1)}, u32[]{:S(2)}, u32[]{:S(2)}) collective-permute-start(bf16[384,128]{1,0:T(8,128)(2,1)S(1)} %get-tuple-element.33), channel_id=1, source_target_pairs={{0,4},{4,8},{8,12},{12,16},{16,20},{20,24},{24,28},{1,5},{5,9},{9,... | collective-permute-start | bytes 294920 | tf_op jit(solution)/shard_map/ppermute | solution.py:383
  13.6 4.6 %collective-permute-start.3 = (bf16[384,128]{1,0:T(8,128)(2,1)S(1)}, bf16[384,128]{1,0:T(8,128)(2,1)S(1)}, u32[]{:S(2)}, u32[]{:S(2)}) collective-permute-start(bf16[384,128]{1,0:T(8,128)(2,1)S(1)} %get-tuple-element.34), channel_id=1, source_target_pairs={{0,8},{4,12},{8,16},{12,20},{16,24},{20,28},{1,9},{5,13},{9,17},{1... | collective-permute-start | bytes 294920 | tf_op jit(solution)/shard_map/ppermute | solution.py:383
  18.2 0.0 copy-start.1
  18.2 6.3 %all-gather = bf16[256,512]{1,0:T(8,128)(2,1)S(1)} all-gather(bf16[64,512]{1,0:T(8,128)(2,1)S(1)} %convert_element_type.36), channel_id=2, replica_groups=mesh['space'=8,'dp'=4] {'dp'}, dimensions={0}, use_global_device_ids=true | all-gather | bytes 327680 | tf_op jit(solution)/shard_map/all_gather | solution.py:439
  24.6 0.0 collective-permute-done.r0
  24.6 0.0 collective-permute-done.1.r1
  24.6 0.0 collective-permute-done.2.r3
  24.6 0.0 collective-permute-done.3.r4
  24.6 0.0 copy-done.1
  24.6 5.7 %forward.1 = (bf16[4,8,8,512]{3,2,1,0:T(8,128)(2,1)}, bf16[4,8,8,512]{3,2,1,0:T(8,128)(2,1)S(1)}, bf16[384,128]{1,0:T(8,128)(2,1)S(1)}, bf16[384,128]{1,0:T(8,12...) custom-call(bf16[4,8,8,512]{3,2,1,0:T(8,128)(2,1)S(1)} %get-tuple-el, ...), custom_call_target="tpu_custom_call" | custom-call | tf_op jit(solution)/shard_map/forward/pallas_call | solution.py:446
  30.3 0.3 collective-permute-start.8
  30.7 1.6 %collective-permute-start.9 = (bf16[64,512]{1,0:T(8,128)(2,1)S(1)}, bf16[64,512]{1,0:T(8,128)(2,1)S(1)}, u32[]{:S(2)}, u32[]{:S(2)}) collective-permute-start(bf16[64,512]{1,0:T(8,128)(2,1)S(1)} %get-tuple-element.44), channel_id=1, source_target_pairs={{0,2},{1,3},{2,0},{3,1},{4,6},{5,7},{6,4},{7,5},{8,10},{9,11},{10,... | collective-permute-start | bytes 196616 | tf_op jit(solution)/shard_map/ppermute | solution.py:387
  32.2 0.0 collective-permute-start.10
  32.2 0.0 collective-permute-done.8
  32.2 2.7 %collective-permute-done.9 = bf16[64,512]{1,0:T(8,128)(2,1)S(1)} collective-permute-done((bf16[64,512]{1,0:T(8,128)(2,1)S(1)}, bf16[64,512]{1,0:T(8,128)(2,1)S(1)}, u32[]{:S(2)}, u32[]{:S(2)}) %collective-permute-start.9) | collective-permute-done | bytes 65568 | tf_op jit(solution)/shard_map/ppermute | solution.py:387
  34.9 1.7 %collective-permute-done.10 = bf16[64,512]{1,0:T(8,128)(2,1)S(1)} collective-permute-done((bf16[64,512]{1,0:T(8,128)(2,1)S(1)}, bf16[64,512]{1,0:T(8,128)(2,1)S(1)}, u32[]{:S(2)}, u32[]{:S(2)}) %collective-permute-start.10) | collective-permute-done | bytes 65568 | tf_op jit(solution)/shard_map/ppermute | solution.py:387
  36.6 2.4 %collective-permute-start.11 = (bf16[64,512]{1,0:T(8,128)(2,1)S(1)}, bf16[64,512]{1,0:T(8,128)(2,1)S(1)}, u32[]{:S(2)}, u32[]{:S(2)}) collective-permute-start(bf16[64,512]{1,0:T(8,128)(2,1)S(1)} %add_convert_fusion.2), channel_id=1, source_target_pairs={{0,4},{4,0},{8,12},{12,8},{16,20},{20,16},{24,28},{28,24},{1,5},{5... | collective-permute-start | bytes 196616 | tf_op jit(solution)/shard_map/ppermute | solution.py:387
  39.0 2.4 %collective-permute-done.11 = bf16[64,512]{1,0:T(8,128)(2,1)S(1)} collective-permute-done((bf16[64,512]{1,0:T(8,128)(2,1)S(1)}, bf16[64,512]{1,0:T(8,128)(2,1)S(1)}, u32[]{:S(2)}, u32[]{:S(2)}) %collective-permute-start.11) | collective-permute-done | bytes 65568 | tf_op jit(solution)/shard_map/ppermute | solution.py:387
  41.4 1.6 %collective-permute-start.12 = (bf16[64,512]{1,0:T(8,128)(2,1)S(1)}, bf16[64,512]{1,0:T(8,128)(2,1)S(1)}, u32[]{:S(2)}, u32[]{:S(2)}) collective-permute-start(bf16[64,512]{1,0:T(8,128)(2,1)S(1)} %add_convert_fusion.1), channel_id=1, source_target_pairs={{0,8},{4,12},{8,0},{12,4},{16,24},{20,28},{24,16},{28,20},{1,9},{5... | collective-permute-start | bytes 196616 | tf_op jit(solution)/shard_map/ppermute | solution.py:387
  43.1 1.3 %collective-permute-start.4 = (bf16[384,128]{1,0:T(8,128)(2,1)S(1)}, bf16[384,128]{1,0:T(8,128)(2,1)S(1)}, u32[]{:S(2)}, u32[]{:S(2)}) collective-permute-start(bf16[384,128]{1,0:T(8,128)(2,1)S(1)} %get-tuple-element.37), channel_id=1, source_target_pairs={{8,0},{12,4},{16,8},{20,12},{24,16},{28,20},{9,1},{13,5},{17,9},{2... | collective-permute-start | bytes 294920 | tf_op jit(solution)/shard_map/ppermute | solution.py:383
  44.4 1.3 %collective-permute-start.5 = (bf16[384,128]{1,0:T(8,128)(2,1)S(1)}, bf16[384,128]{1,0:T(8,128)(2,1)S(1)}, u32[]{:S(2)}, u32[]{:S(2)}) collective-permute-start(bf16[384,128]{1,0:T(8,128)(2,1)S(1)} %get-tuple-element.38), channel_id=1, source_target_pairs={{4,0},{8,4},{12,8},{16,12},{20,16},{24,20},{28,24},{5,1},{9,5},{13... | collective-permute-start | bytes 294920 | tf_op jit(solution)/shard_map/ppermute | solution.py:383
  45.7 4.6 %collective-permute-start.6 = (bf16[384,128]{1,0:T(8,128)(2,1)S(1)}, bf16[384,128]{1,0:T(8,128)(2,1)S(1)}, u32[]{:S(2)}, u32[]{:S(2)}) collective-permute-start(bf16[384,128]{1,0:T(8,128)(2,1)S(1)} %get-tuple-element.40), channel_id=1, source_target_pairs={{0,4},{4,8},{8,12},{12,16},{16,20},{20,24},{24,28},{1,5},{5,9},{9,... | collective-permute-start | bytes 294920 | tf_op jit(solution)/shard_map/ppermute | solution.py:383
  50.2 4.6 %collective-permute-start.7 = (bf16[384,128]{1,0:T(8,128)(2,1)S(1)}, bf16[384,128]{1,0:T(8,128)(2,1)S(1)}, u32[]{:S(2)}, u32[]{:S(2)}) collective-permute-start(bf16[384,128]{1,0:T(8,128)(2,1)S(1)} %get-tuple-element.41), channel_id=1, source_target_pairs={{0,8},{4,12},{8,16},{12,20},{16,24},{20,28},{1,9},{5,13},{9,17},{1... | collective-permute-start | bytes 294920 | tf_op jit(solution)/shard_map/ppermute | solution.py:383
  54.8 0.0 collective-permute-done.12
  54.8 1.3 %collective-permute-start.13 = (bf16[64,512]{1,0:T(8,128)(2,1)S(1)}, bf16[64,512]{1,0:T(8,128)(2,1)S(1)}, u32[]{:S(2)}, u32[]{:S(2)}) collective-permute-start(bf16[64,512]{1,0:T(8,128)(2,1)S(1)} %add_convert_fusion.mine), channel_id=1, source_target_pairs={{0,16},{4,20},{8,24},{12,28},{16,0},{20,4},{24,8},{28,12},{1,17},{... | collective-permute-start | bytes 196616 | tf_op jit(solution)/shard_map/ppermute | solution.py:387
  56.1 0.0 collective-permute-done.4.r0
  56.1 0.0 collective-permute-done.5.r1
  56.1 0.0 collective-permute-done.6.r3
  56.1 0.9 %collective-permute-done.7.r4 = bf16[384,128]{1,0:T(8,128)(2,1)S(1)} collective-permute-done((bf16[384,128]{1,0:T(8,128)(2,1)S(1)}, bf16[384,128]{1,0:T(8,128)(2,1)S(1)}, u32[]{:S(2)}, u32[]{:S(2)}) %collective-permute-start.7) | collective-permute-done | bytes 98336 | tf_op jit(solution)/shard_map/ppermute | solution.py:383
  57.0 4.0 %backward.1 = bf16[4,8,8,512]{3,2,1,0:T(8,128)(2,1)} custom-call(bf16[4,8,8,512]{3,2,1,0:T(8,128)(2,1)S(1)} %get-tuple-element.36.grad, bf16[4,8,8,512]{3,2,1,0:T(8,128)(2,1)S(1)} %get-tuple-element.27.mask, bf16[4,64,512]{2,1,0:T(8,128)(2,1)S(1)} %bitcast.15, s32[4,26]{1,0:T(4,128)S(1)} %get-tuple-element.29.rows, ...), custom_call_target="tpu_custom_call" | custom-call | tf_op jit(solution)/shard_map/backward/pallas_call | solution.py:472
  60.9 0.0 collective-permute-done.13.other
  60.9 0.7 %finish.1 = (f32[64,432]{1,0:T(8,128)}, f32[1,16]{1,0:T(1,128)}) custom-call(bf16[64,512]{1,0:T(8,128)(2,1)S(1)} %add_convert_fusion.mine, bf16[64,512]{1,0:T(8,128)(2,1)S(1)} %collective-permute-done.13.other), custom_call_target="tpu_custom_call" | custom-call | tf_op jit(solution)/shard_map/finish/pallas_call | solution.py:496
  (4 shorter events, 0.1 us)
Async XLA Ops:
  1.3 0.7 %copy-start.3 = (s32[1,4,512]{2,1,0:T(4,128)S(1)}, s32[1,4,512]{2,1,0:T(4,128)}, u32[]{:S(2)}) copy-start(s32[1,4,512]{2,1,0:T(4,128)} %param.9) | copy-start | bytes 24580
  2.0 0.7 %copy-start.4 = (s32[1,4,26]{2,1,0:T(4,128)S(1)}, s32[1,4,26]{2,1,0:T(4,128)}, u32[]{:S(2)}) copy-start(s32[1,4,26]{2,1,0:T(4,128)} %param.12) | copy-start | bytes 1252
  2.0 0.7 %copy-start.5 = (bf16[16]{0:T(256)(128)(2,1)S(1)}, bf16[16]{0:T(256)(128)(2,1)}, u32[]{:S(2)}) copy-start(bf16[16]{0:T(256)(128)(2,1)} %param.14) | copy-start | bytes 100
  2.7 1.0 %copy-start = (bf16[1,4,8,8,512]{4,3,2,1,0:T(8,128)(2,1)S(1)}, bf16[1,4,8,8,512]{4,3,2,1,0:T(8,128)(2,1)}, u32[]{:S(2)}) copy-start(bf16[1,4,8,8,512]{4,3,2,1,0:T(8,128)(2,1)} %param.8) | copy-start | bytes 786436
  3.6 0.8 %copy-start.2 = (bf16[432,64]{0,1:T(8,128)(2,1)S(1)}, bf16[432,64]{0,1:T(8,128)(2,1)}, u32[]{:S(2)}) copy-start(bf16[432,64]{0,1:T(8,128)(2,1)} %param.13) | copy-start | bytes 165892
  5.5 19.1 %collective-permute-start = (bf16[384,128]{1,0:T(8,128)(2,1)S(1)}, bf16[384,128]{1,0:T(8,128)(2,1)S(1)}, u32[]{:S(2)}, u32[]{:S(2)}) collective-permute-start(bf16[384,128]{1,0:T(8,128)(2,1)S(1)} %get-tuple-element.30), channel_id=1, source_target_pairs={{8,0},{12,4},{16,8},{20,12},{24,16},{28,20},{9,1},{13,5},{17,9},{2... | collective-permute-start | bytes 294920 | tf_op jit(solution)/shard_map/ppermute | solution.py:383
  6.8 17.8 %collective-permute-start.1 = (bf16[384,128]{1,0:T(8,128)(2,1)S(1)}, bf16[384,128]{1,0:T(8,128)(2,1)S(1)}, u32[]{:S(2)}, u32[]{:S(2)}) collective-permute-start(bf16[384,128]{1,0:T(8,128)(2,1)S(1)} %get-tuple-element.31), channel_id=1, source_target_pairs={{4,0},{8,4},{12,8},{16,12},{20,16},{24,20},{28,24},{5,1},{9,5},{13... | collective-permute-start | bytes 294920 | tf_op jit(solution)/shard_map/ppermute | solution.py:383
  8.1 16.5 %collective-permute-start.2 = (bf16[384,128]{1,0:T(8,128)(2,1)S(1)}, bf16[384,128]{1,0:T(8,128)(2,1)S(1)}, u32[]{:S(2)}, u32[]{:S(2)}) collective-permute-start(bf16[384,128]{1,0:T(8,128)(2,1)S(1)} %get-tuple-element.33), channel_id=1, source_target_pairs={{0,4},{4,8},{8,12},{12,16},{16,20},{20,24},{24,28},{1,5},{5,9},{9,... | collective-permute-start | bytes 294920 | tf_op jit(solution)/shard_map/ppermute | solution.py:383
  13.6 11.0 %collective-permute-start.3 = (bf16[384,128]{1,0:T(8,128)(2,1)S(1)}, bf16[384,128]{1,0:T(8,128)(2,1)S(1)}, u32[]{:S(2)}, u32[]{:S(2)}) collective-permute-start(bf16[384,128]{1,0:T(8,128)(2,1)S(1)} %get-tuple-element.34), channel_id=1, source_target_pairs={{0,8},{4,12},{8,16},{12,20},{16,24},{20,28},{1,9},{5,13},{9,17},{1... | collective-permute-start | bytes 294920 | tf_op jit(solution)/shard_map/ppermute | solution.py:383
  18.2 6.4 %copy-start.1 = (bf16[1,4,8,8,512]{4,3,2,1,0:T(8,128)(2,1)S(1)}, bf16[1,4,8,8,512]{4,3,2,1,0:T(8,128)(2,1)}, u32[]{:S(2)}) copy-start(bf16[1,4,8,8,512]{4,3,2,1,0:T(8,128)(2,1)} %param.15) | copy-start | bytes 786436
  30.3 1.9 %collective-permute-start.8 = (bf16[64,512]{1,0:T(8,128)(2,1)S(1)}, bf16[64,512]{1,0:T(8,128)(2,1)S(1)}, u32[]{:S(2)}, u32[]{:S(2)}) collective-permute-start(bf16[64,512]{1,0:T(8,128)(2,1)S(1)} %get-tuple-element.43), channel_id=1, source_target_pairs={{0,1},{1,0},{2,3},{3,2},{4,5},{5,4},{6,7},{7,6},{8,9},{9,8},{10,11... | collective-permute-start | bytes 196616 | tf_op jit(solution)/shard_map/ppermute | solution.py:387
  30.7 4.3 %collective-permute-start.9 = (bf16[64,512]{1,0:T(8,128)(2,1)S(1)}, bf16[64,512]{1,0:T(8,128)(2,1)S(1)}, u32[]{:S(2)}, u32[]{:S(2)}) collective-permute-start(bf16[64,512]{1,0:T(8,128)(2,1)S(1)} %get-tuple-element.44), channel_id=1, source_target_pairs={{0,2},{1,3},{2,0},{3,1},{4,6},{5,7},{6,4},{7,5},{8,10},{9,11},{10,... | collective-permute-start | bytes 196616 | tf_op jit(solution)/shard_map/ppermute | solution.py:387
  32.2 4.4 %collective-permute-start.10 = (bf16[64,512]{1,0:T(8,128)(2,1)S(1)}, bf16[64,512]{1,0:T(8,128)(2,1)S(1)}, u32[]{:S(2)}, u32[]{:S(2)}) collective-permute-start(bf16[64,512]{1,0:T(8,128)(2,1)S(1)} %get-tuple-element.45), channel_id=1, source_target_pairs={{0,3},{1,2},{2,1},{3,0},{4,7},{5,6},{6,5},{7,4},{8,11},{9,10},{10,... | collective-permute-start | bytes 196616 | tf_op jit(solution)/shard_map/ppermute | solution.py:387
  36.6 4.8 %collective-permute-start.11 = (bf16[64,512]{1,0:T(8,128)(2,1)S(1)}, bf16[64,512]{1,0:T(8,128)(2,1)S(1)}, u32[]{:S(2)}, u32[]{:S(2)}) collective-permute-start(bf16[64,512]{1,0:T(8,128)(2,1)S(1)} %add_convert_fusion.2), channel_id=1, source_target_pairs={{0,4},{4,0},{8,12},{12,8},{16,20},{20,16},{24,28},{28,24},{1,5},{5... | collective-permute-start | bytes 196616 | tf_op jit(solution)/shard_map/ppermute | solution.py:387
  41.4 13.4 %collective-permute-start.12 = (bf16[64,512]{1,0:T(8,128)(2,1)S(1)}, bf16[64,512]{1,0:T(8,128)(2,1)S(1)}, u32[]{:S(2)}, u32[]{:S(2)}) collective-permute-start(bf16[64,512]{1,0:T(8,128)(2,1)S(1)} %add_convert_fusion.1), channel_id=1, source_target_pairs={{0,8},{4,12},{8,0},{12,4},{16,24},{20,28},{24,16},{28,20},{1,9},{5... | collective-permute-start | bytes 196616 | tf_op jit(solution)/shard_map/ppermute | solution.py:387
  43.1 13.0 %collective-permute-start.4 = (bf16[384,128]{1,0:T(8,128)(2,1)S(1)}, bf16[384,128]{1,0:T(8,128)(2,1)S(1)}, u32[]{:S(2)}, u32[]{:S(2)}) collective-permute-start(bf16[384,128]{1,0:T(8,128)(2,1)S(1)} %get-tuple-element.37), channel_id=1, source_target_pairs={{8,0},{12,4},{16,8},{20,12},{24,16},{28,20},{9,1},{13,5},{17,9},{2... | collective-permute-start | bytes 294920 | tf_op jit(solution)/shard_map/ppermute | solution.py:383
  44.4 11.7 %collective-permute-start.5 = (bf16[384,128]{1,0:T(8,128)(2,1)S(1)}, bf16[384,128]{1,0:T(8,128)(2,1)S(1)}, u32[]{:S(2)}, u32[]{:S(2)}) collective-permute-start(bf16[384,128]{1,0:T(8,128)(2,1)S(1)} %get-tuple-element.38), channel_id=1, source_target_pairs={{4,0},{8,4},{12,8},{16,12},{20,16},{24,20},{28,24},{5,1},{9,5},{13... | collective-permute-start | bytes 294920 | tf_op jit(solution)/shard_map/ppermute | solution.py:383
  45.7 10.5 %collective-permute-start.6 = (bf16[384,128]{1,0:T(8,128)(2,1)S(1)}, bf16[384,128]{1,0:T(8,128)(2,1)S(1)}, u32[]{:S(2)}, u32[]{:S(2)}) collective-permute-start(bf16[384,128]{1,0:T(8,128)(2,1)S(1)} %get-tuple-element.40), channel_id=1, source_target_pairs={{0,4},{4,8},{8,12},{12,16},{16,20},{20,24},{24,28},{1,5},{5,9},{9,... | collective-permute-start | bytes 294920 | tf_op jit(solution)/shard_map/ppermute | solution.py:383
  50.2 6.7 %collective-permute-start.7 = (bf16[384,128]{1,0:T(8,128)(2,1)S(1)}, bf16[384,128]{1,0:T(8,128)(2,1)S(1)}, u32[]{:S(2)}, u32[]{:S(2)}) collective-permute-start(bf16[384,128]{1,0:T(8,128)(2,1)S(1)} %get-tuple-element.41), channel_id=1, source_target_pairs={{0,8},{4,12},{8,16},{12,20},{16,24},{20,28},{1,9},{5,13},{9,17},{1... | collective-permute-start | bytes 294920 | tf_op jit(solution)/shard_map/ppermute | solution.py:383
  54.8 6.1 %collective-permute-start.13 = (bf16[64,512]{1,0:T(8,128)(2,1)S(1)}, bf16[64,512]{1,0:T(8,128)(2,1)S(1)}, u32[]{:S(2)}, u32[]{:S(2)}) collective-permute-start(bf16[64,512]{1,0:T(8,128)(2,1)S(1)} %add_convert_fusion.mine), channel_id=1, source_target_pairs={{0,16},{4,20},{8,24},{12,28},{16,0},{20,4},{24,8},{28,12},{1,17},{... | collective-permute-start | bytes 196616 | tf_op jit(solution)/shard_map/ppermute | solution.py:387

commit v2 on v1

--- a/solution.py
+++ b/solution.py
@@ -37,13 +37,24 @@
     return [block[8 * q : 8 * q + 8] for q in range(4)]
 
 
+def upward(device, distance):
+    return lax.rem(lax.div(device, distance), 2)
+
+
 def pack_units(values, send, outs):
     slots = values.shape[1] // 64 - 1
+    reach = len(outs) // 2
     low = low_half((64, LANES))
-    for column, out in enumerate(outs):
+    device = lax.axis_index("space")
+    for number, out in enumerate(outs):
+        column = reach
+        if number > 0:
+            distance = (number + 1) // 2
+            up = upward(device, distance) == (number + 1) % 2
+            column = jnp.where(up, reach + distance, reach - distance)
 
         def base(link):
-            unit = send[column, link]
+            unit = send[column, 0, link]
             slot = jnp.where(unit < 0, slots, (unit * 43) >> 8)
             return pl.multiple_of(slot * 64, 64)
 
@@ -64,47 +75,92 @@
 
 
 def prepare_kernel(
-    features, occupancy, counts, send, listing, weight_t, bias,
-    masked_out, mask_out, rows_out, shard_out, u0, u1, u2, u3, u4, values,
+    features_hbm, occupancy_hbm, counts_hbm, send_hbm, listing_hbm, weight_hbm, bias_hbm,
+    masked_out, mask_out, rows_out, send_out, shard_out, u0, u1, u2, u3, u4,
+    values, features, occupancy, counts, listing, weight_t, bias, rows, sems,
 ):
+    copies = [
+        pltpu.make_async_copy(src, dst, sems.at[i])
+        for i, (src, dst) in enumerate(
+            (
+                (occupancy_hbm, occupancy),
+                (counts_hbm, counts),
+                (features_hbm, features),
+                (send_hbm, send_out),
+                (listing_hbm, listing),
+                (weight_hbm, weight_t),
+                (bias_hbm, bias),
+            )
+        )
+    ]
+    for copy in copies:
+        copy.start()
     bricks = features.shape[0]
-    live = lax.broadcasted_iota(jnp.int32, (bricks, 512), 0) < counts[0, 0]
-    occ = jnp.where(live, occupancy[...], 0).astype(F32)
+    shard_out[...] = jnp.zeros(shard_out.shape, BF16)
+    values[:, bricks * 64 :, :] = jnp.zeros((4, 64, LANES), F32)
     row = lax.broadcasted_iota(jnp.int32, (64, 512), 0)
     col = lax.broadcasted_iota(jnp.int32, (64, 512), 1)
     same = (col >> 3) == row
+    z_row = lax.broadcasted_iota(jnp.int32, (512, 512), 0) & 7
+    z_col = lax.broadcasted_iota(jnp.int32, (512, 512), 1) >> 6
+    expand = jnp.where(z_row == z_col, 1.0, 0.0).astype(BF16)
+
+    copies[0].wait()
+    copies[1].wait()
+    live = lax.broadcasted_iota(jnp.int32, (bricks, 512), 0) < counts[0, 0]
+    occ = jnp.where(live, occupancy[...], 0).astype(F32)
     spread = jnp.concatenate(
         [jnp.where(same, occ[b : b + 1, :], 0.0) for b in range(bricks)], axis=0
     ).astype(BF16)
-    z_row = lax.broadcasted_iota(jnp.int32, (512, 512), 0) & 7
-    z_col = lax.broadcasted_iota(jnp.int32, (512, 512), 1) >> 6
-    expand = jnp.where(z_row == z_col, 1.0, 0.0).astype(BF16)
     mask = jnp.dot(spread, expand, preferred_element_type=F32)
     mask_out[...] = mask.astype(BF16).reshape(mask_out.shape)
+    copies[2].wait()
     value = features[...].astype(F32).reshape(bricks * 64, 512) * mask
     masked_out[...] = value.astype(BF16).reshape(masked_out.shape)
     for q in range(4):
         values[q, 0 : bricks * 64, :] = value[:, q * LANES : (q + 1) * LANES]
-    values[:, bricks * 64 :, :] = jnp.zeros((4, 64, LANES), F32)
-    pack_units(values, send, (u0, u1, u2, u3, u4))
-
+    copies[3].wait()
+    pack_units(values, send_out, (u0, u1, u2, u3, u4))
+
+    copies[4].wait()
+    device = lax.axis_index("space")
     number = listing[...]
     column = (number * 43) >> 9
     link = number - column * 12
     half = (link >= 6).astype(jnp.int32)
     face = link - 6 * half
-    base = column * (8 * UNIT_ROWS + 2 * Z_ROWS)
+    block = jnp.zeros(number.shape, jnp.int32)
+    for distance in (1, 2):
+        up = upward(device, distance)
+        block = jnp.where(column == 2 - distance, 2 * distance - 1 + up, block)
+        block = jnp.where(column == 2 + distance, 2 * distance - up, block)
+    base = block * (8 * UNIT_ROWS + 2 * Z_ROWS)
     plain = base + (half * 4 + face) * UNIT_ROWS
     paired = base + 8 * UNIT_ROWS + half * Z_ROWS
     none = 5 * (8 * UNIT_ROWS + 2 * Z_ROWS)
-    rows_out[...] = jnp.where(number < 0, none, jnp.where(face < 4, plain, paired))
-
+    rows[...] = jnp.where(number < 0, none, jnp.where(face < 4, plain, paired))
+    last = pltpu.make_async_copy(rows, rows_out, sems.at[len(copies)])
+    last.start()
+
+    copies[5].wait()
+    copies[6].wait()
     shard = weight_t.shape[1]
-    width = shard_out.shape[1]
+    lead = shard // LANES * LANES
     count = bias.shape[1]
-    shard_out[...] = jnp.zeros(shard_out.shape, F32)
-    shard_out[:, 0:shard] = weight_t[...].astype(F32)
-    shard_out[0:1, shard : shard + count] = bias[...].astype(F32)
+    shard_out[:, 0:lead] = weight_t[:, 0:lead]
+    tile = jnp.concatenate(
+        [weight_t[:, lead:shard].astype(F32), jnp.zeros((64, lead + LANES - shard), F32)], axis=1
+    )
+    offset = shard - lead
+    behind = jnp.concatenate(
+        [bias[...].astype(F32), jnp.zeros((1, LANES - count), F32)], axis=1
+    )
+    behind = pltpu.roll(jnp.broadcast_to(behind, (64, LANES)), offset, 1)
+    first = lax.broadcasted_iota(jnp.int32, (64, LANES), 0) == 0
+    lane = lax.broadcasted_iota(jnp.int32, (64, LANES), 1)
+    behind = jnp.where(first & (lane >= offset) & (lane < offset + count), behind, 0.0)
+    shard_out[:, lead : lead + LANES] = (tile + behind).astype(BF16)
+    last.wait()
 
 
 def gather_units(table, received):
@@ -210,51 +266,66 @@
     lax.fori_loop(0, windows.shape[2], one_pair, 0)
 
 
-def spread_weights(gathered, flat, shifted, shard):
-    for k in range(gathered.shape[0]):
-        flat[:, k * shard : (k + 1) * shard] = gathered[k][:, 0:shard].astype(F32)
-    total = gathered.shape[0] * shard
+def weights_kernel(*refs, shard, groups):
+    shards = refs[:groups]
+    forward_out, backward_out, bias_out, gathered, flat, shifted = refs[groups:]
+    me = lax.axis_index("dp")
+    for m, part in enumerate(shards):
+        gathered[m] = part[...]
+    for k in range(groups):
+        flat[:, k * shard : (k + 1) * shard] = gathered[me ^ k][:, 0:shard].astype(F32)
+    total = groups * shard
     flat[:, total:] = jnp.zeros((64, flat.shape[1] - total), F32)
     shifted[:, :] = pltpu.roll(flat[...], flat.shape[1] - 64, 1)
-
-
-def taps_pair(flat, shifted, first):
-    if first % 2 == 0:
-        return flat[:, first * 64 : first * 64 + LANES]
-    return shifted[:, (first - 1) * 64 : (first - 1) * 64 + LANES]
-
-
-def forward_kernel(
-    masked, mask, cotangent, gathered, rows, send, r0, r1, r2, r3, r4,
-    block_out, grad_out, u0, u1, u2, u3, u4, *rest, shard,
-):
-    chunk_outs = rest[:-9]
-    table, windows, sides, walls, flat, shifted, toeplitz, values, flipped = rest[-9:]
-    groups = gathered.shape[0]
-    bricks = masked.shape[0]
-    pairs = bricks // 2
-    gather_units(table, (r0, r1, r2, r3, r4))
-    assemble(masked, table, rows, windows, sides, walls)
-    spread_weights(gathered, flat, shifted, shard)
     low = low_half((64, LANES))
     for ae in range(9):
         one = taps_pair(flat, shifted, 3 * ae)
         two = jnp.where(low, taps_pair(flat, shifted, 3 * ae + 2), 0.0)
         late = jnp.concatenate([one, two], axis=1)
-        toeplitz[ae, 64:128, :] = late.astype(BF16)
-        toeplitz[ae, 0:64, :] = pltpu.roll(late, 192, 1).astype(BF16)
-
-    lane = lax.broadcasted_iota(jnp.int32, (1, LANES), 1)
+        forward_out[ae, 64:128, :] = late.astype(BF16)
+        forward_out[ae, 0:64, :] = pltpu.roll(late, 192, 1).astype(BF16)
+    for ae in range(9):
+        m = 3 * (8 - ae)
+        first = taps_pair(flat, shifted, m)
+        second = taps_pair(flat, shifted, m + 1)
+        third = taps_pair(flat, shifted, m + 2)
+        backward_out[ae, 0:64, :] = second.astype(BF16)
+        backward_out[ae, 64:128, :] = first.astype(BF16)
+        backward_out[ae, 128:192, :] = jnp.where(low, 0.0, pltpu.roll(first, 64, 1)).astype(BF16)
+        backward_out[ae, 192:256, :] = jnp.where(low, third, 0.0).astype(BF16)
+
+    lane = lax.broadcasted_iota(jnp.int32, (8, LANES), 1)
     bias_lane = shard % LANES
     bias_tile = shard - bias_lane
     count = 64 // groups
-    bias_row = jnp.zeros((1, LANES), F32)
+    bias_row = jnp.zeros((8, LANES), F32)
     for k in range(groups):
-        tile = gathered[k][0:16, bias_tile : bias_tile + LANES].astype(F32)[0:8]
-        moved = pltpu.roll(tile, (count * k - bias_lane) % LANES, 1)[0:1]
+        tile = gathered[me ^ k][0:16, bias_tile : bias_tile + LANES].astype(F32)[0:8]
+        moved = pltpu.roll(tile, (count * k - bias_lane) % LANES, 1)
         bias_row += jnp.where((lane >= count * k) & (lane < count * (k + 1)), moved, 0.0)
-    bias_row += pltpu.roll(jnp.broadcast_to(bias_row, (8, LANES)), 64, 1)[0:1]
-
+    bias_out[...] = bias_row + pltpu.roll(bias_row, 64, 1)
+
+
+def taps_pair(flat, shifted, first):
+    if first % 2 == 0:
+        return flat[:, first * 64 : first * 64 + LANES]
+    return shifted[:, (first - 1) * 64 : (first - 1) * 64 + LANES]
+
+
+def forward_kernel(
+    masked, mask, cotangent, toeplitz, bias, rows, send, r0, r1, r2, r3, r4,
+    block_out, grad_out, u0, u1, u2, u3, u4, *rest, shard,
+):
+    chunk_outs = rest[:-8]
+    table, windows, sides, walls, flat, shifted, values, flipped = rest[-8:]
+    groups = len(chunk_outs)
+    bricks = masked.shape[0]
+    pairs = bricks // 2
+    gather_units(table, (r0, r1, r2, r3, r4))
+    assemble(masked, table, rows, windows, sides, walls)
+    bias_lane = shard % LANES
+    bias_tile = shard - bias_lane
+    bias_row = bias[0:1, :]
     values[:, bricks * 64 :, :] = jnp.zeros((4, 64, LANES), F32)
 
     def one_chunk(q, bias_sum):
@@ -329,24 +400,12 @@
 
 
 def backward_kernel(
-    grad, mask, gathered, rows, r0, r1, r2, r3, r4, out,
-    table, windows, sides, walls, flat, shifted, toeplitz, *, shard,
+    grad, mask, toeplitz, rows, r0, r1, r2, r3, r4, out, table, windows, sides, walls
 ):
     bricks = grad.shape[0]
     pairs = bricks // 2
     gather_units(table, (r0, r1, r2, r3, r4))
     assemble(grad, table, rows, windows, sides, walls)
-    spread_weights(gathered, flat, shifted, shard)
-    low = low_half((64, LANES))
-    for ae in range(9):
-        m = 3 * (8 - ae)
-        first = taps_pair(flat, shifted, m)
-        second = taps_pair(flat, shifted, m + 1)
-        third = taps_pair(flat, shifted, m + 2)
-        toeplitz[ae, 0:64, :] = second.astype(BF16)
-        toeplitz[ae, 64:128, :] = first.astype(BF16)
-        toeplitz[ae, 128:192, :] = jnp.where(low, 0.0, pltpu.roll(first, 64, 1)).astype(BF16)
-        toeplitz[ae, 192:256, :] = jnp.where(low, third, 0.0).astype(BF16)
 
     def one_chunk(q, carry):
         total = jnp.zeros((pairs * LANES, LANES), F32)
@@ -377,79 +436,103 @@
     bias_out[...] = moved[0:1, 0:count]
 
 
-def passed_along(block, axis, distance):
-    devices = range(lax.axis_size(axis))
-    route = [(i - distance, i) for i in devices if i - distance in devices]
-    return lax.ppermute(block, axis, route)
-
-
 def swapped(block, axis, bit):
     return lax.ppermute(block, axis, [(i, i ^ bit) for i in range(lax.axis_size(axis))])
 
 
 def exchanged(units):
-    reach = len(units) // 2
-    return [
-        unit if column == reach else passed_along(unit, "space", column - reach)
-        for column, unit in enumerate(units)
-    ]
+    devices = lax.axis_size("space")
+    received = [units[0]]
+    for number in range(1, len(units)):
+        distance = (number + 1) // 2
+        turn = (number + 1) % 2
+        route = []
+        for low in range(devices - distance):
+            if low // distance % 2 == turn:
+                route += [(low, low + distance), (low + distance, low)]
+        received.append(lax.ppermute(units[number], "space", route))
+    return received
 
 
 def body(features, occupancy, counts, send_units, neighbours, weight, conv_bias, cotangent):
     grid_shape = features.shape[1:]
     bricks = grid_shape[0]
     pairs = bricks // 2
-    spread = send_units.shape[2]
-    shard = weight.shape[0]
-    channels = weight.shape[1]
+    spread, links = send_units.shape[2:]
+    shard, channels = weight.shape
     groups = lax.axis_size("dp")
     count = conv_bias.shape[0]
     width = -(-(shard + channels) // LANES) * LANES
     unit_rows = 8 * UNIT_ROWS + 2 * Z_ROWS
     units_type = jax.ShapeDtypeStruct((unit_rows, LANES), BF16)
     grid_type = jax.ShapeDtypeStruct(grid_shape, BF16)
-    send = send_units[0, 0]
+    shard_type = jax.ShapeDtypeStruct((channels, width), BF16)
     params = pltpu.CompilerParams(vmem_limit_bytes=48 * 1024 * 1024)
-
-    masked, mask, rows, own_shard, *units = pl.pallas_call(
+    rows_shape = neighbours.shape[1:]
+    send_shape = (spread, 1, links)
+
+    masked, mask, rows, send, own_shard, *units = pl.pallas_call(
         prepare_kernel,
         name="prepare",
         out_shape=[
             grid_type,
             grid_type,
-            jax.ShapeDtypeStruct(neighbours.shape[1:], jnp.int32),
-            jax.ShapeDtypeStruct((channels, width), F32),
+            jax.ShapeDtypeStruct(rows_shape, jnp.int32),
+            jax.ShapeDtypeStruct(send_shape, jnp.int32),
+            shard_type,
         ]
         + [units_type] * spread,
-        in_specs=[vmem(), vmem(), smem(), smem(), vmem(), vmem(), vmem()],
-        out_specs=[vmem()] * (4 + spread),
-        scratch_shapes=[pltpu.VMEM((4, (bricks + 1) * 64, LANES), F32)],
+        in_specs=[pl.BlockSpec(memory_space=pltpu.HBM)] * 7,
+        out_specs=[vmem(), vmem(), smem(), smem(), vmem()] + [vmem()] * spread,
+        scratch_shapes=[
+            pltpu.VMEM((4, (bricks + 1) * 64, LANES), F32),
+            pltpu.VMEM(grid_shape, BF16),
+            pltpu.VMEM(occupancy.shape[1:], jnp.int32),
+            pltpu.SMEM((1, 1), jnp.int32),
+            pltpu.VMEM(rows_shape, jnp.int32),
+            pltpu.VMEM((channels, shard), BF16),
+            pltpu.VMEM((1, count), BF16),
+            pltpu.VMEM(rows_shape, jnp.int32),
+            pltpu.SemaphoreType.DMA((8,)),
+        ],
         compiler_params=params,
     )(
         features[0],
         occupancy[0],
         counts,
-        send,
+        send_units.transpose(0, 2, 1, 3).reshape(send_shape),
         neighbours[0],
         weight.T,
         conv_bias.reshape(1, count),
     )
 
+    shards = [own_shard] + [swapped(own_shard, "dp", m) for m in range(1, groups)]
     received = exchanged(units)
-    gathered = lax.all_gather(own_shard.astype(BF16), "dp", axis=0)
+
+    flat = pltpu.VMEM((channels, 28 * 64), F32)
+    band_forward, band_backward, bias = pl.pallas_call(
+        functools.partial(weights_kernel, shard=shard, groups=groups),
+        name="weights",
+        out_shape=[
+            jax.ShapeDtypeStruct((9, LANES, 256), BF16),
+            jax.ShapeDtypeStruct((9, 256, LANES), BF16),
+            jax.ShapeDtypeStruct((8, LANES), F32),
+        ],
+        in_specs=[vmem()] * groups,
+        out_specs=[vmem()] * 3,
+        scratch_shapes=[pltpu.VMEM((groups, channels, width), BF16), flat, flat],
+        compiler_params=params,
+    )(*shards)
 
     table = pltpu.VMEM((spread * unit_rows + Z_ROWS, LANES), BF16)
     windows = pltpu.VMEM((3, 4, pairs, 10, 16, 256), BF16)
     sides = pltpu.VMEM((2, 2, 5, 8, LANES), F32)
     walls = pltpu.VMEM((2, 64, LANES), F32)
-    flat = pltpu.VMEM((channels, 28 * 64), F32)
     block_output, grad, *rest = pl.pallas_call(
         functools.partial(forward_kernel, shard=shard),
         name="forward",
-        out_shape=[grid_type, grid_type]
-        + [units_type] * spread
-        + [jax.ShapeDtypeStruct((channels, width), BF16)] * groups,
-        in_specs=[vmem()] * 4 + [smem(), smem()] + [vmem()] * spread,
+        out_shape=[grid_type, grid_type] + [units_type] * spread + [shard_type] * groups,
+        in_specs=[vmem()] * 5 + [smem(), smem()] + [vmem()] * spread,
         out_specs=[vmem()] * (2 + spread + groups),
         scratch_shapes=[
             table,
@@ -458,34 +541,25 @@
             walls,
             flat,
             flat,
-            pltpu.VMEM((9, LANES, 256), BF16),
             pltpu.VMEM((4, (bricks + 1) * 64, LANES), F32),
             pltpu.VMEM((4, LANES, pairs * LANES), BF16),
         ],
         compiler_params=params,
-    )(masked, mask, cotangent[0], gathered, rows, send, *received)
+    )(masked, mask, cotangent[0], band_forward, bias, rows, send, *received)
     grad_units, blocks = rest[:spread], rest[spread:]
 
+    shares = [blocks[0]] + [swapped(blocks[m], "dp", m) for m in range(1, groups)]
     grad_received = exchanged(grad_units)
-    shares = [blocks[0]] + [swapped(blocks[m], "dp", m) for m in range(1, groups)]
 
     grad_input = pl.pallas_call(
-        functools.partial(backward_kernel, shard=shard),
+        backward_kernel,
         name="backward",
         out_shape=grid_type,
         in_specs=[vmem()] * 3 + [smem()] + [vmem()] * spread,
         out_specs=vmem(),
-        scratch_shapes=[
-            table,
-            windows,
-            sides,
-            walls,
-            flat,
-            flat,
-            pltpu.VMEM((9, 256, LANES), BF16),
-        ],
+        scratch_shapes=[table, windows, sides, walls],
         compiler_params=params,
-    )(grad, mask, gathered, rows, *grad_received)
+    )(grad, mask, band_backward, rows, *grad_received)
 
     total = sum(share.astype(F32) for share in shares).astype(BF16)
     devices = lax.axis_size("space")

time: 62.8 us -> 52.2 us (0.83)
  starting transfers between devices: 31.6 us -> 24.2 us
  blocking collectives: 6.32 us -> 0 us
  waiting for transfers between devices: 7.6 us -> 10.8 us
  Pallas kernels: 11.4 us -> 12.5 us
  local copies, waits for them, and re-layouts: 3.17 us -> 2.46 us
    ppermute x8, starting transfers between devices: 24.4 us -> 12.2 us  [exchanged(): received.append(lax.ppermute(units[number], 'space', route))]
    all_gather x1 -> x0, blocking collectives: 6.32 us -> none  [body(): gathered = lax.all_gather(own_shard.astype(BF16), 'dp', axis=0)]
    ppermute x6 -> x9, starting transfers between devices: 7.24 us -> 12 us  [swapped(): lax.ppermute(block, axis, [(i, i ^ bit) for i in range(lax.axis_size(axis...]
    ppermute x6 -> x9, waiting for transfers between devices: 6.73 us -> 8.37 us  [swapped(): lax.ppermute(block, axis, [(i, i ^ bit) for i in range(lax.axis_size(axis...]
    ppermute x8, waiting for transfers between devices: 0.87 us -> 2.44 us  [exchanged(): received.append(lax.ppermute(units[number], 'space', route))]
    pallas_call x1, Pallas kernels: 1.03 us -> 2.4 us  [body(): pl.pallas_call(prepare_kernel, name='prepare', out_shape=[grid_type, grid...]
    unnamed x13 -> x14, local copies, waits for them, and re-layouts: 3.17 us -> 2.46 us
    pallas_call x1 -> x2, Pallas kernels: 3.96 us -> 4.09 us  [the longest x1 3.68 us: body(): pl.pallas_call(backward_kernel, name='backward', out_shape=grid_type, in_...]
  transfers between devices with their start and end apart: 14 -> 17, of which waited for: 4 -> 6; matrix products, arithmetic and copies ran while one was open for 0% -> 0% of each run, Pallas kernels for 6% -> 8%
where the time goes in v2:
time: 52.2 us; the launch traced here: 51.5 us
  starting transfers between devices  24.2 us (46%)
  Pallas kernels  12.5 us (24%)
  waiting for transfers between devices  10.8 us (21%)
  local copies, waits for them, and re-layouts  2.46 us (5%)
  between operations  1.43 us (3%)
    ppermute x8, starting transfers between devices, exchanged(): received.append(lax.ppermute(units[number], 'space', route))  12.2 us
    ppermute x9, starting transfers between devices, swapped(): lax.ppermute(block, axis, [(i, i ^ bit) for i in range(lax.axis_size(axis...  12 us
    ppermute x9, waiting for transfers between devices, swapped(): lax.ppermute(block, axis, [(i, i ^ bit) for i in range(lax.axis_size(axis...  8.37 us
    pallas_call x1, Pallas kernels, body(): pl.pallas_call(functools.partial(forward_kernel, shard=shard), name='forw...  5.37 us
    pallas_call x1, Pallas kernels, body(): pl.pallas_call(backward_kernel, name='backward', out_shape=grid_type, in_...  3.68 us
    unnamed x14, local copies, waits for them, and re-layouts  2.46 us
    ppermute x8, waiting for transfers between devices, exchanged(): received.append(lax.ppermute(units[number], 'space', route))  2.44 us
    pallas_call x1, Pallas kernels, body(): pl.pallas_call(prepare_kernel, name='prepare', out_shape=[grid_type, grid...  2.4 us
  transfers between devices with their start and end apart: 17, of which 6 were waited for; matrix products, arithmetic and copies ran while one was open for 0% of the time, Pallas kernels for 8%

profile of v2, /device:TPU:0, one launch (start us, length us, event | category | flops | bytes accessed | tf_op | source)
XLA Modules:
  0.0 51.5 jit_solution(7267252044960940883)
XLA Ops:
  0.6 0.0 copy-start.3
  1.3 0.0 copy-start.4
  1.3 0.0 copy-start.5
  1.3 0.0 copy-start.6
  1.3 0.6 %copy-done.4 = s32[1,1,5,12]{3,1,2,0:T(1,128)S(1)} copy-done((s32[1,1,5,12]{3,1,2,0:T(1,128)S(1)}, s32[1,1,5,12]{3,1,2,0:T(1,128)}, u32[]{:S(2)}) %copy-start.4) | copy-done | bytes 264
  2.0 0.0 copy-done.5
  2.0 0.0 copy-done.6
  2.0 0.9 %copy-done = bf16[1,4,8,8,512]{4,3,2,1,0:T(8,128)(2,1)S(1)} copy-done((bf16[1,4,8,8,512]{4,3,2,1,0:T(8,128)(2,1)S(1)}, bf16[1,4,8,8,512]{4,3,2,1,0:T(8,128)(2,1)}, u32[]{:S(2)}) %copy-start) | copy-done | bytes 262168
  3.0 0.8 %copy-done.2 = bf16[432,64]{0,1:T(8,128)(2,1)S(1)} copy-done((bf16[432,64]{0,1:T(8,128)(2,1)S(1)}, bf16[432,64]{0,1:T(8,128)(2,1)}, u32[]{:S(2)}) %copy-start.2) | copy-done | bytes 55320
  3.8 2.4 %prepare.1 = (bf16[4,8,8,512]{3,2,1,0:T(8,128)(2,1)S(1)}, bf16[4,8,8,512]{3,2,1,0:T(8,128)(2,1)S(1)}, s32[4,26]{1,0:T(4,128)S(1)}, s32[5,1,12]{2,1,0:T(1,128)S(1...) custom-call(bf16[4,8,8,512]{3,2,1,0:T(8,128)(2,1)S(1)} %bitcast.11, ...), custom_call_target="tpu_custom_call" | custom-call | tf_op jit(solution)/shard_map/prepare/pallas_call | solution.py:474
  6.2 2.4 %collective-permute-start.2 = (bf16[64,512]{1,0:T(8,128)(2,1)S(1)}, bf16[64,512]{1,0:T(8,128)(2,1)S(1)}, u32[]{:S(2)}, u32[]{:S(2)}) collective-permute-start(bf16[64,512]{1,0:T(8,128)(2,1)S(1)} %get-tuple-element.32.refs_0_), channel_id=1, source_target_pairs={{0,3},{1,2},{2,1},{3,0},{4,7},{5,6},{6,5},{7,4},{8,11},{9,10},{10,... | collective-permute-start | bytes 196616 | tf_op jit(solution)/shard_map/ppermute | solution.py:440
  8.6 0.6 %collective-permute-start.1 = (bf16[64,512]{1,0:T(8,128)(2,1)S(1)}, bf16[64,512]{1,0:T(8,128)(2,1)S(1)}, u32[]{:S(2)}, u32[]{:S(2)}) collective-permute-start(bf16[64,512]{1,0:T(8,128)(2,1)S(1)} %get-tuple-element.32.refs_0_), channel_id=1, source_target_pairs={{0,2},{1,3},{2,0},{3,1},{4,6},{5,7},{6,4},{7,5},{8,10},{9,11},{10,... | collective-permute-start | bytes 196616 | tf_op jit(solution)/shard_map/ppermute | solution.py:440
  9.3 1.5 %collective-permute-start.3 = (bf16[384,128]{1,0:T(8,128)(2,1)S(1)}, bf16[384,128]{1,0:T(8,128)(2,1)S(1)}, u32[]{:S(2)}, u32[]{:S(2)}) collective-permute-start(bf16[384,128]{1,0:T(8,128)(2,1)S(1)} %get-tuple-element.38), channel_id=1, source_target_pairs={{0,4},{4,0},{8,12},{12,8},{16,20},{20,16},{24,28},{28,24},{1,5},{5... | collective-permute-start | bytes 294920 | tf_op jit(solution)/shard_map/ppermute | solution.py:453
  10.8 0.7 %collective-permute-start.4 = (bf16[384,128]{1,0:T(8,128)(2,1)S(1)}, bf16[384,128]{1,0:T(8,128)(2,1)S(1)}, u32[]{:S(2)}, u32[]{:S(2)}) collective-permute-start(bf16[384,128]{1,0:T(8,128)(2,1)S(1)} %get-tuple-element.39), channel_id=1, source_target_pairs={{4,8},{8,4},{12,16},{16,12},{20,24},{24,20},{5,9},{9,5},{13,17},{1... | collective-permute-start | bytes 294920 | tf_op jit(solution)/shard_map/ppermute | solution.py:453
  11.5 3.3 %collective-permute-start.5 = (bf16[384,128]{1,0:T(8,128)(2,1)S(1)}, bf16[384,128]{1,0:T(8,128)(2,1)S(1)}, u32[]{:S(2)}, u32[]{:S(2)}) collective-permute-start(bf16[384,128]{1,0:T(8,128)(2,1)S(1)} %get-tuple-element.40), channel_id=1, source_target_pairs={{0,8},{8,0},{4,12},{12,4},{16,24},{24,16},{20,28},{28,20},{1,9},{9... | collective-permute-start | bytes 294920 | tf_op jit(solution)/shard_map/ppermute | solution.py:453
  14.7 0.0 collective-permute-done.2.refs_3_
  14.7 0.7 %collective-permute-start.6 = (bf16[384,128]{1,0:T(8,128)(2,1)S(1)}, bf16[384,128]{1,0:T(8,128)(2,1)S(1)}, u32[]{:S(2)}, u32[]{:S(2)}) collective-permute-start(bf16[384,128]{1,0:T(8,128)(2,1)S(1)} %get-tuple-element.41), channel_id=1, source_target_pairs={{8,16},{16,8},{12,20},{20,12},{9,17},{17,9},{13,21},{21,13},{10,18... | collective-permute-start | bytes 294920 | tf_op jit(solution)/shard_map/ppermute | solution.py:453
  15.4 0.0 collective-permute-done.1.refs_2_
  15.4 0.1 collective-permute-start
  15.5 1.2 %collective-permute-done.refs_1_ = bf16[64,512]{1,0:T(8,128)(2,1)S(1)} collective-permute-done((bf16[64,512]{1,0:T(8,128)(2,1)S(1)}, bf16[64,512]{1,0:T(8,128)(2,1)S(1)}, u32[]{:S(2)}, u32[]{:S(2)}) %collective-permute-start) | collective-permute-done | bytes 65568 | tf_op jit(solution)/shard_map/ppermute | solution.py:440
  16.7 0.4 weights.1
  17.2 0.0 collective-permute-done.3.r1
  17.2 0.0 collective-permute-done.4.r2
  17.2 2.2 %collective-permute-done.5.r3 = bf16[384,128]{1,0:T(8,128)(2,1)S(1)} collective-permute-done((bf16[384,128]{1,0:T(8,128)(2,1)S(1)}, bf16[384,128]{1,0:T(8,128)(2,1)S(1)}, u32[]{:S(2)}, u32[]{:S(2)}) %collective-permute-start.5) | collective-permute-done | bytes 98336 | tf_op jit(solution)/shard_map/ppermute | solution.py:453
  19.3 0.0 collective-permute-done.6.r4
  19.4 5.4 %forward.1 = (bf16[4,8,8,512]{3,2,1,0:T(8,128)(2,1)}, bf16[4,8,8,512]{3,2,1,0:T(8,128)(2,1)S(1)}, bf16[384,128]{1,0:T(8,128)(2,1)S(1)}, bf16[384,128]{1,0:T(8,12...) custom-call(bf16[4,8,8,512]{3,2,1,0:T(8,128)(2,1)S(1)} %get-tuple-el, ...), custom_call_target="tpu_custom_call" | custom-call | tf_op jit(solution)/shard_map/forward/pallas_call | solution.py:531
  24.7 0.0 collective-permute-start.11
  24.7 1.6 %collective-permute-start.12 = (bf16[64,512]{1,0:T(8,128)(2,1)S(1)}, bf16[64,512]{1,0:T(8,128)(2,1)S(1)}, u32[]{:S(2)}, u32[]{:S(2)}) collective-permute-start(bf16[64,512]{1,0:T(8,128)(2,1)S(1)} %get-tuple-element.52), channel_id=1, source_target_pairs={{0,2},{1,3},{2,0},{3,1},{4,6},{5,7},{6,4},{7,5},{8,10},{9,11},{10,... | collective-permute-start | bytes 196616 | tf_op jit(solution)/shard_map/ppermute | solution.py:440
  26.4 0.2 collective-permute-start.13
  26.6 0.0 collective-permute-done.11
  26.6 2.6 %collective-permute-done.12 = bf16[64,512]{1,0:T(8,128)(2,1)S(1)} collective-permute-done((bf16[64,512]{1,0:T(8,128)(2,1)S(1)}, bf16[64,512]{1,0:T(8,128)(2,1)S(1)}, u32[]{:S(2)}, u32[]{:S(2)}) %collective-permute-start.12) | collective-permute-done | bytes 65568 | tf_op jit(solution)/shard_map/ppermute | solution.py:440
  29.2 1.2 %collective-permute-done.13 = bf16[64,512]{1,0:T(8,128)(2,1)S(1)} collective-permute-done((bf16[64,512]{1,0:T(8,128)(2,1)S(1)}, bf16[64,512]{1,0:T(8,128)(2,1)S(1)}, u32[]{:S(2)}, u32[]{:S(2)}) %collective-permute-start.13) | collective-permute-done | bytes 65568 | tf_op jit(solution)/shard_map/ppermute | solution.py:440
  30.5 1.1 %collective-permute-start.14 = (bf16[64,512]{1,0:T(8,128)(2,1)S(1)}, bf16[64,512]{1,0:T(8,128)(2,1)S(1)}, u32[]{:S(2)}, u32[]{:S(2)}) collective-permute-start(bf16[64,512]{1,0:T(8,128)(2,1)S(1)} %add_convert_fusion.2), channel_id=1, source_target_pairs={{0,4},{4,0},{8,12},{12,8},{16,20},{20,16},{24,28},{28,24},{1,5},{5... | collective-permute-start | bytes 196616 | tf_op jit(solution)/shard_map/ppermute | solution.py:440
  31.5 3.3 %collective-permute-done.14 = bf16[64,512]{1,0:T(8,128)(2,1)S(1)} collective-permute-done((bf16[64,512]{1,0:T(8,128)(2,1)S(1)}, bf16[64,512]{1,0:T(8,128)(2,1)S(1)}, u32[]{:S(2)}, u32[]{:S(2)}) %collective-permute-start.14) | collective-permute-done | bytes 65568 | tf_op jit(solution)/shard_map/ppermute | solution.py:440
  34.8 3.1 %collective-permute-start.15 = (bf16[64,512]{1,0:T(8,128)(2,1)S(1)}, bf16[64,512]{1,0:T(8,128)(2,1)S(1)}, u32[]{:S(2)}, u32[]{:S(2)}) collective-permute-start(bf16[64,512]{1,0:T(8,128)(2,1)S(1)} %add_convert_fusion.1), channel_id=1, source_target_pairs={{0,8},{4,12},{8,0},{12,4},{16,24},{20,28},{24,16},{28,20},{1,9},{5... | collective-permute-start | bytes 196616 | tf_op jit(solution)/shard_map/ppermute | solution.py:440
  38.0 1.9 %collective-permute-start.7 = (bf16[384,128]{1,0:T(8,128)(2,1)S(1)}, bf16[384,128]{1,0:T(8,128)(2,1)S(1)}, u32[]{:S(2)}, u32[]{:S(2)}) collective-permute-start(bf16[384,128]{1,0:T(8,128)(2,1)S(1)} %get-tuple-element.46), channel_id=1, source_target_pairs={{0,4},{4,0},{8,12},{12,8},{16,20},{20,16},{24,28},{28,24},{1,5},{5... | collective-permute-start | bytes 294920 | tf_op jit(solution)/shard_map/ppermute | solution.py:453
  39.8 0.7 %collective-permute-start.8 = (bf16[384,128]{1,0:T(8,128)(2,1)S(1)}, bf16[384,128]{1,0:T(8,128)(2,1)S(1)}, u32[]{:S(2)}, u32[]{:S(2)}) collective-permute-start(bf16[384,128]{1,0:T(8,128)(2,1)S(1)} %get-tuple-element.47), channel_id=1, source_target_pairs={{4,8},{8,4},{12,16},{16,12},{20,24},{24,20},{5,9},{9,5},{13,17},{1... | collective-permute-start | bytes 294920 | tf_op jit(solution)/shard_map/ppermute | solution.py:453
  40.5 2.9 %collective-permute-start.9 = (bf16[384,128]{1,0:T(8,128)(2,1)S(1)}, bf16[384,128]{1,0:T(8,128)(2,1)S(1)}, u32[]{:S(2)}, u32[]{:S(2)}) collective-permute-start(bf16[384,128]{1,0:T(8,128)(2,1)S(1)} %get-tuple-element.48), channel_id=1, source_target_pairs={{0,8},{8,0},{4,12},{12,4},{16,24},{24,16},{20,28},{28,20},{1,9},{9... | collective-permute-start | bytes 294920 | tf_op jit(solution)/shard_map/ppermute | solution.py:453
  43.4 0.7 %collective-permute-start.10 = (bf16[384,128]{1,0:T(8,128)(2,1)S(1)}, bf16[384,128]{1,0:T(8,128)(2,1)S(1)}, u32[]{:S(2)}, u32[]{:S(2)}) collective-permute-start(bf16[384,128]{1,0:T(8,128)(2,1)S(1)} %get-tuple-element.49), channel_id=1, source_target_pairs={{8,16},{16,8},{12,20},{20,12},{9,17},{17,9},{13,21},{21,13},{10,18... | collective-permute-start | bytes 294920 | tf_op jit(solution)/shard_map/ppermute | solution.py:453
  44.1 0.0 collective-permute-done.15
  44.1 2.8 %collective-permute-start.16 = (bf16[64,512]{1,0:T(8,128)(2,1)S(1)}, bf16[64,512]{1,0:T(8,128)(2,1)S(1)}, u32[]{:S(2)}, u32[]{:S(2)}) collective-permute-start(bf16[64,512]{1,0:T(8,128)(2,1)S(1)} %add_convert_fusion.mine), channel_id=1, source_target_pairs={{0,16},{4,20},{8,24},{12,28},{16,0},{20,4},{24,8},{28,12},{1,17},{... | collective-permute-start | bytes 196616 | tf_op jit(solution)/shard_map/ppermute | solution.py:440
  46.9 0.0 collective-permute-done.7.r1
  46.9 0.0 collective-permute-done.8.r2
  46.9 0.2 collective-permute-done.9.r3
  47.2 0.0 collective-permute-done.10.r4
  47.2 3.7 %backward.1 = bf16[4,8,8,512]{3,2,1,0:T(8,128)(2,1)} custom-call(bf16[4,8,8,512]{3,2,1,0:T(8,128)(2,1)S(1)} %get-tuple-element.43.grad, bf16[4,8,8,512]{3,2,1,0:T(8,128)(2,1)S(1)} %get-tuple-element.31.mask, bf16[9,256,128]{2,1,0:T(8,128)(2,1)S(1)} %get-tuple-element.44.toeplitz, s32[4,26]{1,0:T(4,128)S(1)} %get-tuple-element.35.rows, ...), custom_call_target="tpu_custom_call" | custom-call | tf_op jit(solution)/shard_map/backward/pallas_call | solution.py:554
  50.8 0.0 collective-permute-done.16.other
  50.8 0.7 %finish.1 = (f32[64,432]{1,0:T(8,128)}, f32[1,16]{1,0:T(1,128)}) custom-call(bf16[64,512]{1,0:T(8,128)(2,1)S(1)} %add_convert_fusion.mine, bf16[64,512]{1,0:T(8,128)(2,1)S(1)} %collective-permute-done.16.other), custom_call_target="tpu_custom_call" | custom-call | tf_op jit(solution)/shard_map/finish/pallas_call | solution.py:570
  (8 shorter events, 0.1 us)
Async XLA Ops:
  0.6 0.7 %copy-start.3 = (s32[1,4,512]{2,1,0:T(4,128)S(1)}, s32[1,4,512]{2,1,0:T(4,128)}, u32[]{:S(2)}) copy-start(s32[1,4,512]{2,1,0:T(4,128)} %param.9) | copy-start | bytes 24580
  1.3 0.7 %copy-start.4 = (s32[1,1,5,12]{3,1,2,0:T(1,128)S(1)}, s32[1,1,5,12]{3,1,2,0:T(1,128)}, u32[]{:S(2)}) copy-start(s32[1,1,5,12]{3,1,2,0:T(1,128)} %param.11) | copy-start | bytes 724
  1.3 0.7 %copy-start.5 = (s32[1,4,26]{2,1,0:T(4,128)S(1)}, s32[1,4,26]{2,1,0:T(4,128)}, u32[]{:S(2)}) copy-start(s32[1,4,26]{2,1,0:T(4,128)} %param.12) | copy-start | bytes 1252
  1.3 0.7 %copy-start.6 = (bf16[16]{0:T(256)(128)(2,1)S(1)}, bf16[16]{0:T(256)(128)(2,1)}, u32[]{:S(2)}) copy-start(bf16[16]{0:T(256)(128)(2,1)} %param.14) | copy-start | bytes 100
  2.0 1.0 %copy-start = (bf16[1,4,8,8,512]{4,3,2,1,0:T(8,128)(2,1)S(1)}, bf16[1,4,8,8,512]{4,3,2,1,0:T(8,128)(2,1)}, u32[]{:S(2)}) copy-start(bf16[1,4,8,8,512]{4,3,2,1,0:T(8,128)(2,1)} %param.8) | copy-start | bytes 786436
  3.0 0.8 %copy-start.2 = (bf16[432,64]{0,1:T(8,128)(2,1)S(1)}, bf16[432,64]{0,1:T(8,128)(2,1)}, u32[]{:S(2)}) copy-start(bf16[432,64]{0,1:T(8,128)(2,1)} %param.13) | copy-start | bytes 165892
  3.8 15.6 %copy-start.1 = (bf16[1,4,8,8,512]{4,3,2,1,0:T(8,128)(2,1)S(1)}, bf16[1,4,8,8,512]{4,3,2,1,0:T(8,128)(2,1)}, u32[]{:S(2)}) copy-start(bf16[1,4,8,8,512]{4,3,2,1,0:T(8,128)(2,1)} %param.15) | copy-start | bytes 786436
  6.2 8.5 %collective-permute-start.2 = (bf16[64,512]{1,0:T(8,128)(2,1)S(1)}, bf16[64,512]{1,0:T(8,128)(2,1)S(1)}, u32[]{:S(2)}, u32[]{:S(2)}) collective-permute-start(bf16[64,512]{1,0:T(8,128)(2,1)S(1)} %get-tuple-element.32.refs_0_), channel_id=1, source_target_pairs={{0,3},{1,2},{2,1},{3,0},{4,7},{5,6},{6,5},{7,4},{8,11},{9,10},{10,... | collective-permute-start | bytes 196616 | tf_op jit(solution)/shard_map/ppermute | solution.py:440
  8.6 6.8 %collective-permute-start.1 = (bf16[64,512]{1,0:T(8,128)(2,1)S(1)}, bf16[64,512]{1,0:T(8,128)(2,1)S(1)}, u32[]{:S(2)}, u32[]{:S(2)}) collective-permute-start(bf16[64,512]{1,0:T(8,128)(2,1)S(1)} %get-tuple-element.32.refs_0_), channel_id=1, source_target_pairs={{0,2},{1,3},{2,0},{3,1},{4,6},{5,7},{6,4},{7,5},{8,10},{9,11},{10,... | collective-permute-start | bytes 196616 | tf_op jit(solution)/shard_map/ppermute | solution.py:440
  9.3 7.9 %collective-permute-start.3 = (bf16[384,128]{1,0:T(8,128)(2,1)S(1)}, bf16[384,128]{1,0:T(8,128)(2,1)S(1)}, u32[]{:S(2)}, u32[]{:S(2)}) collective-permute-start(bf16[384,128]{1,0:T(8,128)(2,1)S(1)} %get-tuple-element.38), channel_id=1, source_target_pairs={{0,4},{4,0},{8,12},{12,8},{16,20},{20,16},{24,28},{28,24},{1,5},{5... | collective-permute-start | bytes 294920 | tf_op jit(solution)/shard_map/ppermute | solution.py:453
  10.8 6.4 %collective-permute-start.4 = (bf16[384,128]{1,0:T(8,128)(2,1)S(1)}, bf16[384,128]{1,0:T(8,128)(2,1)S(1)}, u32[]{:S(2)}, u32[]{:S(2)}) collective-permute-start(bf16[384,128]{1,0:T(8,128)(2,1)S(1)} %get-tuple-element.39), channel_id=1, source_target_pairs={{4,8},{8,4},{12,16},{16,12},{20,24},{24,20},{5,9},{9,5},{13,17},{1... | collective-permute-start | bytes 294920 | tf_op jit(solution)/shard_map/ppermute | solution.py:453
  11.5 7.9 %collective-permute-start.5 = (bf16[384,128]{1,0:T(8,128)(2,1)S(1)}, bf16[384,128]{1,0:T(8,128)(2,1)S(1)}, u32[]{:S(2)}, u32[]{:S(2)}) collective-permute-start(bf16[384,128]{1,0:T(8,128)(2,1)S(1)} %get-tuple-element.40), channel_id=1, source_target_pairs={{0,8},{8,0},{4,12},{12,4},{16,24},{24,16},{20,28},{28,20},{1,9},{9... | collective-permute-start | bytes 294920 | tf_op jit(solution)/shard_map/ppermute | solution.py:453
  14.7 4.6 %collective-permute-start.6 = (bf16[384,128]{1,0:T(8,128)(2,1)S(1)}, bf16[384,128]{1,0:T(8,128)(2,1)S(1)}, u32[]{:S(2)}, u32[]{:S(2)}) collective-permute-start(bf16[384,128]{1,0:T(8,128)(2,1)S(1)} %get-tuple-element.41), channel_id=1, source_target_pairs={{8,16},{16,8},{12,20},{20,12},{9,17},{17,9},{13,21},{21,13},{10,18... | collective-permute-start | bytes 294920 | tf_op jit(solution)/shard_map/ppermute | solution.py:453
  15.4 1.3 %collective-permute-start = (bf16[64,512]{1,0:T(8,128)(2,1)S(1)}, bf16[64,512]{1,0:T(8,128)(2,1)S(1)}, u32[]{:S(2)}, u32[]{:S(2)}) collective-permute-start(bf16[64,512]{1,0:T(8,128)(2,1)S(1)} %get-tuple-element.32.refs_0_), channel_id=1, source_target_pairs={{0,1},{1,0},{2,3},{3,2},{4,5},{5,4},{6,7},{7,6},{8,9},{9,8},{10,11... | collective-permute-start | bytes 196616 | tf_op jit(solution)/shard_map/ppermute | solution.py:440
  24.7 1.9 %collective-permute-start.11 = (bf16[64,512]{1,0:T(8,128)(2,1)S(1)}, bf16[64,512]{1,0:T(8,128)(2,1)S(1)}, u32[]{:S(2)}, u32[]{:S(2)}) collective-permute-start(bf16[64,512]{1,0:T(8,128)(2,1)S(1)} %get-tuple-element.51), channel_id=1, source_target_pairs={{0,1},{1,0},{2,3},{3,2},{4,5},{5,4},{6,7},{7,6},{8,9},{9,8},{10,11... | collective-permute-start | bytes 196616 | tf_op jit(solution)/shard_map/ppermute | solution.py:440
  24.7 4.5 %collective-permute-start.12 = (bf16[64,512]{1,0:T(8,128)(2,1)S(1)}, bf16[64,512]{1,0:T(8,128)(2,1)S(1)}, u32[]{:S(2)}, u32[]{:S(2)}) collective-permute-start(bf16[64,512]{1,0:T(8,128)(2,1)S(1)} %get-tuple-element.52), channel_id=1, source_target_pairs={{0,2},{1,3},{2,0},{3,1},{4,6},{5,7},{6,4},{7,5},{8,10},{9,11},{10,... | collective-permute-start | bytes 196616 | tf_op jit(solution)/shard_map/ppermute | solution.py:440
  26.4 4.1 %collective-permute-start.13 = (bf16[64,512]{1,0:T(8,128)(2,1)S(1)}, bf16[64,512]{1,0:T(8,128)(2,1)S(1)}, u32[]{:S(2)}, u32[]{:S(2)}) collective-permute-start(bf16[64,512]{1,0:T(8,128)(2,1)S(1)} %get-tuple-element.53), channel_id=1, source_target_pairs={{0,3},{1,2},{2,1},{3,0},{4,7},{5,6},{6,5},{7,4},{8,11},{9,10},{10,... | collective-permute-start | bytes 196616 | tf_op jit(solution)/shard_map/ppermute | solution.py:440
  30.5 4.3 %collective-permute-start.14 = (bf16[64,512]{1,0:T(8,128)(2,1)S(1)}, bf16[64,512]{1,0:T(8,128)(2,1)S(1)}, u32[]{:S(2)}, u32[]{:S(2)}) collective-permute-start(bf16[64,512]{1,0:T(8,128)(2,1)S(1)} %add_convert_fusion.2), channel_id=1, source_target_pairs={{0,4},{4,0},{8,12},{12,8},{16,20},{20,16},{24,28},{28,24},{1,5},{5... | collective-permute-start | bytes 196616 | tf_op jit(solution)/shard_map/ppermute | solution.py:440
  34.8 9.3 %collective-permute-start.15 = (bf16[64,512]{1,0:T(8,128)(2,1)S(1)}, bf16[64,512]{1,0:T(8,128)(2,1)S(1)}, u32[]{:S(2)}, u32[]{:S(2)}) collective-permute-start(bf16[64,512]{1,0:T(8,128)(2,1)S(1)} %add_convert_fusion.1), channel_id=1, source_target_pairs={{0,8},{4,12},{8,0},{12,4},{16,24},{20,28},{24,16},{28,20},{1,9},{5... | collective-permute-start | bytes 196616 | tf_op jit(solution)/shard_map/ppermute | solution.py:440
  38.0 9.0 %collective-permute-start.7 = (bf16[384,128]{1,0:T(8,128)(2,1)S(1)}, bf16[384,128]{1,0:T(8,128)(2,1)S(1)}, u32[]{:S(2)}, u32[]{:S(2)}) collective-permute-start(bf16[384,128]{1,0:T(8,128)(2,1)S(1)} %get-tuple-element.46), channel_id=1, source_target_pairs={{0,4},{4,0},{8,12},{12,8},{16,20},{20,16},{24,28},{28,24},{1,5},{5... | collective-permute-start | bytes 294920 | tf_op jit(solution)/shard_map/ppermute | solution.py:453
  39.8 7.1 %collective-permute-start.8 = (bf16[384,128]{1,0:T(8,128)(2,1)S(1)}, bf16[384,128]{1,0:T(8,128)(2,1)S(1)}, u32[]{:S(2)}, u32[]{:S(2)}) collective-permute-start(bf16[384,128]{1,0:T(8,128)(2,1)S(1)} %get-tuple-element.47), channel_id=1, source_target_pairs={{4,8},{8,4},{12,16},{16,12},{20,24},{24,20},{5,9},{9,5},{13,17},{1... | collective-permute-start | bytes 294920 | tf_op jit(solution)/shard_map/ppermute | solution.py:453
  40.5 6.6 %collective-permute-start.9 = (bf16[384,128]{1,0:T(8,128)(2,1)S(1)}, bf16[384,128]{1,0:T(8,128)(2,1)S(1)}, u32[]{:S(2)}, u32[]{:S(2)}) collective-permute-start(bf16[384,128]{1,0:T(8,128)(2,1)S(1)} %get-tuple-element.48), channel_id=1, source_target_pairs={{0,8},{8,0},{4,12},{12,4},{16,24},{24,16},{20,28},{28,20},{1,9},{9... | collective-permute-start | bytes 294920 | tf_op jit(solution)/shard_map/ppermute | solution.py:453
  43.4 3.7 %collective-permute-start.10 = (bf16[384,128]{1,0:T(8,128)(2,1)S(1)}, bf16[384,128]{1,0:T(8,128)(2,1)S(1)}, u32[]{:S(2)}, u32[]{:S(2)}) collective-permute-start(bf16[384,128]{1,0:T(8,128)(2,1)S(1)} %get-tuple-element.49), channel_id=1, source_target_pairs={{8,16},{16,8},{12,20},{20,12},{9,17},{17,9},{13,21},{21,13},{10,18... | collective-permute-start | bytes 294920 | tf_op jit(solution)/shard_map/ppermute | solution.py:453
  44.1 6.7 %collective-permute-start.16 = (bf16[64,512]{1,0:T(8,128)(2,1)S(1)}, bf16[64,512]{1,0:T(8,128)(2,1)S(1)}, u32[]{:S(2)}, u32[]{:S(2)}) collective-permute-start(bf16[64,512]{1,0:T(8,128)(2,1)S(1)} %add_convert_fusion.mine), channel_id=1, source_target_pairs={{0,16},{4,20},{8,24},{12,28},{16,0},{20,4},{24,8},{28,12},{1,17},{... | collective-permute-start | bytes 196616 | tf_op jit(solution)/shard_map/ppermute | solution.py:440

commit v3 on v2

--- a/solution.py
+++ b/solution.py
@@ -12,6 +12,7 @@
 LANES = 128
 UNIT_ROWS = 32
 Z_ROWS = 64
+SWAPS = ((1, 0), (2, 0), (2, 1), (1, 1))
 DN_NT = (((1,), (1,)), ((), ()))
 DN_NN = (((1,), (0,)), ((), ()))
 
@@ -22,6 +23,10 @@
 
 def smem():
     return pl.BlockSpec(memory_space=pltpu.SMEM)
+
+
+def untouched():
+    return pl.BlockSpec(memory_space=pl.ANY)
 
 
 def offset_number(ox, oy, oz):
@@ -49,8 +54,8 @@
     for number, out in enumerate(outs):
         column = reach
         if number > 0:
-            distance = (number + 1) // 2
-            up = upward(device, distance) == (number + 1) % 2
+            distance, turn = SWAPS[number - 1]
+            up = upward(device, distance) == turn
             column = jnp.where(up, reach + distance, reach - distance)
 
         def base(link):
@@ -75,16 +80,15 @@
 
 
 def prepare_kernel(
-    features_hbm, occupancy_hbm, counts_hbm, send_hbm, listing_hbm, weight_hbm, bias_hbm,
+    features_hbm, occupancy_hbm, send_hbm, listing_hbm, weight_hbm, bias_hbm, counts,
     masked_out, mask_out, rows_out, send_out, shard_out, u0, u1, u2, u3, u4,
-    values, features, occupancy, counts, listing, weight_t, bias, rows, sems,
+    values, features, occupancy, listing, weight_t, bias, rows, sems,
 ):
     copies = [
         pltpu.make_async_copy(src, dst, sems.at[i])
         for i, (src, dst) in enumerate(
             (
                 (occupancy_hbm, occupancy),
-                (counts_hbm, counts),
                 (features_hbm, features),
                 (send_hbm, send_out),
                 (listing_hbm, listing),
@@ -106,7 +110,6 @@
     expand = jnp.where(z_row == z_col, 1.0, 0.0).astype(BF16)
 
     copies[0].wait()
-    copies[1].wait()
     live = lax.broadcasted_iota(jnp.int32, (bricks, 512), 0) < counts[0, 0]
     occ = jnp.where(live, occupancy[...], 0).astype(F32)
     spread = jnp.concatenate(
@@ -114,15 +117,15 @@
     ).astype(BF16)
     mask = jnp.dot(spread, expand, preferred_element_type=F32)
     mask_out[...] = mask.astype(BF16).reshape(mask_out.shape)
-    copies[2].wait()
+    copies[1].wait()
     value = features[...].astype(F32).reshape(bricks * 64, 512) * mask
     masked_out[...] = value.astype(BF16).reshape(masked_out.shape)
     for q in range(4):
         values[q, 0 : bricks * 64, :] = value[:, q * LANES : (q + 1) * LANES]
+    copies[2].wait()
+    pack_units(values, send_out, (u0, u1, u2, u3, u4))
+
     copies[3].wait()
-    pack_units(values, send_out, (u0, u1, u2, u3, u4))
-
-    copies[4].wait()
     device = lax.axis_index("space")
     number = listing[...]
     column = (number * 43) >> 9
@@ -132,8 +135,9 @@
     block = jnp.zeros(number.shape, jnp.int32)
     for distance in (1, 2):
         up = upward(device, distance)
-        block = jnp.where(column == 2 - distance, 2 * distance - 1 + up, block)
-        block = jnp.where(column == 2 + distance, 2 * distance - up, block)
+        even, odd = (SWAPS.index((distance, turn)) + 1 for turn in range(2))
+        block = jnp.where(column == 2 - distance, jnp.where(up == 0, even, odd), block)
+        block = jnp.where(column == 2 + distance, jnp.where(up == 0, odd, even), block)
     base = block * (8 * UNIT_ROWS + 2 * Z_ROWS)
     plain = base + (half * 4 + face) * UNIT_ROWS
     paired = base + 8 * UNIT_ROWS + half * Z_ROWS
@@ -142,8 +146,8 @@
     last = pltpu.make_async_copy(rows, rows_out, sems.at[len(copies)])
     last.start()
 
+    copies[4].wait()
     copies[5].wait()
-    copies[6].wait()
     shard = weight_t.shape[1]
     lead = shard // LANES * LANES
     count = bias.shape[1]
@@ -399,13 +403,23 @@
                 chunk_outs[m][...] = block
 
 
-def backward_kernel(
-    grad, mask, toeplitz, rows, r0, r1, r2, r3, r4, out, table, windows, sides, walls
-):
-    bricks = grad.shape[0]
-    pairs = bricks // 2
+def assemble_kernel(grad, rows, r0, r1, r2, r3, r4, after, windows, table, sides, walls):
+    del after
     gather_units(table, (r0, r1, r2, r3, r4))
     assemble(grad, table, rows, windows, sides, walls)
+
+
+def sum_kernel(*refs, terms):
+    total = refs[0][...].astype(F32)
+    for share in refs[1:terms]:
+        total += share[...].astype(F32)
+    refs[terms + 4][...] = total.astype(BF16)
+
+
+def backward_kernel(windows, mask, toeplitz, after, out):
+    del after
+    bricks = mask.shape[0]
+    pairs = bricks // 2
 
     def one_chunk(q, carry):
         total = jnp.zeros((pairs * LANES, LANES), F32)
@@ -440,18 +454,13 @@
     return lax.ppermute(block, axis, [(i, i ^ bit) for i in range(lax.axis_size(axis))])
 
 
-def exchanged(units):
-    devices = lax.axis_size("space")
-    received = [units[0]]
-    for number in range(1, len(units)):
-        distance = (number + 1) // 2
-        turn = (number + 1) % 2
-        route = []
-        for low in range(devices - distance):
-            if low // distance % 2 == turn:
-                route += [(low, low + distance), (low + distance, low)]
-        received.append(lax.ppermute(units[number], "space", route))
-    return received
+def exchanged(number, unit):
+    distance, turn = SWAPS[number - 1]
+    route = []
+    for low in range(lax.axis_size("space") - distance):
+        if low // distance % 2 == turn:
+            route += [(low, low + distance), (low + distance, low)]
+    return lax.ppermute(unit, "space", route)
 
 
 def body(features, occupancy, counts, send_units, neighbours, weight, conv_bias, cotangent):
@@ -482,32 +491,36 @@
             shard_type,
         ]
         + [units_type] * spread,
-        in_specs=[pl.BlockSpec(memory_space=pltpu.HBM)] * 7,
+        in_specs=[pl.BlockSpec(memory_space=pltpu.HBM)] * 6 + [smem()],
         out_specs=[vmem(), vmem(), smem(), smem(), vmem()] + [vmem()] * spread,
         scratch_shapes=[
             pltpu.VMEM((4, (bricks + 1) * 64, LANES), F32),
             pltpu.VMEM(grid_shape, BF16),
             pltpu.VMEM(occupancy.shape[1:], jnp.int32),
-            pltpu.SMEM((1, 1), jnp.int32),
             pltpu.VMEM(rows_shape, jnp.int32),
             pltpu.VMEM((channels, shard), BF16),
             pltpu.VMEM((1, count), BF16),
             pltpu.VMEM(rows_shape, jnp.int32),
-            pltpu.SemaphoreType.DMA((8,)),
+            pltpu.SemaphoreType.DMA((7,)),
         ],
         compiler_params=params,
     )(
-        features[0],
-        occupancy[0],
+        *(
+            pltpu.with_memory_space_constraint(operand, pltpu.HBM)
+            for operand in (
+                features[0],
+                occupancy[0],
+                send_units.transpose(0, 2, 1, 3).reshape(send_shape),
+                neighbours[0],
+                weight.T,
+                conv_bias.reshape(1, count),
+            )
+        ),
         counts,
-        send_units.transpose(0, 2, 1, 3).reshape(send_shape),
-        neighbours[0],
-        weight.T,
-        conv_bias.reshape(1, count),
     )
 
     shards = [own_shard] + [swapped(own_shard, "dp", m) for m in range(1, groups)]
-    received = exchanged(units)
+    received = units[:1] + [exchanged(number, units[number]) for number in range(1, spread)]
 
     flat = pltpu.VMEM((channels, 28 * 64), F32)
     band_forward, band_backward, bias = pl.pallas_call(
@@ -549,24 +562,50 @@
     grad_units, blocks = rest[:spread], rest[spread:]
 
     shares = [blocks[0]] + [swapped(blocks[m], "dp", m) for m in range(1, groups)]
-    grad_received = exchanged(grad_units)
-
+    grad_received = grad_units[:1] + [exchanged(n, grad_units[n]) for n in range(1, 3)]
+    total, *later = pl.pallas_call(
+        functools.partial(sum_kernel, terms=groups),
+        name="sum",
+        out_shape=[shard_type, units_type, units_type],
+        in_specs=[vmem()] * groups + [untouched()] * 4,
+        out_specs=[vmem(), untouched(), untouched()],
+        input_output_aliases={groups: 1, groups + 1: 2},
+        compiler_params=params,
+    )(*shares, *grad_units[3:], *grad_received[1:])
+    steps = []
+    bit = 1
+    while bit < lax.axis_size("space"):
+        steps.append(bit)
+        bit *= 2
+
+    def stepped(total, bit):
+        return (total.astype(F32) + swapped(total, "space", bit).astype(F32)).astype(BF16)
+
+    for bit in steps[:-1][:1]:
+        total = stepped(total, bit)
+    grad_received += [exchanged(n, unit) for n, unit in zip(range(3, spread), later)]
+
+    padded_grad = pl.pallas_call(
+        assemble_kernel,
+        name="assemble",
+        out_shape=jax.ShapeDtypeStruct(windows.shape, BF16),
+        in_specs=[vmem()] + [smem()] + [vmem()] * spread + [untouched()],
+        out_specs=vmem(),
+        scratch_shapes=[table, sides, walls],
+        compiler_params=params,
+    )(grad, rows, *grad_received, total)
+
+    for bit in steps[1:-1]:
+        total = stepped(total, bit)
     grad_input = pl.pallas_call(
         backward_kernel,
         name="backward",
         out_shape=grid_type,
-        in_specs=[vmem()] * 3 + [smem()] + [vmem()] * spread,
+        in_specs=[vmem()] * 3 + [untouched()],
         out_specs=vmem(),
-        scratch_shapes=[table, windows, sides, walls],
         compiler_params=params,
-    )(grad, mask, band_backward, rows, *grad_received)
-
-    total = sum(share.astype(F32) for share in shares).astype(BF16)
-    devices = lax.axis_size("space")
-    bit = 1
-    while 2 * bit < devices:
-        total = (total.astype(F32) + swapped(total, "space", bit).astype(F32)).astype(BF16)
-        bit *= 2
+    )(padded_grad, mask, band_backward, total)
+
     weight_share, bias_share = pl.pallas_call(
         finish_kernel,
         name="finish",
@@ -577,7 +616,7 @@
         in_specs=[vmem()] * 2,
         out_specs=[vmem()] * 2,
         compiler_params=params,
-    )(total, swapped(total, "space", bit))
+    )(total, swapped(total, "space", steps[-1]))
     return (
         block_output[None],
         grad_input[None],

time: 52.2 us -> 53.7 us (1.029)
  starting transfers between devices: 24.2 us -> 25.8 us
  local copies, waits for them, and re-layouts: 2.46 us -> 0.95 us
  waiting for transfers between devices: 10.8 us -> 11.8 us
    ppermute x9, waiting for transfers between devices: 8.37 us -> 11.8 us  [swapped(): lax.ppermute(block, axis, [(i, i ^ bit) for i in range(lax.axis_size(axis...]
    ppermute x8, waiting for transfers between devices: 2.44 us -> 0.02 us  [exchanged(): return lax.ppermute(unit, 'space', route)]
    unnamed x14 -> x2, local copies, waits for them, and re-layouts: 2.46 us -> 0.95 us
    pallas_call x0 -> x2, Pallas kernels: none -> 1.15 us  [the longest x1 1.11 us: body(): pl.pallas_call(assemble_kernel, name='assemble', out_shape=jax.ShapeDtype...]
    ppermute x9, starting transfers between devices: 12 us -> 13.1 us  [swapped(): lax.ppermute(block, axis, [(i, i ^ bit) for i in range(lax.axis_size(axis...]
    pallas_call x1, Pallas kernels: 3.68 us -> 2.57 us  [body(): pl.pallas_call(backward_kernel, name='backward', out_shape=grid_type, in_...]
  transfers between devices with their start and end apart: 17 -> 17, of which waited for: 6 -> 5; matrix products, arithmetic and copies ran while one was open for 0% -> 0% of each run, Pallas kernels for 8% -> 8%
where the time goes in v3:
time: 53.7 us; the launch traced here: 52.7 us
  starting transfers between devices  25.8 us (48%)
  Pallas kernels  12.7 us (24%)
  waiting for transfers between devices  11.8 us (22%)
  between operations  1.4 us (3%)
  local copies, waits for them, and re-layouts  0.95 us (2%)
    ppermute x9, starting transfers between devices, swapped(): lax.ppermute(block, axis, [(i, i ^ bit) for i in range(lax.axis_size(axis...  13.1 us
    ppermute x8, starting transfers between devices, exchanged(): return lax.ppermute(unit, 'space', route)  12.7 us
    ppermute x9, waiting for transfers between devices, swapped(): lax.ppermute(block, axis, [(i, i ^ bit) for i in range(lax.axis_size(axis...  11.8 us
    pallas_call x1, Pallas kernels, body(): pl.pallas_call(functools.partial(forward_kernel, shard=shard), name='forw...  5.36 us
    pallas_call x1, Pallas kernels, body(): pl.pallas_call(backward_kernel, name='backward', out_shape=grid_type, in_...  2.57 us
    pallas_call x1, Pallas kernels, body(): pl.pallas_call(prepare_kernel, name='prepare', out_shape=[grid_type, grid...  2.52 us
    pallas_call x1, Pallas kernels, body(): pl.pallas_call(assemble_kernel, name='assemble', out_shape=jax.ShapeDtype...  1.11 us
  transfers between devices with their start and end apart: 17, of which 5 were waited for; matrix products, arithmetic and copies ran while one was open for 0% of the time, Pallas kernels for 8%

profile of v3, /device:TPU:0, one launch (start us, length us, event | category | flops | bytes accessed | tf_op | source)
XLA Modules:
  0.0 52.7 jit_solution(16105296569185377016)
XLA Ops:
  1.3 2.5 %prepare.1 = (bf16[4,8,8,512]{3,2,1,0:T(8,128)(2,1)S(1)}, bf16[4,8,8,512]{3,2,1,0:T(8,128)(2,1)S(1)}, s32[4,26]{1,0:T(4,128)S(1)}, s32[5,1,12]{2,1,0:T(1,128)S(1...) custom-call(bf16[4,8,8,512]{3,2,1,0:T(8,128)(2,1)} %bitcast.13, ...), custom_call_target="tpu_custom_call" | custom-call | tf_op jit(solution)/shard_map/prepare/pallas_call | solution.py:483
  3.8 0.5 collective-permute-start
  4.3 2.6 %collective-permute-start.1 = (bf16[64,512]{1,0:T(8,128)(2,1)S(1)}, bf16[64,512]{1,0:T(8,128)(2,1)S(1)}, u32[]{:S(2)}, u32[]{:S(2)}) collective-permute-start(bf16[64,512]{1,0:T(8,128)(2,1)S(1)} %get-tuple-element.35.refs_0_), channel_id=1, source_target_pairs={{0,2},{1,3},{2,0},{3,1},{4,6},{5,7},{6,4},{7,5},{8,10},{9,11},{10,... | collective-permute-start | bytes 196616 | tf_op jit(solution)/shard_map/ppermute | solution.py:454
  6.9 1.5 %collective-permute-start.3 = (bf16[384,128]{1,0:T(8,128)(2,1)S(1)}, bf16[384,128]{1,0:T(8,128)(2,1)S(1)}, u32[]{:S(2)}, u32[]{:S(2)}) collective-permute-start(bf16[384,128]{1,0:T(8,128)(2,1)S(1)} %get-tuple-element.41), channel_id=1, source_target_pairs={{0,4},{4,0},{8,12},{12,8},{16,20},{20,16},{24,28},{28,24},{1,5},{5... | collective-permute-start | bytes 294920 | tf_op jit(solution)/shard_map/ppermute | solution.py:463
  8.4 1.6 %collective-permute-start.4 = (bf16[384,128]{1,0:T(8,128)(2,1)S(1)}, bf16[384,128]{1,0:T(8,128)(2,1)S(1)}, u32[]{:S(2)}, u32[]{:S(2)}) collective-permute-start(bf16[384,128]{1,0:T(8,128)(2,1)S(1)} %get-tuple-element.42), channel_id=1, source_target_pairs={{0,8},{8,0},{4,12},{12,4},{16,24},{24,16},{20,28},{28,20},{1,9},{9... | collective-permute-start | bytes 294920 | tf_op jit(solution)/shard_map/ppermute | solution.py:463
  10.0 0.7 %collective-permute-start.5 = (bf16[384,128]{1,0:T(8,128)(2,1)S(1)}, bf16[384,128]{1,0:T(8,128)(2,1)S(1)}, u32[]{:S(2)}, u32[]{:S(2)}) collective-permute-start(bf16[384,128]{1,0:T(8,128)(2,1)S(1)} %get-tuple-element.43), channel_id=1, source_target_pairs={{8,16},{16,8},{12,20},{20,12},{9,17},{17,9},{13,21},{21,13},{10,18... | collective-permute-start | bytes 294920 | tf_op jit(solution)/shard_map/ppermute | solution.py:463
  10.6 0.0 collective-permute-done.refs_1_
  10.7 0.7 %collective-permute-start.6 = (bf16[384,128]{1,0:T(8,128)(2,1)S(1)}, bf16[384,128]{1,0:T(8,128)(2,1)S(1)}, u32[]{:S(2)}, u32[]{:S(2)}) collective-permute-start(bf16[384,128]{1,0:T(8,128)(2,1)S(1)} %get-tuple-element.44), channel_id=1, source_target_pairs={{4,8},{8,4},{12,16},{16,12},{20,24},{24,20},{5,9},{9,5},{13,17},{1... | collective-permute-start | bytes 294920 | tf_op jit(solution)/shard_map/ppermute | solution.py:463
  11.3 0.0 collective-permute-done.1.refs_2_
  11.3 0.1 collective-permute-start.2
  11.4 4.2 %collective-permute-done.2.refs_3_ = bf16[64,512]{1,0:T(8,128)(2,1)S(1)} collective-permute-done((bf16[64,512]{1,0:T(8,128)(2,1)S(1)}, bf16[64,512]{1,0:T(8,128)(2,1)S(1)}, u32[]{:S(2)}, u32[]{:S(2)}) %collective-permute-start.2) | collective-permute-done | bytes 65568 | tf_op jit(solution)/shard_map/ppermute | solution.py:454
  15.6 0.4 weights.1
  16.0 0.0 collective-permute-done.3.r1
  16.0 0.0 collective-permute-done.4.r2
  16.0 0.0 collective-permute-done.5.r3
  16.0 0.0 collective-permute-done.6.r4
  16.0 0.0 copy-start
  16.0 0.9 %copy-done = bf16[1,4,8,8,512]{4,3,2,1,0:T(8,128)(2,1)S(1)} copy-done((bf16[1,4,8,8,512]{4,3,2,1,0:T(8,128)(2,1)S(1)}, bf16[1,4,8,8,512]{4,3,2,1,0:T(8,128)(2,1)}, u32[]{:S(2)}) %copy-start) | copy-done | bytes 262168
  17.0 5.4 %forward.1 = (bf16[4,8,8,512]{3,2,1,0:T(8,128)(2,1)}, bf16[4,8,8,512]{3,2,1,0:T(8,128)(2,1)S(1)}, bf16[384,128]{1,0:T(8,128)(2,1)S(1)}, bf16[384,128]{1,0:T(8,12...) custom-call(bf16[4,8,8,512]{3,2,1,0:T(8,128)(2,1)S(1)} %get-tuple-el, ...), custom_call_target="tpu_custom_call" | custom-call | tf_op jit(solution)/shard_map/forward/pallas_call | solution.py:544
  22.3 6.6 %collective-permute-start.7 = (bf16[384,128]{1,0:T(8,128)(2,1)S(1)}, bf16[384,128]{1,0:T(8,128)(2,1)S(1)}, u32[]{:S(2)}, u32[]{:S(2)}) collective-permute-start(bf16[384,128]{1,0:T(8,128)(2,1)S(1)} %get-tuple-element.48), channel_id=1, source_target_pairs={{0,4},{4,0},{8,12},{12,8},{16,20},{20,16},{24,28},{28,24},{1,5},{5... | collective-permute-start | bytes 294920 | tf_op jit(solution)/shard_map/ppermute | solution.py:463
  29.0 0.3 collective-permute-start.8
  29.3 0.0 collective-permute-start.9
  29.3 0.9 %collective-permute-start.10 = (bf16[64,512]{1,0:T(8,128)(2,1)S(1)}, bf16[64,512]{1,0:T(8,128)(2,1)S(1)}, u32[]{:S(2)}, u32[]{:S(2)}) collective-permute-start(bf16[64,512]{1,0:T(8,128)(2,1)S(1)} %get-tuple-element.52), channel_id=1, source_target_pairs={{0,2},{1,3},{2,0},{3,1},{4,6},{5,7},{6,4},{7,5},{8,10},{9,11},{10,... | collective-permute-start | bytes 196616 | tf_op jit(solution)/shard_map/ppermute | solution.py:454
  30.2 1.0 %collective-permute-start.11 = (bf16[64,512]{1,0:T(8,128)(2,1)S(1)}, bf16[64,512]{1,0:T(8,128)(2,1)S(1)}, u32[]{:S(2)}, u32[]{:S(2)}) collective-permute-start(bf16[64,512]{1,0:T(8,128)(2,1)S(1)} %get-tuple-element.53), channel_id=1, source_target_pairs={{0,3},{1,2},{2,1},{3,0},{4,7},{5,6},{6,5},{7,4},{8,11},{9,10},{10,... | collective-permute-start | bytes 196616 | tf_op jit(solution)/shard_map/ppermute | solution.py:454
  31.1 0.0 collective-permute-done.9.refs_1_
  31.2 3.0 %collective-permute-done.10.refs_2_ = bf16[64,512]{1,0:T(8,128)(2,1)S(1)} collective-permute-done((bf16[64,512]{1,0:T(8,128)(2,1)S(1)}, bf16[64,512]{1,0:T(8,128)(2,1)S(1)}, u32[]{:S(2)}, u32[]{:S(2)}) %collective-permute-start.10) | collective-permute-done | bytes 65568 | tf_op jit(solution)/shard_map/ppermute | solution.py:454
  34.2 0.6 %collective-permute-done.11.refs_3_ = bf16[64,512]{1,0:T(8,128)(2,1)S(1)} collective-permute-done((bf16[64,512]{1,0:T(8,128)(2,1)S(1)}, bf16[64,512]{1,0:T(8,128)(2,1)S(1)}, u32[]{:S(2)}, u32[]{:S(2)}) %collective-permute-start.11) | collective-permute-done | bytes 65568 | tf_op jit(solution)/shard_map/ppermute | solution.py:454
  34.8 0.0 collective-permute-done.7.refs_6_.r1
  34.8 0.0 collective-permute-done.8.refs_7_.r2
  34.9 1.6 %collective-permute-start.14 = (bf16[64,512]{1,0:T(8,128)(2,1)S(1)}, bf16[64,512]{1,0:T(8,128)(2,1)S(1)}, u32[]{:S(2)}, u32[]{:S(2)}) collective-permute-start(bf16[64,512]{1,0:T(8,128)(2,1)S(1)} %get-tuple-element.58), channel_id=1, source_target_pairs={{0,4},{4,0},{8,12},{12,8},{16,20},{20,16},{24,28},{28,24},{1,5},{5... | collective-permute-start | bytes 196616 | tf_op jit(solution)/shard_map/ppermute | solution.py:454
  36.4 2.8 %collective-permute-done.14 = bf16[64,512]{1,0:T(8,128)(2,1)S(1)} collective-permute-done((bf16[64,512]{1,0:T(8,128)(2,1)S(1)}, bf16[64,512]{1,0:T(8,128)(2,1)S(1)}, u32[]{:S(2)}, u32[]{:S(2)}) %collective-permute-start.14) | collective-permute-done | bytes 65568 | tf_op jit(solution)/shard_map/ppermute | solution.py:454
  39.2 1.8 %collective-permute-start.15 = (bf16[64,512]{1,0:T(8,128)(2,1)S(1)}, bf16[64,512]{1,0:T(8,128)(2,1)S(1)}, u32[]{:S(2)}, u32[]{:S(2)}) collective-permute-start(bf16[64,512]{1,0:T(8,128)(2,1)S(1)} %add_convert_fusion.1.after), channel_id=1, source_target_pairs={{0,8},{4,12},{8,0},{12,4},{16,24},{20,28},{24,16},{28,20},{1,9},{5... | collective-permute-start | bytes 196616 | tf_op jit(solution)/shard_map/ppermute | solution.py:454
  41.0 0.7 %collective-permute-start.12 = (bf16[384,128]{1,0:T(8,128)(2,1)S(1)}, bf16[384,128]{1,0:T(8,128)(2,1)S(1)}, u32[]{:S(2)}, u32[]{:S(2)}) collective-permute-start(bf16[384,128]{1,0:T(8,128)(2,1)S(1)} %get-tuple-element.56), channel_id=1, source_target_pairs={{8,16},{16,8},{12,20},{20,12},{9,17},{17,9},{13,21},{21,13},{10,18... | collective-permute-start | bytes 294920 | tf_op jit(solution)/shard_map/ppermute | solution.py:463
  41.7 0.7 %collective-permute-start.13 = (bf16[384,128]{1,0:T(8,128)(2,1)S(1)}, bf16[384,128]{1,0:T(8,128)(2,1)S(1)}, u32[]{:S(2)}, u32[]{:S(2)}) collective-permute-start(bf16[384,128]{1,0:T(8,128)(2,1)S(1)} %get-tuple-element.57), channel_id=1, source_target_pairs={{4,8},{8,4},{12,16},{16,12},{20,24},{24,20},{5,9},{9,5},{13,17},{1... | collective-permute-start | bytes 294920 | tf_op jit(solution)/shard_map/ppermute | solution.py:463
  42.3 1.2 %collective-permute-done.15 = bf16[64,512]{1,0:T(8,128)(2,1)S(1)} collective-permute-done((bf16[64,512]{1,0:T(8,128)(2,1)S(1)}, bf16[64,512]{1,0:T(8,128)(2,1)S(1)}, u32[]{:S(2)}, u32[]{:S(2)}) %collective-permute-start.15) | collective-permute-done | bytes 65568 | tf_op jit(solution)/shard_map/ppermute | solution.py:454
  43.6 4.7 %collective-permute-start.16 = (bf16[64,512]{1,0:T(8,128)(2,1)S(1)}, bf16[64,512]{1,0:T(8,128)(2,1)S(1)}, u32[]{:S(2)}, u32[]{:S(2)}) collective-permute-start(bf16[64,512]{1,0:T(8,128)(2,1)S(1)} %add_convert_fusion.after.mine), channel_id=1, source_target_pairs={{0,16},{4,20},{8,24},{12,28},{16,0},{20,4},{24,8},{28,12},{1,17},{... | collective-permute-start | bytes 196616 | tf_op jit(solution)/shard_map/ppermute | solution.py:454
  48.3 0.0 collective-permute-done.12.r3
  48.3 0.0 collective-permute-done.13.r4
  48.3 1.1 %assemble.1.windows = bf16[3,4,2,10,16,256]{5,4,3,2,1,0:T(8,128)(2,1)S(1)} custom-call(bf16[4,8,8,512]{3,2,1,0:T(8,128)(2,1)S(1)} %get-tuple-element.46.grad, s32[4,26]{1,0:T(4,128)S(1)} %get-tuple-element.38.rows, bf16[384,128]{1,0:T(8,128)(2,1)S(1)} %get-tuple-element.47.r0, bf16[384,128]{1,0:T(8,128)(2,1)S(1)} %collective-permute-done.7.refs_6_.r1, ...), custom_call_target="tpu_custom_call" | custom-call | tf_op jit(solution)/shard_map/assemble/pallas_call | solution.py:588
  49.4 2.6 %backward.1 = bf16[4,8,8,512]{3,2,1,0:T(8,128)(2,1)} custom-call(bf16[3,4,2,10,16,256]{5,4,3,2,1,0:T(8,128)(2,1)S(1)} %assemble.1.windows, bf16[4,8,8,512]{3,2,1,0:T(8,128)(2,1)S(1)} %get-tuple-element.34.mask, bf16[9,256,128]{2,1,0:T(8,128)(2,1)S(1)} %get-tuple-element.59.toeplitz, bf16[64,512]{1,0:T(8,128)(2,1)S(1)} %add_convert_fusion.after.mine), custom_call_target="tpu_custom_call" | custom-call | tf_op jit(solution)/shard_map/backward/pallas_call | solution.py:600
  52.0 0.0 collective-permute-done.16.other
  52.0 0.7 %finish.1 = (f32[64,432]{1,0:T(8,128)}, f32[1,16]{1,0:T(1,128)}) custom-call(bf16[64,512]{1,0:T(8,128)(2,1)S(1)} %add_convert_fusion.after.mine, bf16[64,512]{1,0:T(8,128)(2,1)S(1)} %collective-permute-done.16.other), custom_call_target="tpu_custom_call" | custom-call | tf_op jit(solution)/shard_map/finish/pallas_call | solution.py:609
  (3 shorter events, 0.1 us)
Async XLA Ops:
  3.8 6.8 %collective-permute-start = (bf16[64,512]{1,0:T(8,128)(2,1)S(1)}, bf16[64,512]{1,0:T(8,128)(2,1)S(1)}, u32[]{:S(2)}, u32[]{:S(2)}) collective-permute-start(bf16[64,512]{1,0:T(8,128)(2,1)S(1)} %get-tuple-element.35.refs_0_), channel_id=1, source_target_pairs={{0,1},{1,0},{2,3},{3,2},{4,5},{5,4},{6,7},{7,6},{8,9},{9,8},{10,11... | collective-permute-start | bytes 196616 | tf_op jit(solution)/shard_map/ppermute | solution.py:454
  4.3 7.0 %collective-permute-start.1 = (bf16[64,512]{1,0:T(8,128)(2,1)S(1)}, bf16[64,512]{1,0:T(8,128)(2,1)S(1)}, u32[]{:S(2)}, u32[]{:S(2)}) collective-permute-start(bf16[64,512]{1,0:T(8,128)(2,1)S(1)} %get-tuple-element.35.refs_0_), channel_id=1, source_target_pairs={{0,2},{1,3},{2,0},{3,1},{4,6},{5,7},{6,4},{7,5},{8,10},{9,11},{10,... | collective-permute-start | bytes 196616 | tf_op jit(solution)/shard_map/ppermute | solution.py:454
  6.9 9.1 %collective-permute-start.3 = (bf16[384,128]{1,0:T(8,128)(2,1)S(1)}, bf16[384,128]{1,0:T(8,128)(2,1)S(1)}, u32[]{:S(2)}, u32[]{:S(2)}) collective-permute-start(bf16[384,128]{1,0:T(8,128)(2,1)S(1)} %get-tuple-element.41), channel_id=1, source_target_pairs={{0,4},{4,0},{8,12},{12,8},{16,20},{20,16},{24,28},{28,24},{1,5},{5... | collective-permute-start | bytes 294920 | tf_op jit(solution)/shard_map/ppermute | solution.py:463
  8.4 7.6 %collective-permute-start.4 = (bf16[384,128]{1,0:T(8,128)(2,1)S(1)}, bf16[384,128]{1,0:T(8,128)(2,1)S(1)}, u32[]{:S(2)}, u32[]{:S(2)}) collective-permute-start(bf16[384,128]{1,0:T(8,128)(2,1)S(1)} %get-tuple-element.42), channel_id=1, source_target_pairs={{0,8},{8,0},{4,12},{12,4},{16,24},{24,16},{20,28},{28,20},{1,9},{9... | collective-permute-start | bytes 294920 | tf_op jit(solution)/shard_map/ppermute | solution.py:463
  10.0 6.0 %collective-permute-start.5 = (bf16[384,128]{1,0:T(8,128)(2,1)S(1)}, bf16[384,128]{1,0:T(8,128)(2,1)S(1)}, u32[]{:S(2)}, u32[]{:S(2)}) collective-permute-start(bf16[384,128]{1,0:T(8,128)(2,1)S(1)} %get-tuple-element.43), channel_id=1, source_target_pairs={{8,16},{16,8},{12,20},{20,12},{9,17},{17,9},{13,21},{21,13},{10,18... | collective-permute-start | bytes 294920 | tf_op jit(solution)/shard_map/ppermute | solution.py:463
  10.7 5.4 %collective-permute-start.6 = (bf16[384,128]{1,0:T(8,128)(2,1)S(1)}, bf16[384,128]{1,0:T(8,128)(2,1)S(1)}, u32[]{:S(2)}, u32[]{:S(2)}) collective-permute-start(bf16[384,128]{1,0:T(8,128)(2,1)S(1)} %get-tuple-element.44), channel_id=1, source_target_pairs={{4,8},{8,4},{12,16},{16,12},{20,24},{24,20},{5,9},{9,5},{13,17},{1... | collective-permute-start | bytes 294920 | tf_op jit(solution)/shard_map/ppermute | solution.py:463
  11.3 4.2 %collective-permute-start.2 = (bf16[64,512]{1,0:T(8,128)(2,1)S(1)}, bf16[64,512]{1,0:T(8,128)(2,1)S(1)}, u32[]{:S(2)}, u32[]{:S(2)}) collective-permute-start(bf16[64,512]{1,0:T(8,128)(2,1)S(1)} %get-tuple-element.35.refs_0_), channel_id=1, source_target_pairs={{0,3},{1,2},{2,1},{3,0},{4,7},{5,6},{6,5},{7,4},{8,11},{9,10},{10,... | collective-permute-start | bytes 196616 | tf_op jit(solution)/shard_map/ppermute | solution.py:454
  16.0 1.0 %copy-start = (bf16[1,4,8,8,512]{4,3,2,1,0:T(8,128)(2,1)S(1)}, bf16[1,4,8,8,512]{4,3,2,1,0:T(8,128)(2,1)}, u32[]{:S(2)}) copy-start(bf16[1,4,8,8,512]{4,3,2,1,0:T(8,128)(2,1)} %param.15) | copy-start | bytes 786436
  22.3 12.5 %collective-permute-start.7 = (bf16[384,128]{1,0:T(8,128)(2,1)S(1)}, bf16[384,128]{1,0:T(8,128)(2,1)S(1)}, u32[]{:S(2)}, u32[]{:S(2)}) collective-permute-start(bf16[384,128]{1,0:T(8,128)(2,1)S(1)} %get-tuple-element.48), channel_id=1, source_target_pairs={{0,4},{4,0},{8,12},{12,8},{16,20},{20,16},{24,28},{28,24},{1,5},{5... | collective-permute-start | bytes 294920 | tf_op jit(solution)/shard_map/ppermute | solution.py:463
  29.0 5.9 %collective-permute-start.8 = (bf16[384,128]{1,0:T(8,128)(2,1)S(1)}, bf16[384,128]{1,0:T(8,128)(2,1)S(1)}, u32[]{:S(2)}, u32[]{:S(2)}) collective-permute-start(bf16[384,128]{1,0:T(8,128)(2,1)S(1)} %get-tuple-element.49), channel_id=1, source_target_pairs={{0,8},{8,0},{4,12},{12,4},{16,24},{24,16},{20,28},{28,20},{1,9},{9... | collective-permute-start | bytes 294920 | tf_op jit(solution)/shard_map/ppermute | solution.py:463
  29.3 1.9 %collective-permute-start.9 = (bf16[64,512]{1,0:T(8,128)(2,1)S(1)}, bf16[64,512]{1,0:T(8,128)(2,1)S(1)}, u32[]{:S(2)}, u32[]{:S(2)}) collective-permute-start(bf16[64,512]{1,0:T(8,128)(2,1)S(1)} %get-tuple-element.51), channel_id=1, source_target_pairs={{0,1},{1,0},{2,3},{3,2},{4,5},{5,4},{6,7},{7,6},{8,9},{9,8},{10,11... | collective-permute-start | bytes 196616 | tf_op jit(solution)/shard_map/ppermute | solution.py:454
  29.3 4.9 %collective-permute-start.10 = (bf16[64,512]{1,0:T(8,128)(2,1)S(1)}, bf16[64,512]{1,0:T(8,128)(2,1)S(1)}, u32[]{:S(2)}, u32[]{:S(2)}) collective-permute-start(bf16[64,512]{1,0:T(8,128)(2,1)S(1)} %get-tuple-element.52), channel_id=1, source_target_pairs={{0,2},{1,3},{2,0},{3,1},{4,6},{5,7},{6,4},{7,5},{8,10},{9,11},{10,... | collective-permute-start | bytes 196616 | tf_op jit(solution)/shard_map/ppermute | solution.py:454
  30.2 4.6 %collective-permute-start.11 = (bf16[64,512]{1,0:T(8,128)(2,1)S(1)}, bf16[64,512]{1,0:T(8,128)(2,1)S(1)}, u32[]{:S(2)}, u32[]{:S(2)}) collective-permute-start(bf16[64,512]{1,0:T(8,128)(2,1)S(1)} %get-tuple-element.53), channel_id=1, source_target_pairs={{0,3},{1,2},{2,1},{3,0},{4,7},{5,6},{6,5},{7,4},{8,11},{9,10},{10,... | collective-permute-start | bytes 196616 | tf_op jit(solution)/shard_map/ppermute | solution.py:454
  34.9 4.3 %collective-permute-start.14 = (bf16[64,512]{1,0:T(8,128)(2,1)S(1)}, bf16[64,512]{1,0:T(8,128)(2,1)S(1)}, u32[]{:S(2)}, u32[]{:S(2)}) collective-permute-start(bf16[64,512]{1,0:T(8,128)(2,1)S(1)} %get-tuple-element.58), channel_id=1, source_target_pairs={{0,4},{4,0},{8,12},{12,8},{16,20},{20,16},{24,28},{28,24},{1,5},{5... | collective-permute-start | bytes 196616 | tf_op jit(solution)/shard_map/ppermute | solution.py:454
  39.2 4.3 %collective-permute-start.15 = (bf16[64,512]{1,0:T(8,128)(2,1)S(1)}, bf16[64,512]{1,0:T(8,128)(2,1)S(1)}, u32[]{:S(2)}, u32[]{:S(2)}) collective-permute-start(bf16[64,512]{1,0:T(8,128)(2,1)S(1)} %add_convert_fusion.1.after), channel_id=1, source_target_pairs={{0,8},{4,12},{8,0},{12,4},{16,24},{20,28},{24,16},{28,20},{1,9},{5... | collective-permute-start | bytes 196616 | tf_op jit(solution)/shard_map/ppermute | solution.py:454
  41.0 7.3 %collective-permute-start.12 = (bf16[384,128]{1,0:T(8,128)(2,1)S(1)}, bf16[384,128]{1,0:T(8,128)(2,1)S(1)}, u32[]{:S(2)}, u32[]{:S(2)}) collective-permute-start(bf16[384,128]{1,0:T(8,128)(2,1)S(1)} %get-tuple-element.56), channel_id=1, source_target_pairs={{8,16},{16,8},{12,20},{20,12},{9,17},{17,9},{13,21},{21,13},{10,18... | collective-permute-start | bytes 294920 | tf_op jit(solution)/shard_map/ppermute | solution.py:463
  41.7 6.7 %collective-permute-start.13 = (bf16[384,128]{1,0:T(8,128)(2,1)S(1)}, bf16[384,128]{1,0:T(8,128)(2,1)S(1)}, u32[]{:S(2)}, u32[]{:S(2)}) collective-permute-start(bf16[384,128]{1,0:T(8,128)(2,1)S(1)} %get-tuple-element.57), channel_id=1, source_target_pairs={{4,8},{8,4},{12,16},{16,12},{20,24},{24,20},{5,9},{9,5},{13,17},{1... | collective-permute-start | bytes 294920 | tf_op jit(solution)/shard_map/ppermute | solution.py:463
  43.6 8.4 %collective-permute-start.16 = (bf16[64,512]{1,0:T(8,128)(2,1)S(1)}, bf16[64,512]{1,0:T(8,128)(2,1)S(1)}, u32[]{:S(2)}, u32[]{:S(2)}) collective-permute-start(bf16[64,512]{1,0:T(8,128)(2,1)S(1)} %add_convert_fusion.after.mine), channel_id=1, source_target_pairs={{0,16},{4,20},{8,24},{12,28},{16,0},{20,4},{24,8},{28,12},{1,17},{... | collective-permute-start | bytes 196616 | tf_op jit(solution)/shard_map/ppermute | solution.py:454

commit v4 on v3

--- a/solution.py
+++ b/solution.py
@@ -12,7 +12,10 @@
 LANES = 128
 UNIT_ROWS = 32
 Z_ROWS = 64
-SWAPS = ((1, 0), (2, 0), (2, 1), (1, 1))
+SWAPS = (
+    ((1, 0), (2, 0), (2, 1), (1, 1)),
+    ((2, 0), (1, 0), (1, 1), (2, 1)),
+)
 DN_NT = (((1,), (1,)), ((), ()))
 DN_NN = (((1,), (0,)), ((), ()))
 
@@ -51,12 +54,15 @@
     reach = len(outs) // 2
     low = low_half((64, LANES))
     device = lax.axis_index("space")
+    odd = lax.rem(lax.axis_index("dp"), 2)
     for number, out in enumerate(outs):
         column = reach
         if number > 0:
-            distance, turn = SWAPS[number - 1]
-            up = upward(device, distance) == turn
-            column = jnp.where(up, reach + distance, reach - distance)
+            columns = []
+            for distance, turn in (SWAPS[0][number - 1], SWAPS[1][number - 1]):
+                up = upward(device, distance) == turn
+                columns.append(jnp.where(up, reach + distance, reach - distance))
+            column = jnp.where(odd == 0, columns[0], columns[1])
 
         def base(link):
             unit = send[column, 0, link]
@@ -133,11 +139,19 @@
     half = (link >= 6).astype(jnp.int32)
     face = link - 6 * half
     block = jnp.zeros(number.shape, jnp.int32)
+    odd = lax.rem(lax.axis_index("dp"), 2)
     for distance in (1, 2):
         up = upward(device, distance)
-        even, odd = (SWAPS.index((distance, turn)) + 1 for turn in range(2))
-        block = jnp.where(column == 2 - distance, jnp.where(up == 0, even, odd), block)
-        block = jnp.where(column == 2 + distance, jnp.where(up == 0, odd, even), block)
+        first, second = (
+            jnp.where(
+                odd == 0,
+                SWAPS[0].index((distance, turn)) + 1,
+                SWAPS[1].index((distance, turn)) + 1,
+            )
+            for turn in range(2)
+        )
+        block = jnp.where(column == 2 - distance, jnp.where(up == 0, first, second), block)
+        block = jnp.where(column == 2 + distance, jnp.where(up == 0, second, first), block)
     base = block * (8 * UNIT_ROWS + 2 * Z_ROWS)
     plain = base + (half * 4 + face) * UNIT_ROWS
     paired = base + 8 * UNIT_ROWS + half * Z_ROWS
@@ -317,12 +331,13 @@
 
 
 def forward_kernel(
-    masked, mask, cotangent, toeplitz, bias, rows, send, r0, r1, r2, r3, r4,
-    block_out, grad_out, u0, u1, u2, u3, u4, *rest, shard,
+    masked, mask, cotangent_hbm, toeplitz, bias, rows, send, r0, r1, r2, r3, r4,
+    block_out, grad_out, keep_out, give_out, u0, u1, u2, u3, u4,
+    table, windows, sides, walls, flat, shifted, values, flipped, cotangent, sem, *, shard,
 ):
-    chunk_outs = rest[:-8]
-    table, windows, sides, walls, flat, shifted, values, flipped = rest[-8:]
-    groups = len(chunk_outs)
+    fetch = pltpu.make_async_copy(cotangent_hbm, cotangent, sem)
+    fetch.start()
+    groups = 2 * keep_out.shape[0]
     bricks = masked.shape[0]
     pairs = bricks // 2
     gather_units(table, (r0, r1, r2, r3, r4))
@@ -330,6 +345,7 @@
     bias_lane = shard % LANES
     bias_tile = shard - bias_lane
     bias_row = bias[0:1, :]
+    fetch.wait()
     values[:, bricks * 64 :, :] = jnp.zeros((4, 64, LANES), F32)
 
     def one_chunk(q, bias_sum):
@@ -380,7 +396,7 @@
             total += jnp.dot(flipped[q], window, preferred_element_type=F32)
         flat[:, 192 * ae : 192 * ae + 256] = total[64:128] + pltpu.roll(total[0:64], 64, 1)
 
-    width = chunk_outs[0].shape[1]
+    width = keep_out.shape[2]
     bias_all = jnp.sum(bias_sum, axis=0, keepdims=True)
     bias_all = jnp.broadcast_to(bias_all, (8, LANES))
     bias_all = bias_all + pltpu.roll(bias_all, 64, 1)
@@ -400,7 +416,7 @@
 
             @pl.when(me ^ m == k)
             def _(m=m, block=block):
-                chunk_outs[m][...] = block
+                (give_out if m % 2 else keep_out)[m // 2] = block
 
 
 def assemble_kernel(grad, rows, r0, r1, r2, r3, r4, after, windows, table, sides, walls):
@@ -409,15 +425,24 @@
     assemble(grad, table, rows, windows, sides, walls)
 
 
-def sum_kernel(*refs, terms):
-    total = refs[0][...].astype(F32)
-    for share in refs[1:terms]:
-        total += share[...].astype(F32)
-    refs[terms + 4][...] = total.astype(BF16)
-
-
-def backward_kernel(windows, mask, toeplitz, after, out):
+def sum_kernel(*refs):
+    refs[-1][...] = (refs[0][...].astype(F32) + refs[1][...].astype(F32)).astype(BF16)
+
+
+def sum_after(mine, other, after):
+    return pl.pallas_call(
+        sum_kernel,
+        name="sum",
+        out_shape=jax.ShapeDtypeStruct(mine.shape, mine.dtype),
+        in_specs=[vmem()] * 2 + [untouched()] * len(after),
+        out_specs=vmem(),
+        compiler_params=pltpu.CompilerParams(vmem_limit_bytes=1024 * 1024),
+    )(mine, other, *after)
+
+
+def backward_kernel(windows, mask, toeplitz, after, out, done):
     del after
+    done[...] = jnp.zeros(done.shape, F32)
     bricks = mask.shape[0]
     pairs = bricks // 2
 
@@ -454,13 +479,38 @@
     return lax.ppermute(block, axis, [(i, i ^ bit) for i in range(lax.axis_size(axis))])
 
 
+def by_parity(block, routes):
+    groups = lax.axis_size("dp")
+    pairs = [
+        (source * groups + group, target * groups + group)
+        for group in range(groups)
+        for source, target in routes[group % 2]
+    ]
+    return lax.ppermute(block, ("space", "dp"), pairs)
+
+
 def exchanged(number, unit):
-    distance, turn = SWAPS[number - 1]
-    route = []
-    for low in range(lax.axis_size("space") - distance):
-        if low // distance % 2 == turn:
-            route += [(low, low + distance), (low + distance, low)]
-    return lax.ppermute(unit, "space", route)
+    routes = []
+    for swaps in SWAPS:
+        distance, turn = swaps[number - 1]
+        route = []
+        for low in range(lax.axis_size("space") - distance):
+            if low // distance % 2 == turn:
+                route += [(low, low + distance), (low + distance, low)]
+        routes.append(route)
+    return by_parity(unit, routes)
+
+
+def space_steps():
+    bits = []
+    while 2 ** len(bits) < lax.axis_size("space"):
+        bits.append(2 ** len(bits))
+    return list(zip(bits, bits[1:] + bits[:1]))
+
+
+def stepped(total, step):
+    devices = range(lax.axis_size("space"))
+    return by_parity(total, [[(i, i ^ bit) for i in devices] for bit in step])
 
 
 def body(features, occupancy, counts, send_units, neighbours, weight, conv_bias, cotangent):
@@ -519,7 +569,12 @@
         counts,
     )
 
-    shards = [own_shard] + [swapped(own_shard, "dp", m) for m in range(1, groups)]
+    shards = {0: own_shard}
+    bit = groups // 2
+    while bit:
+        for m in list(shards):
+            shards[m | bit] = swapped(shards[m], "dp", bit)
+        bit //= 2
     received = units[:1] + [exchanged(number, units[number]) for number in range(1, spread)]
 
     flat = pltpu.VMEM((channels, 28 * 64), F32)
@@ -535,18 +590,21 @@
         out_specs=[vmem()] * 3,
         scratch_shapes=[pltpu.VMEM((groups, channels, width), BF16), flat, flat],
         compiler_params=params,
-    )(*shards)
+    )(*(shards[m] for m in range(groups)))
 
     table = pltpu.VMEM((spread * unit_rows + Z_ROWS, LANES), BF16)
     windows = pltpu.VMEM((3, 4, pairs, 10, 16, 256), BF16)
     sides = pltpu.VMEM((2, 2, 5, 8, LANES), F32)
     walls = pltpu.VMEM((2, 64, LANES), F32)
-    block_output, grad, *rest = pl.pallas_call(
+    half_type = jax.ShapeDtypeStruct((groups // 2, channels, width), BF16)
+    block_output, grad, keep, give, *grad_units = pl.pallas_call(
         functools.partial(forward_kernel, shard=shard),
         name="forward",
-        out_shape=[grid_type, grid_type] + [units_type] * spread + [shard_type] * groups,
-        in_specs=[vmem()] * 5 + [smem(), smem()] + [vmem()] * spread,
-        out_specs=[vmem()] * (2 + spread + groups),
+        out_shape=[grid_type, grid_type, half_type, half_type] + [units_type] * spread,
+        in_specs=[vmem(), vmem(), pl.BlockSpec(memory_space=pltpu.HBM), vmem(), vmem()]
+        + [smem(), smem()]
+        + [vmem()] * spread,
+        out_specs=[vmem()] * (4 + spread),
         scratch_shapes=[
             table,
             windows,
@@ -556,35 +614,33 @@
             flat,
             pltpu.VMEM((4, (bricks + 1) * 64, LANES), F32),
             pltpu.VMEM((4, LANES, pairs * LANES), BF16),
+            pltpu.VMEM(grid_shape, BF16),
+            pltpu.SemaphoreType.DMA,
         ],
         compiler_params=params,
-    )(masked, mask, cotangent[0], band_forward, bias, rows, send, *received)
-    grad_units, blocks = rest[:spread], rest[spread:]
-
-    shares = [blocks[0]] + [swapped(blocks[m], "dp", m) for m in range(1, groups)]
+    )(
+        masked,
+        mask,
+        pltpu.with_memory_space_constraint(cotangent[0], pltpu.HBM),
+        band_forward,
+        bias,
+        rows,
+        send,
+        *received,
+    )
+
     grad_received = grad_units[:1] + [exchanged(n, grad_units[n]) for n in range(1, 3)]
-    total, *later = pl.pallas_call(
-        functools.partial(sum_kernel, terms=groups),
-        name="sum",
-        out_shape=[shard_type, units_type, units_type],
-        in_specs=[vmem()] * groups + [untouched()] * 4,
-        out_specs=[vmem(), untouched(), untouched()],
-        input_output_aliases={groups: 1, groups + 1: 2},
-        compiler_params=params,
-    )(*shares, *grad_units[3:], *grad_received[1:])
-    steps = []
-    bit = 1
-    while bit < lax.axis_size("space"):
-        steps.append(bit)
+    total = sum_after(keep, swapped(give, "dp", 1), grad_received[1:])
+    grad_received += [exchanged(n, grad_units[n]) for n in range(3, spread)]
+    bit = 2
+    while bit < groups:
+        far = swapped(total[1::2], "dp", bit)
+        total = sum_after(total[0::2], far, grad_received[3:] if 2 * bit >= groups else [])
         bit *= 2
-
-    def stepped(total, bit):
-        return (total.astype(F32) + swapped(total, "space", bit).astype(F32)).astype(BF16)
-
-    for bit in steps[:-1][:1]:
-        total = stepped(total, bit)
-    grad_received += [exchanged(n, unit) for n, unit in zip(range(3, spread), later)]
-
+    total = total[0]
+
+    steps = space_steps()
+    other = stepped(total, steps[0])
     padded_grad = pl.pallas_call(
         assemble_kernel,
         name="assemble",
@@ -595,17 +651,22 @@
         compiler_params=params,
     )(grad, rows, *grad_received, total)
 
-    for bit in steps[1:-1]:
-        total = stepped(total, bit)
-    grad_input = pl.pallas_call(
+    if len(steps) > 1:
+        total = sum_after(total, other, [padded_grad])
+        other = stepped(total, steps[1])
+
+    grad_input, done = pl.pallas_call(
         backward_kernel,
         name="backward",
-        out_shape=grid_type,
+        out_shape=[grid_type, jax.ShapeDtypeStruct((8, LANES), F32)],
         in_specs=[vmem()] * 3 + [untouched()],
-        out_specs=vmem(),
+        out_specs=[vmem()] * 2,
         compiler_params=params,
     )(padded_grad, mask, band_backward, total)
 
+    for number, step in enumerate(steps[2:]):
+        total = sum_after(total, other, [done] if number == 0 else [])
+        other = stepped(total, step)
     weight_share, bias_share = pl.pallas_call(
         finish_kernel,
         name="finish",
@@ -616,7 +677,7 @@
         in_specs=[vmem()] * 2,
         out_specs=[vmem()] * 2,
         compiler_params=params,
-    )(total, swapped(total, "space", steps[-1]))
+    )(total, other)
     return (
         block_output[None],
         grad_input[None],

time: 53.7 us -> 52.6 us (0.980); the launches traced: 52.7 us -> 52.3 us
  starting transfers between devices: 25.8 us -> 27.3 us
  waiting for transfers between devices: 11.8 us -> 10.6 us
  local copies, waits for them, and re-layouts: 0.95 us -> 0.01 us
    ppermute x8 -> x11, starting transfers between devices: 12.7 us -> 23.3 us  [by_parity(): return lax.ppermute(block, ('space', 'dp'), pairs)]
    ppermute x9 -> x5, starting transfers between devices: 13.1 us -> 3.96 us  [swapped(): lax.ppermute(block, axis, [(i, i ^ bit) for i in range(lax.axis_size(axis...]
    ppermute x9 -> x5, waiting for transfers between devices: 11.8 us -> 4.98 us  [swapped(): lax.ppermute(block, axis, [(i, i ^ bit) for i in range(lax.axis_size(axis...]
    ppermute x8 -> x11, waiting for transfers between devices: 0.02 us -> 5.58 us  [by_parity(): return lax.ppermute(block, ('space', 'dp'), pairs)]
    unnamed x2 -> x0, local copies, waits for them, and re-layouts: 0.95 us -> none
    pallas_call x2 -> x5, Pallas kernels: 2.61 us -> 2.64 us  [the longest x1 2.55 us: body(): pl.pallas_call(backward_kernel, name='backward', out_shape=[grid_type, ja...]
  transfers between devices with their start and end apart: 17 -> 16, of which waited for: 5 -> 5; matrix products, arithmetic and copies ran while one was open for 0% -> 0% of each run, Pallas kernels for 8% -> 8%
where the time goes in v4:
time: 52.6 us; the launch traced here: 52.3 us
  starting transfers between devices  27.3 us (52%)
  Pallas kernels  13.1 us (25%)
  waiting for transfers between devices  10.6 us (20%)
  between operations  1.41 us (3%)
    ppermute x11, starting transfers between devices, by_parity(): return lax.ppermute(block, ('space', 'dp'), pairs)  23.3 us
    pallas_call x1, Pallas kernels, body(): pl.pallas_call(functools.partial(forward_kernel, shard=shard), name='forw...  5.71 us
    ppermute x11, waiting for transfers between devices, by_parity(): return lax.ppermute(block, ('space', 'dp'), pairs)  5.58 us
    ppermute x5, waiting for transfers between devices, swapped(): lax.ppermute(block, axis, [(i, i ^ bit) for i in range(lax.axis_size(axis...  4.98 us
    ppermute x5, starting transfers between devices, swapped(): lax.ppermute(block, axis, [(i, i ^ bit) for i in range(lax.axis_size(axis...  3.96 us
    pallas_call x1, Pallas kernels, body(): pl.pallas_call(backward_kernel, name='backward', out_shape=[grid_type, ja...  2.55 us
    pallas_call x1, Pallas kernels, body(): pl.pallas_call(prepare_kernel, name='prepare', out_shape=[grid_type, grid...  2.52 us
    pallas_call x1, Pallas kernels, body(): pl.pallas_call(assemble_kernel, name='assemble', out_shape=jax.ShapeDtype...  1.11 us
  transfers between devices with their start and end apart: 16, of which 5 were waited for; matrix products, arithmetic and copies ran while one was open for 0% of the time, Pallas kernels for 8%

profile of v4, /device:TPU:0, one launch (start us, length us, event | category | flops | bytes accessed | tf_op | source)
XLA Modules:
  0.0 52.3 jit_solution(7544878519908366541)
XLA Ops:
  1.3 2.5 %prepare.1 = (bf16[4,8,8,512]{3,2,1,0:T(8,128)(2,1)S(1)}, bf16[4,8,8,512]{3,2,1,0:T(8,128)(2,1)S(1)}, s32[4,26]{1,0:T(4,128)S(1)}, s32[5,1,12]{2,1,0:T(1,128)S(1...) custom-call(bf16[4,8,8,512]{3,2,1,0:T(8,128)(2,1)} %bitcast.15, ...), custom_call_target="tpu_custom_call" | custom-call | tf_op jit(solution)/shard_map/prepare/pallas_call | solution.py:533
  3.8 0.5 collective-permute-start
  4.3 2.6 %collective-permute-start.1 = (bf16[64,512]{1,0:T(8,128)(2,1)S(1)}, bf16[64,512]{1,0:T(8,128)(2,1)S(1)}, u32[]{:S(2)}, u32[]{:S(2)}) collective-permute-start(bf16[64,512]{1,0:T(8,128)(2,1)S(1)} %get-tuple-element.32.refs_0_), channel_id=1, source_target_pairs={{0,2},{1,3},{2,0},{3,1},{4,6},{5,7},{6,4},{7,5},{8,10},{9,11},{10,... | collective-permute-start | bytes 196616 | tf_op jit(solution)/shard_map/ppermute | solution.py:479
  6.9 1.5 %collective-permute-start.3 = (bf16[384,128]{1,0:T(8,128)(2,1)S(1)}, bf16[384,128]{1,0:T(8,128)(2,1)S(1)}, u32[]{:S(2)}, u32[]{:S(2)}) collective-permute-start(bf16[384,128]{1,0:T(8,128)(2,1)S(1)} %get-tuple-element.38), channel_id=1, source_target_pairs={{0,4},{4,0},{8,12},{12,8},{16,20},{20,16},{24,28},{28,24},{1,9},{9... | collective-permute-start | bytes 294920 | tf_op jit(solution)/shard_map/ppermute | solution.py:489
  8.4 1.6 %collective-permute-start.4 = (bf16[384,128]{1,0:T(8,128)(2,1)S(1)}, bf16[384,128]{1,0:T(8,128)(2,1)S(1)}, u32[]{:S(2)}, u32[]{:S(2)}) collective-permute-start(bf16[384,128]{1,0:T(8,128)(2,1)S(1)} %get-tuple-element.39), channel_id=1, source_target_pairs={{0,8},{8,0},{4,12},{12,4},{16,24},{24,16},{20,28},{28,20},{1,5},{5... | collective-permute-start | bytes 294920 | tf_op jit(solution)/shard_map/ppermute | solution.py:489
  10.0 0.7 %collective-permute-start.5 = (bf16[384,128]{1,0:T(8,128)(2,1)S(1)}, bf16[384,128]{1,0:T(8,128)(2,1)S(1)}, u32[]{:S(2)}, u32[]{:S(2)}) collective-permute-start(bf16[384,128]{1,0:T(8,128)(2,1)S(1)} %get-tuple-element.40), channel_id=1, source_target_pairs={{8,16},{16,8},{12,20},{20,12},{5,9},{9,5},{13,17},{17,13},{21,25},... | collective-permute-start | bytes 294920 | tf_op jit(solution)/shard_map/ppermute | solution.py:489
  10.7 0.0 collective-permute-done.refs_1_
  10.7 0.7 %collective-permute-start.6 = (bf16[384,128]{1,0:T(8,128)(2,1)S(1)}, bf16[384,128]{1,0:T(8,128)(2,1)S(1)}, u32[]{:S(2)}, u32[]{:S(2)}) collective-permute-start(bf16[384,128]{1,0:T(8,128)(2,1)S(1)} %get-tuple-element.41), channel_id=1, source_target_pairs={{4,8},{8,4},{12,16},{16,12},{20,24},{24,20},{9,17},{17,9},{13,21},... | collective-permute-start | bytes 294920 | tf_op jit(solution)/shard_map/ppermute | solution.py:489
  11.3 0.0 collective-permute-done.1.refs_2_
  11.3 0.1 collective-permute-start.2
  11.4 1.2 %collective-permute-done.2.refs_3_ = bf16[64,512]{1,0:T(8,128)(2,1)S(1)} collective-permute-done((bf16[64,512]{1,0:T(8,128)(2,1)S(1)}, bf16[64,512]{1,0:T(8,128)(2,1)S(1)}, u32[]{:S(2)}, u32[]{:S(2)}) %collective-permute-start.2) | collective-permute-done | bytes 65568 | tf_op jit(solution)/shard_map/ppermute | solution.py:479
  12.7 0.4 weights.1
  13.1 0.0 collective-permute-done.3.r1
  13.1 0.0 collective-permute-done.4.r2
  13.1 0.0 collective-permute-done.5.r3
  13.1 0.0 collective-permute-done.6.r4
  13.1 5.7 %forward.1 = (bf16[4,8,8,512]{3,2,1,0:T(8,128)(2,1)}, bf16[4,8,8,512]{3,2,1,0:T(8,128)(2,1)S(1)}, bf16[2,64,512]{2,1,0:T(8,128)(2,1)S(1)}, bf16[2,64,512]{2,1,0:...) custom-call(bf16[4,8,8,512]{3,2,1,0:T(8,128)(2,1)S(1)} %get-tuple-el, ...), custom_call_target="tpu_custom_call" | custom-call | tf_op jit(solution)/shard_map/forward/pallas_call | solution.py:600
  18.8 0.2 collective-permute-start.11
  19.0 7.8 %collective-permute-start.7 = (bf16[384,128]{1,0:T(8,128)(2,1)S(1)}, bf16[384,128]{1,0:T(8,128)(2,1)S(1)}, u32[]{:S(2)}, u32[]{:S(2)}) collective-permute-start(bf16[384,128]{1,0:T(8,128)(2,1)S(1)} %get-tuple-element.45), channel_id=1, source_target_pairs={{0,4},{4,0},{8,12},{12,8},{16,20},{20,16},{24,28},{28,24},{1,9},{9... | collective-permute-start | bytes 294920 | tf_op jit(solution)/shard_map/ppermute | solution.py:489
  26.9 2.0 %collective-permute-start.8 = (bf16[384,128]{1,0:T(8,128)(2,1)S(1)}, bf16[384,128]{1,0:T(8,128)(2,1)S(1)}, u32[]{:S(2)}, u32[]{:S(2)}) collective-permute-start(bf16[384,128]{1,0:T(8,128)(2,1)S(1)} %get-tuple-element.46), channel_id=1, source_target_pairs={{0,8},{8,0},{4,12},{12,4},{16,24},{24,16},{20,28},{28,20},{1,5},{5... | collective-permute-start | bytes 294920 | tf_op jit(solution)/shard_map/ppermute | solution.py:489
  28.8 0.7 %collective-permute-start.9 = (bf16[384,128]{1,0:T(8,128)(2,1)S(1)}, bf16[384,128]{1,0:T(8,128)(2,1)S(1)}, u32[]{:S(2)}, u32[]{:S(2)}) collective-permute-start(bf16[384,128]{1,0:T(8,128)(2,1)S(1)} %get-tuple-element.47), channel_id=1, source_target_pairs={{8,16},{16,8},{12,20},{20,12},{5,9},{9,5},{13,17},{17,13},{21,25},... | collective-permute-start | bytes 294920 | tf_op jit(solution)/shard_map/ppermute | solution.py:489
  29.5 0.7 %collective-permute-start.10 = (bf16[384,128]{1,0:T(8,128)(2,1)S(1)}, bf16[384,128]{1,0:T(8,128)(2,1)S(1)}, u32[]{:S(2)}, u32[]{:S(2)}) collective-permute-start(bf16[384,128]{1,0:T(8,128)(2,1)S(1)} %get-tuple-element.48), channel_id=1, source_target_pairs={{4,8},{8,4},{12,16},{16,12},{20,24},{24,20},{9,17},{17,9},{13,21},... | collective-permute-start | bytes 294920 | tf_op jit(solution)/shard_map/ppermute | solution.py:489
  30.2 0.0 collective-permute-done.7.refs_2_.r1
  30.2 1.5 %collective-permute-done.8.refs_3_.r2 = bf16[384,128]{1,0:T(8,128)(2,1)S(1)} collective-permute-done((bf16[384,128]{1,0:T(8,128)(2,1)S(1)}, bf16[384,128]{1,0:T(8,128)(2,1)S(1)}, u32[]{:S(2)}, u32[]{:S(2)}) %collective-permute-start.8) | collective-permute-done | bytes 98336 | tf_op jit(solution)/shard_map/ppermute | solution.py:489
  31.7 0.0 collective-permute-done.11.refs_1_
  31.8 0.6 %collective-permute-start.12 = (bf16[1,64,512]{2,1,0:T(8,128)(2,1)S(1)}, bf16[1,64,512]{2,1,0:T(8,128)(2,1)S(1)}, u32[]{:S(2)}, u32[]{:S(2)}) collective-permute-start(bf16[1,64,512]{2,1,0:T(8,128)(2,1)S(1)} %get-tuple-element.56), channel_id=1, source_target_pairs={{0,2},{1,3},{2,0},{3,1},{4,6},{5,7},{6,4},{7,5},{8,10},{9,11},{10,... | collective-permute-start | bytes 196616 | tf_op jit(solution)/shard_map/ppermute | solution.py:479
  32.4 0.0 collective-permute-done.9.refs_2_.r3
  32.4 0.0 collective-permute-done.10.refs_3_.r4
  32.4 3.7 %collective-permute-done.12.refs_1_ = bf16[1,64,512]{2,1,0:T(8,128)(2,1)S(1)} collective-permute-done((bf16[1,64,512]{2,1,0:T(8,128)(2,1)S(1)}, bf16[1,64,512]{2,1,0:T(8,128)(2,1)S(1)}, u32[]{:S(2)}, u32[]{:S(2)}) %collective-permute-start.12) | collective-permute-done | bytes 65568 | tf_op jit(solution)/shard_map/ppermute | solution.py:479
  36.1 2.6 %collective-permute-start.13 = (bf16[64,512]{1,0:T(8,128)(2,1)S(1)}, bf16[64,512]{1,0:T(8,128)(2,1)S(1)}, u32[]{:S(2)}, u32[]{:S(2)}) collective-permute-start(bf16[64,512]{1,0:T(8,128)(2,1)S(1)} %bitcast.12), channel_id=1, source_target_pairs={{0,4},{4,0},{8,12},{12,8},{16,20},{20,16},{24,28},{28,24},{1,9},{5... | collective-permute-start | bytes 196616 | tf_op jit(solution)/shard_map/ppermute | solution.py:489
  38.7 1.1 %assemble.1.refs_2_.windows = bf16[3,4,2,10,16,256]{5,4,3,2,1,0:T(8,128)(2,1)S(1)} custom-call(bf16[4,8,8,512]{3,2,1,0:T(8,128)(2,1)S(1)} %get-tuple-element.43.grad, s32[4,26]{1,0:T(4,128)S(1)} %get-tuple-element.35.rows, bf16[384,128]{1,0:T(8,128)(2,1)S(1)} %get-tuple-element.44.r0, bf16[384,128]{1,0:T(8,128)(2,1)S(1)} %collective-permute-done.7.refs_2_.r1, ...), custom_call_target="tpu_custom_call" | custom-call | tf_op jit(solution)/shard_map/assemble/pallas_call | solution.py:644
  39.8 1.1 %collective-permute-done.13.refs_1_ = bf16[64,512]{1,0:T(8,128)(2,1)S(1)} collective-permute-done((bf16[64,512]{1,0:T(8,128)(2,1)S(1)}, bf16[64,512]{1,0:T(8,128)(2,1)S(1)}, u32[]{:S(2)}, u32[]{:S(2)}) %collective-permute-start.13) | collective-permute-done | bytes 65568 | tf_op jit(solution)/shard_map/ppermute | solution.py:489
  41.0 2.9 %collective-permute-start.14 = (bf16[64,512]{1,0:T(8,128)(2,1)S(1)}, bf16[64,512]{1,0:T(8,128)(2,1)S(1)}, u32[]{:S(2)}, u32[]{:S(2)}) collective-permute-start(bf16[64,512]{1,0:T(8,128)(2,1)S(1)} %sum.6.after.refs_0_), channel_id=1, source_target_pairs={{0,8},{4,12},{8,0},{12,4},{16,24},{20,28},{24,16},{28,20},{1,17},{... | collective-permute-start | bytes 196616 | tf_op jit(solution)/shard_map/ppermute | solution.py:489
  43.8 2.5 %backward.1 = (bf16[4,8,8,512]{3,2,1,0:T(8,128)(2,1)}, f32[8,128]{1,0:T(8,128)S(1)}) custom-call(bf16[3,4,2,10,16,256]{5,4,3,2,1,0:T(8,128)(2,1)S(1)} %assemble.1.refs_2_.windows, bf16[4,8,8,512]{3,2,1,0:T(8,128)(2,1)S(1)} %get-tuple-element.31.mask, bf16[9,256,128]{2,1,0:T(8,128)(2,1)S(1)} %get-tuple-element.51.toeplitz, bf16[64,512]{1,0:T(8,128)(2,1)S(1)} %sum.6.after.refs_0_), custom_call_target="tpu_custom_call" | custom-call | tf_op jit(solution)/shard_map/backward/pallas_call | solution.py:658
  46.4 0.0 collective-permute-done.14.refs_1_
  46.4 2.3 %collective-permute-start.15 = (bf16[64,512]{1,0:T(8,128)(2,1)S(1)}, bf16[64,512]{1,0:T(8,128)(2,1)S(1)}, u32[]{:S(2)}, u32[]{:S(2)}) collective-permute-start(bf16[64,512]{1,0:T(8,128)(2,1)S(1)} %sum.7.mine), channel_id=1, source_target_pairs={{0,16},{4,20},{8,24},{12,28},{16,0},{20,4},{24,8},{28,12},{1,5},{5... | collective-permute-start | bytes 196616 | tf_op jit(solution)/shard_map/ppermute | solution.py:489
  48.7 2.9 %collective-permute-done.15.other = bf16[64,512]{1,0:T(8,128)(2,1)S(1)} collective-permute-done((bf16[64,512]{1,0:T(8,128)(2,1)S(1)}, bf16[64,512]{1,0:T(8,128)(2,1)S(1)}, u32[]{:S(2)}, u32[]{:S(2)}) %collective-permute-start.15) | collective-permute-done | bytes 65568 | tf_op jit(solution)/shard_map/ppermute | solution.py:489
  51.6 0.7 %finish.1 = (f32[64,432]{1,0:T(8,128)}, f32[1,16]{1,0:T(1,128)}) custom-call(bf16[64,512]{1,0:T(8,128)(2,1)S(1)} %sum.7.mine, bf16[64,512]{1,0:T(8,128)(2,1)S(1)} %collective-permute-done.15.other), custom_call_target="tpu_custom_call" | custom-call | tf_op jit(solution)/shard_map/finish/pallas_call | solution.py:670
  (5 shorter events, 0.1 us)
Async XLA Ops:
  3.8 6.8 %collective-permute-start = (bf16[64,512]{1,0:T(8,128)(2,1)S(1)}, bf16[64,512]{1,0:T(8,128)(2,1)S(1)}, u32[]{:S(2)}, u32[]{:S(2)}) collective-permute-start(bf16[64,512]{1,0:T(8,128)(2,1)S(1)} %get-tuple-element.32.refs_0_), channel_id=1, source_target_pairs={{0,1},{1,0},{2,3},{3,2},{4,5},{5,4},{6,7},{7,6},{8,9},{9,8},{10,11... | collective-permute-start | bytes 196616 | tf_op jit(solution)/shard_map/ppermute | solution.py:479
  4.3 7.0 %collective-permute-start.1 = (bf16[64,512]{1,0:T(8,128)(2,1)S(1)}, bf16[64,512]{1,0:T(8,128)(2,1)S(1)}, u32[]{:S(2)}, u32[]{:S(2)}) collective-permute-start(bf16[64,512]{1,0:T(8,128)(2,1)S(1)} %get-tuple-element.32.refs_0_), channel_id=1, source_target_pairs={{0,2},{1,3},{2,0},{3,1},{4,6},{5,7},{6,4},{7,5},{8,10},{9,11},{10,... | collective-permute-start | bytes 196616 | tf_op jit(solution)/shard_map/ppermute | solution.py:479
  6.9 6.2 %collective-permute-start.3 = (bf16[384,128]{1,0:T(8,128)(2,1)S(1)}, bf16[384,128]{1,0:T(8,128)(2,1)S(1)}, u32[]{:S(2)}, u32[]{:S(2)}) collective-permute-start(bf16[384,128]{1,0:T(8,128)(2,1)S(1)} %get-tuple-element.38), channel_id=1, source_target_pairs={{0,4},{4,0},{8,12},{12,8},{16,20},{20,16},{24,28},{28,24},{1,9},{9... | collective-permute-start | bytes 294920 | tf_op jit(solution)/shard_map/ppermute | solution.py:489
  8.4 4.7 %collective-permute-start.4 = (bf16[384,128]{1,0:T(8,128)(2,1)S(1)}, bf16[384,128]{1,0:T(8,128)(2,1)S(1)}, u32[]{:S(2)}, u32[]{:S(2)}) collective-permute-start(bf16[384,128]{1,0:T(8,128)(2,1)S(1)} %get-tuple-element.39), channel_id=1, source_target_pairs={{0,8},{8,0},{4,12},{12,4},{16,24},{24,16},{20,28},{28,20},{1,5},{5... | collective-permute-start | bytes 294920 | tf_op jit(solution)/shard_map/ppermute | solution.py:489
  10.0 3.1 %collective-permute-start.5 = (bf16[384,128]{1,0:T(8,128)(2,1)S(1)}, bf16[384,128]{1,0:T(8,128)(2,1)S(1)}, u32[]{:S(2)}, u32[]{:S(2)}) collective-permute-start(bf16[384,128]{1,0:T(8,128)(2,1)S(1)} %get-tuple-element.40), channel_id=1, source_target_pairs={{8,16},{16,8},{12,20},{20,12},{5,9},{9,5},{13,17},{17,13},{21,25},... | collective-permute-start | bytes 294920 | tf_op jit(solution)/shard_map/ppermute | solution.py:489
  10.7 2.4 %collective-permute-start.6 = (bf16[384,128]{1,0:T(8,128)(2,1)S(1)}, bf16[384,128]{1,0:T(8,128)(2,1)S(1)}, u32[]{:S(2)}, u32[]{:S(2)}) collective-permute-start(bf16[384,128]{1,0:T(8,128)(2,1)S(1)} %get-tuple-element.41), channel_id=1, source_target_pairs={{4,8},{8,4},{12,16},{16,12},{20,24},{24,20},{9,17},{17,9},{13,21},... | collective-permute-start | bytes 294920 | tf_op jit(solution)/shard_map/ppermute | solution.py:489
  11.3 1.3 %collective-permute-start.2 = (bf16[64,512]{1,0:T(8,128)(2,1)S(1)}, bf16[64,512]{1,0:T(8,128)(2,1)S(1)}, u32[]{:S(2)}, u32[]{:S(2)}) collective-permute-start(bf16[64,512]{1,0:T(8,128)(2,1)S(1)} %collective-permute-done.1.refs_2_), channel_id=1, source_target_pairs={{0,1},{1,0},{2,3},{3,2},{4,5},{5,4},{6,7},{7,6},{8,9},{9,8},{10,11... | collective-permute-start | bytes 196616 | tf_op jit(solution)/shard_map/ppermute | solution.py:479
  18.8 12.9 %collective-permute-start.11 = (bf16[2,64,512]{2,1,0:T(8,128)(2,1)S(1)}, bf16[2,64,512]{2,1,0:T(8,128)(2,1)S(1)}, u32[]{:S(2)}, u32[]{:S(2)}) collective-permute-start(bf16[2,64,512]{2,1,0:T(8,128)(2,1)S(1)} %get-tuple-element.50), channel_id=1, source_target_pairs={{0,1},{1,0},{2,3},{3,2},{4,5},{5,4},{6,7},{7,6},{8,9},{9,8},{10,11... | collective-permute-start | bytes 393224 | tf_op jit(solution)/shard_map/ppermute | solution.py:479
  19.0 11.1 %collective-permute-start.7 = (bf16[384,128]{1,0:T(8,128)(2,1)S(1)}, bf16[384,128]{1,0:T(8,128)(2,1)S(1)}, u32[]{:S(2)}, u32[]{:S(2)}) collective-permute-start(bf16[384,128]{1,0:T(8,128)(2,1)S(1)} %get-tuple-element.45), channel_id=1, source_target_pairs={{0,4},{4,0},{8,12},{12,8},{16,20},{20,16},{24,28},{28,24},{1,9},{9... | collective-permute-start | bytes 294920 | tf_op jit(solution)/shard_map/ppermute | solution.py:489
  26.9 4.8 %collective-permute-start.8 = (bf16[384,128]{1,0:T(8,128)(2,1)S(1)}, bf16[384,128]{1,0:T(8,128)(2,1)S(1)}, u32[]{:S(2)}, u32[]{:S(2)}) collective-permute-start(bf16[384,128]{1,0:T(8,128)(2,1)S(1)} %get-tuple-element.46), channel_id=1, source_target_pairs={{0,8},{8,0},{4,12},{12,4},{16,24},{24,16},{20,28},{28,20},{1,5},{5... | collective-permute-start | bytes 294920 | tf_op jit(solution)/shard_map/ppermute | solution.py:489
  28.8 3.5 %collective-permute-start.9 = (bf16[384,128]{1,0:T(8,128)(2,1)S(1)}, bf16[384,128]{1,0:T(8,128)(2,1)S(1)}, u32[]{:S(2)}, u32[]{:S(2)}) collective-permute-start(bf16[384,128]{1,0:T(8,128)(2,1)S(1)} %get-tuple-element.47), channel_id=1, source_target_pairs={{8,16},{16,8},{12,20},{20,12},{5,9},{9,5},{13,17},{17,13},{21,25},... | collective-permute-start | bytes 294920 | tf_op jit(solution)/shard_map/ppermute | solution.py:489
  29.5 2.9 %collective-permute-start.10 = (bf16[384,128]{1,0:T(8,128)(2,1)S(1)}, bf16[384,128]{1,0:T(8,128)(2,1)S(1)}, u32[]{:S(2)}, u32[]{:S(2)}) collective-permute-start(bf16[384,128]{1,0:T(8,128)(2,1)S(1)} %get-tuple-element.48), channel_id=1, source_target_pairs={{4,8},{8,4},{12,16},{16,12},{20,24},{24,20},{9,17},{17,9},{13,21},... | collective-permute-start | bytes 294920 | tf_op jit(solution)/shard_map/ppermute | solution.py:489
  31.8 4.3 %collective-permute-start.12 = (bf16[1,64,512]{2,1,0:T(8,128)(2,1)S(1)}, bf16[1,64,512]{2,1,0:T(8,128)(2,1)S(1)}, u32[]{:S(2)}, u32[]{:S(2)}) collective-permute-start(bf16[1,64,512]{2,1,0:T(8,128)(2,1)S(1)} %get-tuple-element.56), channel_id=1, source_target_pairs={{0,2},{1,3},{2,0},{3,1},{4,6},{5,7},{6,4},{7,5},{8,10},{9,11},{10,... | collective-permute-start | bytes 196616 | tf_op jit(solution)/shard_map/ppermute | solution.py:479
  36.1 4.8 %collective-permute-start.13 = (bf16[64,512]{1,0:T(8,128)(2,1)S(1)}, bf16[64,512]{1,0:T(8,128)(2,1)S(1)}, u32[]{:S(2)}, u32[]{:S(2)}) collective-permute-start(bf16[64,512]{1,0:T(8,128)(2,1)S(1)} %bitcast.12), channel_id=1, source_target_pairs={{0,4},{4,0},{8,12},{12,8},{16,20},{20,16},{24,28},{28,24},{1,9},{5... | collective-permute-start | bytes 196616 | tf_op jit(solution)/shard_map/ppermute | solution.py:489
  41.0 5.4 %collective-permute-start.14 = (bf16[64,512]{1,0:T(8,128)(2,1)S(1)}, bf16[64,512]{1,0:T(8,128)(2,1)S(1)}, u32[]{:S(2)}, u32[]{:S(2)}) collective-permute-start(bf16[64,512]{1,0:T(8,128)(2,1)S(1)} %sum.6.after.refs_0_), channel_id=1, source_target_pairs={{0,8},{4,12},{8,0},{12,4},{16,24},{20,28},{24,16},{28,20},{1,17},{... | collective-permute-start | bytes 196616 | tf_op jit(solution)/shard_map/ppermute | solution.py:489
  46.4 5.2 %collective-permute-start.15 = (bf16[64,512]{1,0:T(8,128)(2,1)S(1)}, bf16[64,512]{1,0:T(8,128)(2,1)S(1)}, u32[]{:S(2)}, u32[]{:S(2)}) collective-permute-start(bf16[64,512]{1,0:T(8,128)(2,1)S(1)} %sum.7.mine), channel_id=1, source_target_pairs={{0,16},{4,20},{8,24},{12,28},{16,0},{20,4},{24,8},{28,12},{1,5},{5... | collective-permute-start | bytes 196616 | tf_op jit(solution)/shard_map/ppermute | solution.py:489

commit v5 on v4

--- a/solution.py
+++ b/solution.py
@@ -419,8 +419,7 @@
                 (give_out if m % 2 else keep_out)[m // 2] = block
 
 
-def assemble_kernel(grad, rows, r0, r1, r2, r3, r4, after, windows, table, sides, walls):
-    del after
+def assemble_kernel(grad, rows, r0, r1, r2, r3, r4, windows, table, sides, walls):
     gather_units(table, (r0, r1, r2, r3, r4))
     assemble(grad, table, rows, windows, sides, walls)
 
@@ -440,9 +439,7 @@
     )(mine, other, *after)
 
 
-def backward_kernel(windows, mask, toeplitz, after, out, done):
-    del after
-    done[...] = jnp.zeros(done.shape, F32)
+def backward_kernel(windows, mask, toeplitz, out):
     bricks = mask.shape[0]
     pairs = bricks // 2
 
@@ -462,10 +459,12 @@
     lax.fori_loop(0, 4, one_chunk, 0)
 
 
-def finish_kernel(mine, other, weight_out, bias_out):
+def finish_kernel(terms, weight_out, bias_out):
     shard = weight_out.shape[1]
     count = bias_out.shape[1]
-    total = mine[...].astype(F32) + other[...].astype(F32)
+    total = jnp.zeros(terms.shape[1:], F32)
+    for number in range(terms.shape[0]):
+        total += terms[number].astype(F32)
     weight_out[...] = total[:, 0:shard]
     bias_lane = shard % LANES
     bias_tile = shard - bias_lane
@@ -499,18 +498,6 @@
                 route += [(low, low + distance), (low + distance, low)]
         routes.append(route)
     return by_parity(unit, routes)
-
-
-def space_steps():
-    bits = []
-    while 2 ** len(bits) < lax.axis_size("space"):
-        bits.append(2 ** len(bits))
-    return list(zip(bits, bits[1:] + bits[:1]))
-
-
-def stepped(total, step):
-    devices = range(lax.axis_size("space"))
-    return by_parity(total, [[(i, i ^ bit) for i in devices] for bit in step])
 
 
 def body(features, occupancy, counts, send_units, neighbours, weight, conv_bias, cotangent):
@@ -630,43 +617,35 @@
     )
 
     grad_received = grad_units[:1] + [exchanged(n, grad_units[n]) for n in range(1, 3)]
-    total = sum_after(keep, swapped(give, "dp", 1), grad_received[1:])
+    total = sum_after(keep, swapped(give, "dp", 1), [])
     grad_received += [exchanged(n, grad_units[n]) for n in range(3, spread)]
     bit = 2
     while bit < groups:
-        far = swapped(total[1::2], "dp", bit)
-        total = sum_after(total[0::2], far, grad_received[3:] if 2 * bit >= groups else [])
+        total = sum_after(total[0::2], swapped(total[1::2], "dp", bit), [])
         bit *= 2
     total = total[0]
 
-    steps = space_steps()
-    other = stepped(total, steps[0])
+    terms = lax.all_gather(total, "space", axis=0)
+
     padded_grad = pl.pallas_call(
         assemble_kernel,
         name="assemble",
         out_shape=jax.ShapeDtypeStruct(windows.shape, BF16),
-        in_specs=[vmem()] + [smem()] + [vmem()] * spread + [untouched()],
+        in_specs=[vmem()] + [smem()] + [vmem()] * spread,
         out_specs=vmem(),
         scratch_shapes=[table, sides, walls],
         compiler_params=params,
-    )(grad, rows, *grad_received, total)
-
-    if len(steps) > 1:
-        total = sum_after(total, other, [padded_grad])
-        other = stepped(total, steps[1])
-
-    grad_input, done = pl.pallas_call(
+    )(grad, rows, *grad_received)
+
+    grad_input = pl.pallas_call(
         backward_kernel,
         name="backward",
-        out_shape=[grid_type, jax.ShapeDtypeStruct((8, LANES), F32)],
-        in_specs=[vmem()] * 3 + [untouched()],
-        out_specs=[vmem()] * 2,
+        out_shape=grid_type,
+        in_specs=[vmem()] * 3,
+        out_specs=vmem(),
         compiler_params=params,
-    )(padded_grad, mask, band_backward, total)
-
-    for number, step in enumerate(steps[2:]):
-        total = sum_after(total, other, [done] if number == 0 else [])
-        other = stepped(total, step)
+    )(padded_grad, mask, band_backward)
+
     weight_share, bias_share = pl.pallas_call(
         finish_kernel,
         name="finish",
@@ -674,10 +653,10 @@
             jax.ShapeDtypeStruct((channels, shard), F32),
             jax.ShapeDtypeStruct((1, count), F32),
         ],
-        in_specs=[vmem()] * 2,
+        in_specs=[vmem()],
         out_specs=[vmem()] * 2,
         compiler_params=params,
-    )(total, other)
+    )(terms)
     return (
         block_output[None],
         grad_input[None],

time: 52.6 us -> 71.9 us (1.37)
  blocking collectives: 0 us -> 35.6 us
  waiting for transfers between devices: 10.6 us -> 2.16 us
  starting transfers between devices: 27.3 us -> 19.4 us
    all_gather x0 -> x1, blocking collectives: none -> 35.6 us  [body(): terms = lax.all_gather(total, 'space', axis=0)]
    ppermute x11 -> x8, starting transfers between devices: 23.3 us -> 15.5 us  [by_parity(): return lax.ppermute(block, ('space', 'dp'), pairs)]
    ppermute x11 -> x8, waiting for transfers between devices: 5.58 us -> 0.91 us  [by_parity(): return lax.ppermute(block, ('space', 'dp'), pairs)]
    ppermute x5, waiting for transfers between devices: 4.98 us -> 1.25 us  [swapped(): lax.ppermute(block, axis, [(i, i ^ bit) for i in range(lax.axis_size(axis...]
  transfers between devices with their start and end apart: 16 -> 13, of which waited for: 5 -> 2; matrix products, arithmetic and copies ran while one was open for 0% -> 0% of each run, Pallas kernels for 8% -> 6%
where the time goes in v5:
time: 71.9 us; the launch traced here: 71.7 us
  blocking collectives  35.6 us (50%)
  starting transfers between devices  19.4 us (27%)
  Pallas kernels  13.1 us (18%)
  waiting for transfers between devices  2.16 us (3%)
  between operations  1.41 us (2%)
    all_gather x1, blocking collectives, body(): terms = lax.all_gather(total, 'space', axis=0)  35.6 us
    ppermute x8, starting transfers between devices, by_parity(): return lax.ppermute(block, ('space', 'dp'), pairs)  15.5 us
    pallas_call x1, Pallas kernels, body(): pl.pallas_call(functools.partial(forward_kernel, shard=shard), name='forw...  5.71 us
    ppermute x5, starting transfers between devices, swapped(): lax.ppermute(block, axis, [(i, i ^ bit) for i in range(lax.axis_size(axis...  3.88 us
    pallas_call x1, Pallas kernels, body(): pl.pallas_call(backward_kernel, name='backward', out_shape=grid_type, in_...  2.55 us
    pallas_call x1, Pallas kernels, body(): pl.pallas_call(prepare_kernel, name='prepare', out_shape=[grid_type, grid...  2.52 us
  transfers between devices with their start and end apart: 13, of which 2 were waited for; matrix products, arithmetic and copies ran while one was open for 0% of the time, Pallas kernels for 6%

profile of v5, /device:TPU:0, one launch (start us, length us, event | category | flops | bytes accessed | tf_op | source)
XLA Modules:
  0.0 71.7 jit_solution(6388388184062277152)
XLA Ops:
  1.3 2.5 %prepare.1 = (bf16[4,8,8,512]{3,2,1,0:T(8,128)(2,1)S(1)}, bf16[4,8,8,512]{3,2,1,0:T(8,128)(2,1)S(1)}, s32[4,26]{1,0:T(4,128)S(1)}, s32[5,1,12]{2,1,0:T(1,128)S(1...) custom-call(bf16[4,8,8,512]{3,2,1,0:T(8,128)(2,1)} %bitcast.12, ...), custom_call_target="tpu_custom_call" | custom-call | tf_op jit(solution)/shard_map/prepare/pallas_call | solution.py:520
  3.8 3.0 %collective-permute-start.1 = (bf16[64,512]{1,0:T(8,128)(2,1)S(1)}, bf16[64,512]{1,0:T(8,128)(2,1)S(1)}, u32[]{:S(2)}, u32[]{:S(2)}) collective-permute-start(bf16[64,512]{1,0:T(8,128)(2,1)S(1)} %get-tuple-element.30.refs_0_), channel_id=1, source_target_pairs={{0,2},{1,3},{2,0},{3,1},{4,6},{5,7},{6,4},{7,5},{8,10},{9,11},{10,... | collective-permute-start | bytes 196616 | tf_op jit(solution)/shard_map/ppermute | solution.py:478
  6.8 0.0 collective-permute-start
  6.8 1.5 %collective-permute-start.3 = (bf16[384,128]{1,0:T(8,128)(2,1)S(1)}, bf16[384,128]{1,0:T(8,128)(2,1)S(1)}, u32[]{:S(2)}, u32[]{:S(2)}) collective-permute-start(bf16[384,128]{1,0:T(8,128)(2,1)S(1)} %get-tuple-element.36), channel_id=1, source_target_pairs={{0,4},{4,0},{8,12},{12,8},{16,20},{20,16},{24,28},{28,24},{1,9},{9... | collective-permute-start | bytes 294920 | tf_op jit(solution)/shard_map/ppermute | solution.py:488
  8.3 1.6 %collective-permute-start.4 = (bf16[384,128]{1,0:T(8,128)(2,1)S(1)}, bf16[384,128]{1,0:T(8,128)(2,1)S(1)}, u32[]{:S(2)}, u32[]{:S(2)}) collective-permute-start(bf16[384,128]{1,0:T(8,128)(2,1)S(1)} %get-tuple-element.37), channel_id=1, source_target_pairs={{0,8},{8,0},{4,12},{12,4},{16,24},{24,16},{20,28},{28,20},{1,5},{5... | collective-permute-start | bytes 294920 | tf_op jit(solution)/shard_map/ppermute | solution.py:488
  9.9 0.7 collective-permute-start.5
  10.6 0.0 collective-permute-done.1.refs_2_
  10.6 0.7 collective-permute-start.6
  11.3 0.0 collective-permute-done.refs_1_
  11.3 0.1 collective-permute-start.2
  11.3 1.2 %collective-permute-done.2.refs_3_ = bf16[64,512]{1,0:T(8,128)(2,1)S(1)} collective-permute-done((bf16[64,512]{1,0:T(8,128)(2,1)S(1)}, bf16[64,512]{1,0:T(8,128)(2,1)S(1)}, u32[]{:S(2)}, u32[]{:S(2)}) %collective-permute-start.2) | collective-permute-done | bytes 65568 | tf_op jit(solution)/shard_map/ppermute | solution.py:478
  12.6 0.4 weights.1
  13.0 0.0 collective-permute-done.3.r1
  13.0 0.0 collective-permute-done.4.r2
  13.0 0.0 collective-permute-done.5.r3
  13.0 0.0 collective-permute-done.6.r4
  13.0 5.7 %forward.1 = (bf16[4,8,8,512]{3,2,1,0:T(8,128)(2,1)}, bf16[4,8,8,512]{3,2,1,0:T(8,128)(2,1)S(1)}, bf16[2,64,512]{2,1,0:T(8,128)(2,1)S(1)}, bf16[2,64,512]{2,1,0:...) custom-call(bf16[4,8,8,512]{3,2,1,0:T(8,128)(2,1)S(1)} %get-tuple-el, ...), custom_call_target="tpu_custom_call" | custom-call | tf_op jit(solution)/shard_map/forward/pallas_call | solution.py:587
  18.8 0.2 collective-permute-start.11
  19.0 7.8 %collective-permute-start.7 = (bf16[384,128]{1,0:T(8,128)(2,1)S(1)}, bf16[384,128]{1,0:T(8,128)(2,1)S(1)}, u32[]{:S(2)}, u32[]{:S(2)}) collective-permute-start(bf16[384,128]{1,0:T(8,128)(2,1)S(1)} %get-tuple-element.43), channel_id=1, source_target_pairs={{0,4},{4,0},{8,12},{12,8},{16,20},{20,16},{24,28},{28,24},{1,9},{9... | collective-permute-start | bytes 294920 | tf_op jit(solution)/shard_map/ppermute | solution.py:488
  26.8 2.0 %collective-permute-start.8 = (bf16[384,128]{1,0:T(8,128)(2,1)S(1)}, bf16[384,128]{1,0:T(8,128)(2,1)S(1)}, u32[]{:S(2)}, u32[]{:S(2)}) collective-permute-start(bf16[384,128]{1,0:T(8,128)(2,1)S(1)} %get-tuple-element.44), channel_id=1, source_target_pairs={{0,8},{8,0},{4,12},{12,4},{16,24},{24,16},{20,28},{28,20},{1,5},{5... | collective-permute-start | bytes 294920 | tf_op jit(solution)/shard_map/ppermute | solution.py:488
  28.8 0.7 collective-permute-start.9
  29.4 0.7 collective-permute-start.10
  30.1 0.0 collective-permute-done.11.refs_1_
  30.2 0.6 collective-permute-start.12
  30.7 0.0 collective-permute-done.7.r1
  30.7 0.9 %collective-permute-done.8.r2 = bf16[384,128]{1,0:T(8,128)(2,1)S(1)} collective-permute-done((bf16[384,128]{1,0:T(8,128)(2,1)S(1)}, bf16[384,128]{1,0:T(8,128)(2,1)S(1)}, u32[]{:S(2)}, u32[]{:S(2)}) %collective-permute-start.8) | collective-permute-done | bytes 98336 | tf_op jit(solution)/shard_map/ppermute | solution.py:488
  31.6 0.0 collective-permute-done.9.r3
  31.6 0.0 collective-permute-done.10.r4
  31.6 1.1 %assemble.1.windows = bf16[3,4,2,10,16,256]{5,4,3,2,1,0:T(8,128)(2,1)S(1)} custom-call(bf16[4,8,8,512]{3,2,1,0:T(8,128)(2,1)S(1)} %get-tuple-element.41.grad, s32[4,26]{1,0:T(4,128)S(1)} %get-tuple-element.33.rows, bf16[384,128]{1,0:T(8,128)(2,1)S(1)} %get-tuple-element.42.r0, bf16[384,128]{1,0:T(8,128)(2,1)S(1)} %collective-permute-done.7.r1, ...), custom_call_target="tpu_custom_call" | custom-call | tf_op jit(solution)/shard_map/assemble/pallas_call | solution.py:630
  32.8 2.5 %backward.1 = bf16[4,8,8,512]{3,2,1,0:T(8,128)(2,1)} custom-call(bf16[3,4,2,10,16,256]{5,4,3,2,1,0:T(8,128)(2,1)S(1)} %assemble.1.windows, bf16[4,8,8,512]{3,2,1,0:T(8,128)(2,1)S(1)} %get-tuple-element.29.mask, bf16[9,256,128]{2,1,0:T(8,128)(2,1)S(1)} %get-tuple-element.47.toeplitz), custom_call_target="tpu_custom_call" | custom-call | tf_op jit(solution)/shard_map/backward/pallas_call | solution.py:640
  35.3 0.0 collective-permute-done.12.refs_1_
  35.3 35.6 %all_gather.3.terms = bf16[8,64,512]{2,1,0:T(8,128)(2,1)S(1)} all-gather(bf16[1,64,512]{2,1,0:T(8,128)(2,1)S(1)} %sum.3), channel_id=1, replica_groups=mesh['space'=8,'dp'=4] {'space'}, dimensions={0}, use_global_device_ids=true | all-gather | bytes 589824 | tf_op jit(solution)/shard_map/all_gather | solution.py:628
  70.9 0.7 %finish.1 = (f32[64,432]{1,0:T(8,128)}, f32[1,16]{1,0:T(1,128)}) custom-call(bf16[8,64,512]{2,1,0:T(8,128)(2,1)S(1)} %all_gather.3.terms), custom_call_target="tpu_custom_call" | custom-call | tf_op jit(solution)/shard_map/finish/pallas_call | solution.py:649
  (3 shorter events, 0.1 us)
Async XLA Ops:
  3.8 6.8 %collective-permute-start.1 = (bf16[64,512]{1,0:T(8,128)(2,1)S(1)}, bf16[64,512]{1,0:T(8,128)(2,1)S(1)}, u32[]{:S(2)}, u32[]{:S(2)}) collective-permute-start(bf16[64,512]{1,0:T(8,128)(2,1)S(1)} %get-tuple-element.30.refs_0_), channel_id=1, source_target_pairs={{0,2},{1,3},{2,0},{3,1},{4,6},{5,7},{6,4},{7,5},{8,10},{9,11},{10,... | collective-permute-start | bytes 196616 | tf_op jit(solution)/shard_map/ppermute | solution.py:478
  6.8 4.5 %collective-permute-start = (bf16[64,512]{1,0:T(8,128)(2,1)S(1)}, bf16[64,512]{1,0:T(8,128)(2,1)S(1)}, u32[]{:S(2)}, u32[]{:S(2)}) collective-permute-start(bf16[64,512]{1,0:T(8,128)(2,1)S(1)} %get-tuple-element.30.refs_0_), channel_id=1, source_target_pairs={{0,1},{1,0},{2,3},{3,2},{4,5},{5,4},{6,7},{7,6},{8,9},{9,8},{10,11... | collective-permute-start | bytes 196616 | tf_op jit(solution)/shard_map/ppermute | solution.py:478
  6.8 6.2 %collective-permute-start.3 = (bf16[384,128]{1,0:T(8,128)(2,1)S(1)}, bf16[384,128]{1,0:T(8,128)(2,1)S(1)}, u32[]{:S(2)}, u32[]{:S(2)}) collective-permute-start(bf16[384,128]{1,0:T(8,128)(2,1)S(1)} %get-tuple-element.36), channel_id=1, source_target_pairs={{0,4},{4,0},{8,12},{12,8},{16,20},{20,16},{24,28},{28,24},{1,9},{9... | collective-permute-start | bytes 294920 | tf_op jit(solution)/shard_map/ppermute | solution.py:488
  8.3 4.7 %collective-permute-start.4 = (bf16[384,128]{1,0:T(8,128)(2,1)S(1)}, bf16[384,128]{1,0:T(8,128)(2,1)S(1)}, u32[]{:S(2)}, u32[]{:S(2)}) collective-permute-start(bf16[384,128]{1,0:T(8,128)(2,1)S(1)} %get-tuple-element.37), channel_id=1, source_target_pairs={{0,8},{8,0},{4,12},{12,4},{16,24},{24,16},{20,28},{28,20},{1,5},{5... | collective-permute-start | bytes 294920 | tf_op jit(solution)/shard_map/ppermute | solution.py:488
  9.9 3.1 %collective-permute-start.5 = (bf16[384,128]{1,0:T(8,128)(2,1)S(1)}, bf16[384,128]{1,0:T(8,128)(2,1)S(1)}, u32[]{:S(2)}, u32[]{:S(2)}) collective-permute-start(bf16[384,128]{1,0:T(8,128)(2,1)S(1)} %get-tuple-element.38), channel_id=1, source_target_pairs={{8,16},{16,8},{12,20},{20,12},{5,9},{9,5},{13,17},{17,13},{21,25},... | collective-permute-start | bytes 294920 | tf_op jit(solution)/shard_map/ppermute | solution.py:488
  10.6 2.4 %collective-permute-start.6 = (bf16[384,128]{1,0:T(8,128)(2,1)S(1)}, bf16[384,128]{1,0:T(8,128)(2,1)S(1)}, u32[]{:S(2)}, u32[]{:S(2)}) collective-permute-start(bf16[384,128]{1,0:T(8,128)(2,1)S(1)} %get-tuple-element.39), channel_id=1, source_target_pairs={{4,8},{8,4},{12,16},{16,12},{20,24},{24,20},{9,17},{17,9},{13,21},... | collective-permute-start | bytes 294920 | tf_op jit(solution)/shard_map/ppermute | solution.py:488
  11.3 1.3 %collective-permute-start.2 = (bf16[64,512]{1,0:T(8,128)(2,1)S(1)}, bf16[64,512]{1,0:T(8,128)(2,1)S(1)}, u32[]{:S(2)}, u32[]{:S(2)}) collective-permute-start(bf16[64,512]{1,0:T(8,128)(2,1)S(1)} %collective-permute-done.1.refs_2_), channel_id=1, source_target_pairs={{0,1},{1,0},{2,3},{3,2},{4,5},{5,4},{6,7},{7,6},{8,9},{9,8},{10,11... | collective-permute-start | bytes 196616 | tf_op jit(solution)/shard_map/ppermute | solution.py:478
  18.8 11.3 %collective-permute-start.11 = (bf16[2,64,512]{2,1,0:T(8,128)(2,1)S(1)}, bf16[2,64,512]{2,1,0:T(8,128)(2,1)S(1)}, u32[]{:S(2)}, u32[]{:S(2)}) collective-permute-start(bf16[2,64,512]{2,1,0:T(8,128)(2,1)S(1)} %get-tuple-element.49), channel_id=1, source_target_pairs={{0,1},{1,0},{2,3},{3,2},{4,5},{5,4},{6,7},{7,6},{8,9},{9,8},{10,11... | collective-permute-start | bytes 393224 | tf_op jit(solution)/shard_map/ppermute | solution.py:478
  19.0 11.8 %collective-permute-start.7 = (bf16[384,128]{1,0:T(8,128)(2,1)S(1)}, bf16[384,128]{1,0:T(8,128)(2,1)S(1)}, u32[]{:S(2)}, u32[]{:S(2)}) collective-permute-start(bf16[384,128]{1,0:T(8,128)(2,1)S(1)} %get-tuple-element.43), channel_id=1, source_target_pairs={{0,4},{4,0},{8,12},{12,8},{16,20},{20,16},{24,28},{28,24},{1,9},{9... | collective-permute-start | bytes 294920 | tf_op jit(solution)/shard_map/ppermute | solution.py:488
  26.8 4.8 %collective-permute-start.8 = (bf16[384,128]{1,0:T(8,128)(2,1)S(1)}, bf16[384,128]{1,0:T(8,128)(2,1)S(1)}, u32[]{:S(2)}, u32[]{:S(2)}) collective-permute-start(bf16[384,128]{1,0:T(8,128)(2,1)S(1)} %get-tuple-element.44), channel_id=1, source_target_pairs={{0,8},{8,0},{4,12},{12,4},{16,24},{24,16},{20,28},{28,20},{1,5},{5... | collective-permute-start | bytes 294920 | tf_op jit(solution)/shard_map/ppermute | solution.py:488
  28.8 2.9 %collective-permute-start.9 = (bf16[384,128]{1,0:T(8,128)(2,1)S(1)}, bf16[384,128]{1,0:T(8,128)(2,1)S(1)}, u32[]{:S(2)}, u32[]{:S(2)}) collective-permute-start(bf16[384,128]{1,0:T(8,128)(2,1)S(1)} %get-tuple-element.45), channel_id=1, source_target_pairs={{8,16},{16,8},{12,20},{20,12},{5,9},{9,5},{13,17},{17,13},{21,25},... | collective-permute-start | bytes 294920 | tf_op jit(solution)/shard_map/ppermute | solution.py:488
  29.4 2.2 %collective-permute-start.10 = (bf16[384,128]{1,0:T(8,128)(2,1)S(1)}, bf16[384,128]{1,0:T(8,128)(2,1)S(1)}, u32[]{:S(2)}, u32[]{:S(2)}) collective-permute-start(bf16[384,128]{1,0:T(8,128)(2,1)S(1)} %get-tuple-element.46), channel_id=1, source_target_pairs={{4,8},{8,4},{12,16},{16,12},{20,24},{24,20},{9,17},{17,9},{13,21},... | collective-permute-start | bytes 294920 | tf_op jit(solution)/shard_map/ppermute | solution.py:488
  30.2 5.2 %collective-permute-start.12 = (bf16[1,64,512]{2,1,0:T(8,128)(2,1)S(1)}, bf16[1,64,512]{2,1,0:T(8,128)(2,1)S(1)}, u32[]{:S(2)}, u32[]{:S(2)}) collective-permute-start(bf16[1,64,512]{2,1,0:T(8,128)(2,1)S(1)} %get-tuple-element.52), channel_id=1, source_target_pairs={{0,2},{1,3},{2,0},{3,1},{4,6},{5,7},{6,4},{7,5},{8,10},{9,11},{10,... | collective-permute-start | bytes 196616 | tf_op jit(solution)/shard_map/ppermute | solution.py:478

commit v6 on v4

--- a/solution.py
+++ b/solution.py
@@ -13,8 +13,8 @@
 UNIT_ROWS = 32
 Z_ROWS = 64
 SWAPS = (
-    ((1, 0), (2, 0), (2, 1), (1, 1)),
-    ((2, 0), (1, 0), (1, 1), (2, 1)),
+    ((1, 1), (2, 1), (1, 0), (2, 0)),
+    ((2, 1), (1, 1), (2, 0), (1, 0)),
 )
 DN_NT = (((1,), (1,)), ((), ()))
 DN_NN = (((1,), (0,)), ((), ()))
@@ -425,24 +425,26 @@
     assemble(grad, table, rows, windows, sides, walls)
 
 
-def sum_kernel(*refs):
-    refs[-1][...] = (refs[0][...].astype(F32) + refs[1][...].astype(F32)).astype(BF16)
-
-
-def sum_after(mine, other, after):
-    return pl.pallas_call(
-        sum_kernel,
+def sum_kernel(*refs, operands):
+    refs[operands][...] = (refs[0][...].astype(F32) + refs[1][...].astype(F32)).astype(BF16)
+
+
+def sum_after(mine, other, after, through=()):
+    operands = 2 + len(after) + len(through)
+    total, *passed = pl.pallas_call(
+        functools.partial(sum_kernel, operands=operands),
         name="sum",
-        out_shape=jax.ShapeDtypeStruct(mine.shape, mine.dtype),
-        in_specs=[vmem()] * 2 + [untouched()] * len(after),
-        out_specs=vmem(),
+        out_shape=[jax.ShapeDtypeStruct(x.shape, x.dtype) for x in (mine, *through)],
+        in_specs=[vmem()] * 2 + [untouched()] * (operands - 2),
+        out_specs=[vmem()] + [untouched()] * len(through),
+        input_output_aliases={2 + len(after) + i: 1 + i for i in range(len(through))},
         compiler_params=pltpu.CompilerParams(vmem_limit_bytes=1024 * 1024),
-    )(mine, other, *after)
-
-
-def backward_kernel(windows, mask, toeplitz, after, out, done):
+    )(mine, other, *after, *through)
+    return total, passed
+
+
+def backward_kernel(windows, mask, toeplitz, after, out):
     del after
-    done[...] = jnp.zeros(done.shape, F32)
     bricks = mask.shape[0]
     pairs = bricks // 2
 
@@ -630,17 +632,25 @@
     )
 
     grad_received = grad_units[:1] + [exchanged(n, grad_units[n]) for n in range(1, 3)]
-    total = sum_after(keep, swapped(give, "dp", 1), grad_received[1:])
-    grad_received += [exchanged(n, grad_units[n]) for n in range(3, spread)]
+    total, _ = sum_after(keep, swapped(give, "dp", 1), [])
+    later = grad_units[3:]
     bit = 2
     while bit < groups:
         far = swapped(total[1::2], "dp", bit)
-        total = sum_after(total[0::2], far, grad_received[3:] if 2 * bit >= groups else [])
+        last = 2 * bit >= groups
+        total, later = sum_after(
+            total[0::2], far, grad_received[1:3] if last else [], later if last else []
+        )
         bit *= 2
     total = total[0]
 
     steps = space_steps()
     other = stepped(total, steps[0])
+    grad_received += [exchanged(n, unit) for n, unit in zip(range(3, spread), later)]
+    if len(steps) > 1:
+        total, _ = sum_after(total, other, grad_received[3:4])
+        other = stepped(total, steps[1])
+
     padded_grad = pl.pallas_call(
         assemble_kernel,
         name="assemble",
@@ -651,22 +661,19 @@
         compiler_params=params,
     )(grad, rows, *grad_received, total)
 
-    if len(steps) > 1:
-        total = sum_after(total, other, [padded_grad])
-        other = stepped(total, steps[1])
-
-    grad_input, done = pl.pallas_call(
+    for number, step in enumerate(steps[2:]):
+        total, _ = sum_after(total, other, [] if number else [padded_grad])
+        other = stepped(total, step)
+
+    grad_input = pl.pallas_call(
         backward_kernel,
         name="backward",
-        out_shape=[grid_type, jax.ShapeDtypeStruct((8, LANES), F32)],
+        out_shape=grid_type,
         in_specs=[vmem()] * 3 + [untouched()],
-        out_specs=[vmem()] * 2,
+        out_specs=vmem(),
         compiler_params=params,
     )(padded_grad, mask, band_backward, total)
 
-    for number, step in enumerate(steps[2:]):
-        total = sum_after(total, other, [done] if number == 0 else [])
-        other = stepped(total, step)
     weight_share, bias_share = pl.pallas_call(
         finish_kernel,
         name="finish",

time: 52.6 us -> 51.8 us (0.985)
  waiting for transfers between devices: 10.6 us -> 8.23 us
  starting transfers between devices: 27.3 us -> 28.9 us
    ppermute x11, waiting for transfers between devices: 5.58 us -> 3.03 us  [by_parity(): return lax.ppermute(block, ('space', 'dp'), pairs)]
    ppermute x11, starting transfers between devices: 23.3 us -> 25.1 us  [by_parity(): return lax.ppermute(block, ('space', 'dp'), pairs)]
  transfers between devices with their start and end apart: 16 -> 16, of which waited for: 5 -> 6; matrix products, arithmetic and copies ran while one was open for 0% -> 0% of each run, Pallas kernels for 8% -> 8%
where the time goes in v6:
time: 51.8 us; the launch traced here: 51.6 us
  starting transfers between devices  28.9 us (56%)
  Pallas kernels  13.1 us (25%)
  waiting for transfers between devices  8.23 us (16%)
  between operations  1.39 us (3%)
    ppermute x11, starting transfers between devices, by_parity(): return lax.ppermute(block, ('space', 'dp'), pairs)  25.1 us
    pallas_call x1, Pallas kernels, body(): pl.pallas_call(functools.partial(forward_kernel, shard=shard), name='forw...  5.71 us
    ppermute x5, waiting for transfers between devices, swapped(): lax.ppermute(block, axis, [(i, i ^ bit) for i in range(lax.axis_size(axis...  5.2 us
    ppermute x5, starting transfers between devices, swapped(): lax.ppermute(block, axis, [(i, i ^ bit) for i in range(lax.axis_size(axis...  3.75 us
    ppermute x11, waiting for transfers between devices, by_parity(): return lax.ppermute(block, ('space', 'dp'), pairs)  3.03 us
    pallas_call x1, Pallas kernels, body(): pl.pallas_call(backward_kernel, name='backward', out_shape=grid_type, in_...  2.54 us
    pallas_call x1, Pallas kernels, body(): pl.pallas_call(prepare_kernel, name='prepare', out_shape=[grid_type, grid...  2.52 us
    pallas_call x1, Pallas kernels, body(): pl.pallas_call(assemble_kernel, name='assemble', out_shape=jax.ShapeDtype...  1.11 us
  transfers between devices with their start and end apart: 16, of which 6 were waited for; matrix products, arithmetic and copies ran while one was open for 0% of the time, Pallas kernels for 8%

profile of v6, /device:TPU:0, one launch (start us, length us, event | category | flops | bytes accessed | tf_op | source)
XLA Modules:
  0.0 51.6 jit_solution(2567568904622582230)
XLA Ops:
  1.3 2.5 %prepare.1 = (bf16[4,8,8,512]{3,2,1,0:T(8,128)(2,1)S(1)}, bf16[4,8,8,512]{3,2,1,0:T(8,128)(2,1)S(1)}, s32[4,26]{1,0:T(4,128)S(1)}, s32[5,1,12]{2,1,0:T(1,128)S(1...) custom-call(bf16[4,8,8,512]{3,2,1,0:T(8,128)(2,1)} %bitcast.15, ...), custom_call_target="tpu_custom_call" | custom-call | tf_op jit(solution)/shard_map/prepare/pallas_call | solution.py:535
  3.8 0.5 %collective-permute-start = (bf16[64,512]{1,0:T(8,128)(2,1)S(1)}, bf16[64,512]{1,0:T(8,128)(2,1)S(1)}, u32[]{:S(2)}, u32[]{:S(2)}) collective-permute-start(bf16[64,512]{1,0:T(8,128)(2,1)S(1)} %get-tuple-element.33.refs_0_), channel_id=1, source_target_pairs={{0,1},{1,0},{2,3},{3,2},{4,5},{5,4},{6,7},{7,6},{8,9},{9,8},{10,11... | collective-permute-start | bytes 196616 | tf_op jit(solution)/shard_map/ppermute | solution.py:481
  4.3 2.6 %collective-permute-start.1 = (bf16[64,512]{1,0:T(8,128)(2,1)S(1)}, bf16[64,512]{1,0:T(8,128)(2,1)S(1)}, u32[]{:S(2)}, u32[]{:S(2)}) collective-permute-start(bf16[64,512]{1,0:T(8,128)(2,1)S(1)} %get-tuple-element.33.refs_0_), channel_id=1, source_target_pairs={{0,2},{1,3},{2,0},{3,1},{4,6},{5,7},{6,4},{7,5},{8,10},{9,11},{10,... | collective-permute-start | bytes 196616 | tf_op jit(solution)/shard_map/ppermute | solution.py:481
  6.9 0.7 %collective-permute-start.3 = (bf16[384,128]{1,0:T(8,128)(2,1)S(1)}, bf16[384,128]{1,0:T(8,128)(2,1)S(1)}, u32[]{:S(2)}, u32[]{:S(2)}) collective-permute-start(bf16[384,128]{1,0:T(8,128)(2,1)S(1)} %get-tuple-element.39), channel_id=1, source_target_pairs={{4,8},{8,4},{12,16},{16,12},{20,24},{24,20},{9,17},{17,9},{13,21},... | collective-permute-start | bytes 294920 | tf_op jit(solution)/shard_map/ppermute | solution.py:491
  7.6 0.7 %collective-permute-start.4 = (bf16[384,128]{1,0:T(8,128)(2,1)S(1)}, bf16[384,128]{1,0:T(8,128)(2,1)S(1)}, u32[]{:S(2)}, u32[]{:S(2)}) collective-permute-start(bf16[384,128]{1,0:T(8,128)(2,1)S(1)} %get-tuple-element.40), channel_id=1, source_target_pairs={{8,16},{16,8},{12,20},{20,12},{5,9},{9,5},{13,17},{17,13},{21,25},... | collective-permute-start | bytes 294920 | tf_op jit(solution)/shard_map/ppermute | solution.py:491
  8.2 4.3 %collective-permute-start.5 = (bf16[384,128]{1,0:T(8,128)(2,1)S(1)}, bf16[384,128]{1,0:T(8,128)(2,1)S(1)}, u32[]{:S(2)}, u32[]{:S(2)}) collective-permute-start(bf16[384,128]{1,0:T(8,128)(2,1)S(1)} %get-tuple-element.41), channel_id=1, source_target_pairs={{0,4},{4,0},{8,12},{12,8},{16,20},{20,16},{24,28},{28,24},{1,9},{9... | collective-permute-start | bytes 294920 | tf_op jit(solution)/shard_map/ppermute | solution.py:491
  12.6 0.0 collective-permute-done.refs_1_
  12.6 4.4 %collective-permute-start.6 = (bf16[384,128]{1,0:T(8,128)(2,1)S(1)}, bf16[384,128]{1,0:T(8,128)(2,1)S(1)}, u32[]{:S(2)}, u32[]{:S(2)}) collective-permute-start(bf16[384,128]{1,0:T(8,128)(2,1)S(1)} %get-tuple-element.42), channel_id=1, source_target_pairs={{0,8},{8,0},{4,12},{12,4},{16,24},{24,16},{20,28},{28,20},{1,5},{5... | collective-permute-start | bytes 294920 | tf_op jit(solution)/shard_map/ppermute | solution.py:491
  17.0 0.0 collective-permute-done.1.refs_2_
  17.0 0.0 collective-permute-start.2
  17.0 1.3 %collective-permute-done.2.refs_3_ = bf16[64,512]{1,0:T(8,128)(2,1)S(1)} collective-permute-done((bf16[64,512]{1,0:T(8,128)(2,1)S(1)}, bf16[64,512]{1,0:T(8,128)(2,1)S(1)}, u32[]{:S(2)}, u32[]{:S(2)}) %collective-permute-start.2) | collective-permute-done | bytes 65568 | tf_op jit(solution)/shard_map/ppermute | solution.py:481
  18.2 0.4 weights.1
  18.6 0.0 collective-permute-done.3.r1
  18.7 0.0 collective-permute-done.4.r2
  18.7 0.0 collective-permute-done.5.r3
  18.7 0.9 %collective-permute-done.6.r4 = bf16[384,128]{1,0:T(8,128)(2,1)S(1)} collective-permute-done((bf16[384,128]{1,0:T(8,128)(2,1)S(1)}, bf16[384,128]{1,0:T(8,128)(2,1)S(1)}, u32[]{:S(2)}, u32[]{:S(2)}) %collective-permute-start.6) | collective-permute-done | bytes 98336 | tf_op jit(solution)/shard_map/ppermute | solution.py:491
  19.6 5.7 %forward.1 = (bf16[4,8,8,512]{3,2,1,0:T(8,128)(2,1)}, bf16[4,8,8,512]{3,2,1,0:T(8,128)(2,1)S(1)}, bf16[2,64,512]{2,1,0:T(8,128)(2,1)S(1)}, bf16[2,64,512]{2,1,0:...) custom-call(bf16[4,8,8,512]{3,2,1,0:T(8,128)(2,1)S(1)} %get-tuple-el, ...), custom_call_target="tpu_custom_call" | custom-call | tf_op jit(solution)/shard_map/forward/pallas_call | solution.py:602
  25.3 0.1 collective-permute-start.9
  25.4 0.7 %collective-permute-start.7 = (bf16[384,128]{1,0:T(8,128)(2,1)S(1)}, bf16[384,128]{1,0:T(8,128)(2,1)S(1)}, u32[]{:S(2)}, u32[]{:S(2)}) collective-permute-start(bf16[384,128]{1,0:T(8,128)(2,1)S(1)} %get-tuple-element.46), channel_id=1, source_target_pairs={{4,8},{8,4},{12,16},{16,12},{20,24},{24,20},{9,17},{17,9},{13,21},... | collective-permute-start | bytes 294920 | tf_op jit(solution)/shard_map/ppermute | solution.py:491
  26.0 0.7 %collective-permute-start.8 = (bf16[384,128]{1,0:T(8,128)(2,1)S(1)}, bf16[384,128]{1,0:T(8,128)(2,1)S(1)}, u32[]{:S(2)}, u32[]{:S(2)}) collective-permute-start(bf16[384,128]{1,0:T(8,128)(2,1)S(1)} %get-tuple-element.47), channel_id=1, source_target_pairs={{8,16},{16,8},{12,20},{20,12},{5,9},{9,5},{13,17},{17,13},{21,25},... | collective-permute-start | bytes 294920 | tf_op jit(solution)/shard_map/ppermute | solution.py:491
  26.7 0.0 collective-permute-done.9.refs_1_
  26.8 0.6 %collective-permute-start.10 = (bf16[1,64,512]{2,1,0:T(8,128)(2,1)S(1)}, bf16[1,64,512]{2,1,0:T(8,128)(2,1)S(1)}, u32[]{:S(2)}, u32[]{:S(2)}) collective-permute-start(bf16[1,64,512]{2,1,0:T(8,128)(2,1)S(1)} %get-tuple-element.58), channel_id=1, source_target_pairs={{0,2},{1,3},{2,0},{3,1},{4,6},{5,7},{6,4},{7,5},{8,10},{9,11},{10,... | collective-permute-start | bytes 196616 | tf_op jit(solution)/shard_map/ppermute | solution.py:481
  27.4 0.0 collective-permute-done.7.refs_2_.r1
  27.4 0.0 collective-permute-done.8.refs_3_.r2
  27.4 3.9 %collective-permute-done.10.refs_1_ = bf16[1,64,512]{2,1,0:T(8,128)(2,1)S(1)} collective-permute-done((bf16[1,64,512]{2,1,0:T(8,128)(2,1)S(1)}, bf16[1,64,512]{2,1,0:T(8,128)(2,1)S(1)}, u32[]{:S(2)}, u32[]{:S(2)}) %collective-permute-start.10) | collective-permute-done | bytes 65568 | tf_op jit(solution)/shard_map/ppermute | solution.py:481
  31.4 4.6 %collective-permute-start.11 = (bf16[384,128]{1,0:T(8,128)(2,1)S(1)}, bf16[384,128]{1,0:T(8,128)(2,1)S(1)}, u32[]{:S(2)}, u32[]{:S(2)}) collective-permute-start(bf16[384,128]{1,0:T(8,128)(2,1)S(1)} %get-tuple-element.52), channel_id=1, source_target_pairs={{0,4},{4,0},{8,12},{12,8},{16,20},{20,16},{24,28},{28,24},{1,9},{9... | collective-permute-start | bytes 294920 | tf_op jit(solution)/shard_map/ppermute | solution.py:491
  36.0 0.1 collective-permute-start.13
  36.1 3.7 %collective-permute-start.12 = (bf16[384,128]{1,0:T(8,128)(2,1)S(1)}, bf16[384,128]{1,0:T(8,128)(2,1)S(1)}, u32[]{:S(2)}, u32[]{:S(2)}) collective-permute-start(bf16[384,128]{1,0:T(8,128)(2,1)S(1)} %get-tuple-element.53), channel_id=1, source_target_pairs={{0,8},{8,0},{4,12},{12,4},{16,24},{24,16},{20,28},{28,20},{1,5},{5... | collective-permute-start | bytes 294920 | tf_op jit(solution)/shard_map/ppermute | solution.py:491
  39.8 0.8 %collective-permute-done.13.refs_1_ = bf16[64,512]{1,0:T(8,128)(2,1)S(1)} collective-permute-done((bf16[64,512]{1,0:T(8,128)(2,1)S(1)}, bf16[64,512]{1,0:T(8,128)(2,1)S(1)}, u32[]{:S(2)}, u32[]{:S(2)}) %collective-permute-start.13) | collective-permute-done | bytes 65568 | tf_op jit(solution)/shard_map/ppermute | solution.py:491
  40.6 0.0 collective-permute-done.11.refs_2_.r3
  40.6 2.8 %collective-permute-start.14 = (bf16[64,512]{1,0:T(8,128)(2,1)S(1)}, bf16[64,512]{1,0:T(8,128)(2,1)S(1)}, u32[]{:S(2)}, u32[]{:S(2)}) collective-permute-start(bf16[64,512]{1,0:T(8,128)(2,1)S(1)} %sum.6.after.refs_0_), channel_id=1, source_target_pairs={{0,8},{4,12},{8,0},{12,4},{16,24},{20,28},{24,16},{28,20},{1,17},{... | collective-permute-start | bytes 196616 | tf_op jit(solution)/shard_map/ppermute | solution.py:491
  43.4 0.0 collective-permute-done.12.r4
  43.4 1.1 %assemble.1.refs_2_.windows = bf16[3,4,2,10,16,256]{5,4,3,2,1,0:T(8,128)(2,1)S(1)} custom-call(bf16[4,8,8,512]{3,2,1,0:T(8,128)(2,1)S(1)} %get-tuple-element.44.grad, s32[4,26]{1,0:T(4,128)S(1)} %get-tuple-element.36.rows, bf16[384,128]{1,0:T(8,128)(2,1)S(1)} %get-tuple-element.45.r0, bf16[384,128]{1,0:T(8,128)(2,1)S(1)} %collective-permute-done.7.refs_2_.r1, ...), custom_call_target="tpu_custom_call" | custom-call | tf_op jit(solution)/shard_map/assemble/pallas_call | solution.py:654
  44.6 1.1 %collective-permute-done.14.refs_1_ = bf16[64,512]{1,0:T(8,128)(2,1)S(1)} collective-permute-done((bf16[64,512]{1,0:T(8,128)(2,1)S(1)}, bf16[64,512]{1,0:T(8,128)(2,1)S(1)}, u32[]{:S(2)}, u32[]{:S(2)}) %collective-permute-start.14) | collective-permute-done | bytes 65568 | tf_op jit(solution)/shard_map/ppermute | solution.py:491
  45.7 2.5 %collective-permute-start.15 = (bf16[64,512]{1,0:T(8,128)(2,1)S(1)}, bf16[64,512]{1,0:T(8,128)(2,1)S(1)}, u32[]{:S(2)}, u32[]{:S(2)}) collective-permute-start(bf16[64,512]{1,0:T(8,128)(2,1)S(1)} %sum.7.after.mine), channel_id=1, source_target_pairs={{0,16},{4,20},{8,24},{12,28},{16,0},{20,4},{24,8},{28,12},{1,5},{5... | collective-permute-start | bytes 196616 | tf_op jit(solution)/shard_map/ppermute | solution.py:491
  48.2 2.5 %backward.1 = bf16[4,8,8,512]{3,2,1,0:T(8,128)(2,1)} custom-call(bf16[3,4,2,10,16,256]{5,4,3,2,1,0:T(8,128)(2,1)S(1)} %assemble.1.refs_2_.windows, bf16[4,8,8,512]{3,2,1,0:T(8,128)(2,1)S(1)} %get-tuple-element.32.mask, bf16[9,256,128]{2,1,0:T(8,128)(2,1)S(1)} %get-tuple-element.55.toeplitz, bf16[64,512]{1,0:T(8,128)(2,1)S(1)} %sum.7.after.mine), custom_call_target="tpu_custom_call" | custom-call | tf_op jit(solution)/shard_map/backward/pallas_call | solution.py:668
  50.8 0.2 collective-permute-done.15.other
  50.9 0.7 %finish.1 = (f32[64,432]{1,0:T(8,128)}, f32[1,16]{1,0:T(1,128)}) custom-call(bf16[64,512]{1,0:T(8,128)(2,1)S(1)} %sum.7.after.mine, bf16[64,512]{1,0:T(8,128)(2,1)S(1)} %collective-permute-done.15.other), custom_call_target="tpu_custom_call" | custom-call | tf_op jit(solution)/shard_map/finish/pallas_call | solution.py:677
  (5 shorter events, 0.1 us)
Async XLA Ops:
  3.8 8.8 %collective-permute-start = (bf16[64,512]{1,0:T(8,128)(2,1)S(1)}, bf16[64,512]{1,0:T(8,128)(2,1)S(1)}, u32[]{:S(2)}, u32[]{:S(2)}) collective-permute-start(bf16[64,512]{1,0:T(8,128)(2,1)S(1)} %get-tuple-element.33.refs_0_), channel_id=1, source_target_pairs={{0,1},{1,0},{2,3},{3,2},{4,5},{5,4},{6,7},{7,6},{8,9},{9,8},{10,11... | collective-permute-start | bytes 196616 | tf_op jit(solution)/shard_map/ppermute | solution.py:481
  4.3 12.6 %collective-permute-start.1 = (bf16[64,512]{1,0:T(8,128)(2,1)S(1)}, bf16[64,512]{1,0:T(8,128)(2,1)S(1)}, u32[]{:S(2)}, u32[]{:S(2)}) collective-permute-start(bf16[64,512]{1,0:T(8,128)(2,1)S(1)} %get-tuple-element.33.refs_0_), channel_id=1, source_target_pairs={{0,2},{1,3},{2,0},{3,1},{4,6},{5,7},{6,4},{7,5},{8,10},{9,11},{10,... | collective-permute-start | bytes 196616 | tf_op jit(solution)/shard_map/ppermute | solution.py:481
  6.9 11.8 %collective-permute-start.3 = (bf16[384,128]{1,0:T(8,128)(2,1)S(1)}, bf16[384,128]{1,0:T(8,128)(2,1)S(1)}, u32[]{:S(2)}, u32[]{:S(2)}) collective-permute-start(bf16[384,128]{1,0:T(8,128)(2,1)S(1)} %get-tuple-element.39), channel_id=1, source_target_pairs={{4,8},{8,4},{12,16},{16,12},{20,24},{24,20},{9,17},{17,9},{13,21},... | collective-permute-start | bytes 294920 | tf_op jit(solution)/shard_map/ppermute | solution.py:491
  7.6 11.1 %collective-permute-start.4 = (bf16[384,128]{1,0:T(8,128)(2,1)S(1)}, bf16[384,128]{1,0:T(8,128)(2,1)S(1)}, u32[]{:S(2)}, u32[]{:S(2)}) collective-permute-start(bf16[384,128]{1,0:T(8,128)(2,1)S(1)} %get-tuple-element.40), channel_id=1, source_target_pairs={{8,16},{16,8},{12,20},{20,12},{5,9},{9,5},{13,17},{17,13},{21,25},... | collective-permute-start | bytes 294920 | tf_op jit(solution)/shard_map/ppermute | solution.py:491
  8.2 10.4 %collective-permute-start.5 = (bf16[384,128]{1,0:T(8,128)(2,1)S(1)}, bf16[384,128]{1,0:T(8,128)(2,1)S(1)}, u32[]{:S(2)}, u32[]{:S(2)}) collective-permute-start(bf16[384,128]{1,0:T(8,128)(2,1)S(1)} %get-tuple-element.41), channel_id=1, source_target_pairs={{0,4},{4,0},{8,12},{12,8},{16,20},{20,16},{24,28},{28,24},{1,9},{9... | collective-permute-start | bytes 294920 | tf_op jit(solution)/shard_map/ppermute | solution.py:491
  12.6 7.0 %collective-permute-start.6 = (bf16[384,128]{1,0:T(8,128)(2,1)S(1)}, bf16[384,128]{1,0:T(8,128)(2,1)S(1)}, u32[]{:S(2)}, u32[]{:S(2)}) collective-permute-start(bf16[384,128]{1,0:T(8,128)(2,1)S(1)} %get-tuple-element.42), channel_id=1, source_target_pairs={{0,8},{8,0},{4,12},{12,4},{16,24},{24,16},{20,28},{28,20},{1,5},{5... | collective-permute-start | bytes 294920 | tf_op jit(solution)/shard_map/ppermute | solution.py:491
  17.0 1.3 %collective-permute-start.2 = (bf16[64,512]{1,0:T(8,128)(2,1)S(1)}, bf16[64,512]{1,0:T(8,128)(2,1)S(1)}, u32[]{:S(2)}, u32[]{:S(2)}) collective-permute-start(bf16[64,512]{1,0:T(8,128)(2,1)S(1)} %collective-permute-done.1.refs_2_), channel_id=1, source_target_pairs={{0,1},{1,0},{2,3},{3,2},{4,5},{5,4},{6,7},{7,6},{8,9},{9,8},{10,11... | collective-permute-start | bytes 196616 | tf_op jit(solution)/shard_map/ppermute | solution.py:481
  25.3 1.4 %collective-permute-start.9 = (bf16[2,64,512]{2,1,0:T(8,128)(2,1)S(1)}, bf16[2,64,512]{2,1,0:T(8,128)(2,1)S(1)}, u32[]{:S(2)}, u32[]{:S(2)}) collective-permute-start(bf16[2,64,512]{2,1,0:T(8,128)(2,1)S(1)} %get-tuple-element.49), channel_id=1, source_target_pairs={{0,1},{1,0},{2,3},{3,2},{4,5},{5,4},{6,7},{7,6},{8,9},{9,8},{10,11... | collective-permute-start | bytes 393224 | tf_op jit(solution)/shard_map/ppermute | solution.py:481
  25.4 2.0 %collective-permute-start.7 = (bf16[384,128]{1,0:T(8,128)(2,1)S(1)}, bf16[384,128]{1,0:T(8,128)(2,1)S(1)}, u32[]{:S(2)}, u32[]{:S(2)}) collective-permute-start(bf16[384,128]{1,0:T(8,128)(2,1)S(1)} %get-tuple-element.46), channel_id=1, source_target_pairs={{4,8},{8,4},{12,16},{16,12},{20,24},{24,20},{9,17},{17,9},{13,21},... | collective-permute-start | bytes 294920 | tf_op jit(solution)/shard_map/ppermute | solution.py:491
  26.0 1.4 %collective-permute-start.8 = (bf16[384,128]{1,0:T(8,128)(2,1)S(1)}, bf16[384,128]{1,0:T(8,128)(2,1)S(1)}, u32[]{:S(2)}, u32[]{:S(2)}) collective-permute-start(bf16[384,128]{1,0:T(8,128)(2,1)S(1)} %get-tuple-element.47), channel_id=1, source_target_pairs={{8,16},{16,8},{12,20},{20,12},{5,9},{9,5},{13,17},{17,13},{21,25},... | collective-permute-start | bytes 294920 | tf_op jit(solution)/shard_map/ppermute | solution.py:491
  26.8 4.5 %collective-permute-start.10 = (bf16[1,64,512]{2,1,0:T(8,128)(2,1)S(1)}, bf16[1,64,512]{2,1,0:T(8,128)(2,1)S(1)}, u32[]{:S(2)}, u32[]{:S(2)}) collective-permute-start(bf16[1,64,512]{2,1,0:T(8,128)(2,1)S(1)} %get-tuple-element.58), channel_id=1, source_target_pairs={{0,2},{1,3},{2,0},{3,1},{4,6},{5,7},{6,4},{7,5},{8,10},{9,11},{10,... | collective-permute-start | bytes 196616 | tf_op jit(solution)/shard_map/ppermute | solution.py:481
  31.4 9.3 %collective-permute-start.11 = (bf16[384,128]{1,0:T(8,128)(2,1)S(1)}, bf16[384,128]{1,0:T(8,128)(2,1)S(1)}, u32[]{:S(2)}, u32[]{:S(2)}) collective-permute-start(bf16[384,128]{1,0:T(8,128)(2,1)S(1)} %get-tuple-element.52), channel_id=1, source_target_pairs={{0,4},{4,0},{8,12},{12,8},{16,20},{20,16},{24,28},{28,24},{1,9},{9... | collective-permute-start | bytes 294920 | tf_op jit(solution)/shard_map/ppermute | solution.py:491
  36.0 4.6 %collective-permute-start.13 = (bf16[64,512]{1,0:T(8,128)(2,1)S(1)}, bf16[64,512]{1,0:T(8,128)(2,1)S(1)}, u32[]{:S(2)}, u32[]{:S(2)}) collective-permute-start(bf16[64,512]{1,0:T(8,128)(2,1)S(1)} %bitcast.12), channel_id=1, source_target_pairs={{0,4},{4,0},{8,12},{12,8},{16,20},{20,16},{24,28},{28,24},{1,9},{5... | collective-permute-start | bytes 196616 | tf_op jit(solution)/shard_map/ppermute | solution.py:491
  36.1 7.4 %collective-permute-start.12 = (bf16[384,128]{1,0:T(8,128)(2,1)S(1)}, bf16[384,128]{1,0:T(8,128)(2,1)S(1)}, u32[]{:S(2)}, u32[]{:S(2)}) collective-permute-start(bf16[384,128]{1,0:T(8,128)(2,1)S(1)} %get-tuple-element.53), channel_id=1, source_target_pairs={{0,8},{8,0},{4,12},{12,4},{16,24},{24,16},{20,28},{28,20},{1,5},{5... | collective-permute-start | bytes 294920 | tf_op jit(solution)/shard_map/ppermute | solution.py:491
  40.6 5.0 %collective-permute-start.14 = (bf16[64,512]{1,0:T(8,128)(2,1)S(1)}, bf16[64,512]{1,0:T(8,128)(2,1)S(1)}, u32[]{:S(2)}, u32[]{:S(2)}) collective-permute-start(bf16[64,512]{1,0:T(8,128)(2,1)S(1)} %sum.6.after.refs_0_), channel_id=1, source_target_pairs={{0,8},{4,12},{8,0},{12,4},{16,24},{20,28},{24,16},{28,20},{1,17},{... | collective-permute-start | bytes 196616 | tf_op jit(solution)/shard_map/ppermute | solution.py:491
  45.7 5.2 %collective-permute-start.15 = (bf16[64,512]{1,0:T(8,128)(2,1)S(1)}, bf16[64,512]{1,0:T(8,128)(2,1)S(1)}, u32[]{:S(2)}, u32[]{:S(2)}) collective-permute-start(bf16[64,512]{1,0:T(8,128)(2,1)S(1)} %sum.7.after.mine), channel_id=1, source_target_pairs={{0,16},{4,20},{8,24},{12,28},{16,0},{20,4},{24,8},{28,12},{1,5},{5... | collective-permute-start | bytes 196616 | tf_op jit(solution)/shard_map/ppermute | solution.py:491

commit v7 on v6

--- a/solution.py
+++ b/solution.py
@@ -194,7 +194,7 @@
     sub = lax.broadcasted_iota(jnp.int32, (8, LANES), 0)
     top, bottom = sub == 0, sub == 7
 
-    def put(pair, xp, per_brick):
+    def put(pair, half, bit, per_brick):
         for e in range(3):
             stacked = [
                 jnp.concatenate([per_brick[0][e][i], per_brick[1][e][i]], axis=0)
@@ -204,8 +204,8 @@
             before = [stacked[4]] + stacked[:3]
             after = stacked[1:4] + [stacked[4]]
             for q in range(4):
-                windows[e, q, pair, xp, :, 0:LANES] = stacked[q].astype(BF16)
-                windows[e, q, pair, xp, :, LANES:] = jnp.where(
+                windows[e, q, pair, half, bit, :, 0:LANES] = stacked[q].astype(BF16)
+                windows[e, q, pair, half, bit, :, LANES:] = jnp.where(
                     low16, after[q], before[q]
                 ).astype(BF16)
 
@@ -249,39 +249,81 @@
                         ],
                     ]
                 )
-            put(pair, 0 if ox < 0 else 9, per_brick)
-
-        def one_x(x, carry):
-            per_brick = []
-            for b2 in range(2):
-                brick = pair * 2 + b2
-                block = source[brick, x].astype(F32)
-                centre = [block[:, q * LANES : (q + 1) * LANES] for q in range(4)]
-                centre.append(walls[b2, pl.ds(pl.multiple_of(x * 8, 8), 8), :])
-                lower = [
-                    jnp.broadcast_to(sides[b2, 0, i, pl.ds(x, 1), :], (8, LANES))
-                    for i in range(5)
-                ]
-                upper = [
-                    jnp.broadcast_to(sides[b2, 1, i, pl.ds(x, 1), :], (8, LANES))
-                    for i in range(5)
-                ]
-                per_brick.append(
-                    [
-                        [jnp.where(top, l, pltpu.roll(c, 1, 0)) for l, c in zip(lower, centre)],
-                        centre,
+            put(pair, 0 if ox < 0 else 4, 0 if ox < 0 else 1, per_brick)
+
+        def two_x(i, carry):
+            for bit in range(2):
+                x = 2 * i + bit
+                per_brick = []
+                for b2 in range(2):
+                    brick = pair * 2 + b2
+                    block = source[brick, i, bit].astype(F32)
+                    centre = [block[:, q * LANES : (q + 1) * LANES] for q in range(4)]
+                    centre.append(walls[b2, pl.ds(pl.multiple_of(x * 8, 8), 8), :])
+                    lower = [
+                        jnp.broadcast_to(sides[b2, 0, n, pl.ds(x, 1), :], (8, LANES))
+                        for n in range(5)
+                    ]
+                    upper = [
+                        jnp.broadcast_to(sides[b2, 1, n, pl.ds(x, 1), :], (8, LANES))
+                        for n in range(5)
+                    ]
+                    per_brick.append(
                         [
-                            jnp.where(bottom, u, pltpu.roll(c, 7, 0))
-                            for u, c in zip(upper, centre)
-                        ],
-                    ]
-                )
-            put(pair, x + 1, per_brick)
+                            [
+                                jnp.where(top, l, pltpu.roll(c, 1, 0))
+                                for l, c in zip(lower, centre)
+                            ],
+                            centre,
+                            [
+                                jnp.where(bottom, u, pltpu.roll(c, 7, 0))
+                                for u, c in zip(upper, centre)
+                            ],
+                        ]
+                    )
+                put(pair, i + bit, 1 - bit, per_brick)
             return carry
 
-        return lax.fori_loop(0, 8, one_x, carry)
+        return lax.fori_loop(0, 4, two_x, carry)
 
     lax.fori_loop(0, windows.shape[2], one_pair, 0)
+
+
+def lane_block(d, e):
+    return slice((3 * d + e) * 256, (3 * d + e + 1) * 256)
+
+
+def tap_rows(windows, d, e):
+    block = windows[e, :, :, d // 2 : d // 2 + 4, d % 2]
+    return block.reshape(-1, block.shape[-1])
+
+
+def all_taps(windows):
+    return jnp.concatenate(
+        [tap_rows(windows, d, e) for d in range(4) for e in range(3)], axis=1
+    )
+
+
+def chunk_places(bricks):
+    return [(2 * pair + b2, i) for pair in range(bricks // 2) for i in range(4) for b2 in range(2)]
+
+
+def chunk_of(ref, q):
+    lanes = slice(q * LANES, (q + 1) * LANES)
+    return jnp.concatenate(
+        [
+            jnp.concatenate([ref[b, i, x, :, lanes].astype(F32) for x in range(2)], axis=1)
+            for b, i in chunk_places(ref.shape[0])
+        ],
+        axis=0,
+    )
+
+
+def put_chunk(ref, q, value):
+    for n, (b, i) in enumerate(chunk_places(ref.shape[0])):
+        for x in range(2):
+            part = value[8 * n : 8 * n + 8, x * LANES : (x + 1) * LANES]
+            ref[b, i, x, :, q * LANES : (q + 1) * LANES] = part.astype(ref.dtype)
 
 
 def weights_kernel(*refs, shard, groups):
@@ -296,21 +338,36 @@
     flat[:, total:] = jnp.zeros((64, flat.shape[1] - total), F32)
     shifted[:, :] = pltpu.roll(flat[...], flat.shape[1] - 64, 1)
     low = low_half((64, LANES))
+    for e in range(3):
+        for x in range(2):
+            half = slice(x * LANES, (x + 1) * LANES)
+            forward_out[half, lane_block(3 * (1 - x), e)] = jnp.zeros((LANES, 256), BF16)
+            backward_out[lane_block(3 * (1 - x), e), half] = jnp.zeros((256, LANES), BF16)
     for ae in range(9):
+        a, e = ae // 3, ae % 3
         one = taps_pair(flat, shifted, 3 * ae)
         two = jnp.where(low, taps_pair(flat, shifted, 3 * ae + 2), 0.0)
         late = jnp.concatenate([one, two], axis=1)
-        forward_out[ae, 64:128, :] = late.astype(BF16)
-        forward_out[ae, 0:64, :] = pltpu.roll(late, 192, 1).astype(BF16)
+        band = jnp.concatenate([pltpu.roll(late, 192, 1), late], axis=0).astype(BF16)
+        for x in range(2):
+            forward_out[x * LANES : (x + 1) * LANES, lane_block(a + x, e)] = band
     for ae in range(9):
+        a, e = ae // 3, ae % 3
         m = 3 * (8 - ae)
         first = taps_pair(flat, shifted, m)
         second = taps_pair(flat, shifted, m + 1)
         third = taps_pair(flat, shifted, m + 2)
-        backward_out[ae, 0:64, :] = second.astype(BF16)
-        backward_out[ae, 64:128, :] = first.astype(BF16)
-        backward_out[ae, 128:192, :] = jnp.where(low, 0.0, pltpu.roll(first, 64, 1)).astype(BF16)
-        backward_out[ae, 192:256, :] = jnp.where(low, third, 0.0).astype(BF16)
+        band = jnp.concatenate(
+            [
+                second,
+                first,
+                jnp.where(low, 0.0, pltpu.roll(first, 64, 1)),
+                jnp.where(low, third, 0.0),
+            ],
+            axis=0,
+        ).astype(BF16)
+        for x in range(2):
+            backward_out[lane_block(a + x, e), x * LANES : (x + 1) * LANES] = band
 
     lane = lax.broadcasted_iota(jnp.int32, (8, LANES), 1)
     bias_lane = shard % LANES
@@ -348,53 +405,43 @@
     fetch.wait()
     values[:, bricks * 64 :, :] = jnp.zeros((4, 64, LANES), F32)
 
-    def one_chunk(q, bias_sum):
-        total = jnp.zeros((pairs * LANES, LANES), F32)
+    bias_row = jnp.concatenate([bias_row, bias_row], axis=1)
+    total = lax.dot_general(all_taps(windows), toeplitz[...], DN_NT, preferred_element_type=F32)
+    rows_of_chunk = total.shape[0] // 4
+    bias_sum = jnp.zeros((8, 256), F32)
+    for q in range(4):
+        p = total[q * rows_of_chunk : (q + 1) * rows_of_chunk] + bias_row
+        active = chunk_of(mask, q)
+        sig = jax.nn.sigmoid(p)
+        put_chunk(block_out, q, p * sig * active)
+        grad = (chunk_of(cotangent, q) * sig * (1.0 + p * (1.0 - sig)) * active).astype(BF16)
+        wide = grad.astype(F32)
+        put_chunk(grad_out, q, wide)
+        for n, (brick, i) in enumerate(chunk_places(bricks)):
+            for x in range(2):
+                at = brick * 64 + (2 * i + x) * 8
+                values[q, at : at + 8, :] = wide[
+                    8 * n : 8 * n + 8, x * LANES : (x + 1) * LANES
+                ]
+        flipped[:, q * rows_of_chunk : (q + 1) * rows_of_chunk] = jnp.transpose(wide).astype(BF16)
+        bias_sum += jnp.sum(wide.reshape(-1, 8, 256), axis=0)
+    bias_sum = bias_sum[:, 0:LANES] + bias_sum[:, LANES:]
+    pack_units(values, send, (u0, u1, u2, u3, u4))
+
+    for e in range(3):
+        products = [
+            jnp.dot(flipped[...], tap_rows(windows, d, e), preferred_element_type=F32)
+            for d in range(4)
+        ]
         for a in range(3):
-            for e in range(3):
-                window = windows[e, q, :, a : a + 8].reshape(pairs * LANES, 256)
-                total += lax.dot_general(
-                    window, toeplitz[3 * a + e], DN_NT, preferred_element_type=F32
-                )
-        pre = (total + bias_row).reshape(pairs, 8, 2, 8, LANES)
-        lanes = pl.ds(pl.multiple_of(q * LANES, LANES), LANES)
-        for brick in range(bricks):
-            p = pre[brick // 2, :, brick % 2]
-            active = mask[brick, :, :, lanes].astype(F32)
-            sig = jax.nn.sigmoid(p)
-            block_out[brick, :, :, lanes] = (p * sig * active).astype(BF16)
-            grad = (
-                cotangent[brick, :, :, lanes].astype(F32)
-                * sig
-                * (1.0 + p * (1.0 - sig))
-                * active
-            ).astype(BF16)
-            grad_out[brick, :, :, lanes] = grad
-            wide = grad.astype(F32).reshape(64, LANES)
-            values[q, brick * 64 : (brick + 1) * 64, :] = wide
-            bias_sum += jnp.sum(wide.reshape(8, 8, LANES), axis=0)
-        return bias_sum
-
-    bias_sum = lax.fori_loop(0, 4, one_chunk, jnp.zeros((8, LANES), F32))
-    pack_units(values, send, (u0, u1, u2, u3, u4))
-
-    for q in range(4):
-        for pair in range(pairs):
-            by_x = []
-            for x in range(8):
-                for b2 in range(2):
-                    at = (pair * 2 + b2) * 64 + x * 8
-                    by_x.append(values[q, at : at + 8, :])
-            flipped[q, :, pair * LANES : (pair + 1) * LANES] = jnp.transpose(
-                jnp.concatenate(by_x, axis=0)
-            ).astype(BF16)
-    for ae in range(9):
-        a, e = ae // 3, ae % 3
-        total = jnp.zeros((LANES, 256), F32)
-        for q in range(4):
-            window = windows[e, q, :, a : a + 8].reshape(pairs * LANES, 256)
-            total += jnp.dot(flipped[q], window, preferred_element_type=F32)
-        flat[:, 192 * ae : 192 * ae + 256] = total[64:128] + pltpu.roll(total[0:64], 64, 1)
+            both = products[a][0:LANES] + products[a + 1][LANES:]
+            shifted[64 * a : 64 * a + 64, 256 * e : 256 * e + 256] = both[64:] + pltpu.roll(
+                both[0:64], 64, 1
+            )
+    for a in range(3):
+        for e in range(3):
+            at = 192 * (3 * a + e)
+            flat[:, at : at + 256] = shifted[64 * a : 64 * a + 64, 256 * e : 256 * e + 256]
 
     width = keep_out.shape[2]
     bias_all = jnp.sum(bias_sum, axis=0, keepdims=True)
@@ -407,11 +454,11 @@
     me = lax.axis_index("dp")
     for k in range(groups):
         part = flat[:, k * shard : (k + 1) * shard]
-        shifted[:, 0:shard] = part
-        shifted[:, shard:width] = jnp.zeros((64, width - shard), F32)
+        shifted[0:64, 0:shard] = part
+        shifted[0:64, shard:width] = jnp.zeros((64, width - shard), F32)
         tile = shifted[0:8, bias_tile : bias_tile + LANES]
         shifted[0:8, bias_tile : bias_tile + LANES] = jnp.where(keep, bias_all, tile)
-        block = shifted[:, 0:width].astype(BF16)
+        block = shifted[0:64, 0:width].astype(BF16)
         for m in range(groups):
 
             @pl.when(me ^ m == k)
@@ -445,23 +492,11 @@
 
 def backward_kernel(windows, mask, toeplitz, after, out):
     del after
-    bricks = mask.shape[0]
-    pairs = bricks // 2
-
-    def one_chunk(q, carry):
-        total = jnp.zeros((pairs * LANES, LANES), F32)
-        for a in range(3):
-            for e in range(3):
-                window = windows[e, q, :, a : a + 8].reshape(pairs * LANES, 256)
-                total += jnp.dot(window, toeplitz[3 * a + e], preferred_element_type=F32)
-        total = total.reshape(pairs, 8, 2, 8, LANES)
-        lanes = pl.ds(pl.multiple_of(q * LANES, LANES), LANES)
-        for brick in range(bricks):
-            active = mask[brick, :, :, lanes].astype(F32)
-            out[brick, :, :, lanes] = (total[brick // 2, :, brick % 2] * active).astype(BF16)
-        return carry
-
-    lax.fori_loop(0, 4, one_chunk, 0)
+    total = jnp.dot(all_taps(windows), toeplitz[...], preferred_element_type=F32)
+    rows_of_chunk = total.shape[0] // 4
+    for q in range(4):
+        part = total[q * rows_of_chunk : (q + 1) * rows_of_chunk]
+        put_chunk(out, q, part * chunk_of(mask, q))
 
 
 def finish_kernel(mine, other, weight_out, bias_out):
@@ -516,8 +551,8 @@
 
 
 def body(features, occupancy, counts, send_units, neighbours, weight, conv_bias, cotangent):
-    grid_shape = features.shape[1:]
-    bricks = grid_shape[0]
+    bricks, edge, _, lanes = features.shape[1:]
+    grid_shape = (bricks, edge // 2, 2, edge, lanes)
     pairs = bricks // 2
     spread, links = send_units.shape[2:]
     shard, channels = weight.shape
@@ -560,7 +595,7 @@
         *(
             pltpu.with_memory_space_constraint(operand, pltpu.HBM)
             for operand in (
-                features[0],
+                features.reshape(grid_shape),
                 occupancy[0],
                 send_units.transpose(0, 2, 1, 3).reshape(send_shape),
                 neighbours[0],
@@ -584,8 +619,8 @@
         functools.partial(weights_kernel, shard=shard, groups=groups),
         name="weights",
         out_shape=[
-            jax.ShapeDtypeStruct((9, LANES, 256), BF16),
-            jax.ShapeDtypeStruct((9, 256, LANES), BF16),
+            jax.ShapeDtypeStruct((256, 12 * 256), BF16),
+            jax.ShapeDtypeStruct((12 * 256, 256), BF16),
             jax.ShapeDtypeStruct((8, LANES), F32),
         ],
         in_specs=[vmem()] * groups,
@@ -595,7 +630,7 @@
     )(*(shards[m] for m in range(groups)))
 
     table = pltpu.VMEM((spread * unit_rows + Z_ROWS, LANES), BF16)
-    windows = pltpu.VMEM((3, 4, pairs, 10, 16, 256), BF16)
+    windows = pltpu.VMEM((3, 4, pairs, 5, 2, 16, 256), BF16)
     sides = pltpu.VMEM((2, 2, 5, 8, LANES), F32)
     walls = pltpu.VMEM((2, 64, LANES), F32)
     half_type = jax.ShapeDtypeStruct((groups // 2, channels, width), BF16)
@@ -613,9 +648,9 @@
             sides,
             walls,
             flat,
-            flat,
+            pltpu.VMEM((192, 3 * 256), F32),
             pltpu.VMEM((4, (bricks + 1) * 64, LANES), F32),
-            pltpu.VMEM((4, LANES, pairs * LANES), BF16),
+            pltpu.VMEM((256, bricks * LANES), BF16),
             pltpu.VMEM(grid_shape, BF16),
             pltpu.SemaphoreType.DMA,
         ],
@@ -623,7 +658,7 @@
     )(
         masked,
         mask,
-        pltpu.with_memory_space_constraint(cotangent[0], pltpu.HBM),
+        pltpu.with_memory_space_constraint(cotangent.reshape(grid_shape), pltpu.HBM),
         band_forward,
         bias,
         rows,
@@ -686,8 +721,8 @@
         compiler_params=params,
     )(total, other)
     return (
-        block_output[None],
-        grad_input[None],
+        block_output.reshape(features.shape),
+        grad_input.reshape(features.shape),
         weight_share.T,
         bias_share.reshape(count),
     )

time: 51.8 us -> 52.7 us (1.017)
    pallas_call x1, Pallas kernels: 5.71 us -> 6.6 us  [body(): pl.pallas_call(functools.partial(forward_kernel, shard=shard), name='forw...]
    pallas_call x1, Pallas kernels: 2.54 us -> 1.68 us  [body(): pl.pallas_call(backward_kernel, name='backward', out_shape=grid_type, in_...]
    ppermute x11, starting transfers between devices: 25.1 us -> 25.7 us  [by_parity(): return lax.ppermute(block, ('space', 'dp'), pairs)]
  transfers between devices with their start and end apart: 16 -> 16, of which waited for: 6 -> 6; matrix products, arithmetic and copies ran while one was open for 0% -> 0% of each run, Pallas kernels for 8% -> 6%
where the time goes in v7:
time: 52.7 us; the launch traced here: 52.5 us
  starting transfers between devices  29.4 us (56%)
  Pallas kernels  13.2 us (25%)
  waiting for transfers between devices  8.45 us (16%)
  between operations  1.42 us (3%)
    ppermute x11, starting transfers between devices, by_parity(): return lax.ppermute(block, ('space', 'dp'), pairs)  25.7 us
    pallas_call x1, Pallas kernels, body(): pl.pallas_call(functools.partial(forward_kernel, shard=shard), name='forw...  6.6 us
    ppermute x5, waiting for transfers between devices, swapped(): lax.ppermute(block, axis, [(i, i ^ bit) for i in range(lax.axis_size(axis...  5.2 us
    ppermute x5, starting transfers between devices, swapped(): lax.ppermute(block, axis, [(i, i ^ bit) for i in range(lax.axis_size(axis...  3.68 us
    ppermute x11, waiting for transfers between devices, by_parity(): return lax.ppermute(block, ('space', 'dp'), pairs)  3.26 us
    pallas_call x1, Pallas kernels, body(): pl.pallas_call(prepare_kernel, name='prepare', out_shape=[grid_type, grid...  2.52 us
    pallas_call x1, Pallas kernels, body(): pl.pallas_call(backward_kernel, name='backward', out_shape=grid_type, in_...  1.68 us
    pallas_call x1, Pallas kernels, body(): pl.pallas_call(assemble_kernel, name='assemble', out_shape=jax.ShapeDtype...  1.07 us
  transfers between devices with their start and end apart: 16, of which 6 were waited for; matrix products, arithmetic and copies ran while one was open for 0% of the time, Pallas kernels for 6%

profile of v7, /device:TPU:0, one launch (start us, length us, event | category | flops | bytes accessed | tf_op | source)
XLA Modules:
  0.0 52.5 jit_solution(5169132240033940981)
XLA Ops:
  1.3 2.5 %prepare.1 = (bf16[4,4,2,8,512]{4,3,2,1,0:T(8,128)(2,1)S(1)}, bf16[4,4,2,8,512]{4,3,2,1,0:T(8,128)(2,1)S(1)}, s32[4,26]{1,0:T(4,128)S(1)}, s32[5,1,12]{2,1,0:T(1...) custom-call(bf16[4,4,2,8,512]{4,3,2,1,0:T(8,128)(2,1)} %bitcast.16, ...), custom_call_target="tpu_custom_call" | custom-call | tf_op jit(solution)/shard_map/prepare/pallas_call | solution.py:570
  3.8 3.0 %collective-permute-start.1 = (bf16[64,512]{1,0:T(8,128)(2,1)S(1)}, bf16[64,512]{1,0:T(8,128)(2,1)S(1)}, u32[]{:S(2)}, u32[]{:S(2)}) collective-permute-start(bf16[64,512]{1,0:T(8,128)(2,1)S(1)} %get-tuple-element.33.refs_0_), channel_id=1, source_target_pairs={{0,2},{1,3},{2,0},{3,1},{4,6},{5,7},{6,4},{7,5},{8,10},{9,11},{10,... | collective-permute-start | bytes 196616 | tf_op jit(solution)/shard_map/ppermute | solution.py:516
  6.8 0.0 collective-permute-start
  6.8 0.7 %collective-permute-start.3 = (bf16[384,128]{1,0:T(8,128)(2,1)S(1)}, bf16[384,128]{1,0:T(8,128)(2,1)S(1)}, u32[]{:S(2)}, u32[]{:S(2)}) collective-permute-start(bf16[384,128]{1,0:T(8,128)(2,1)S(1)} %get-tuple-element.39), channel_id=1, source_target_pairs={{4,8},{8,4},{12,16},{16,12},{20,24},{24,20},{9,17},{17,9},{13,21},... | collective-permute-start | bytes 294920 | tf_op jit(solution)/shard_map/ppermute | solution.py:526
  7.5 0.7 %collective-permute-start.4 = (bf16[384,128]{1,0:T(8,128)(2,1)S(1)}, bf16[384,128]{1,0:T(8,128)(2,1)S(1)}, u32[]{:S(2)}, u32[]{:S(2)}) collective-permute-start(bf16[384,128]{1,0:T(8,128)(2,1)S(1)} %get-tuple-element.40), channel_id=1, source_target_pairs={{8,16},{16,8},{12,20},{20,12},{5,9},{9,5},{13,17},{17,13},{21,25},... | collective-permute-start | bytes 294920 | tf_op jit(solution)/shard_map/ppermute | solution.py:526
  8.2 4.3 %collective-permute-start.5 = (bf16[384,128]{1,0:T(8,128)(2,1)S(1)}, bf16[384,128]{1,0:T(8,128)(2,1)S(1)}, u32[]{:S(2)}, u32[]{:S(2)}) collective-permute-start(bf16[384,128]{1,0:T(8,128)(2,1)S(1)} %get-tuple-element.41), channel_id=1, source_target_pairs={{0,4},{4,0},{8,12},{12,8},{16,20},{20,16},{24,28},{28,24},{1,9},{9... | collective-permute-start | bytes 294920 | tf_op jit(solution)/shard_map/ppermute | solution.py:526
  12.5 0.0 collective-permute-done.1.refs_2_
  12.5 4.4 %collective-permute-start.6 = (bf16[384,128]{1,0:T(8,128)(2,1)S(1)}, bf16[384,128]{1,0:T(8,128)(2,1)S(1)}, u32[]{:S(2)}, u32[]{:S(2)}) collective-permute-start(bf16[384,128]{1,0:T(8,128)(2,1)S(1)} %get-tuple-element.42), channel_id=1, source_target_pairs={{0,8},{8,0},{4,12},{12,4},{16,24},{24,16},{20,28},{28,20},{1,5},{5... | collective-permute-start | bytes 294920 | tf_op jit(solution)/shard_map/ppermute | solution.py:526
  16.9 0.0 collective-permute-done.refs_1_
  16.9 0.0 collective-permute-start.2
  16.9 1.3 %collective-permute-done.2.refs_3_ = bf16[64,512]{1,0:T(8,128)(2,1)S(1)} collective-permute-done((bf16[64,512]{1,0:T(8,128)(2,1)S(1)}, bf16[64,512]{1,0:T(8,128)(2,1)S(1)}, u32[]{:S(2)}, u32[]{:S(2)}) %collective-permute-start.2) | collective-permute-done | bytes 65568 | tf_op jit(solution)/shard_map/ppermute | solution.py:516
  18.2 0.5 %weights.1 = (bf16[256,3072]{1,0:T(8,128)(2,1)S(1)}, bf16[3072,256]{1,0:T(8,128)(2,1)S(1)}, f32[8,128]{1,0:T(8,128)S(1)}) custom-call(bf16[64,512]{1,0:T(8,128)(2,1)S(1)} %get-tuple-element.33.refs_0_, bf16[64,512]{1,0:T(8,128)(2,1)S(1)} %collective-permute-done.refs_1_, bf16[64,512]{1,0:T(8,128)(2,1)S(1)} %collective-permute-done.1.refs_2_, ...), custom_call_target="tpu_custom_call" | custom-call | tf_op jit(solution)/shard_map/weights/pallas_call | solution.py:618
  18.7 0.0 collective-permute-done.3.r1
  18.7 0.0 collective-permute-done.4.r2
  18.7 0.0 collective-permute-done.5.r3
  18.7 0.8 %collective-permute-done.6.r4 = bf16[384,128]{1,0:T(8,128)(2,1)S(1)} collective-permute-done((bf16[384,128]{1,0:T(8,128)(2,1)S(1)}, bf16[384,128]{1,0:T(8,128)(2,1)S(1)}, u32[]{:S(2)}, u32[]{:S(2)}) %collective-permute-start.6) | collective-permute-done | bytes 98336 | tf_op jit(solution)/shard_map/ppermute | solution.py:526
  19.5 6.6 %forward.1 = (bf16[4,4,2,8,512]{4,3,2,1,0:T(8,128)(2,1)}, bf16[4,4,2,8,512]{4,3,2,1,0:T(8,128)(2,1)S(1)}, bf16[2,64,512]{2,1,0:T(8,128)(2,1)S(1)}, bf16[2,64,512...) custom-call(bf16[4,4,2,8,512]{4,3,2,1,0:T(8,128)(2,1)S(1)} %get-tupl, ...), custom_call_target="tpu_custom_call" | custom-call | tf_op jit(solution)/shard_map/forward/pallas_call | solution.py:637
  26.1 0.1 collective-permute-start.9
  26.2 0.7 %collective-permute-start.7 = (bf16[384,128]{1,0:T(8,128)(2,1)S(1)}, bf16[384,128]{1,0:T(8,128)(2,1)S(1)}, u32[]{:S(2)}, u32[]{:S(2)}) collective-permute-start(bf16[384,128]{1,0:T(8,128)(2,1)S(1)} %get-tuple-element.46), channel_id=1, source_target_pairs={{4,8},{8,4},{12,16},{16,12},{20,24},{24,20},{9,17},{17,9},{13,21},... | collective-permute-start | bytes 294920 | tf_op jit(solution)/shard_map/ppermute | solution.py:526
  26.9 0.7 %collective-permute-start.8 = (bf16[384,128]{1,0:T(8,128)(2,1)S(1)}, bf16[384,128]{1,0:T(8,128)(2,1)S(1)}, u32[]{:S(2)}, u32[]{:S(2)}) collective-permute-start(bf16[384,128]{1,0:T(8,128)(2,1)S(1)} %get-tuple-element.47), channel_id=1, source_target_pairs={{8,16},{16,8},{12,20},{20,12},{5,9},{9,5},{13,17},{17,13},{21,25},... | collective-permute-start | bytes 294920 | tf_op jit(solution)/shard_map/ppermute | solution.py:526
  27.5 0.0 collective-permute-done.9.refs_1_
  27.6 0.6 %collective-permute-start.10 = (bf16[1,64,512]{2,1,0:T(8,128)(2,1)S(1)}, bf16[1,64,512]{2,1,0:T(8,128)(2,1)S(1)}, u32[]{:S(2)}, u32[]{:S(2)}) collective-permute-start(bf16[1,64,512]{2,1,0:T(8,128)(2,1)S(1)} %get-tuple-element.58), channel_id=1, source_target_pairs={{0,2},{1,3},{2,0},{3,1},{4,6},{5,7},{6,4},{7,5},{8,10},{9,11},{10,... | collective-permute-start | bytes 196616 | tf_op jit(solution)/shard_map/ppermute | solution.py:516
  28.2 0.0 collective-permute-done.7.refs_2_.r1
  28.2 0.0 collective-permute-done.8.refs_3_.r2
  28.2 3.9 %collective-permute-done.10.refs_1_ = bf16[1,64,512]{2,1,0:T(8,128)(2,1)S(1)} collective-permute-done((bf16[1,64,512]{2,1,0:T(8,128)(2,1)S(1)}, bf16[1,64,512]{2,1,0:T(8,128)(2,1)S(1)}, u32[]{:S(2)}, u32[]{:S(2)}) %collective-permute-start.10) | collective-permute-done | bytes 65568 | tf_op jit(solution)/shard_map/ppermute | solution.py:516
  32.2 4.7 %collective-permute-start.11 = (bf16[384,128]{1,0:T(8,128)(2,1)S(1)}, bf16[384,128]{1,0:T(8,128)(2,1)S(1)}, u32[]{:S(2)}, u32[]{:S(2)}) collective-permute-start(bf16[384,128]{1,0:T(8,128)(2,1)S(1)} %get-tuple-element.52), channel_id=1, source_target_pairs={{0,4},{4,0},{8,12},{12,8},{16,20},{20,16},{24,28},{28,24},{1,9},{9... | collective-permute-start | bytes 294920 | tf_op jit(solution)/shard_map/ppermute | solution.py:526
  36.9 0.1 collective-permute-start.13
  36.9 4.0 %collective-permute-start.12 = (bf16[384,128]{1,0:T(8,128)(2,1)S(1)}, bf16[384,128]{1,0:T(8,128)(2,1)S(1)}, u32[]{:S(2)}, u32[]{:S(2)}) collective-permute-start(bf16[384,128]{1,0:T(8,128)(2,1)S(1)} %get-tuple-element.53), channel_id=1, source_target_pairs={{0,8},{8,0},{4,12},{12,4},{16,24},{24,16},{20,28},{28,20},{1,5},{5... | collective-permute-start | bytes 294920 | tf_op jit(solution)/shard_map/ppermute | solution.py:526
  40.9 0.5 %collective-permute-done.13.refs_1_ = bf16[64,512]{1,0:T(8,128)(2,1)S(1)} collective-permute-done((bf16[64,512]{1,0:T(8,128)(2,1)S(1)}, bf16[64,512]{1,0:T(8,128)(2,1)S(1)}, u32[]{:S(2)}, u32[]{:S(2)}) %collective-permute-start.13) | collective-permute-done | bytes 65568 | tf_op jit(solution)/shard_map/ppermute | solution.py:526
  41.5 0.0 collective-permute-done.11.refs_2_.r3
  41.5 2.8 %collective-permute-start.14 = (bf16[64,512]{1,0:T(8,128)(2,1)S(1)}, bf16[64,512]{1,0:T(8,128)(2,1)S(1)}, u32[]{:S(2)}, u32[]{:S(2)}) collective-permute-start(bf16[64,512]{1,0:T(8,128)(2,1)S(1)} %sum.6.after.refs_0_), channel_id=1, source_target_pairs={{0,8},{4,12},{8,0},{12,4},{16,24},{20,28},{24,16},{28,20},{1,17},{... | collective-permute-start | bytes 196616 | tf_op jit(solution)/shard_map/ppermute | solution.py:526
  44.3 0.0 collective-permute-done.12.r4
  44.3 1.1 %assemble.1.refs_2_.windows = bf16[3,4,2,5,2,16,256]{6,5,4,3,2,1,0:T(8,128)(2,1)S(1)} custom-call(bf16[4,4,2,8,512]{4,3,2,1,0:T(8,128)(2,1)S(1)} %get-tuple-element.44.grad, s32[4,26]{1,0:T(4,128)S(1)} %get-tuple-element.36.rows, bf16[384,128]{1,0:T(8,128)(2,1)S(1)} %get-tuple-element.45.r0, bf16[384,128]{1,0:T(8,128)(2,1)S(1)} %collective-permute-done.7.refs_2_.r1, ...), custom_call_target="tpu_custom_call" | custom-call | tf_op jit(solution)/shard_map/assemble/pallas_call | solution.py:689
  45.4 1.2 %collective-permute-done.14.refs_1_ = bf16[64,512]{1,0:T(8,128)(2,1)S(1)} collective-permute-done((bf16[64,512]{1,0:T(8,128)(2,1)S(1)}, bf16[64,512]{1,0:T(8,128)(2,1)S(1)}, u32[]{:S(2)}, u32[]{:S(2)}) %collective-permute-start.14) | collective-permute-done | bytes 65568 | tf_op jit(solution)/shard_map/ppermute | solution.py:526
  46.6 2.8 %collective-permute-start.15 = (bf16[64,512]{1,0:T(8,128)(2,1)S(1)}, bf16[64,512]{1,0:T(8,128)(2,1)S(1)}, u32[]{:S(2)}, u32[]{:S(2)}) collective-permute-start(bf16[64,512]{1,0:T(8,128)(2,1)S(1)} %sum.7.after.mine), channel_id=1, source_target_pairs={{0,16},{4,20},{8,24},{12,28},{16,0},{20,4},{24,8},{28,12},{1,5},{5... | collective-permute-start | bytes 196616 | tf_op jit(solution)/shard_map/ppermute | solution.py:526
  49.3 1.7 %backward.1 = bf16[4,4,2,8,512]{4,3,2,1,0:T(8,128)(2,1)} custom-call(bf16[3,4,2,5,2,16,256]{6,5,4,3,2,1,0:T(8,128)(2,1)S(1)} %assemble.1.refs_2_.windows, bf16[4,4,2,8,512]{4,3,2,1,0:T(8,128)(2,1)S(1)} %get-tuple-element.32.mask, bf16[3072,256]{1,0:T(8,128)(2,1)S(1)} %get-tuple-element.55.toeplitz, bf16[64,512]{1,0:T(8,128)(2,1)S(1)} %sum.7.after.mine), custom_call_target="tpu_custom_call" | custom-call | tf_op jit(solution)/shard_map/backward/pallas_call | solution.py:703
  51.0 0.8 %collective-permute-done.15.other = bf16[64,512]{1,0:T(8,128)(2,1)S(1)} collective-permute-done((bf16[64,512]{1,0:T(8,128)(2,1)S(1)}, bf16[64,512]{1,0:T(8,128)(2,1)S(1)}, u32[]{:S(2)}, u32[]{:S(2)}) %collective-permute-start.15) | collective-permute-done | bytes 65568 | tf_op jit(solution)/shard_map/ppermute | solution.py:526
  51.8 0.7 %finish.1 = (f32[64,432]{1,0:T(8,128)}, f32[1,16]{1,0:T(1,128)}) custom-call(bf16[64,512]{1,0:T(8,128)(2,1)S(1)} %sum.7.after.mine, bf16[64,512]{1,0:T(8,128)(2,1)S(1)} %collective-permute-done.15.other), custom_call_target="tpu_custom_call" | custom-call | tf_op jit(solution)/shard_map/finish/pallas_call | solution.py:712
  (5 shorter events, 0.1 us)
Async XLA Ops:
  3.8 8.7 %collective-permute-start.1 = (bf16[64,512]{1,0:T(8,128)(2,1)S(1)}, bf16[64,512]{1,0:T(8,128)(2,1)S(1)}, u32[]{:S(2)}, u32[]{:S(2)}) collective-permute-start(bf16[64,512]{1,0:T(8,128)(2,1)S(1)} %get-tuple-element.33.refs_0_), channel_id=1, source_target_pairs={{0,2},{1,3},{2,0},{3,1},{4,6},{5,7},{6,4},{7,5},{8,10},{9,11},{10,... | collective-permute-start | bytes 196616 | tf_op jit(solution)/shard_map/ppermute | solution.py:516
  6.8 10.1 %collective-permute-start = (bf16[64,512]{1,0:T(8,128)(2,1)S(1)}, bf16[64,512]{1,0:T(8,128)(2,1)S(1)}, u32[]{:S(2)}, u32[]{:S(2)}) collective-permute-start(bf16[64,512]{1,0:T(8,128)(2,1)S(1)} %get-tuple-element.33.refs_0_), channel_id=1, source_target_pairs={{0,1},{1,0},{2,3},{3,2},{4,5},{5,4},{6,7},{7,6},{8,9},{9,8},{10,11... | collective-permute-start | bytes 196616 | tf_op jit(solution)/shard_map/ppermute | solution.py:516
  6.8 11.9 %collective-permute-start.3 = (bf16[384,128]{1,0:T(8,128)(2,1)S(1)}, bf16[384,128]{1,0:T(8,128)(2,1)S(1)}, u32[]{:S(2)}, u32[]{:S(2)}) collective-permute-start(bf16[384,128]{1,0:T(8,128)(2,1)S(1)} %get-tuple-element.39), channel_id=1, source_target_pairs={{4,8},{8,4},{12,16},{16,12},{20,24},{24,20},{9,17},{17,9},{13,21},... | collective-permute-start | bytes 294920 | tf_op jit(solution)/shard_map/ppermute | solution.py:526
  7.5 11.2 %collective-permute-start.4 = (bf16[384,128]{1,0:T(8,128)(2,1)S(1)}, bf16[384,128]{1,0:T(8,128)(2,1)S(1)}, u32[]{:S(2)}, u32[]{:S(2)}) collective-permute-start(bf16[384,128]{1,0:T(8,128)(2,1)S(1)} %get-tuple-element.40), channel_id=1, source_target_pairs={{8,16},{16,8},{12,20},{20,12},{5,9},{9,5},{13,17},{17,13},{21,25},... | collective-permute-start | bytes 294920 | tf_op jit(solution)/shard_map/ppermute | solution.py:526
  8.2 10.6 %collective-permute-start.5 = (bf16[384,128]{1,0:T(8,128)(2,1)S(1)}, bf16[384,128]{1,0:T(8,128)(2,1)S(1)}, u32[]{:S(2)}, u32[]{:S(2)}) collective-permute-start(bf16[384,128]{1,0:T(8,128)(2,1)S(1)} %get-tuple-element.41), channel_id=1, source_target_pairs={{0,4},{4,0},{8,12},{12,8},{16,20},{20,16},{24,28},{28,24},{1,9},{9... | collective-permute-start | bytes 294920 | tf_op jit(solution)/shard_map/ppermute | solution.py:526
  12.5 7.0 %collective-permute-start.6 = (bf16[384,128]{1,0:T(8,128)(2,1)S(1)}, bf16[384,128]{1,0:T(8,128)(2,1)S(1)}, u32[]{:S(2)}, u32[]{:S(2)}) collective-permute-start(bf16[384,128]{1,0:T(8,128)(2,1)S(1)} %get-tuple-element.42), channel_id=1, source_target_pairs={{0,8},{8,0},{4,12},{12,4},{16,24},{24,16},{20,28},{28,20},{1,5},{5... | collective-permute-start | bytes 294920 | tf_op jit(solution)/shard_map/ppermute | solution.py:526
  16.9 1.3 %collective-permute-start.2 = (bf16[64,512]{1,0:T(8,128)(2,1)S(1)}, bf16[64,512]{1,0:T(8,128)(2,1)S(1)}, u32[]{:S(2)}, u32[]{:S(2)}) collective-permute-start(bf16[64,512]{1,0:T(8,128)(2,1)S(1)} %collective-permute-done.1.refs_2_), channel_id=1, source_target_pairs={{0,1},{1,0},{2,3},{3,2},{4,5},{5,4},{6,7},{7,6},{8,9},{9,8},{10,11... | collective-permute-start | bytes 196616 | tf_op jit(solution)/shard_map/ppermute | solution.py:516
  26.1 1.4 %collective-permute-start.9 = (bf16[2,64,512]{2,1,0:T(8,128)(2,1)S(1)}, bf16[2,64,512]{2,1,0:T(8,128)(2,1)S(1)}, u32[]{:S(2)}, u32[]{:S(2)}) collective-permute-start(bf16[2,64,512]{2,1,0:T(8,128)(2,1)S(1)} %get-tuple-element.49), channel_id=1, source_target_pairs={{0,1},{1,0},{2,3},{3,2},{4,5},{5,4},{6,7},{7,6},{8,9},{9,8},{10,11... | collective-permute-start | bytes 393224 | tf_op jit(solution)/shard_map/ppermute | solution.py:516
  26.2 2.0 %collective-permute-start.7 = (bf16[384,128]{1,0:T(8,128)(2,1)S(1)}, bf16[384,128]{1,0:T(8,128)(2,1)S(1)}, u32[]{:S(2)}, u32[]{:S(2)}) collective-permute-start(bf16[384,128]{1,0:T(8,128)(2,1)S(1)} %get-tuple-element.46), channel_id=1, source_target_pairs={{4,8},{8,4},{12,16},{16,12},{20,24},{24,20},{9,17},{17,9},{13,21},... | collective-permute-start | bytes 294920 | tf_op jit(solution)/shard_map/ppermute | solution.py:526
  26.9 1.4 %collective-permute-start.8 = (bf16[384,128]{1,0:T(8,128)(2,1)S(1)}, bf16[384,128]{1,0:T(8,128)(2,1)S(1)}, u32[]{:S(2)}, u32[]{:S(2)}) collective-permute-start(bf16[384,128]{1,0:T(8,128)(2,1)S(1)} %get-tuple-element.47), channel_id=1, source_target_pairs={{8,16},{16,8},{12,20},{20,12},{5,9},{9,5},{13,17},{17,13},{21,25},... | collective-permute-start | bytes 294920 | tf_op jit(solution)/shard_map/ppermute | solution.py:526
  27.6 4.5 %collective-permute-start.10 = (bf16[1,64,512]{2,1,0:T(8,128)(2,1)S(1)}, bf16[1,64,512]{2,1,0:T(8,128)(2,1)S(1)}, u32[]{:S(2)}, u32[]{:S(2)}) collective-permute-start(bf16[1,64,512]{2,1,0:T(8,128)(2,1)S(1)} %get-tuple-element.58), channel_id=1, source_target_pairs={{0,2},{1,3},{2,0},{3,1},{4,6},{5,7},{6,4},{7,5},{8,10},{9,11},{10,... | collective-permute-start | bytes 196616 | tf_op jit(solution)/shard_map/ppermute | solution.py:516
  32.2 9.3 %collective-permute-start.11 = (bf16[384,128]{1,0:T(8,128)(2,1)S(1)}, bf16[384,128]{1,0:T(8,128)(2,1)S(1)}, u32[]{:S(2)}, u32[]{:S(2)}) collective-permute-start(bf16[384,128]{1,0:T(8,128)(2,1)S(1)} %get-tuple-element.52), channel_id=1, source_target_pairs={{0,4},{4,0},{8,12},{12,8},{16,20},{20,16},{24,28},{28,24},{1,9},{9... | collective-permute-start | bytes 294920 | tf_op jit(solution)/shard_map/ppermute | solution.py:526
  36.9 4.6 %collective-permute-start.13 = (bf16[64,512]{1,0:T(8,128)(2,1)S(1)}, bf16[64,512]{1,0:T(8,128)(2,1)S(1)}, u32[]{:S(2)}, u32[]{:S(2)}) collective-permute-start(bf16[64,512]{1,0:T(8,128)(2,1)S(1)} %bitcast.12), channel_id=1, source_target_pairs={{0,4},{4,0},{8,12},{12,8},{16,20},{20,16},{24,28},{28,24},{1,9},{5... | collective-permute-start | bytes 196616 | tf_op jit(solution)/shard_map/ppermute | solution.py:526
  36.9 7.4 %collective-permute-start.12 = (bf16[384,128]{1,0:T(8,128)(2,1)S(1)}, bf16[384,128]{1,0:T(8,128)(2,1)S(1)}, u32[]{:S(2)}, u32[]{:S(2)}) collective-permute-start(bf16[384,128]{1,0:T(8,128)(2,1)S(1)} %get-tuple-element.53), channel_id=1, source_target_pairs={{0,8},{8,0},{4,12},{12,4},{16,24},{24,16},{20,28},{28,20},{1,5},{5... | collective-permute-start | bytes 294920 | tf_op jit(solution)/shard_map/ppermute | solution.py:526
  41.5 5.1 %collective-permute-start.14 = (bf16[64,512]{1,0:T(8,128)(2,1)S(1)}, bf16[64,512]{1,0:T(8,128)(2,1)S(1)}, u32[]{:S(2)}, u32[]{:S(2)}) collective-permute-start(bf16[64,512]{1,0:T(8,128)(2,1)S(1)} %sum.6.after.refs_0_), channel_id=1, source_target_pairs={{0,8},{4,12},{8,0},{12,4},{16,24},{20,28},{24,16},{28,20},{1,17},{... | collective-permute-start | bytes 196616 | tf_op jit(solution)/shard_map/ppermute | solution.py:526
  46.6 5.2 %collective-permute-start.15 = (bf16[64,512]{1,0:T(8,128)(2,1)S(1)}, bf16[64,512]{1,0:T(8,128)(2,1)S(1)}, u32[]{:S(2)}, u32[]{:S(2)}) collective-permute-start(bf16[64,512]{1,0:T(8,128)(2,1)S(1)} %sum.7.after.mine), channel_id=1, source_target_pairs={{0,16},{4,20},{8,24},{12,28},{16,0},{20,4},{24,8},{28,12},{1,5},{5... | collective-permute-start | bytes 196616 | tf_op jit(solution)/shard_map/ppermute | solution.py:526

commit v8 on v7

--- a/solution.py
+++ b/solution.py
@@ -16,8 +16,6 @@
     ((1, 1), (2, 1), (1, 0), (2, 0)),
     ((2, 1), (1, 1), (2, 0), (1, 0)),
 )
-DN_NT = (((1,), (1,)), ((), ()))
-DN_NN = (((1,), (0,)), ((), ()))
 
 
 def vmem():
@@ -115,22 +113,6 @@
     z_col = lax.broadcasted_iota(jnp.int32, (512, 512), 1) >> 6
     expand = jnp.where(z_row == z_col, 1.0, 0.0).astype(BF16)
 
-    copies[0].wait()
-    live = lax.broadcasted_iota(jnp.int32, (bricks, 512), 0) < counts[0, 0]
-    occ = jnp.where(live, occupancy[...], 0).astype(F32)
-    spread = jnp.concatenate(
-        [jnp.where(same, occ[b : b + 1, :], 0.0) for b in range(bricks)], axis=0
-    ).astype(BF16)
-    mask = jnp.dot(spread, expand, preferred_element_type=F32)
-    mask_out[...] = mask.astype(BF16).reshape(mask_out.shape)
-    copies[1].wait()
-    value = features[...].astype(F32).reshape(bricks * 64, 512) * mask
-    masked_out[...] = value.astype(BF16).reshape(masked_out.shape)
-    for q in range(4):
-        values[q, 0 : bricks * 64, :] = value[:, q * LANES : (q + 1) * LANES]
-    copies[2].wait()
-    pack_units(values, send_out, (u0, u1, u2, u3, u4))
-
     copies[3].wait()
     device = lax.axis_index("space")
     number = listing[...]
@@ -159,6 +141,22 @@
     rows[...] = jnp.where(number < 0, none, jnp.where(face < 4, plain, paired))
     last = pltpu.make_async_copy(rows, rows_out, sems.at[len(copies)])
     last.start()
+
+    copies[0].wait()
+    live = lax.broadcasted_iota(jnp.int32, (bricks, 512), 0) < counts[0, 0]
+    occ = jnp.where(live, occupancy[...], 0).astype(F32)
+    spread = jnp.concatenate(
+        [jnp.where(same, occ[b : b + 1, :], 0.0) for b in range(bricks)], axis=0
+    ).astype(BF16)
+    mask = jnp.dot(spread, expand, preferred_element_type=F32)
+    mask_out[...] = mask.astype(BF16).reshape(mask_out.shape)
+    copies[1].wait()
+    value = features[...].astype(F32).reshape(bricks * 64, 512) * mask
+    masked_out[...] = value.astype(BF16).reshape(masked_out.shape)
+    for q in range(4):
+        values[q, 0 : bricks * 64, :] = value[:, q * LANES : (q + 1) * LANES]
+    copies[2].wait()
+    pack_units(values, send_out, (u0, u1, u2, u3, u4))
 
     copies[4].wait()
     copies[5].wait()
@@ -289,7 +287,7 @@
     lax.fori_loop(0, windows.shape[2], one_pair, 0)
 
 
-def lane_block(d, e):
+def row_block(d, e):
     return slice((3 * d + e) * 256, (3 * d + e + 1) * 256)
 
 
@@ -341,16 +339,16 @@
     for e in range(3):
         for x in range(2):
             half = slice(x * LANES, (x + 1) * LANES)
-            forward_out[half, lane_block(3 * (1 - x), e)] = jnp.zeros((LANES, 256), BF16)
-            backward_out[lane_block(3 * (1 - x), e), half] = jnp.zeros((256, LANES), BF16)
+            for out in (forward_out, backward_out):
+                out[row_block(3 * (1 - x), e), half] = jnp.zeros((256, LANES), BF16)
     for ae in range(9):
         a, e = ae // 3, ae % 3
         one = taps_pair(flat, shifted, 3 * ae)
         two = jnp.where(low, taps_pair(flat, shifted, 3 * ae + 2), 0.0)
         late = jnp.concatenate([one, two], axis=1)
-        band = jnp.concatenate([pltpu.roll(late, 192, 1), late], axis=0).astype(BF16)
+        band = jnp.transpose(jnp.concatenate([pltpu.roll(late, 192, 1), late], axis=0)).astype(BF16)
         for x in range(2):
-            forward_out[x * LANES : (x + 1) * LANES, lane_block(a + x, e)] = band
+            forward_out[row_block(a + x, e), x * LANES : (x + 1) * LANES] = band
     for ae in range(9):
         a, e = ae // 3, ae % 3
         m = 3 * (8 - ae)
@@ -367,7 +365,7 @@
             axis=0,
         ).astype(BF16)
         for x in range(2):
-            backward_out[lane_block(a + x, e), x * LANES : (x + 1) * LANES] = band
+            backward_out[row_block(a + x, e), x * LANES : (x + 1) * LANES] = band
 
     lane = lax.broadcasted_iota(jnp.int32, (8, LANES), 1)
     bias_lane = shard % LANES
@@ -406,7 +404,7 @@
     values[:, bricks * 64 :, :] = jnp.zeros((4, 64, LANES), F32)
 
     bias_row = jnp.concatenate([bias_row, bias_row], axis=1)
-    total = lax.dot_general(all_taps(windows), toeplitz[...], DN_NT, preferred_element_type=F32)
+    total = jnp.dot(all_taps(windows), toeplitz[...], preferred_element_type=F32)
     rows_of_chunk = total.shape[0] // 4
     bias_sum = jnp.zeros((8, 256), F32)
     for q in range(4):
@@ -472,22 +470,26 @@
     assemble(grad, table, rows, windows, sides, walls)
 
 
-def sum_kernel(*refs, operands):
-    refs[operands][...] = (refs[0][...].astype(F32) + refs[1][...].astype(F32)).astype(BF16)
-
-
-def sum_after(mine, other, after, through=()):
+def sum_kernel(*refs, operands, parts):
+    total = (refs[0][...].astype(F32) + refs[1][...].astype(F32)).astype(BF16)
+    for part in range(parts):
+        for row in range(part, total.shape[0], parts):
+            refs[operands + part][row // parts] = total[row]
+
+
+def sum_after(mine, other, after=(), through=(), parts=1):
     operands = 2 + len(after) + len(through)
-    total, *passed = pl.pallas_call(
-        functools.partial(sum_kernel, operands=operands),
+    share = jax.ShapeDtypeStruct((mine.shape[0] // parts, *mine.shape[1:]), mine.dtype)
+    outs = pl.pallas_call(
+        functools.partial(sum_kernel, operands=operands, parts=parts),
         name="sum",
-        out_shape=[jax.ShapeDtypeStruct(x.shape, x.dtype) for x in (mine, *through)],
+        out_shape=[share] * parts + [jax.ShapeDtypeStruct(x.shape, x.dtype) for x in through],
         in_specs=[vmem()] * 2 + [untouched()] * (operands - 2),
-        out_specs=[vmem()] + [untouched()] * len(through),
-        input_output_aliases={2 + len(after) + i: 1 + i for i in range(len(through))},
+        out_specs=[vmem()] * parts + [untouched()] * len(through),
+        input_output_aliases={2 + len(after) + i: parts + i for i in range(len(through))},
         compiler_params=pltpu.CompilerParams(vmem_limit_bytes=1024 * 1024),
     )(mine, other, *after, *through)
-    return total, passed
+    return list(outs[:parts]), list(outs[parts:])
 
 
 def backward_kernel(windows, mask, toeplitz, after, out):
@@ -619,7 +621,7 @@
         functools.partial(weights_kernel, shard=shard, groups=groups),
         name="weights",
         out_shape=[
-            jax.ShapeDtypeStruct((256, 12 * 256), BF16),
+            jax.ShapeDtypeStruct((12 * 256, 256), BF16),
             jax.ShapeDtypeStruct((12 * 256, 256), BF16),
             jax.ShapeDtypeStruct((8, LANES), F32),
         ],
@@ -666,24 +668,22 @@
         *received,
     )
 
-    grad_received = grad_units[:1] + [exchanged(n, grad_units[n]) for n in range(1, 3)]
-    total, _ = sum_after(keep, swapped(give, "dp", 1), [])
-    later = grad_units[3:]
-    bit = 2
-    while bit < groups:
-        far = swapped(total[1::2], "dp", bit)
-        last = 2 * bit >= groups
-        total, later = sum_after(
-            total[0::2], far, grad_received[1:3] if last else [], later if last else []
-        )
+    later = grad_units[2:]
+    bit = 1
+    while 2 * bit < groups:
+        first = later[:1] if bit == 1 else []
+        (keep, give), first = sum_after(keep, swapped(give, "dp", bit), through=first, parts=2)
+        later = first + later[1:] if bit == 1 else later
         bit *= 2
-    total = total[0]
+    grad_received = [grad_units[0], exchanged(1, grad_units[1])]
+    (total,), last = sum_after(keep, swapped(give, "dp", bit), grad_received[1:], later[1:])
+    for number, unit in enumerate([later[0], *last], 2):
+        grad_received.append(exchanged(number, unit))
 
     steps = space_steps()
     other = stepped(total, steps[0])
-    grad_received += [exchanged(n, unit) for n, unit in zip(range(3, spread), later)]
     if len(steps) > 1:
-        total, _ = sum_after(total, other, grad_received[3:4])
+        (total,), _ = sum_after(total, other, grad_received[3:4])
         other = stepped(total, steps[1])
 
     padded_grad = pl.pallas_call(
@@ -697,7 +697,7 @@
     )(grad, rows, *grad_received, total)
 
     for number, step in enumerate(steps[2:]):
-        total, _ = sum_after(total, other, [] if number else [padded_grad])
+        (total,), _ = sum_after(total, other, [] if number else [padded_grad])
         other = stepped(total, step)
 
     grad_input = pl.pallas_call(
@@ -719,7 +719,7 @@
         in_specs=[vmem()] * 2,
         out_specs=[vmem()] * 2,
         compiler_params=params,
-    )(total, other)
+    )(total[0], other[0])
     return (
         block_output.reshape(features.shape),
         grad_input.reshape(features.shape),

time: 52.7 us -> 51.2 us (0.972)
  starting transfers between devices: 29.4 us -> 25.3 us
  waiting for transfers between devices: 8.45 us -> 11.3 us
    ppermute x11, starting transfers between devices: 25.7 us -> 21.6 us  [by_parity(): return lax.ppermute(block, ('space', 'dp'), pairs)]
    ppermute x11, waiting for transfers between devices: 3.26 us -> 5.62 us  [by_parity(): return lax.ppermute(block, ('space', 'dp'), pairs)]
  transfers between devices with their start and end apart: 16 -> 16, of which waited for: 6 -> 7; matrix products, arithmetic and copies ran while one was open for 0% -> 0% of each run, Pallas kernels for 6% -> 7%
where the time goes in v8:
time: 51.2 us; the launch traced here: 50.9 us
  starting transfers between devices  25.3 us (49%)
  Pallas kernels  12.9 us (25%)
  waiting for transfers between devices  11.3 us (22%)
  between operations  1.4 us (3%)
    ppermute x11, starting transfers between devices, by_parity(): return lax.ppermute(block, ('space', 'dp'), pairs)  21.6 us
    pallas_call x1, Pallas kernels, body(): pl.pallas_call(functools.partial(forward_kernel, shard=shard), name='forw...  6.57 us
    ppermute x5, waiting for transfers between devices, swapped(): lax.ppermute(block, axis, [(i, i ^ bit) for i in range(lax.axis_size(axis...  5.64 us
    ppermute x11, waiting for transfers between devices, by_parity(): return lax.ppermute(block, ('space', 'dp'), pairs)  5.62 us
    ppermute x5, starting transfers between devices, swapped(): lax.ppermute(block, axis, [(i, i ^ bit) for i in range(lax.axis_size(axis...  3.69 us
    pallas_call x1, Pallas kernels, body(): pl.pallas_call(prepare_kernel, name='prepare', out_shape=[grid_type, grid...  2.15 us
    pallas_call x1, Pallas kernels, body(): pl.pallas_call(backward_kernel, name='backward', out_shape=grid_type, in_...  1.68 us
    pallas_call x1, Pallas kernels, body(): pl.pallas_call(assemble_kernel, name='assemble', out_shape=jax.ShapeDtype...  1.07 us
  transfers between devices with their start and end apart: 16, of which 7 were waited for; matrix products, arithmetic and copies ran while one was open for 0% of the time, Pallas kernels for 7%

profile of v8, /device:TPU:0, one launch (start us, length us, event | category | flops | bytes accessed | tf_op | source)
XLA Modules:
  0.0 50.9 jit_solution(15499500159920013671)
XLA Ops:
  1.3 2.1 %prepare.1 = (bf16[4,4,2,8,512]{4,3,2,1,0:T(8,128)(2,1)S(1)}, bf16[4,4,2,8,512]{4,3,2,1,0:T(8,128)(2,1)S(1)}, s32[4,26]{1,0:T(4,128)S(1)}, s32[5,1,12]{2,1,0:T(1...) custom-call(bf16[4,4,2,8,512]{4,3,2,1,0:T(8,128)(2,1)} %bitcast.17, ...), custom_call_target="tpu_custom_call" | custom-call | tf_op jit(solution)/shard_map/prepare/pallas_call | solution.py:572
  3.4 3.0 %collective-permute-start.1 = (bf16[64,512]{1,0:T(8,128)(2,1)S(1)}, bf16[64,512]{1,0:T(8,128)(2,1)S(1)}, u32[]{:S(2)}, u32[]{:S(2)}) collective-permute-start(bf16[64,512]{1,0:T(8,128)(2,1)S(1)} %get-tuple-element.36.refs_0_), channel_id=1, source_target_pairs={{0,2},{1,3},{2,0},{3,1},{4,6},{5,7},{6,4},{7,5},{8,10},{9,11},{10,... | collective-permute-start | bytes 196616 | tf_op jit(solution)/shard_map/ppermute | solution.py:518
  6.4 0.0 collective-permute-start
  6.4 0.7 %collective-permute-start.3 = (bf16[384,128]{1,0:T(8,128)(2,1)S(1)}, bf16[384,128]{1,0:T(8,128)(2,1)S(1)}, u32[]{:S(2)}, u32[]{:S(2)}) collective-permute-start(bf16[384,128]{1,0:T(8,128)(2,1)S(1)} %get-tuple-element.42), channel_id=1, source_target_pairs={{4,8},{8,4},{12,16},{16,12},{20,24},{24,20},{9,17},{17,9},{13,21},... | collective-permute-start | bytes 294920 | tf_op jit(solution)/shard_map/ppermute | solution.py:528
  7.1 0.7 %collective-permute-start.4 = (bf16[384,128]{1,0:T(8,128)(2,1)S(1)}, bf16[384,128]{1,0:T(8,128)(2,1)S(1)}, u32[]{:S(2)}, u32[]{:S(2)}) collective-permute-start(bf16[384,128]{1,0:T(8,128)(2,1)S(1)} %get-tuple-element.43), channel_id=1, source_target_pairs={{8,16},{16,8},{12,20},{20,12},{5,9},{9,5},{13,17},{17,13},{21,25},... | collective-permute-start | bytes 294920 | tf_op jit(solution)/shard_map/ppermute | solution.py:528
  7.8 4.3 %collective-permute-start.5 = (bf16[384,128]{1,0:T(8,128)(2,1)S(1)}, bf16[384,128]{1,0:T(8,128)(2,1)S(1)}, u32[]{:S(2)}, u32[]{:S(2)}) collective-permute-start(bf16[384,128]{1,0:T(8,128)(2,1)S(1)} %get-tuple-element.44), channel_id=1, source_target_pairs={{0,4},{4,0},{8,12},{12,8},{16,20},{20,16},{24,28},{28,24},{1,9},{9... | collective-permute-start | bytes 294920 | tf_op jit(solution)/shard_map/ppermute | solution.py:528
  12.1 0.0 collective-permute-done.1.refs_2_
  12.1 4.4 %collective-permute-start.6 = (bf16[384,128]{1,0:T(8,128)(2,1)S(1)}, bf16[384,128]{1,0:T(8,128)(2,1)S(1)}, u32[]{:S(2)}, u32[]{:S(2)}) collective-permute-start(bf16[384,128]{1,0:T(8,128)(2,1)S(1)} %get-tuple-element.45), channel_id=1, source_target_pairs={{0,8},{8,0},{4,12},{12,4},{16,24},{24,16},{20,28},{28,20},{1,5},{5... | collective-permute-start | bytes 294920 | tf_op jit(solution)/shard_map/ppermute | solution.py:528
  16.5 0.0 collective-permute-done.refs_1_
  16.5 0.0 collective-permute-start.2
  16.5 1.3 %collective-permute-done.2.refs_3_ = bf16[64,512]{1,0:T(8,128)(2,1)S(1)} collective-permute-done((bf16[64,512]{1,0:T(8,128)(2,1)S(1)}, bf16[64,512]{1,0:T(8,128)(2,1)S(1)}, u32[]{:S(2)}, u32[]{:S(2)}) %collective-permute-start.2) | collective-permute-done | bytes 65568 | tf_op jit(solution)/shard_map/ppermute | solution.py:518
  17.8 0.7 %weights.1 = (bf16[3072,256]{1,0:T(8,128)(2,1)S(1)}, bf16[3072,256]{1,0:T(8,128)(2,1)S(1)}, f32[8,128]{1,0:T(8,128)S(1)}) custom-call(bf16[64,512]{1,0:T(8,128)(2,1)S(1)} %get-tuple-element.36.refs_0_, bf16[64,512]{1,0:T(8,128)(2,1)S(1)} %collective-permute-done.refs_1_, bf16[64,512]{1,0:T(8,128)(2,1)S(1)} %collective-permute-done.1.refs_2_, ...), custom_call_target="tpu_custom_call" | custom-call | tf_op jit(solution)/shard_map/weights/pallas_call | solution.py:620
  18.5 0.0 collective-permute-done.3.r1
  18.5 0.0 collective-permute-done.4.r2
  18.5 0.0 collective-permute-done.5.r3
  18.5 0.6 %collective-permute-done.6.r4 = bf16[384,128]{1,0:T(8,128)(2,1)S(1)} collective-permute-done((bf16[384,128]{1,0:T(8,128)(2,1)S(1)}, bf16[384,128]{1,0:T(8,128)(2,1)S(1)}, u32[]{:S(2)}, u32[]{:S(2)}) %collective-permute-start.6) | collective-permute-done | bytes 98336 | tf_op jit(solution)/shard_map/ppermute | solution.py:528
  19.1 6.6 %forward.1 = (bf16[4,4,2,8,512]{4,3,2,1,0:T(8,128)(2,1)}, bf16[4,4,2,8,512]{4,3,2,1,0:T(8,128)(2,1)S(1)}, bf16[2,64,512]{2,1,0:T(8,128)(2,1)S(1)}, bf16[2,64,512...) custom-call(bf16[4,4,2,8,512]{4,3,2,1,0:T(8,128)(2,1)S(1)} %get-tupl, ...), custom_call_target="tpu_custom_call" | custom-call | tf_op jit(solution)/shard_map/forward/pallas_call | solution.py:639
  25.7 0.1 collective-permute-start.8
  25.8 0.7 %collective-permute-start.7 = (bf16[384,128]{1,0:T(8,128)(2,1)S(1)}, bf16[384,128]{1,0:T(8,128)(2,1)S(1)}, u32[]{:S(2)}, u32[]{:S(2)}) collective-permute-start(bf16[384,128]{1,0:T(8,128)(2,1)S(1)} %get-tuple-element.49), channel_id=1, source_target_pairs={{4,8},{8,4},{12,16},{16,12},{20,24},{24,20},{9,17},{17,9},{13,21},... | collective-permute-start | bytes 294920 | tf_op jit(solution)/shard_map/ppermute | solution.py:528
  26.4 0.7 %collective-permute-done.8.refs_1_ = bf16[2,64,512]{2,1,0:T(8,128)(2,1)S(1)} collective-permute-done((bf16[2,64,512]{2,1,0:T(8,128)(2,1)S(1)}, bf16[2,64,512]{2,1,0:T(8,128)(2,1)S(1)}, u32[]{:S(2)}, u32[]{:S(2)}) %collective-permute-start.8) | collective-permute-done | bytes 131104 | tf_op jit(solution)/shard_map/ppermute | solution.py:518
  27.1 0.6 %collective-permute-start.10 = (bf16[1,64,512]{2,1,0:T(8,128)(2,1)S(1)}, bf16[1,64,512]{2,1,0:T(8,128)(2,1)S(1)}, u32[]{:S(2)}, u32[]{:S(2)}) collective-permute-start(bf16[1,64,512]{2,1,0:T(8,128)(2,1)S(1)} %get-tuple-element.55), channel_id=1, source_target_pairs={{0,2},{1,3},{2,0},{3,1},{4,6},{5,7},{6,4},{7,5},{8,10},{9,11},{10,... | collective-permute-start | bytes 196616 | tf_op jit(solution)/shard_map/ppermute | solution.py:518
  27.8 0.0 collective-permute-done.7.refs_2_.r1
  27.8 3.7 %collective-permute-done.10.refs_1_ = bf16[1,64,512]{2,1,0:T(8,128)(2,1)S(1)} collective-permute-done((bf16[1,64,512]{2,1,0:T(8,128)(2,1)S(1)}, bf16[1,64,512]{2,1,0:T(8,128)(2,1)S(1)}, u32[]{:S(2)}, u32[]{:S(2)}) %collective-permute-start.10) | collective-permute-done | bytes 65568 | tf_op jit(solution)/shard_map/ppermute | solution.py:518
  31.5 4.1 %collective-permute-start.11 = (bf16[384,128]{1,0:T(8,128)(2,1)S(1)}, bf16[384,128]{1,0:T(8,128)(2,1)S(1)}, u32[]{:S(2)}, u32[]{:S(2)}) collective-permute-start(bf16[384,128]{1,0:T(8,128)(2,1)S(1)} %get-tuple-element.58), channel_id=1, source_target_pairs={{0,4},{4,0},{8,12},{12,8},{16,20},{20,16},{24,28},{28,24},{1,9},{9... | collective-permute-start | bytes 294920 | tf_op jit(solution)/shard_map/ppermute | solution.py:528
  35.6 0.1 collective-permute-start.13
  35.7 0.7 %collective-permute-start.9 = (bf16[384,128]{1,0:T(8,128)(2,1)S(1)}, bf16[384,128]{1,0:T(8,128)(2,1)S(1)}, u32[]{:S(2)}, u32[]{:S(2)}) collective-permute-start(bf16[384,128]{1,0:T(8,128)(2,1)S(1)} %get-tuple-element.53), channel_id=1, source_target_pairs={{8,16},{16,8},{12,20},{20,12},{5,9},{9,5},{13,17},{17,13},{21,25},... | collective-permute-start | bytes 294920 | tf_op jit(solution)/shard_map/ppermute | solution.py:528
  36.4 4.2 %collective-permute-start.12 = (bf16[384,128]{1,0:T(8,128)(2,1)S(1)}, bf16[384,128]{1,0:T(8,128)(2,1)S(1)}, u32[]{:S(2)}, u32[]{:S(2)}) collective-permute-start(bf16[384,128]{1,0:T(8,128)(2,1)S(1)} %get-tuple-element.59), channel_id=1, source_target_pairs={{0,8},{8,0},{4,12},{12,4},{16,24},{24,16},{20,28},{28,20},{1,5},{5... | collective-permute-start | bytes 294920 | tf_op jit(solution)/shard_map/ppermute | solution.py:528
  40.6 0.0 collective-permute-done.13.refs_1_
  40.6 0.0 collective-permute-done.11.refs_2_.r3
  40.6 0.2 collective-permute-start.14
  40.8 0.0 collective-permute-done.9.r2
  40.8 2.7 %collective-permute-done.12.r4 = bf16[384,128]{1,0:T(8,128)(2,1)S(1)} collective-permute-done((bf16[384,128]{1,0:T(8,128)(2,1)S(1)}, bf16[384,128]{1,0:T(8,128)(2,1)S(1)}, u32[]{:S(2)}, u32[]{:S(2)}) %collective-permute-start.12) | collective-permute-done | bytes 98336 | tf_op jit(solution)/shard_map/ppermute | solution.py:528
  43.5 1.1 %assemble.1.refs_2_.windows = bf16[3,4,2,5,2,16,256]{6,5,4,3,2,1,0:T(8,128)(2,1)S(1)} custom-call(bf16[4,4,2,8,512]{4,3,2,1,0:T(8,128)(2,1)S(1)} %get-tuple-element.47.grad, s32[4,26]{1,0:T(4,128)S(1)} %get-tuple-element.39.rows, bf16[384,128]{1,0:T(8,128)(2,1)S(1)} %get-tuple-element.48.r0, bf16[384,128]{1,0:T(8,128)(2,1)S(1)} %collective-permute-done.7.refs_2_.r1, ...), custom_call_target="tpu_custom_call" | custom-call | tf_op jit(solution)/shard_map/assemble/pallas_call | solution.py:689
  44.6 0.4 collective-permute-done.14.refs_1_
  45.0 1.7 %collective-permute-start.15 = (bf16[1,64,512]{2,1,0:T(8,128)(2,1)S(1)}, bf16[1,64,512]{2,1,0:T(8,128)(2,1)S(1)}, u32[]{:S(2)}, u32[]{:S(2)}) collective-permute-start(bf16[1,64,512]{2,1,0:T(8,128)(2,1)S(1)} %sum.7.after), channel_id=1, source_target_pairs={{0,16},{4,20},{8,24},{12,28},{16,0},{20,4},{24,8},{28,12},{1,5},{5... | collective-permute-start | bytes 196616 | tf_op jit(solution)/shard_map/ppermute | solution.py:528
  46.7 1.7 %backward.1 = bf16[4,4,2,8,512]{4,3,2,1,0:T(8,128)(2,1)} custom-call(bf16[3,4,2,5,2,16,256]{6,5,4,3,2,1,0:T(8,128)(2,1)S(1)} %assemble.1.refs_2_.windows, bf16[4,4,2,8,512]{4,3,2,1,0:T(8,128)(2,1)S(1)} %get-tuple-element.35.mask, bf16[3072,256]{1,0:T(8,128)(2,1)S(1)} %get-tuple-element.61.toeplitz, bf16[1,64,512]{2,1,0:T(8,128)(2,1)S(1)} %sum.7.after), custom_call_target="tpu_custom_call" | custom-call | tf_op jit(solution)/shard_map/backward/pallas_call | solution.py:703
  48.4 1.9 %collective-permute-done.15 = bf16[1,64,512]{2,1,0:T(8,128)(2,1)S(1)} collective-permute-done((bf16[1,64,512]{2,1,0:T(8,128)(2,1)S(1)}, bf16[1,64,512]{2,1,0:T(8,128)(2,1)S(1)}, u32[]{:S(2)}, u32[]{:S(2)}) %collective-permute-start.15) | collective-permute-done | bytes 65568 | tf_op jit(solution)/shard_map/ppermute | solution.py:528
  50.3 0.7 %finish.1 = (f32[64,432]{1,0:T(8,128)}, f32[1,16]{1,0:T(1,128)}) custom-call(bf16[64,512]{1,0:T(8,128)(2,1)S(1)} %bitcast.13, bf16[64,512]{1,0:T(8,128)(2,1)S(1)} %bitcast.14), custom_call_target="tpu_custom_call" | custom-call | tf_op jit(solution)/shard_map/finish/pallas_call | solution.py:712
  (4 shorter events, 0.1 us)
Async XLA Ops:
  3.4 8.7 %collective-permute-start.1 = (bf16[64,512]{1,0:T(8,128)(2,1)S(1)}, bf16[64,512]{1,0:T(8,128)(2,1)S(1)}, u32[]{:S(2)}, u32[]{:S(2)}) collective-permute-start(bf16[64,512]{1,0:T(8,128)(2,1)S(1)} %get-tuple-element.36.refs_0_), channel_id=1, source_target_pairs={{0,2},{1,3},{2,0},{3,1},{4,6},{5,7},{6,4},{7,5},{8,10},{9,11},{10,... | collective-permute-start | bytes 196616 | tf_op jit(solution)/shard_map/ppermute | solution.py:518
  6.4 10.1 %collective-permute-start = (bf16[64,512]{1,0:T(8,128)(2,1)S(1)}, bf16[64,512]{1,0:T(8,128)(2,1)S(1)}, u32[]{:S(2)}, u32[]{:S(2)}) collective-permute-start(bf16[64,512]{1,0:T(8,128)(2,1)S(1)} %get-tuple-element.36.refs_0_), channel_id=1, source_target_pairs={{0,1},{1,0},{2,3},{3,2},{4,5},{5,4},{6,7},{7,6},{8,9},{9,8},{10,11... | collective-permute-start | bytes 196616 | tf_op jit(solution)/shard_map/ppermute | solution.py:518
  6.4 12.1 %collective-permute-start.3 = (bf16[384,128]{1,0:T(8,128)(2,1)S(1)}, bf16[384,128]{1,0:T(8,128)(2,1)S(1)}, u32[]{:S(2)}, u32[]{:S(2)}) collective-permute-start(bf16[384,128]{1,0:T(8,128)(2,1)S(1)} %get-tuple-element.42), channel_id=1, source_target_pairs={{4,8},{8,4},{12,16},{16,12},{20,24},{24,20},{9,17},{17,9},{13,21},... | collective-permute-start | bytes 294920 | tf_op jit(solution)/shard_map/ppermute | solution.py:528
  7.1 11.4 %collective-permute-start.4 = (bf16[384,128]{1,0:T(8,128)(2,1)S(1)}, bf16[384,128]{1,0:T(8,128)(2,1)S(1)}, u32[]{:S(2)}, u32[]{:S(2)}) collective-permute-start(bf16[384,128]{1,0:T(8,128)(2,1)S(1)} %get-tuple-element.43), channel_id=1, source_target_pairs={{8,16},{16,8},{12,20},{20,12},{5,9},{9,5},{13,17},{17,13},{21,25},... | collective-permute-start | bytes 294920 | tf_op jit(solution)/shard_map/ppermute | solution.py:528
  7.8 10.8 %collective-permute-start.5 = (bf16[384,128]{1,0:T(8,128)(2,1)S(1)}, bf16[384,128]{1,0:T(8,128)(2,1)S(1)}, u32[]{:S(2)}, u32[]{:S(2)}) collective-permute-start(bf16[384,128]{1,0:T(8,128)(2,1)S(1)} %get-tuple-element.44), channel_id=1, source_target_pairs={{0,4},{4,0},{8,12},{12,8},{16,20},{20,16},{24,28},{28,24},{1,9},{9... | collective-permute-start | bytes 294920 | tf_op jit(solution)/shard_map/ppermute | solution.py:528
  12.1 7.0 %collective-permute-start.6 = (bf16[384,128]{1,0:T(8,128)(2,1)S(1)}, bf16[384,128]{1,0:T(8,128)(2,1)S(1)}, u32[]{:S(2)}, u32[]{:S(2)}) collective-permute-start(bf16[384,128]{1,0:T(8,128)(2,1)S(1)} %get-tuple-element.45), channel_id=1, source_target_pairs={{0,8},{8,0},{4,12},{12,4},{16,24},{24,16},{20,28},{28,20},{1,5},{5... | collective-permute-start | bytes 294920 | tf_op jit(solution)/shard_map/ppermute | solution.py:528
  16.5 1.3 %collective-permute-start.2 = (bf16[64,512]{1,0:T(8,128)(2,1)S(1)}, bf16[64,512]{1,0:T(8,128)(2,1)S(1)}, u32[]{:S(2)}, u32[]{:S(2)}) collective-permute-start(bf16[64,512]{1,0:T(8,128)(2,1)S(1)} %collective-permute-done.1.refs_2_), channel_id=1, source_target_pairs={{0,1},{1,0},{2,3},{3,2},{4,5},{5,4},{6,7},{7,6},{8,9},{9,8},{10,11... | collective-permute-start | bytes 196616 | tf_op jit(solution)/shard_map/ppermute | solution.py:518
  25.7 1.4 %collective-permute-start.8 = (bf16[2,64,512]{2,1,0:T(8,128)(2,1)S(1)}, bf16[2,64,512]{2,1,0:T(8,128)(2,1)S(1)}, u32[]{:S(2)}, u32[]{:S(2)}) collective-permute-start(bf16[2,64,512]{2,1,0:T(8,128)(2,1)S(1)} %get-tuple-element.51), channel_id=1, source_target_pairs={{0,1},{1,0},{2,3},{3,2},{4,5},{5,4},{6,7},{7,6},{8,9},{9,8},{10,11... | collective-permute-start | bytes 393224 | tf_op jit(solution)/shard_map/ppermute | solution.py:518
  25.8 2.0 %collective-permute-start.7 = (bf16[384,128]{1,0:T(8,128)(2,1)S(1)}, bf16[384,128]{1,0:T(8,128)(2,1)S(1)}, u32[]{:S(2)}, u32[]{:S(2)}) collective-permute-start(bf16[384,128]{1,0:T(8,128)(2,1)S(1)} %get-tuple-element.49), channel_id=1, source_target_pairs={{4,8},{8,4},{12,16},{16,12},{20,24},{24,20},{9,17},{17,9},{13,21},... | collective-permute-start | bytes 294920 | tf_op jit(solution)/shard_map/ppermute | solution.py:528
  27.1 4.3 %collective-permute-start.10 = (bf16[1,64,512]{2,1,0:T(8,128)(2,1)S(1)}, bf16[1,64,512]{2,1,0:T(8,128)(2,1)S(1)}, u32[]{:S(2)}, u32[]{:S(2)}) collective-permute-start(bf16[1,64,512]{2,1,0:T(8,128)(2,1)S(1)} %get-tuple-element.55), channel_id=1, source_target_pairs={{0,2},{1,3},{2,0},{3,1},{4,6},{5,7},{6,4},{7,5},{8,10},{9,11},{10,... | collective-permute-start | bytes 196616 | tf_op jit(solution)/shard_map/ppermute | solution.py:518
  31.5 9.1 %collective-permute-start.11 = (bf16[384,128]{1,0:T(8,128)(2,1)S(1)}, bf16[384,128]{1,0:T(8,128)(2,1)S(1)}, u32[]{:S(2)}, u32[]{:S(2)}) collective-permute-start(bf16[384,128]{1,0:T(8,128)(2,1)S(1)} %get-tuple-element.58), channel_id=1, source_target_pairs={{0,4},{4,0},{8,12},{12,8},{16,20},{20,16},{24,28},{28,24},{1,9},{9... | collective-permute-start | bytes 294920 | tf_op jit(solution)/shard_map/ppermute | solution.py:528
  35.6 4.9 %collective-permute-start.13 = (bf16[1,64,512]{2,1,0:T(8,128)(2,1)S(1)}, bf16[1,64,512]{2,1,0:T(8,128)(2,1)S(1)}, u32[]{:S(2)}, u32[]{:S(2)}) collective-permute-start(bf16[1,64,512]{2,1,0:T(8,128)(2,1)S(1)} %get-tuple-element.60.refs_0_), channel_id=1, source_target_pairs={{0,4},{4,0},{8,12},{12,8},{16,20},{20,16},{24,28},{28,24},{1,9},{5... | collective-permute-start | bytes 196616 | tf_op jit(solution)/shard_map/ppermute | solution.py:528
  35.7 5.1 %collective-permute-start.9 = (bf16[384,128]{1,0:T(8,128)(2,1)S(1)}, bf16[384,128]{1,0:T(8,128)(2,1)S(1)}, u32[]{:S(2)}, u32[]{:S(2)}) collective-permute-start(bf16[384,128]{1,0:T(8,128)(2,1)S(1)} %get-tuple-element.53), channel_id=1, source_target_pairs={{8,16},{16,8},{12,20},{20,12},{5,9},{9,5},{13,17},{17,13},{21,25},... | collective-permute-start | bytes 294920 | tf_op jit(solution)/shard_map/ppermute | solution.py:528
  36.4 7.1 %collective-permute-start.12 = (bf16[384,128]{1,0:T(8,128)(2,1)S(1)}, bf16[384,128]{1,0:T(8,128)(2,1)S(1)}, u32[]{:S(2)}, u32[]{:S(2)}) collective-permute-start(bf16[384,128]{1,0:T(8,128)(2,1)S(1)} %get-tuple-element.59), channel_id=1, source_target_pairs={{0,8},{8,0},{4,12},{12,4},{16,24},{24,16},{20,28},{28,20},{1,5},{5... | collective-permute-start | bytes 294920 | tf_op jit(solution)/shard_map/ppermute | solution.py:528
  40.6 4.4 %collective-permute-start.14 = (bf16[1,64,512]{2,1,0:T(8,128)(2,1)S(1)}, bf16[1,64,512]{2,1,0:T(8,128)(2,1)S(1)}, u32[]{:S(2)}, u32[]{:S(2)}) collective-permute-start(bf16[1,64,512]{2,1,0:T(8,128)(2,1)S(1)} %sum.6.after.refs_0_), channel_id=1, source_target_pairs={{0,8},{4,12},{8,0},{12,4},{16,24},{20,28},{24,16},{28,20},{1,17},{... | collective-permute-start | bytes 196616 | tf_op jit(solution)/shard_map/ppermute | solution.py:528
  45.0 5.2 %collective-permute-start.15 = (bf16[1,64,512]{2,1,0:T(8,128)(2,1)S(1)}, bf16[1,64,512]{2,1,0:T(8,128)(2,1)S(1)}, u32[]{:S(2)}, u32[]{:S(2)}) collective-permute-start(bf16[1,64,512]{2,1,0:T(8,128)(2,1)S(1)} %sum.7.after), channel_id=1, source_target_pairs={{0,16},{4,20},{8,24},{12,28},{16,0},{20,4},{24,8},{28,12},{1,5},{5... | collective-permute-start | bytes 196616 | tf_op jit(solution)/shard_map/ppermute | solution.py:528

commit v9 on v8

--- a/solution.py
+++ b/solution.py
@@ -10,6 +10,7 @@
 F32 = jnp.float32
 BF16 = jnp.bfloat16
 LANES = 128
+BIAS_LANE = 96
 UNIT_ROWS = 32
 Z_ROWS = 64
 SWAPS = (
@@ -104,7 +105,6 @@
     for copy in copies:
         copy.start()
     bricks = features.shape[0]
-    shard_out[...] = jnp.zeros(shard_out.shape, BF16)
     values[:, bricks * 64 :, :] = jnp.zeros((4, 64, LANES), F32)
     row = lax.broadcasted_iota(jnp.int32, (64, 512), 0)
     col = lax.broadcasted_iota(jnp.int32, (64, 512), 1)
@@ -163,20 +163,44 @@
     shard = weight_t.shape[1]
     lead = shard // LANES * LANES
     count = bias.shape[1]
-    shard_out[:, 0:lead] = weight_t[:, 0:lead]
-    tile = jnp.concatenate(
+    tail = jnp.concatenate(
         [weight_t[:, lead:shard].astype(F32), jnp.zeros((64, lead + LANES - shard), F32)], axis=1
     )
-    offset = shard - lead
     behind = jnp.concatenate(
         [bias[...].astype(F32), jnp.zeros((1, LANES - count), F32)], axis=1
     )
-    behind = pltpu.roll(jnp.broadcast_to(behind, (64, LANES)), offset, 1)
-    first = lax.broadcasted_iota(jnp.int32, (64, LANES), 0) == 0
-    lane = lax.broadcasted_iota(jnp.int32, (64, LANES), 1)
-    behind = jnp.where(first & (lane >= offset) & (lane < offset + count), behind, 0.0)
-    shard_out[:, lead : lead + LANES] = (tile + behind).astype(BF16)
+    behind = pltpu.roll(jnp.broadcast_to(behind, (32, LANES)), BIAS_LANE, 1)
+    packed = pack_shard(weight_t[:, 0:lead].astype(F32), (tail, shard - lead), behind, 0.0)
+    shard_out[...] = packed.astype(BF16)
     last.wait()
+
+
+def pack_shard(block, rest, bias_low, bias_high):
+    tail, count = rest
+    tiles = [block[:, i : i + LANES] for i in range(0, block.shape[1], LANES)]
+    beside = tail[0:32] + pltpu.roll(tail[32:64], count, 1)
+    row = lax.broadcasted_iota(jnp.int32, (32, LANES), 0)
+    lane = lax.broadcasted_iota(jnp.int32, (32, LANES), 1)
+    behind = jnp.where(row == 0, bias_low, bias_high)
+    beside = jnp.where((lane >= BIAS_LANE) & (row < 2), behind, beside)
+    return jnp.concatenate(tiles + [beside], axis=0)
+
+
+def unpack_shard(rows, shard):
+    lead = shard // LANES
+    tiles = [rows[64 * i : 64 * i + 64] for i in range(lead)]
+    beside = rows[64 * lead :]
+    count = shard - lead * LANES
+    tail = jnp.concatenate([beside, pltpu.roll(beside, LANES - count, 1)], axis=0)
+    return jnp.concatenate(tiles + [tail[:, 0:count]], axis=1)
+
+
+def unpack_bias(rows):
+    edge = rows[rows.shape[0] - 32 : rows.shape[0] - 24]
+    lane = lax.broadcasted_iota(jnp.int32, (1, LANES), 1)
+    low = pltpu.roll(edge, LANES - BIAS_LANE, 1)[0:1]
+    high = pltpu.roll(edge, 2 * (LANES - BIAS_LANE), 1)[1:2]
+    return jnp.where(lane < 32, low, jnp.where(lane < 64, high, 0.0))
 
 
 def gather_units(table, received):
@@ -331,7 +355,8 @@
     for m, part in enumerate(shards):
         gathered[m] = part[...]
     for k in range(groups):
-        flat[:, k * shard : (k + 1) * shard] = gathered[me ^ k][:, 0:shard].astype(F32)
+        rows = gathered[me ^ k].astype(F32)
+        flat[:, k * shard : (k + 1) * shard] = unpack_shard(rows, shard)
     total = groups * shard
     flat[:, total:] = jnp.zeros((64, flat.shape[1] - total), F32)
     shifted[:, :] = pltpu.roll(flat[...], flat.shape[1] - 64, 1)
@@ -368,13 +393,11 @@
             backward_out[row_block(a + x, e), x * LANES : (x + 1) * LANES] = band
 
     lane = lax.broadcasted_iota(jnp.int32, (8, LANES), 1)
-    bias_lane = shard % LANES
-    bias_tile = shard - bias_lane
     count = 64 // groups
     bias_row = jnp.zeros((8, LANES), F32)
     for k in range(groups):
-        tile = gathered[me ^ k][0:16, bias_tile : bias_tile + LANES].astype(F32)[0:8]
-        moved = pltpu.roll(tile, (count * k - bias_lane) % LANES, 1)
+        row = unpack_bias(gathered[me ^ k].astype(F32))
+        moved = pltpu.roll(jnp.broadcast_to(row, (8, LANES)), count * k, 1)
         bias_row += jnp.where((lane >= count * k) & (lane < count * (k + 1)), moved, 0.0)
     bias_out[...] = bias_row + pltpu.roll(bias_row, 64, 1)
 
@@ -388,7 +411,8 @@
 def forward_kernel(
     masked, mask, cotangent_hbm, toeplitz, bias, rows, send, r0, r1, r2, r3, r4,
     block_out, grad_out, keep_out, give_out, u0, u1, u2, u3, u4,
-    table, windows, sides, walls, flat, shifted, values, flipped, cotangent, sem, *, shard,
+    table, windows, sides, walls, flat, shifted, values, flipped, cotangent, product, sem,
+    *, shard,
 ):
     fetch = pltpu.make_async_copy(cotangent_hbm, cotangent, sem)
     fetch.start()
@@ -397,66 +421,84 @@
     pairs = bricks // 2
     gather_units(table, (r0, r1, r2, r3, r4))
     assemble(masked, table, rows, windows, sides, walls)
-    bias_lane = shard % LANES
-    bias_tile = shard - bias_lane
     bias_row = bias[0:1, :]
     fetch.wait()
     values[:, bricks * 64 :, :] = jnp.zeros((4, 64, LANES), F32)
 
     bias_row = jnp.concatenate([bias_row, bias_row], axis=1)
-    total = jnp.dot(all_taps(windows), toeplitz[...], preferred_element_type=F32)
-    rows_of_chunk = total.shape[0] // 4
-    bias_sum = jnp.zeros((8, 256), F32)
-    for q in range(4):
-        p = total[q * rows_of_chunk : (q + 1) * rows_of_chunk] + bias_row
-        active = chunk_of(mask, q)
-        sig = jax.nn.sigmoid(p)
-        put_chunk(block_out, q, p * sig * active)
-        grad = (chunk_of(cotangent, q) * sig * (1.0 + p * (1.0 - sig)) * active).astype(BF16)
-        wide = grad.astype(F32)
-        put_chunk(grad_out, q, wide)
-        for n, (brick, i) in enumerate(chunk_places(bricks)):
-            for x in range(2):
-                at = brick * 64 + (2 * i + x) * 8
-                values[q, at : at + 8, :] = wide[
-                    8 * n : 8 * n + 8, x * LANES : (x + 1) * LANES
-                ]
-        flipped[:, q * rows_of_chunk : (q + 1) * rows_of_chunk] = jnp.transpose(wide).astype(BF16)
-        bias_sum += jnp.sum(wide.reshape(-1, 8, 256), axis=0)
+    product[...] = jnp.dot(all_taps(windows), toeplitz[...], preferred_element_type=F32)
+    rows_of_chunk = product.shape[0] // 4
+
+    def one_chunk(q, bias_sum):
+        lanes = pl.ds(pl.multiple_of(q * LANES, LANES), LANES)
+        for pair in range(pairs):
+            for i in range(4):
+                at = pl.multiple_of(q * rows_of_chunk + (pair * 4 + i) * 16, 16)
+                p = product[pl.ds(at, 16), :] + bias_row
+
+                def both(ref, i=i, pair=pair):
+                    return jnp.concatenate(
+                        [
+                            jnp.concatenate(
+                                [ref[2 * pair + b, i, x, :, lanes].astype(F32) for b in range(2)],
+                                axis=0,
+                            )
+                            for x in range(2)
+                        ],
+                        axis=1,
+                    )
+
+                active = both(mask)
+                sig = jax.nn.sigmoid(p)
+                out = p * sig * active
+                grad = both(cotangent) * sig * (1.0 + p * (1.0 - sig)) * active
+                wide = grad.astype(BF16).astype(F32)
+                product[pl.ds(at, 16), :] = wide
+                bias_sum += wide[0:8] + wide[8:16]
+                for b in range(2):
+                    brick = 2 * pair + b
+                    for x in range(2):
+                        rows_, half = slice(8 * b, 8 * b + 8), slice(x * LANES, (x + 1) * LANES)
+                        block_out[brick, i, x, :, lanes] = out[rows_, half].astype(BF16)
+                        grad_out[brick, i, x, :, lanes] = wide[rows_, half].astype(BF16)
+                        to = brick * 64 + (2 * i + x) * 8
+                        values[q, to : to + 8, :] = wide[rows_, half]
+        return bias_sum
+
+    bias_sum = lax.fori_loop(0, 4, one_chunk, jnp.zeros((8, 256), F32))
     bias_sum = bias_sum[:, 0:LANES] + bias_sum[:, LANES:]
     pack_units(values, send, (u0, u1, u2, u3, u4))
+    for q in range(4):
+        rows_of_q = slice(q * rows_of_chunk, (q + 1) * rows_of_chunk)
+        flipped[:, rows_of_q] = jnp.transpose(product[rows_of_q, :]).astype(BF16)
 
     for e in range(3):
-        products = [
-            jnp.dot(flipped[...], tap_rows(windows, d, e), preferred_element_type=F32)
-            for d in range(4)
-        ]
-        for a in range(3):
-            both = products[a][0:LANES] + products[a + 1][LANES:]
-            shifted[64 * a : 64 * a + 64, 256 * e : 256 * e + 256] = both[64:] + pltpu.roll(
-                both[0:64], 64, 1
-            )
+        upper = None
+        for d in range(4):
+            terms = jnp.dot(flipped[...], tap_rows(windows, d, e), preferred_element_type=F32)
+            if d > 0:
+                both = upper + terms[LANES:]
+                shifted[64 * d - 64 : 64 * d, 256 * e : 256 * e + 256] = both[64:] + pltpu.roll(
+                    both[0:64], 64, 1
+                )
+            upper = terms[0:LANES]
     for a in range(3):
         for e in range(3):
             at = 192 * (3 * a + e)
             flat[:, at : at + 256] = shifted[64 * a : 64 * a + 64, 256 * e : 256 * e + 256]
 
-    width = keep_out.shape[2]
     bias_all = jnp.sum(bias_sum, axis=0, keepdims=True)
-    bias_all = jnp.broadcast_to(bias_all, (8, LANES))
+    bias_all = jnp.broadcast_to(bias_all, (32, LANES))
     bias_all = bias_all + pltpu.roll(bias_all, 64, 1)
-    bias_all = pltpu.roll(bias_all, bias_lane, 1)
-    row8 = lax.broadcasted_iota(jnp.int32, (8, LANES), 0)
-    lane8 = lax.broadcasted_iota(jnp.int32, (8, LANES), 1)
-    keep = (row8 == 0) & (lane8 >= bias_lane) & (lane8 < bias_lane + 64)
+    bias_low = pltpu.roll(bias_all, BIAS_LANE, 1)
+    bias_high = pltpu.roll(bias_all, BIAS_LANE - 32, 1)
+    lead = shard // LANES * LANES
     me = lax.axis_index("dp")
     for k in range(groups):
-        part = flat[:, k * shard : (k + 1) * shard]
-        shifted[0:64, 0:shard] = part
-        shifted[0:64, shard:width] = jnp.zeros((64, width - shard), F32)
-        tile = shifted[0:8, bias_tile : bias_tile + LANES]
-        shifted[0:8, bias_tile : bias_tile + LANES] = jnp.where(keep, bias_all, tile)
-        block = shifted[0:64, 0:width].astype(BF16)
+        shifted[0:64, 0:shard] = flat[:, k * shard : (k + 1) * shard]
+        shifted[0:64, shard : lead + LANES] = jnp.zeros((64, lead + LANES - shard), F32)
+        tail = (shifted[0:64, lead : lead + LANES], shard - lead)
+        block = pack_shard(shifted[0:64, 0:lead], tail, bias_low, bias_high).astype(BF16)
         for m in range(groups):
 
             @pl.when(me ^ m == k)
@@ -502,16 +544,11 @@
 
 
 def finish_kernel(mine, other, weight_out, bias_out):
-    shard = weight_out.shape[1]
+    total = mine[...].astype(F32) + other[...].astype(F32)
+    weight_out[...] = unpack_shard(total, weight_out.shape[1])
     count = bias_out.shape[1]
-    total = mine[...].astype(F32) + other[...].astype(F32)
-    weight_out[...] = total[:, 0:shard]
-    bias_lane = shard % LANES
-    bias_tile = shard - bias_lane
-    tile = total[0:8, bias_tile : bias_tile + LANES]
-    me = lax.axis_index("dp")
-    moved = pltpu.roll(tile, 2 * LANES - bias_lane - me * count, 1)
-    bias_out[...] = moved[0:1, 0:count]
+    row = jnp.broadcast_to(unpack_bias(total), (8, LANES))
+    bias_out[...] = pltpu.roll(row, LANES - lax.axis_index("dp") * count, 1)[0:1, 0:count]
 
 
 def swapped(block, axis, bit):
@@ -560,11 +597,11 @@
     shard, channels = weight.shape
     groups = lax.axis_size("dp")
     count = conv_bias.shape[0]
-    width = -(-(shard + channels) // LANES) * LANES
+    shard_rows = channels * (shard // LANES) + channels // 2
     unit_rows = 8 * UNIT_ROWS + 2 * Z_ROWS
     units_type = jax.ShapeDtypeStruct((unit_rows, LANES), BF16)
     grid_type = jax.ShapeDtypeStruct(grid_shape, BF16)
-    shard_type = jax.ShapeDtypeStruct((channels, width), BF16)
+    shard_type = jax.ShapeDtypeStruct((shard_rows, LANES), BF16)
     params = pltpu.CompilerParams(vmem_limit_bytes=48 * 1024 * 1024)
     rows_shape = neighbours.shape[1:]
     send_shape = (spread, 1, links)
@@ -627,7 +664,7 @@
         ],
         in_specs=[vmem()] * groups,
         out_specs=[vmem()] * 3,
-        scratch_shapes=[pltpu.VMEM((groups, channels, width), BF16), flat, flat],
+        scratch_shapes=[pltpu.VMEM((groups, shard_rows, LANES), BF16), flat, flat],
         compiler_params=params,
     )(*(shards[m] for m in range(groups)))
 
@@ -635,7 +672,7 @@
     windows = pltpu.VMEM((3, 4, pairs, 5, 2, 16, 256), BF16)
     sides = pltpu.VMEM((2, 2, 5, 8, LANES), F32)
     walls = pltpu.VMEM((2, 64, LANES), F32)
-    half_type = jax.ShapeDtypeStruct((groups // 2, channels, width), BF16)
+    half_type = jax.ShapeDtypeStruct((groups // 2, shard_rows, LANES), BF16)
     block_output, grad, keep, give, *grad_units = pl.pallas_call(
         functools.partial(forward_kernel, shard=shard),
         name="forward",
@@ -654,6 +691,7 @@
             pltpu.VMEM((4, (bricks + 1) * 64, LANES), F32),
             pltpu.VMEM((256, bricks * LANES), BF16),
             pltpu.VMEM(grid_shape, BF16),
+            pltpu.VMEM((bricks * LANES, 256), F32),
             pltpu.SemaphoreType.DMA,
         ],
         compiler_params=params,

time: 51.2 us -> 51.3 us (level)
  waiting for transfers between devices: 11.3 us -> 10.7 us
  Pallas kernels: 12.9 us -> 13.5 us
where the time goes in v9:
time: 51.3 us; the launch traced here: 51.1 us
  starting transfers between devices  25.5 us (50%)
  Pallas kernels  13.5 us (26%)
  waiting for transfers between devices  10.7 us (21%)
  between operations  1.4 us (3%)
    ppermute x11, starting transfers between devices, by_parity(): return lax.ppermute(block, ('space', 'dp'), pairs)  21.8 us
    pallas_call x1, Pallas kernels, body(): pl.pallas_call(functools.partial(forward_kernel, shard=shard), name='forw...  7.04 us
    ppermute x5, waiting for transfers between devices, swapped(): lax.ppermute(block, axis, [(i, i ^ bit) for i in range(lax.axis_size(axis...  5.53 us
    ppermute x11, waiting for transfers between devices, by_parity(): return lax.ppermute(block, ('space', 'dp'), pairs)  5.16 us
    ppermute x5, starting transfers between devices, swapped(): lax.ppermute(block, axis, [(i, i ^ bit) for i in range(lax.axis_size(axis...  3.67 us
    pallas_call x1, Pallas kernels, body(): pl.pallas_call(prepare_kernel, name='prepare', out_shape=[grid_type, grid...  2.15 us
    pallas_call x1, Pallas kernels, body(): pl.pallas_call(backward_kernel, name='backward', out_shape=grid_type, in_...  1.68 us
    pallas_call x1, Pallas kernels, body(): pl.pallas_call(assemble_kernel, name='assemble', out_shape=jax.ShapeDtype...  1.07 us
  transfers between devices with their start and end apart: 16, of which 7 were waited for; matrix products, arithmetic and copies ran while one was open for 0% of the time, Pallas kernels for 7%

profile of v9, /device:TPU:0, one launch (start us, length us, event | category | flops | bytes accessed | tf_op | source)
XLA Modules:
  0.0 51.1 jit_solution(13078498465461757677)
XLA Ops:
  1.3 2.1 %prepare.1 = (bf16[4,4,2,8,512]{4,3,2,1,0:T(8,128)(2,1)S(1)}, bf16[4,4,2,8,512]{4,3,2,1,0:T(8,128)(2,1)S(1)}, s32[4,26]{1,0:T(4,128)S(1)}, s32[5,1,12]{2,1,0:T(1...) custom-call(bf16[4,4,2,8,512]{4,3,2,1,0:T(8,128)(2,1)} %bitcast.17, ...), custom_call_target="tpu_custom_call" | custom-call | tf_op jit(solution)/shard_map/prepare/pallas_call | solution.py:609
  3.4 3.0 %collective-permute-start.1 = (bf16[224,128]{1,0:T(8,128)(2,1)S(1)}, bf16[224,128]{1,0:T(8,128)(2,1)S(1)}, u32[]{:S(2)}, u32[]{:S(2)}) collective-permute-start(bf16[224,128]{1,0:T(8,128)(2,1)S(1)} %get-tuple-element.36.refs_0_), channel_id=1, source_target_pairs={{0,2},{1,3},{2,0},{3,1},{4,6},{5,7},{6,4},{7,5},{8,10},{9,11},{10,... | collective-permute-start | bytes 172040 | tf_op jit(solution)/shard_map/ppermute | solution.py:555
  6.4 0.0 collective-permute-start
  6.4 0.7 %collective-permute-start.3 = (bf16[384,128]{1,0:T(8,128)(2,1)S(1)}, bf16[384,128]{1,0:T(8,128)(2,1)S(1)}, u32[]{:S(2)}, u32[]{:S(2)}) collective-permute-start(bf16[384,128]{1,0:T(8,128)(2,1)S(1)} %get-tuple-element.42), channel_id=1, source_target_pairs={{4,8},{8,4},{12,16},{16,12},{20,24},{24,20},{9,17},{17,9},{13,21},... | collective-permute-start | bytes 294920 | tf_op jit(solution)/shard_map/ppermute | solution.py:565
  7.1 0.7 %collective-permute-start.4 = (bf16[384,128]{1,0:T(8,128)(2,1)S(1)}, bf16[384,128]{1,0:T(8,128)(2,1)S(1)}, u32[]{:S(2)}, u32[]{:S(2)}) collective-permute-start(bf16[384,128]{1,0:T(8,128)(2,1)S(1)} %get-tuple-element.43), channel_id=1, source_target_pairs={{8,16},{16,8},{12,20},{20,12},{5,9},{9,5},{13,17},{17,13},{21,25},... | collective-permute-start | bytes 294920 | tf_op jit(solution)/shard_map/ppermute | solution.py:565
  7.8 4.3 %collective-permute-start.5 = (bf16[384,128]{1,0:T(8,128)(2,1)S(1)}, bf16[384,128]{1,0:T(8,128)(2,1)S(1)}, u32[]{:S(2)}, u32[]{:S(2)}) collective-permute-start(bf16[384,128]{1,0:T(8,128)(2,1)S(1)} %get-tuple-element.44), channel_id=1, source_target_pairs={{0,4},{4,0},{8,12},{12,8},{16,20},{20,16},{24,28},{28,24},{1,9},{9... | collective-permute-start | bytes 294920 | tf_op jit(solution)/shard_map/ppermute | solution.py:565
  12.1 0.0 collective-permute-done.1.refs_2_
  12.1 4.4 %collective-permute-start.6 = (bf16[384,128]{1,0:T(8,128)(2,1)S(1)}, bf16[384,128]{1,0:T(8,128)(2,1)S(1)}, u32[]{:S(2)}, u32[]{:S(2)}) collective-permute-start(bf16[384,128]{1,0:T(8,128)(2,1)S(1)} %get-tuple-element.45), channel_id=1, source_target_pairs={{0,8},{8,0},{4,12},{12,4},{16,24},{24,16},{20,28},{28,20},{1,5},{5... | collective-permute-start | bytes 294920 | tf_op jit(solution)/shard_map/ppermute | solution.py:565
  16.5 0.0 collective-permute-done.refs_1_
  16.5 0.0 collective-permute-start.2
  16.5 1.2 %collective-permute-done.2.refs_3_ = bf16[224,128]{1,0:T(8,128)(2,1)S(1)} collective-permute-done((bf16[224,128]{1,0:T(8,128)(2,1)S(1)}, bf16[224,128]{1,0:T(8,128)(2,1)S(1)}, u32[]{:S(2)}, u32[]{:S(2)}) %collective-permute-start.2) | collective-permute-done | bytes 57376 | tf_op jit(solution)/shard_map/ppermute | solution.py:555
  17.8 0.8 %weights.1 = (bf16[3072,256]{1,0:T(8,128)(2,1)S(1)}, bf16[3072,256]{1,0:T(8,128)(2,1)S(1)}, f32[8,128]{1,0:T(8,128)S(1)}) custom-call(bf16[224,128]{1,0:T(8,128)(2,1)S(1)} %get-tuple-element.36.refs_0_, bf16[224,128]{1,0:T(8,128)(2,1)S(1)} %collective-permute-done.refs_1_, bf16[224,128]{1,0:T(8,128)(2,1)S(1)} %collective-permute-done.1.refs_2_, ...), custom_call_target="tpu_custom_call" | custom-call | tf_op jit(solution)/shard_map/weights/pallas_call | solution.py:657
  18.6 0.0 collective-permute-done.3.r1
  18.6 0.0 collective-permute-done.4.r2
  18.6 0.0 collective-permute-done.5.r3
  18.6 0.5 %collective-permute-done.6.r4 = bf16[384,128]{1,0:T(8,128)(2,1)S(1)} collective-permute-done((bf16[384,128]{1,0:T(8,128)(2,1)S(1)}, bf16[384,128]{1,0:T(8,128)(2,1)S(1)}, u32[]{:S(2)}, u32[]{:S(2)}) %collective-permute-start.6) | collective-permute-done | bytes 98336 | tf_op jit(solution)/shard_map/ppermute | solution.py:565
  19.1 7.0 %forward.1 = (bf16[4,4,2,8,512]{4,3,2,1,0:T(8,128)(2,1)}, bf16[4,4,2,8,512]{4,3,2,1,0:T(8,128)(2,1)S(1)}, bf16[2,224,128]{2,1,0:T(8,128)(2,1)S(1)}, bf16[2,224,1...) custom-call(bf16[4,4,2,8,512]{4,3,2,1,0:T(8,128)(2,1)S(1)} %get-tupl, ...), custom_call_target="tpu_custom_call" | custom-call | tf_op jit(solution)/shard_map/forward/pallas_call | solution.py:676
  26.2 0.1 collective-permute-start.8
  26.2 0.7 %collective-permute-start.7 = (bf16[384,128]{1,0:T(8,128)(2,1)S(1)}, bf16[384,128]{1,0:T(8,128)(2,1)S(1)}, u32[]{:S(2)}, u32[]{:S(2)}) collective-permute-start(bf16[384,128]{1,0:T(8,128)(2,1)S(1)} %get-tuple-element.49), channel_id=1, source_target_pairs={{4,8},{8,4},{12,16},{16,12},{20,24},{24,20},{9,17},{17,9},{13,21},... | collective-permute-start | bytes 294920 | tf_op jit(solution)/shard_map/ppermute | solution.py:565
  26.9 0.6 %collective-permute-done.8.refs_1_ = bf16[2,224,128]{2,1,0:T(8,128)(2,1)S(1)} collective-permute-done((bf16[2,224,128]{2,1,0:T(8,128)(2,1)S(1)}, bf16[2,224,128]{2,1,0:T(8,128)(2,1)S(1)}, u32[]{:S(2)}, u32[]{:S(2)}) %collective-permute-start.8) | collective-permute-done | bytes 114720 | tf_op jit(solution)/shard_map/ppermute | solution.py:555
  27.6 0.6 %collective-permute-start.10 = (bf16[1,224,128]{2,1,0:T(8,128)(2,1)S(1)}, bf16[1,224,128]{2,1,0:T(8,128)(2,1)S(1)}, u32[]{:S(2)}, u32[]{:S(2)}) collective-permute-start(bf16[1,224,128]{2,1,0:T(8,128)(2,1)S(1)} %get-tuple-element.55), channel_id=1, source_target_pairs={{0,2},{1,3},{2,0},{3,1},{4,6},{5,7},{6,4},{7,5},{8,10},{9,11},{10,... | collective-permute-start | bytes 172040 | tf_op jit(solution)/shard_map/ppermute | solution.py:555
  28.2 0.0 collective-permute-done.7.refs_2_.r1
  28.2 3.6 %collective-permute-done.10.refs_1_ = bf16[1,224,128]{2,1,0:T(8,128)(2,1)S(1)} collective-permute-done((bf16[1,224,128]{2,1,0:T(8,128)(2,1)S(1)}, bf16[1,224,128]{2,1,0:T(8,128)(2,1)S(1)}, u32[]{:S(2)}, u32[]{:S(2)}) %collective-permute-start.10) | collective-permute-done | bytes 57376 | tf_op jit(solution)/shard_map/ppermute | solution.py:555
  31.9 4.2 %collective-permute-start.11 = (bf16[384,128]{1,0:T(8,128)(2,1)S(1)}, bf16[384,128]{1,0:T(8,128)(2,1)S(1)}, u32[]{:S(2)}, u32[]{:S(2)}) collective-permute-start(bf16[384,128]{1,0:T(8,128)(2,1)S(1)} %get-tuple-element.58), channel_id=1, source_target_pairs={{0,4},{4,0},{8,12},{12,8},{16,20},{20,16},{24,28},{28,24},{1,9},{9... | collective-permute-start | bytes 294920 | tf_op jit(solution)/shard_map/ppermute | solution.py:565
  36.0 0.1 collective-permute-start.13
  36.1 0.7 %collective-permute-start.9 = (bf16[384,128]{1,0:T(8,128)(2,1)S(1)}, bf16[384,128]{1,0:T(8,128)(2,1)S(1)}, u32[]{:S(2)}, u32[]{:S(2)}) collective-permute-start(bf16[384,128]{1,0:T(8,128)(2,1)S(1)} %get-tuple-element.53), channel_id=1, source_target_pairs={{8,16},{16,8},{12,20},{20,12},{5,9},{9,5},{13,17},{17,13},{21,25},... | collective-permute-start | bytes 294920 | tf_op jit(solution)/shard_map/ppermute | solution.py:565
  36.8 4.2 %collective-permute-start.12 = (bf16[384,128]{1,0:T(8,128)(2,1)S(1)}, bf16[384,128]{1,0:T(8,128)(2,1)S(1)}, u32[]{:S(2)}, u32[]{:S(2)}) collective-permute-start(bf16[384,128]{1,0:T(8,128)(2,1)S(1)} %get-tuple-element.59), channel_id=1, source_target_pairs={{0,8},{8,0},{4,12},{12,4},{16,24},{24,16},{20,28},{28,20},{1,5},{5... | collective-permute-start | bytes 294920 | tf_op jit(solution)/shard_map/ppermute | solution.py:565
  40.9 0.0 collective-permute-done.13.refs_1_
  40.9 0.0 collective-permute-done.11.refs_2_.r3
  41.0 0.2 collective-permute-start.14
  41.2 0.0 collective-permute-done.9.r2
  41.2 2.7 %collective-permute-done.12.r4 = bf16[384,128]{1,0:T(8,128)(2,1)S(1)} collective-permute-done((bf16[384,128]{1,0:T(8,128)(2,1)S(1)}, bf16[384,128]{1,0:T(8,128)(2,1)S(1)}, u32[]{:S(2)}, u32[]{:S(2)}) %collective-permute-start.12) | collective-permute-done | bytes 98336 | tf_op jit(solution)/shard_map/ppermute | solution.py:565
  43.9 1.1 %assemble.1.refs_2_.windows = bf16[3,4,2,5,2,16,256]{6,5,4,3,2,1,0:T(8,128)(2,1)S(1)} custom-call(bf16[4,4,2,8,512]{4,3,2,1,0:T(8,128)(2,1)S(1)} %get-tuple-element.47.grad, s32[4,26]{1,0:T(4,128)S(1)} %get-tuple-element.39.rows, bf16[384,128]{1,0:T(8,128)(2,1)S(1)} %get-tuple-element.48.r0, bf16[384,128]{1,0:T(8,128)(2,1)S(1)} %collective-permute-done.7.refs_2_.r1, ...), custom_call_target="tpu_custom_call" | custom-call | tf_op jit(solution)/shard_map/assemble/pallas_call | solution.py:727
  45.0 0.2 collective-permute-done.14.refs_1_
  45.2 1.8 %collective-permute-start.15 = (bf16[1,224,128]{2,1,0:T(8,128)(2,1)S(1)}, bf16[1,224,128]{2,1,0:T(8,128)(2,1)S(1)}, u32[]{:S(2)}, u32[]{:S(2)}) collective-permute-start(bf16[1,224,128]{2,1,0:T(8,128)(2,1)S(1)} %sum.7.after), channel_id=1, source_target_pairs={{0,16},{4,20},{8,24},{12,28},{16,0},{20,4},{24,8},{28,12},{1,5},{5... | collective-permute-start | bytes 172040 | tf_op jit(solution)/shard_map/ppermute | solution.py:565
  47.0 1.7 %backward.1 = bf16[4,4,2,8,512]{4,3,2,1,0:T(8,128)(2,1)} custom-call(bf16[3,4,2,5,2,16,256]{6,5,4,3,2,1,0:T(8,128)(2,1)S(1)} %assemble.1.refs_2_.windows, bf16[4,4,2,8,512]{4,3,2,1,0:T(8,128)(2,1)S(1)} %get-tuple-element.35.mask, bf16[3072,256]{1,0:T(8,128)(2,1)S(1)} %get-tuple-element.61.toeplitz, bf16[1,224,128]{2,1,0:T(8,128)(2,1)S(1)} %sum.7.after), custom_call_target="tpu_custom_call" | custom-call | tf_op jit(solution)/shard_map/backward/pallas_call | solution.py:741
  48.7 1.7 %collective-permute-done.15 = bf16[1,224,128]{2,1,0:T(8,128)(2,1)S(1)} collective-permute-done((bf16[1,224,128]{2,1,0:T(8,128)(2,1)S(1)}, bf16[1,224,128]{2,1,0:T(8,128)(2,1)S(1)}, u32[]{:S(2)}, u32[]{:S(2)}) %collective-permute-start.15) | collective-permute-done | bytes 57376 | tf_op jit(solution)/shard_map/ppermute | solution.py:565
  50.4 0.7 %finish.1 = (f32[64,432]{1,0:T(8,128)}, f32[1,16]{1,0:T(1,128)}) custom-call(bf16[224,128]{1,0:T(8,128)(2,1)S(1)} %bitcast.13, bf16[224,128]{1,0:T(8,128)(2,1)S(1)} %bitcast.14), custom_call_target="tpu_custom_call" | custom-call | tf_op jit(solution)/shard_map/finish/pallas_call | solution.py:750
  (4 shorter events, 0.1 us)
Async XLA Ops:
  3.4 8.7 %collective-permute-start.1 = (bf16[224,128]{1,0:T(8,128)(2,1)S(1)}, bf16[224,128]{1,0:T(8,128)(2,1)S(1)}, u32[]{:S(2)}, u32[]{:S(2)}) collective-permute-start(bf16[224,128]{1,0:T(8,128)(2,1)S(1)} %get-tuple-element.36.refs_0_), channel_id=1, source_target_pairs={{0,2},{1,3},{2,0},{3,1},{4,6},{5,7},{6,4},{7,5},{8,10},{9,11},{10,... | collective-permute-start | bytes 172040 | tf_op jit(solution)/shard_map/ppermute | solution.py:555
  6.4 10.1 %collective-permute-start = (bf16[224,128]{1,0:T(8,128)(2,1)S(1)}, bf16[224,128]{1,0:T(8,128)(2,1)S(1)}, u32[]{:S(2)}, u32[]{:S(2)}) collective-permute-start(bf16[224,128]{1,0:T(8,128)(2,1)S(1)} %get-tuple-element.36.refs_0_), channel_id=1, source_target_pairs={{0,1},{1,0},{2,3},{3,2},{4,5},{5,4},{6,7},{7,6},{8,9},{9,8},{10,11... | collective-permute-start | bytes 172040 | tf_op jit(solution)/shard_map/ppermute | solution.py:555
  6.4 12.1 %collective-permute-start.3 = (bf16[384,128]{1,0:T(8,128)(2,1)S(1)}, bf16[384,128]{1,0:T(8,128)(2,1)S(1)}, u32[]{:S(2)}, u32[]{:S(2)}) collective-permute-start(bf16[384,128]{1,0:T(8,128)(2,1)S(1)} %get-tuple-element.42), channel_id=1, source_target_pairs={{4,8},{8,4},{12,16},{16,12},{20,24},{24,20},{9,17},{17,9},{13,21},... | collective-permute-start | bytes 294920 | tf_op jit(solution)/shard_map/ppermute | solution.py:565
  7.1 11.5 %collective-permute-start.4 = (bf16[384,128]{1,0:T(8,128)(2,1)S(1)}, bf16[384,128]{1,0:T(8,128)(2,1)S(1)}, u32[]{:S(2)}, u32[]{:S(2)}) collective-permute-start(bf16[384,128]{1,0:T(8,128)(2,1)S(1)} %get-tuple-element.43), channel_id=1, source_target_pairs={{8,16},{16,8},{12,20},{20,12},{5,9},{9,5},{13,17},{17,13},{21,25},... | collective-permute-start | bytes 294920 | tf_op jit(solution)/shard_map/ppermute | solution.py:565
  7.8 10.8 %collective-permute-start.5 = (bf16[384,128]{1,0:T(8,128)(2,1)S(1)}, bf16[384,128]{1,0:T(8,128)(2,1)S(1)}, u32[]{:S(2)}, u32[]{:S(2)}) collective-permute-start(bf16[384,128]{1,0:T(8,128)(2,1)S(1)} %get-tuple-element.44), channel_id=1, source_target_pairs={{0,4},{4,0},{8,12},{12,8},{16,20},{20,16},{24,28},{28,24},{1,9},{9... | collective-permute-start | bytes 294920 | tf_op jit(solution)/shard_map/ppermute | solution.py:565
  12.1 7.0 %collective-permute-start.6 = (bf16[384,128]{1,0:T(8,128)(2,1)S(1)}, bf16[384,128]{1,0:T(8,128)(2,1)S(1)}, u32[]{:S(2)}, u32[]{:S(2)}) collective-permute-start(bf16[384,128]{1,0:T(8,128)(2,1)S(1)} %get-tuple-element.45), channel_id=1, source_target_pairs={{0,8},{8,0},{4,12},{12,4},{16,24},{24,16},{20,28},{28,20},{1,5},{5... | collective-permute-start | bytes 294920 | tf_op jit(solution)/shard_map/ppermute | solution.py:565
  16.5 1.2 %collective-permute-start.2 = (bf16[224,128]{1,0:T(8,128)(2,1)S(1)}, bf16[224,128]{1,0:T(8,128)(2,1)S(1)}, u32[]{:S(2)}, u32[]{:S(2)}) collective-permute-start(bf16[224,128]{1,0:T(8,128)(2,1)S(1)} %collective-permute-done.1.refs_2_), channel_id=1, source_target_pairs={{0,1},{1,0},{2,3},{3,2},{4,5},{5,4},{6,7},{7,6},{8,9},{9,8},{10,11... | collective-permute-start | bytes 172040 | tf_op jit(solution)/shard_map/ppermute | solution.py:555
  26.2 1.4 %collective-permute-start.8 = (bf16[2,224,128]{2,1,0:T(8,128)(2,1)S(1)}, bf16[2,224,128]{2,1,0:T(8,128)(2,1)S(1)}, u32[]{:S(2)}, u32[]{:S(2)}) collective-permute-start(bf16[2,224,128]{2,1,0:T(8,128)(2,1)S(1)} %get-tuple-element.51), channel_id=1, source_target_pairs={{0,1},{1,0},{2,3},{3,2},{4,5},{5,4},{6,7},{7,6},{8,9},{9,8},{10,11... | collective-permute-start | bytes 344072 | tf_op jit(solution)/shard_map/ppermute | solution.py:555
  26.2 1.9 %collective-permute-start.7 = (bf16[384,128]{1,0:T(8,128)(2,1)S(1)}, bf16[384,128]{1,0:T(8,128)(2,1)S(1)}, u32[]{:S(2)}, u32[]{:S(2)}) collective-permute-start(bf16[384,128]{1,0:T(8,128)(2,1)S(1)} %get-tuple-element.49), channel_id=1, source_target_pairs={{4,8},{8,4},{12,16},{16,12},{20,24},{24,20},{9,17},{17,9},{13,21},... | collective-permute-start | bytes 294920 | tf_op jit(solution)/shard_map/ppermute | solution.py:565
  27.6 4.2 %collective-permute-start.10 = (bf16[1,224,128]{2,1,0:T(8,128)(2,1)S(1)}, bf16[1,224,128]{2,1,0:T(8,128)(2,1)S(1)}, u32[]{:S(2)}, u32[]{:S(2)}) collective-permute-start(bf16[1,224,128]{2,1,0:T(8,128)(2,1)S(1)} %get-tuple-element.55), channel_id=1, source_target_pairs={{0,2},{1,3},{2,0},{3,1},{4,6},{5,7},{6,4},{7,5},{8,10},{9,11},{10,... | collective-permute-start | bytes 172040 | tf_op jit(solution)/shard_map/ppermute | solution.py:555
  31.9 9.1 %collective-permute-start.11 = (bf16[384,128]{1,0:T(8,128)(2,1)S(1)}, bf16[384,128]{1,0:T(8,128)(2,1)S(1)}, u32[]{:S(2)}, u32[]{:S(2)}) collective-permute-start(bf16[384,128]{1,0:T(8,128)(2,1)S(1)} %get-tuple-element.58), channel_id=1, source_target_pairs={{0,4},{4,0},{8,12},{12,8},{16,20},{20,16},{24,28},{28,24},{1,9},{9... | collective-permute-start | bytes 294920 | tf_op jit(solution)/shard_map/ppermute | solution.py:565
  36.0 4.9 %collective-permute-start.13 = (bf16[1,224,128]{2,1,0:T(8,128)(2,1)S(1)}, bf16[1,224,128]{2,1,0:T(8,128)(2,1)S(1)}, u32[]{:S(2)}, u32[]{:S(2)}) collective-permute-start(bf16[1,224,128]{2,1,0:T(8,128)(2,1)S(1)} %get-tuple-element.60.refs_0_), channel_id=1, source_target_pairs={{0,4},{4,0},{8,12},{12,8},{16,20},{20,16},{24,28},{28,24},{1,9},{5... | collective-permute-start | bytes 172040 | tf_op jit(solution)/shard_map/ppermute | solution.py:565
  36.1 5.1 %collective-permute-start.9 = (bf16[384,128]{1,0:T(8,128)(2,1)S(1)}, bf16[384,128]{1,0:T(8,128)(2,1)S(1)}, u32[]{:S(2)}, u32[]{:S(2)}) collective-permute-start(bf16[384,128]{1,0:T(8,128)(2,1)S(1)} %get-tuple-element.53), channel_id=1, source_target_pairs={{8,16},{16,8},{12,20},{20,12},{5,9},{9,5},{13,17},{17,13},{21,25},... | collective-permute-start | bytes 294920 | tf_op jit(solution)/shard_map/ppermute | solution.py:565
  36.8 7.1 %collective-permute-start.12 = (bf16[384,128]{1,0:T(8,128)(2,1)S(1)}, bf16[384,128]{1,0:T(8,128)(2,1)S(1)}, u32[]{:S(2)}, u32[]{:S(2)}) collective-permute-start(bf16[384,128]{1,0:T(8,128)(2,1)S(1)} %get-tuple-element.59), channel_id=1, source_target_pairs={{0,8},{8,0},{4,12},{12,4},{16,24},{24,16},{20,28},{28,20},{1,5},{5... | collective-permute-start | bytes 294920 | tf_op jit(solution)/shard_map/ppermute | solution.py:565
  41.0 4.2 %collective-permute-start.14 = (bf16[1,224,128]{2,1,0:T(8,128)(2,1)S(1)}, bf16[1,224,128]{2,1,0:T(8,128)(2,1)S(1)}, u32[]{:S(2)}, u32[]{:S(2)}) collective-permute-start(bf16[1,224,128]{2,1,0:T(8,128)(2,1)S(1)} %sum.6.after.refs_0_), channel_id=1, source_target_pairs={{0,8},{4,12},{8,0},{12,4},{16,24},{20,28},{24,16},{28,20},{1,17},{... | collective-permute-start | bytes 172040 | tf_op jit(solution)/shard_map/ppermute | solution.py:565
  45.2 5.1 %collective-permute-start.15 = (bf16[1,224,128]{2,1,0:T(8,128)(2,1)S(1)}, bf16[1,224,128]{2,1,0:T(8,128)(2,1)S(1)}, u32[]{:S(2)}, u32[]{:S(2)}) collective-permute-start(bf16[1,224,128]{2,1,0:T(8,128)(2,1)S(1)} %sum.7.after), channel_id=1, source_target_pairs={{0,16},{4,20},{8,24},{12,28},{16,0},{20,4},{24,8},{28,12},{1,5},{5... | collective-permute-start | bytes 172040 | tf_op jit(solution)/shard_map/ppermute | solution.py:565

commit v10 on v8

--- a/solution.py
+++ b/solution.py
@@ -426,20 +426,18 @@
     bias_sum = bias_sum[:, 0:LANES] + bias_sum[:, LANES:]
     pack_units(values, send, (u0, u1, u2, u3, u4))
 
-    for e in range(3):
-        products = [
-            jnp.dot(flipped[...], tap_rows(windows, d, e), preferred_element_type=F32)
-            for d in range(4)
-        ]
-        for a in range(3):
-            both = products[a][0:LANES] + products[a + 1][LANES:]
-            shifted[64 * a : 64 * a + 64, 256 * e : 256 * e + 256] = both[64:] + pltpu.roll(
-                both[0:64], 64, 1
-            )
-    for a in range(3):
-        for e in range(3):
-            at = 192 * (3 * a + e)
-            flat[:, at : at + 256] = shifted[64 * a : 64 * a + 64, 256 * e : 256 * e + 256]
+    for ae in range(9):
+        a, e = ae // 3, ae % 3
+        both = jnp.zeros((LANES, 256), F32)
+        for x in range(2):
+            rows = tap_rows(windows, a + x, e)
+            for part in range(0, rows.shape[0], 256):
+                both += jnp.dot(
+                    flipped[x * LANES : (x + 1) * LANES, part : part + 256],
+                    rows[part : part + 256],
+                    preferred_element_type=F32,
+                )
+        flat[:, 192 * ae : 192 * ae + 256] = both[64:] + pltpu.roll(both[0:64], 64, 1)
 
     width = keep_out.shape[2]
     bias_all = jnp.sum(bias_sum, axis=0, keepdims=True)
@@ -650,7 +648,7 @@
             sides,
             walls,
             flat,
-            pltpu.VMEM((192, 3 * 256), F32),
+            pltpu.VMEM((channels, 4 * LANES), F32),
             pltpu.VMEM((4, (bricks + 1) * 64, LANES), F32),
             pltpu.VMEM((256, bricks * LANES), BF16),
             pltpu.VMEM(grid_shape, BF16),

time: 51.2 us -> 50.6 us (0.988)
    pallas_call x1, Pallas kernels: 6.57 us -> 5.99 us  [body(): pl.pallas_call(functools.partial(forward_kernel, shard=shard), name='forw...]
where the time goes in v10:
time: 50.6 us; the launch traced here: 50.4 us
  starting transfers between devices  25.3 us (50%)
  Pallas kernels  12.4 us (25%)
  waiting for transfers between devices  11.3 us (22%)
  between operations  1.4 us (3%)
    ppermute x11, starting transfers between devices, by_parity(): return lax.ppermute(block, ('space', 'dp'), pairs)  21.6 us
    pallas_call x1, Pallas kernels, body(): pl.pallas_call(functools.partial(forward_kernel, shard=shard), name='forw...  5.99 us
    ppermute x5, waiting for transfers between devices, swapped(): lax.ppermute(block, axis, [(i, i ^ bit) for i in range(lax.axis_size(axis...  5.64 us
    ppermute x11, waiting for transfers between devices, by_parity(): return lax.ppermute(block, ('space', 'dp'), pairs)  5.63 us
    ppermute x5, starting transfers between devices, swapped(): lax.ppermute(block, axis, [(i, i ^ bit) for i in range(lax.axis_size(axis...  3.69 us
    pallas_call x1, Pallas kernels, body(): pl.pallas_call(prepare_kernel, name='prepare', out_shape=[grid_type, grid...  2.15 us
    pallas_call x1, Pallas kernels, body(): pl.pallas_call(backward_kernel, name='backward', out_shape=grid_type, in_...  1.68 us
    pallas_call x1, Pallas kernels, body(): pl.pallas_call(assemble_kernel, name='assemble', out_shape=jax.ShapeDtype...  1.07 us
  transfers between devices with their start and end apart: 16, of which 7 were waited for; matrix products, arithmetic and copies ran while one was open for 0% of the time, Pallas kernels for 7%

profile of v10, /device:TPU:0, one launch (start us, length us, event | category | flops | bytes accessed | tf_op | source)
XLA Modules:
  0.0 50.4 jit_solution(2827236678841576063)
XLA Ops:
  1.3 2.1 %prepare.1 = (bf16[4,4,2,8,512]{4,3,2,1,0:T(8,128)(2,1)S(1)}, bf16[4,4,2,8,512]{4,3,2,1,0:T(8,128)(2,1)S(1)}, s32[4,26]{1,0:T(4,128)S(1)}, s32[5,1,12]{2,1,0:T(1...) custom-call(bf16[4,4,2,8,512]{4,3,2,1,0:T(8,128)(2,1)} %bitcast.17, ...), custom_call_target="tpu_custom_call" | custom-call | tf_op jit(solution)/shard_map/prepare/pallas_call | solution.py:570
  3.4 3.0 %collective-permute-start.1 = (bf16[64,512]{1,0:T(8,128)(2,1)S(1)}, bf16[64,512]{1,0:T(8,128)(2,1)S(1)}, u32[]{:S(2)}, u32[]{:S(2)}) collective-permute-start(bf16[64,512]{1,0:T(8,128)(2,1)S(1)} %get-tuple-element.36.refs_0_), channel_id=1, source_target_pairs={{0,2},{1,3},{2,0},{3,1},{4,6},{5,7},{6,4},{7,5},{8,10},{9,11},{10,... | collective-permute-start | bytes 196616 | tf_op jit(solution)/shard_map/ppermute | solution.py:516
  6.4 0.0 collective-permute-start
  6.4 0.7 %collective-permute-start.3 = (bf16[384,128]{1,0:T(8,128)(2,1)S(1)}, bf16[384,128]{1,0:T(8,128)(2,1)S(1)}, u32[]{:S(2)}, u32[]{:S(2)}) collective-permute-start(bf16[384,128]{1,0:T(8,128)(2,1)S(1)} %get-tuple-element.42), channel_id=1, source_target_pairs={{4,8},{8,4},{12,16},{16,12},{20,24},{24,20},{9,17},{17,9},{13,21},... | collective-permute-start | bytes 294920 | tf_op jit(solution)/shard_map/ppermute | solution.py:526
  7.1 0.7 %collective-permute-start.4 = (bf16[384,128]{1,0:T(8,128)(2,1)S(1)}, bf16[384,128]{1,0:T(8,128)(2,1)S(1)}, u32[]{:S(2)}, u32[]{:S(2)}) collective-permute-start(bf16[384,128]{1,0:T(8,128)(2,1)S(1)} %get-tuple-element.43), channel_id=1, source_target_pairs={{8,16},{16,8},{12,20},{20,12},{5,9},{9,5},{13,17},{17,13},{21,25},... | collective-permute-start | bytes 294920 | tf_op jit(solution)/shard_map/ppermute | solution.py:526
  7.8 4.3 %collective-permute-start.5 = (bf16[384,128]{1,0:T(8,128)(2,1)S(1)}, bf16[384,128]{1,0:T(8,128)(2,1)S(1)}, u32[]{:S(2)}, u32[]{:S(2)}) collective-permute-start(bf16[384,128]{1,0:T(8,128)(2,1)S(1)} %get-tuple-element.44), channel_id=1, source_target_pairs={{0,4},{4,0},{8,12},{12,8},{16,20},{20,16},{24,28},{28,24},{1,9},{9... | collective-permute-start | bytes 294920 | tf_op jit(solution)/shard_map/ppermute | solution.py:526
  12.1 0.0 collective-permute-done.1.refs_2_
  12.1 4.4 %collective-permute-start.6 = (bf16[384,128]{1,0:T(8,128)(2,1)S(1)}, bf16[384,128]{1,0:T(8,128)(2,1)S(1)}, u32[]{:S(2)}, u32[]{:S(2)}) collective-permute-start(bf16[384,128]{1,0:T(8,128)(2,1)S(1)} %get-tuple-element.45), channel_id=1, source_target_pairs={{0,8},{8,0},{4,12},{12,4},{16,24},{24,16},{20,28},{28,20},{1,5},{5... | collective-permute-start | bytes 294920 | tf_op jit(solution)/shard_map/ppermute | solution.py:526
  16.5 0.0 collective-permute-done.refs_1_
  16.5 0.0 collective-permute-start.2
  16.5 1.3 %collective-permute-done.2.refs_3_ = bf16[64,512]{1,0:T(8,128)(2,1)S(1)} collective-permute-done((bf16[64,512]{1,0:T(8,128)(2,1)S(1)}, bf16[64,512]{1,0:T(8,128)(2,1)S(1)}, u32[]{:S(2)}, u32[]{:S(2)}) %collective-permute-start.2) | collective-permute-done | bytes 65568 | tf_op jit(solution)/shard_map/ppermute | solution.py:516
  17.8 0.7 %weights.1 = (bf16[3072,256]{1,0:T(8,128)(2,1)S(1)}, bf16[3072,256]{1,0:T(8,128)(2,1)S(1)}, f32[8,128]{1,0:T(8,128)S(1)}) custom-call(bf16[64,512]{1,0:T(8,128)(2,1)S(1)} %get-tuple-element.36.refs_0_, bf16[64,512]{1,0:T(8,128)(2,1)S(1)} %collective-permute-done.refs_1_, bf16[64,512]{1,0:T(8,128)(2,1)S(1)} %collective-permute-done.1.refs_2_, ...), custom_call_target="tpu_custom_call" | custom-call | tf_op jit(solution)/shard_map/weights/pallas_call | solution.py:618
  18.5 0.0 collective-permute-done.3.r1
  18.5 0.0 collective-permute-done.4.r2
  18.5 0.0 collective-permute-done.5.r3
  18.5 0.6 %collective-permute-done.6.r4 = bf16[384,128]{1,0:T(8,128)(2,1)S(1)} collective-permute-done((bf16[384,128]{1,0:T(8,128)(2,1)S(1)}, bf16[384,128]{1,0:T(8,128)(2,1)S(1)}, u32[]{:S(2)}, u32[]{:S(2)}) %collective-permute-start.6) | collective-permute-done | bytes 98336 | tf_op jit(solution)/shard_map/ppermute | solution.py:526
  19.1 6.0 %forward.1 = (bf16[4,4,2,8,512]{4,3,2,1,0:T(8,128)(2,1)}, bf16[4,4,2,8,512]{4,3,2,1,0:T(8,128)(2,1)S(1)}, bf16[2,64,512]{2,1,0:T(8,128)(2,1)S(1)}, bf16[2,64,512...) custom-call(bf16[4,4,2,8,512]{4,3,2,1,0:T(8,128)(2,1)S(1)} %get-tupl, ...), custom_call_target="tpu_custom_call" | custom-call | tf_op jit(solution)/shard_map/forward/pallas_call | solution.py:637
  25.1 0.1 collective-permute-start.8
  25.2 0.7 %collective-permute-start.7 = (bf16[384,128]{1,0:T(8,128)(2,1)S(1)}, bf16[384,128]{1,0:T(8,128)(2,1)S(1)}, u32[]{:S(2)}, u32[]{:S(2)}) collective-permute-start(bf16[384,128]{1,0:T(8,128)(2,1)S(1)} %get-tuple-element.49), channel_id=1, source_target_pairs={{4,8},{8,4},{12,16},{16,12},{20,24},{24,20},{9,17},{17,9},{13,21},... | collective-permute-start | bytes 294920 | tf_op jit(solution)/shard_map/ppermute | solution.py:526
  25.9 0.7 %collective-permute-done.8.refs_1_ = bf16[2,64,512]{2,1,0:T(8,128)(2,1)S(1)} collective-permute-done((bf16[2,64,512]{2,1,0:T(8,128)(2,1)S(1)}, bf16[2,64,512]{2,1,0:T(8,128)(2,1)S(1)}, u32[]{:S(2)}, u32[]{:S(2)}) %collective-permute-start.8) | collective-permute-done | bytes 131104 | tf_op jit(solution)/shard_map/ppermute | solution.py:516
  26.6 0.6 %collective-permute-start.10 = (bf16[1,64,512]{2,1,0:T(8,128)(2,1)S(1)}, bf16[1,64,512]{2,1,0:T(8,128)(2,1)S(1)}, u32[]{:S(2)}, u32[]{:S(2)}) collective-permute-start(bf16[1,64,512]{2,1,0:T(8,128)(2,1)S(1)} %get-tuple-element.55), channel_id=1, source_target_pairs={{0,2},{1,3},{2,0},{3,1},{4,6},{5,7},{6,4},{7,5},{8,10},{9,11},{10,... | collective-permute-start | bytes 196616 | tf_op jit(solution)/shard_map/ppermute | solution.py:516
  27.2 0.0 collective-permute-done.7.refs_2_.r1
  27.2 3.7 %collective-permute-done.10.refs_1_ = bf16[1,64,512]{2,1,0:T(8,128)(2,1)S(1)} collective-permute-done((bf16[1,64,512]{2,1,0:T(8,128)(2,1)S(1)}, bf16[1,64,512]{2,1,0:T(8,128)(2,1)S(1)}, u32[]{:S(2)}, u32[]{:S(2)}) %collective-permute-start.10) | collective-permute-done | bytes 65568 | tf_op jit(solution)/shard_map/ppermute | solution.py:516
  30.9 4.1 %collective-permute-start.11 = (bf16[384,128]{1,0:T(8,128)(2,1)S(1)}, bf16[384,128]{1,0:T(8,128)(2,1)S(1)}, u32[]{:S(2)}, u32[]{:S(2)}) collective-permute-start(bf16[384,128]{1,0:T(8,128)(2,1)S(1)} %get-tuple-element.58), channel_id=1, source_target_pairs={{0,4},{4,0},{8,12},{12,8},{16,20},{20,16},{24,28},{28,24},{1,9},{9... | collective-permute-start | bytes 294920 | tf_op jit(solution)/shard_map/ppermute | solution.py:526
  35.1 0.1 collective-permute-start.13
  35.1 0.7 %collective-permute-start.9 = (bf16[384,128]{1,0:T(8,128)(2,1)S(1)}, bf16[384,128]{1,0:T(8,128)(2,1)S(1)}, u32[]{:S(2)}, u32[]{:S(2)}) collective-permute-start(bf16[384,128]{1,0:T(8,128)(2,1)S(1)} %get-tuple-element.53), channel_id=1, source_target_pairs={{8,16},{16,8},{12,20},{20,12},{5,9},{9,5},{13,17},{17,13},{21,25},... | collective-permute-start | bytes 294920 | tf_op jit(solution)/shard_map/ppermute | solution.py:526
  35.8 4.2 %collective-permute-start.12 = (bf16[384,128]{1,0:T(8,128)(2,1)S(1)}, bf16[384,128]{1,0:T(8,128)(2,1)S(1)}, u32[]{:S(2)}, u32[]{:S(2)}) collective-permute-start(bf16[384,128]{1,0:T(8,128)(2,1)S(1)} %get-tuple-element.59), channel_id=1, source_target_pairs={{0,8},{8,0},{4,12},{12,4},{16,24},{24,16},{20,28},{28,20},{1,5},{5... | collective-permute-start | bytes 294920 | tf_op jit(solution)/shard_map/ppermute | solution.py:526
  40.0 0.0 collective-permute-done.13.refs_1_
  40.0 0.0 collective-permute-done.11.refs_2_.r3
  40.0 0.2 collective-permute-start.14
  40.2 0.0 collective-permute-done.9.r2
  40.2 2.7 %collective-permute-done.12.r4 = bf16[384,128]{1,0:T(8,128)(2,1)S(1)} collective-permute-done((bf16[384,128]{1,0:T(8,128)(2,1)S(1)}, bf16[384,128]{1,0:T(8,128)(2,1)S(1)}, u32[]{:S(2)}, u32[]{:S(2)}) %collective-permute-start.12) | collective-permute-done | bytes 98336 | tf_op jit(solution)/shard_map/ppermute | solution.py:526
  42.9 1.1 %assemble.1.refs_2_.windows = bf16[3,4,2,5,2,16,256]{6,5,4,3,2,1,0:T(8,128)(2,1)S(1)} custom-call(bf16[4,4,2,8,512]{4,3,2,1,0:T(8,128)(2,1)S(1)} %get-tuple-element.47.grad, s32[4,26]{1,0:T(4,128)S(1)} %get-tuple-element.39.rows, bf16[384,128]{1,0:T(8,128)(2,1)S(1)} %get-tuple-element.48.r0, bf16[384,128]{1,0:T(8,128)(2,1)S(1)} %collective-permute-done.7.refs_2_.r1, ...), custom_call_target="tpu_custom_call" | custom-call | tf_op jit(solution)/shard_map/assemble/pallas_call | solution.py:687
  44.0 0.4 collective-permute-done.14.refs_1_
  44.4 1.7 %collective-permute-start.15 = (bf16[1,64,512]{2,1,0:T(8,128)(2,1)S(1)}, bf16[1,64,512]{2,1,0:T(8,128)(2,1)S(1)}, u32[]{:S(2)}, u32[]{:S(2)}) collective-permute-start(bf16[1,64,512]{2,1,0:T(8,128)(2,1)S(1)} %sum.7.after), channel_id=1, source_target_pairs={{0,16},{4,20},{8,24},{12,28},{16,0},{20,4},{24,8},{28,12},{1,5},{5... | collective-permute-start | bytes 196616 | tf_op jit(solution)/shard_map/ppermute | solution.py:526
  46.1 1.7 %backward.1 = bf16[4,4,2,8,512]{4,3,2,1,0:T(8,128)(2,1)} custom-call(bf16[3,4,2,5,2,16,256]{6,5,4,3,2,1,0:T(8,128)(2,1)S(1)} %assemble.1.refs_2_.windows, bf16[4,4,2,8,512]{4,3,2,1,0:T(8,128)(2,1)S(1)} %get-tuple-element.35.mask, bf16[3072,256]{1,0:T(8,128)(2,1)S(1)} %get-tuple-element.61.toeplitz, bf16[1,64,512]{2,1,0:T(8,128)(2,1)S(1)} %sum.7.after), custom_call_target="tpu_custom_call" | custom-call | tf_op jit(solution)/shard_map/backward/pallas_call | solution.py:701
  47.8 1.9 %collective-permute-done.15 = bf16[1,64,512]{2,1,0:T(8,128)(2,1)S(1)} collective-permute-done((bf16[1,64,512]{2,1,0:T(8,128)(2,1)S(1)}, bf16[1,64,512]{2,1,0:T(8,128)(2,1)S(1)}, u32[]{:S(2)}, u32[]{:S(2)}) %collective-permute-start.15) | collective-permute-done | bytes 65568 | tf_op jit(solution)/shard_map/ppermute | solution.py:526
  49.7 0.7 %finish.1 = (f32[64,432]{1,0:T(8,128)}, f32[1,16]{1,0:T(1,128)}) custom-call(bf16[64,512]{1,0:T(8,128)(2,1)S(1)} %bitcast.13, bf16[64,512]{1,0:T(8,128)(2,1)S(1)} %bitcast.14), custom_call_target="tpu_custom_call" | custom-call | tf_op jit(solution)/shard_map/finish/pallas_call | solution.py:710
  (4 shorter events, 0.1 us)
Async XLA Ops:
  3.4 8.7 %collective-permute-start.1 = (bf16[64,512]{1,0:T(8,128)(2,1)S(1)}, bf16[64,512]{1,0:T(8,128)(2,1)S(1)}, u32[]{:S(2)}, u32[]{:S(2)}) collective-permute-start(bf16[64,512]{1,0:T(8,128)(2,1)S(1)} %get-tuple-element.36.refs_0_), channel_id=1, source_target_pairs={{0,2},{1,3},{2,0},{3,1},{4,6},{5,7},{6,4},{7,5},{8,10},{9,11},{10,... | collective-permute-start | bytes 196616 | tf_op jit(solution)/shard_map/ppermute | solution.py:516
  6.4 10.1 %collective-permute-start = (bf16[64,512]{1,0:T(8,128)(2,1)S(1)}, bf16[64,512]{1,0:T(8,128)(2,1)S(1)}, u32[]{:S(2)}, u32[]{:S(2)}) collective-permute-start(bf16[64,512]{1,0:T(8,128)(2,1)S(1)} %get-tuple-element.36.refs_0_), channel_id=1, source_target_pairs={{0,1},{1,0},{2,3},{3,2},{4,5},{5,4},{6,7},{7,6},{8,9},{9,8},{10,11... | collective-permute-start | bytes 196616 | tf_op jit(solution)/shard_map/ppermute | solution.py:516
  6.4 12.1 %collective-permute-start.3 = (bf16[384,128]{1,0:T(8,128)(2,1)S(1)}, bf16[384,128]{1,0:T(8,128)(2,1)S(1)}, u32[]{:S(2)}, u32[]{:S(2)}) collective-permute-start(bf16[384,128]{1,0:T(8,128)(2,1)S(1)} %get-tuple-element.42), channel_id=1, source_target_pairs={{4,8},{8,4},{12,16},{16,12},{20,24},{24,20},{9,17},{17,9},{13,21},... | collective-permute-start | bytes 294920 | tf_op jit(solution)/shard_map/ppermute | solution.py:526
  7.1 11.4 %collective-permute-start.4 = (bf16[384,128]{1,0:T(8,128)(2,1)S(1)}, bf16[384,128]{1,0:T(8,128)(2,1)S(1)}, u32[]{:S(2)}, u32[]{:S(2)}) collective-permute-start(bf16[384,128]{1,0:T(8,128)(2,1)S(1)} %get-tuple-element.43), channel_id=1, source_target_pairs={{8,16},{16,8},{12,20},{20,12},{5,9},{9,5},{13,17},{17,13},{21,25},... | collective-permute-start | bytes 294920 | tf_op jit(solution)/shard_map/ppermute | solution.py:526
  7.8 10.8 %collective-permute-start.5 = (bf16[384,128]{1,0:T(8,128)(2,1)S(1)}, bf16[384,128]{1,0:T(8,128)(2,1)S(1)}, u32[]{:S(2)}, u32[]{:S(2)}) collective-permute-start(bf16[384,128]{1,0:T(8,128)(2,1)S(1)} %get-tuple-element.44), channel_id=1, source_target_pairs={{0,4},{4,0},{8,12},{12,8},{16,20},{20,16},{24,28},{28,24},{1,9},{9... | collective-permute-start | bytes 294920 | tf_op jit(solution)/shard_map/ppermute | solution.py:526
  12.1 7.0 %collective-permute-start.6 = (bf16[384,128]{1,0:T(8,128)(2,1)S(1)}, bf16[384,128]{1,0:T(8,128)(2,1)S(1)}, u32[]{:S(2)}, u32[]{:S(2)}) collective-permute-start(bf16[384,128]{1,0:T(8,128)(2,1)S(1)} %get-tuple-element.45), channel_id=1, source_target_pairs={{0,8},{8,0},{4,12},{12,4},{16,24},{24,16},{20,28},{28,20},{1,5},{5... | collective-permute-start | bytes 294920 | tf_op jit(solution)/shard_map/ppermute | solution.py:526
  16.5 1.3 %collective-permute-start.2 = (bf16[64,512]{1,0:T(8,128)(2,1)S(1)}, bf16[64,512]{1,0:T(8,128)(2,1)S(1)}, u32[]{:S(2)}, u32[]{:S(2)}) collective-permute-start(bf16[64,512]{1,0:T(8,128)(2,1)S(1)} %collective-permute-done.1.refs_2_), channel_id=1, source_target_pairs={{0,1},{1,0},{2,3},{3,2},{4,5},{5,4},{6,7},{7,6},{8,9},{9,8},{10,11... | collective-permute-start | bytes 196616 | tf_op jit(solution)/shard_map/ppermute | solution.py:516
  25.1 1.4 %collective-permute-start.8 = (bf16[2,64,512]{2,1,0:T(8,128)(2,1)S(1)}, bf16[2,64,512]{2,1,0:T(8,128)(2,1)S(1)}, u32[]{:S(2)}, u32[]{:S(2)}) collective-permute-start(bf16[2,64,512]{2,1,0:T(8,128)(2,1)S(1)} %get-tuple-element.51), channel_id=1, source_target_pairs={{0,1},{1,0},{2,3},{3,2},{4,5},{5,4},{6,7},{7,6},{8,9},{9,8},{10,11... | collective-permute-start | bytes 393224 | tf_op jit(solution)/shard_map/ppermute | solution.py:516
  25.2 2.0 %collective-permute-start.7 = (bf16[384,128]{1,0:T(8,128)(2,1)S(1)}, bf16[384,128]{1,0:T(8,128)(2,1)S(1)}, u32[]{:S(2)}, u32[]{:S(2)}) collective-permute-start(bf16[384,128]{1,0:T(8,128)(2,1)S(1)} %get-tuple-element.49), channel_id=1, source_target_pairs={{4,8},{8,4},{12,16},{16,12},{20,24},{24,20},{9,17},{17,9},{13,21},... | collective-permute-start | bytes 294920 | tf_op jit(solution)/shard_map/ppermute | solution.py:526
  26.6 4.3 %collective-permute-start.10 = (bf16[1,64,512]{2,1,0:T(8,128)(2,1)S(1)}, bf16[1,64,512]{2,1,0:T(8,128)(2,1)S(1)}, u32[]{:S(2)}, u32[]{:S(2)}) collective-permute-start(bf16[1,64,512]{2,1,0:T(8,128)(2,1)S(1)} %get-tuple-element.55), channel_id=1, source_target_pairs={{0,2},{1,3},{2,0},{3,1},{4,6},{5,7},{6,4},{7,5},{8,10},{9,11},{10,... | collective-permute-start | bytes 196616 | tf_op jit(solution)/shard_map/ppermute | solution.py:516
  30.9 9.1 %collective-permute-start.11 = (bf16[384,128]{1,0:T(8,128)(2,1)S(1)}, bf16[384,128]{1,0:T(8,128)(2,1)S(1)}, u32[]{:S(2)}, u32[]{:S(2)}) collective-permute-start(bf16[384,128]{1,0:T(8,128)(2,1)S(1)} %get-tuple-element.58), channel_id=1, source_target_pairs={{0,4},{4,0},{8,12},{12,8},{16,20},{20,16},{24,28},{28,24},{1,9},{9... | collective-permute-start | bytes 294920 | tf_op jit(solution)/shard_map/ppermute | solution.py:526
  35.1 4.9 %collective-permute-start.13 = (bf16[1,64,512]{2,1,0:T(8,128)(2,1)S(1)}, bf16[1,64,512]{2,1,0:T(8,128)(2,1)S(1)}, u32[]{:S(2)}, u32[]{:S(2)}) collective-permute-start(bf16[1,64,512]{2,1,0:T(8,128)(2,1)S(1)} %get-tuple-element.60.refs_0_), channel_id=1, source_target_pairs={{0,4},{4,0},{8,12},{12,8},{16,20},{20,16},{24,28},{28,24},{1,9},{5... | collective-permute-start | bytes 196616 | tf_op jit(solution)/shard_map/ppermute | solution.py:526
  35.1 5.1 %collective-permute-start.9 = (bf16[384,128]{1,0:T(8,128)(2,1)S(1)}, bf16[384,128]{1,0:T(8,128)(2,1)S(1)}, u32[]{:S(2)}, u32[]{:S(2)}) collective-permute-start(bf16[384,128]{1,0:T(8,128)(2,1)S(1)} %get-tuple-element.53), channel_id=1, source_target_pairs={{8,16},{16,8},{12,20},{20,12},{5,9},{9,5},{13,17},{17,13},{21,25},... | collective-permute-start | bytes 294920 | tf_op jit(solution)/shard_map/ppermute | solution.py:526
  35.8 7.1 %collective-permute-start.12 = (bf16[384,128]{1,0:T(8,128)(2,1)S(1)}, bf16[384,128]{1,0:T(8,128)(2,1)S(1)}, u32[]{:S(2)}, u32[]{:S(2)}) collective-permute-start(bf16[384,128]{1,0:T(8,128)(2,1)S(1)} %get-tuple-element.59), channel_id=1, source_target_pairs={{0,8},{8,0},{4,12},{12,4},{16,24},{24,16},{20,28},{28,20},{1,5},{5... | collective-permute-start | bytes 294920 | tf_op jit(solution)/shard_map/ppermute | solution.py:526
  40.0 4.4 %collective-permute-start.14 = (bf16[1,64,512]{2,1,0:T(8,128)(2,1)S(1)}, bf16[1,64,512]{2,1,0:T(8,128)(2,1)S(1)}, u32[]{:S(2)}, u32[]{:S(2)}) collective-permute-start(bf16[1,64,512]{2,1,0:T(8,128)(2,1)S(1)} %sum.6.after.refs_0_), channel_id=1, source_target_pairs={{0,8},{4,12},{8,0},{12,4},{16,24},{20,28},{24,16},{28,20},{1,17},{... | collective-permute-start | bytes 196616 | tf_op jit(solution)/shard_map/ppermute | solution.py:526
  44.4 5.2 %collective-permute-start.15 = (bf16[1,64,512]{2,1,0:T(8,128)(2,1)S(1)}, bf16[1,64,512]{2,1,0:T(8,128)(2,1)S(1)}, u32[]{:S(2)}, u32[]{:S(2)}) collective-permute-start(bf16[1,64,512]{2,1,0:T(8,128)(2,1)S(1)} %sum.7.after), channel_id=1, source_target_pairs={{0,16},{4,20},{8,24},{12,28},{16,0},{20,4},{24,8},{28,12},{1,5},{5... | collective-permute-start | bytes 196616 | tf_op jit(solution)/shard_map/ppermute | solution.py:526

commit v11 on v10

--- a/solution.py
+++ b/solution.py
@@ -666,22 +666,26 @@
         *received,
     )
 
-    later = grad_units[2:]
+    early, late = 3, (1, 2, 4)
+    grad_received = {0: grad_units[0]}
+    unit = [grad_units[early]]
     bit = 1
     while 2 * bit < groups:
-        first = later[:1] if bit == 1 else []
-        (keep, give), first = sum_after(keep, swapped(give, "dp", bit), through=first, parts=2)
-        later = first + later[1:] if bit == 1 else later
+        (keep, give), unit = sum_after(keep, swapped(give, "dp", bit), through=unit, parts=2)
         bit *= 2
-    grad_received = [grad_units[0], exchanged(1, grad_units[1])]
-    (total,), last = sum_after(keep, swapped(give, "dp", bit), grad_received[1:], later[1:])
-    for number, unit in enumerate([later[0], *last], 2):
-        grad_received.append(exchanged(number, unit))
+    far = swapped(give, "dp", bit)
+    grad_received[early] = exchanged(early, unit[0])
+    (total,), units_left = sum_after(
+        keep, far, [grad_received[early]], [grad_units[n] for n in late]
+    )
 
     steps = space_steps()
     other = stepped(total, steps[0])
+    for number, unit in zip(late, units_left):
+        grad_received[number] = exchanged(number, unit)
+    grad_received = [grad_received[number] for number in range(spread)]
     if len(steps) > 1:
-        (total,), _ = sum_after(total, other, grad_received[3:4])
+        (total,), _ = sum_after(total, other, [grad_received[late[0]]])
         other = stepped(total, steps[1])
 
     padded_grad = pl.pallas_call(

time: 50.6 us -> 52.1 us (1.030)
  starting transfers between devices: 25.3 us -> 27.8 us
  waiting for transfers between devices: 11.3 us -> 10.3 us
    ppermute x11, starting transfers between devices: 21.6 us -> 24.1 us  [by_parity(): return lax.ppermute(block, ('space', 'dp'), pairs)]
    ppermute x11, waiting for transfers between devices: 5.63 us -> 3.68 us  [by_parity(): return lax.ppermute(block, ('space', 'dp'), pairs)]
    ppermute x5, waiting for transfers between devices: 5.64 us -> 6.65 us  [swapped(): lax.ppermute(block, axis, [(i, i ^ bit) for i in range(lax.axis_size(axis...]
where the time goes in v11:
time: 52.1 us; the launch traced here: 51.9 us
  starting transfers between devices  27.8 us (53%)
  Pallas kernels  12.4 us (24%)
  waiting for transfers between devices  10.3 us (20%)
  between operations  1.4 us (3%)
    ppermute x11, starting transfers between devices, by_parity(): return lax.ppermute(block, ('space', 'dp'), pairs)  24.1 us
    ppermute x5, waiting for transfers between devices, swapped(): lax.ppermute(block, axis, [(i, i ^ bit) for i in range(lax.axis_size(axis...  6.65 us
    pallas_call x1, Pallas kernels, body(): pl.pallas_call(functools.partial(forward_kernel, shard=shard), name='forw...  5.99 us
    ppermute x11, waiting for transfers between devices, by_parity(): return lax.ppermute(block, ('space', 'dp'), pairs)  3.68 us
    ppermute x5, starting transfers between devices, swapped(): lax.ppermute(block, axis, [(i, i ^ bit) for i in range(lax.axis_size(axis...  3.62 us
    pallas_call x1, Pallas kernels, body(): pl.pallas_call(prepare_kernel, name='prepare', out_shape=[grid_type, grid...  2.15 us
    pallas_call x1, Pallas kernels, body(): pl.pallas_call(backward_kernel, name='backward', out_shape=grid_type, in_...  1.68 us
    pallas_call x1, Pallas kernels, body(): pl.pallas_call(assemble_kernel, name='assemble', out_shape=jax.ShapeDtype...  1.07 us
  transfers between devices with their start and end apart: 16, of which 7 were waited for; matrix products, arithmetic and copies ran while one was open for 0% of the time, Pallas kernels for 7%

profile of v11, /device:TPU:0, one launch (start us, length us, event | category | flops | bytes accessed | tf_op | source)
XLA Modules:
  0.0 51.9 jit_solution(16318007297246768918)
XLA Ops:
  1.3 2.1 %prepare.1 = (bf16[4,4,2,8,512]{4,3,2,1,0:T(8,128)(2,1)S(1)}, bf16[4,4,2,8,512]{4,3,2,1,0:T(8,128)(2,1)S(1)}, s32[4,26]{1,0:T(4,128)S(1)}, s32[5,1,12]{2,1,0:T(1...) custom-call(bf16[4,4,2,8,512]{4,3,2,1,0:T(8,128)(2,1)} %bitcast.17, ...), custom_call_target="tpu_custom_call" | custom-call | tf_op jit(solution)/shard_map/prepare/pallas_call | solution.py:570
  3.4 3.0 %collective-permute-start.1 = (bf16[64,512]{1,0:T(8,128)(2,1)S(1)}, bf16[64,512]{1,0:T(8,128)(2,1)S(1)}, u32[]{:S(2)}, u32[]{:S(2)}) collective-permute-start(bf16[64,512]{1,0:T(8,128)(2,1)S(1)} %get-tuple-element.37.refs_0_), channel_id=1, source_target_pairs={{0,2},{1,3},{2,0},{3,1},{4,6},{5,7},{6,4},{7,5},{8,10},{9,11},{10,... | collective-permute-start | bytes 196616 | tf_op jit(solution)/shard_map/ppermute | solution.py:516
  6.4 0.0 collective-permute-start
  6.4 0.7 %collective-permute-start.3 = (bf16[384,128]{1,0:T(8,128)(2,1)S(1)}, bf16[384,128]{1,0:T(8,128)(2,1)S(1)}, u32[]{:S(2)}, u32[]{:S(2)}) collective-permute-start(bf16[384,128]{1,0:T(8,128)(2,1)S(1)} %get-tuple-element.43), channel_id=1, source_target_pairs={{4,8},{8,4},{12,16},{16,12},{20,24},{24,20},{9,17},{17,9},{13,21},... | collective-permute-start | bytes 294920 | tf_op jit(solution)/shard_map/ppermute | solution.py:526
  7.1 0.7 %collective-permute-start.4 = (bf16[384,128]{1,0:T(8,128)(2,1)S(1)}, bf16[384,128]{1,0:T(8,128)(2,1)S(1)}, u32[]{:S(2)}, u32[]{:S(2)}) collective-permute-start(bf16[384,128]{1,0:T(8,128)(2,1)S(1)} %get-tuple-element.44), channel_id=1, source_target_pairs={{8,16},{16,8},{12,20},{20,12},{5,9},{9,5},{13,17},{17,13},{21,25},... | collective-permute-start | bytes 294920 | tf_op jit(solution)/shard_map/ppermute | solution.py:526
  7.8 4.3 %collective-permute-start.5 = (bf16[384,128]{1,0:T(8,128)(2,1)S(1)}, bf16[384,128]{1,0:T(8,128)(2,1)S(1)}, u32[]{:S(2)}, u32[]{:S(2)}) collective-permute-start(bf16[384,128]{1,0:T(8,128)(2,1)S(1)} %get-tuple-element.45), channel_id=1, source_target_pairs={{0,4},{4,0},{8,12},{12,8},{16,20},{20,16},{24,28},{28,24},{1,9},{9... | collective-permute-start | bytes 294920 | tf_op jit(solution)/shard_map/ppermute | solution.py:526
  12.1 0.0 collective-permute-done.1.refs_2_
  12.1 4.4 %collective-permute-start.6 = (bf16[384,128]{1,0:T(8,128)(2,1)S(1)}, bf16[384,128]{1,0:T(8,128)(2,1)S(1)}, u32[]{:S(2)}, u32[]{:S(2)}) collective-permute-start(bf16[384,128]{1,0:T(8,128)(2,1)S(1)} %get-tuple-element.46), channel_id=1, source_target_pairs={{0,8},{8,0},{4,12},{12,4},{16,24},{24,16},{20,28},{28,20},{1,5},{5... | collective-permute-start | bytes 294920 | tf_op jit(solution)/shard_map/ppermute | solution.py:526
  16.5 0.0 collective-permute-done.refs_1_
  16.5 0.0 collective-permute-start.2
  16.5 1.3 %collective-permute-done.2.refs_3_ = bf16[64,512]{1,0:T(8,128)(2,1)S(1)} collective-permute-done((bf16[64,512]{1,0:T(8,128)(2,1)S(1)}, bf16[64,512]{1,0:T(8,128)(2,1)S(1)}, u32[]{:S(2)}, u32[]{:S(2)}) %collective-permute-start.2) | collective-permute-done | bytes 65568 | tf_op jit(solution)/shard_map/ppermute | solution.py:516
  17.8 0.7 %weights.1 = (bf16[3072,256]{1,0:T(8,128)(2,1)S(1)}, bf16[3072,256]{1,0:T(8,128)(2,1)S(1)}, f32[8,128]{1,0:T(8,128)S(1)}) custom-call(bf16[64,512]{1,0:T(8,128)(2,1)S(1)} %get-tuple-element.37.refs_0_, bf16[64,512]{1,0:T(8,128)(2,1)S(1)} %collective-permute-done.refs_1_, bf16[64,512]{1,0:T(8,128)(2,1)S(1)} %collective-permute-done.1.refs_2_, ...), custom_call_target="tpu_custom_call" | custom-call | tf_op jit(solution)/shard_map/weights/pallas_call | solution.py:618
  18.5 0.0 collective-permute-done.3.r1
  18.5 0.0 collective-permute-done.4.r2
  18.5 0.0 collective-permute-done.5.r3
  18.5 0.6 %collective-permute-done.6.r4 = bf16[384,128]{1,0:T(8,128)(2,1)S(1)} collective-permute-done((bf16[384,128]{1,0:T(8,128)(2,1)S(1)}, bf16[384,128]{1,0:T(8,128)(2,1)S(1)}, u32[]{:S(2)}, u32[]{:S(2)}) %collective-permute-start.6) | collective-permute-done | bytes 98336 | tf_op jit(solution)/shard_map/ppermute | solution.py:526
  19.1 6.0 %forward.1 = (bf16[4,4,2,8,512]{4,3,2,1,0:T(8,128)(2,1)}, bf16[4,4,2,8,512]{4,3,2,1,0:T(8,128)(2,1)S(1)}, bf16[2,64,512]{2,1,0:T(8,128)(2,1)S(1)}, bf16[2,64,512...) custom-call(bf16[4,4,2,8,512]{4,3,2,1,0:T(8,128)(2,1)S(1)} %get-tupl, ...), custom_call_target="tpu_custom_call" | custom-call | tf_op jit(solution)/shard_map/forward/pallas_call | solution.py:637
  25.1 0.1 collective-permute-start.7
  25.2 1.3 %collective-permute-done.7.refs_1_ = bf16[2,64,512]{2,1,0:T(8,128)(2,1)S(1)} collective-permute-done((bf16[2,64,512]{2,1,0:T(8,128)(2,1)S(1)}, bf16[2,64,512]{2,1,0:T(8,128)(2,1)S(1)}, u32[]{:S(2)}, u32[]{:S(2)}) %collective-permute-start.7) | collective-permute-done | bytes 131104 | tf_op jit(solution)/shard_map/ppermute | solution.py:516
  26.6 0.5 %collective-permute-start.9 = (bf16[384,128]{1,0:T(8,128)(2,1)S(1)}, bf16[384,128]{1,0:T(8,128)(2,1)S(1)}, u32[]{:S(2)}, u32[]{:S(2)}) collective-permute-start(bf16[384,128]{1,0:T(8,128)(2,1)S(1)} %get-tuple-element.55), channel_id=1, source_target_pairs={{0,4},{4,0},{8,12},{12,8},{16,20},{20,16},{24,28},{28,24},{1,9},{9... | collective-permute-start | bytes 294920 | tf_op jit(solution)/shard_map/ppermute | solution.py:526
  27.1 0.5 %collective-permute-start.8 = (bf16[1,64,512]{2,1,0:T(8,128)(2,1)S(1)}, bf16[1,64,512]{2,1,0:T(8,128)(2,1)S(1)}, u32[]{:S(2)}, u32[]{:S(2)}) collective-permute-start(bf16[1,64,512]{2,1,0:T(8,128)(2,1)S(1)} %get-tuple-element.54), channel_id=1, source_target_pairs={{0,2},{1,3},{2,0},{3,1},{4,6},{5,7},{6,4},{7,5},{8,10},{9,11},{10,... | collective-permute-start | bytes 196616 | tf_op jit(solution)/shard_map/ppermute | solution.py:516
  27.6 4.1 %collective-permute-done.8.refs_1_ = bf16[1,64,512]{2,1,0:T(8,128)(2,1)S(1)} collective-permute-done((bf16[1,64,512]{2,1,0:T(8,128)(2,1)S(1)}, bf16[1,64,512]{2,1,0:T(8,128)(2,1)S(1)}, u32[]{:S(2)}, u32[]{:S(2)}) %collective-permute-start.8) | collective-permute-done | bytes 65568 | tf_op jit(solution)/shard_map/ppermute | solution.py:516
  31.7 0.0 collective-permute-done.9.refs_2_.r3
  31.7 0.7 %collective-permute-start.10 = (bf16[384,128]{1,0:T(8,128)(2,1)S(1)}, bf16[384,128]{1,0:T(8,128)(2,1)S(1)}, u32[]{:S(2)}, u32[]{:S(2)}) collective-permute-start(bf16[384,128]{1,0:T(8,128)(2,1)S(1)} %get-tuple-element.59), channel_id=1, source_target_pairs={{4,8},{8,4},{12,16},{16,12},{20,24},{24,20},{9,17},{17,9},{13,21},... | collective-permute-start | bytes 294920 | tf_op jit(solution)/shard_map/ppermute | solution.py:526
  32.4 4.9 %collective-permute-start.13 = (bf16[1,64,512]{2,1,0:T(8,128)(2,1)S(1)}, bf16[1,64,512]{2,1,0:T(8,128)(2,1)S(1)}, u32[]{:S(2)}, u32[]{:S(2)}) collective-permute-start(bf16[1,64,512]{2,1,0:T(8,128)(2,1)S(1)} %get-tuple-element.62.refs_0_), channel_id=1, source_target_pairs={{0,4},{4,0},{8,12},{12,8},{16,20},{20,16},{24,28},{28,24},{1,9},{5... | collective-permute-start | bytes 196616 | tf_op jit(solution)/shard_map/ppermute | solution.py:526
  37.3 0.7 %collective-permute-start.11 = (bf16[384,128]{1,0:T(8,128)(2,1)S(1)}, bf16[384,128]{1,0:T(8,128)(2,1)S(1)}, u32[]{:S(2)}, u32[]{:S(2)}) collective-permute-start(bf16[384,128]{1,0:T(8,128)(2,1)S(1)} %get-tuple-element.60), channel_id=1, source_target_pairs={{8,16},{16,8},{12,20},{20,12},{5,9},{9,5},{13,17},{17,13},{21,25},... | collective-permute-start | bytes 294920 | tf_op jit(solution)/shard_map/ppermute | solution.py:526
  38.0 2.4 %collective-permute-start.12 = (bf16[384,128]{1,0:T(8,128)(2,1)S(1)}, bf16[384,128]{1,0:T(8,128)(2,1)S(1)}, u32[]{:S(2)}, u32[]{:S(2)}) collective-permute-start(bf16[384,128]{1,0:T(8,128)(2,1)S(1)} %get-tuple-element.61), channel_id=1, source_target_pairs={{0,8},{8,0},{4,12},{12,4},{16,24},{24,16},{20,28},{28,20},{1,5},{5... | collective-permute-start | bytes 294920 | tf_op jit(solution)/shard_map/ppermute | solution.py:526
  40.4 0.5 collective-permute-done.13.refs_1_
  40.9 0.0 collective-permute-done.10.refs_2_.r1
  40.9 2.8 %collective-permute-start.14 = (bf16[1,64,512]{2,1,0:T(8,128)(2,1)S(1)}, bf16[1,64,512]{2,1,0:T(8,128)(2,1)S(1)}, u32[]{:S(2)}, u32[]{:S(2)}) collective-permute-start(bf16[1,64,512]{2,1,0:T(8,128)(2,1)S(1)} %sum.6.after.refs_0_), channel_id=1, source_target_pairs={{0,8},{4,12},{8,0},{12,4},{16,24},{20,28},{24,16},{28,20},{1,17},{... | collective-permute-start | bytes 196616 | tf_op jit(solution)/shard_map/ppermute | solution.py:526
  43.7 0.0 collective-permute-done.11.r2
  43.7 0.0 collective-permute-done.12.r4
  43.7 1.1 %assemble.1.refs_2_.windows = bf16[3,4,2,5,2,16,256]{6,5,4,3,2,1,0:T(8,128)(2,1)S(1)} custom-call(bf16[4,4,2,8,512]{4,3,2,1,0:T(8,128)(2,1)S(1)} %get-tuple-element.48.grad, s32[4,26]{1,0:T(4,128)S(1)} %get-tuple-element.40.rows, bf16[384,128]{1,0:T(8,128)(2,1)S(1)} %get-tuple-element.49.r0, bf16[384,128]{1,0:T(8,128)(2,1)S(1)} %collective-permute-done.10.refs_2_.r1, ...), custom_call_target="tpu_custom_call" | custom-call | tf_op jit(solution)/shard_map/assemble/pallas_call | solution.py:691
  44.8 1.2 %collective-permute-done.14.refs_1_ = bf16[1,64,512]{2,1,0:T(8,128)(2,1)S(1)} collective-permute-done((bf16[1,64,512]{2,1,0:T(8,128)(2,1)S(1)}, bf16[1,64,512]{2,1,0:T(8,128)(2,1)S(1)}, u32[]{:S(2)}, u32[]{:S(2)}) %collective-permute-start.14) | collective-permute-done | bytes 65568 | tf_op jit(solution)/shard_map/ppermute | solution.py:526
  46.0 2.1 %collective-permute-start.15 = (bf16[1,64,512]{2,1,0:T(8,128)(2,1)S(1)}, bf16[1,64,512]{2,1,0:T(8,128)(2,1)S(1)}, u32[]{:S(2)}, u32[]{:S(2)}) collective-permute-start(bf16[1,64,512]{2,1,0:T(8,128)(2,1)S(1)} %sum.7.after), channel_id=1, source_target_pairs={{0,16},{4,20},{8,24},{12,28},{16,0},{20,4},{24,8},{28,12},{1,5},{5... | collective-permute-start | bytes 196616 | tf_op jit(solution)/shard_map/ppermute | solution.py:526
  48.0 1.7 %backward.1 = bf16[4,4,2,8,512]{4,3,2,1,0:T(8,128)(2,1)} custom-call(bf16[3,4,2,5,2,16,256]{6,5,4,3,2,1,0:T(8,128)(2,1)S(1)} %assemble.1.refs_2_.windows, bf16[4,4,2,8,512]{4,3,2,1,0:T(8,128)(2,1)S(1)} %get-tuple-element.36.mask, bf16[3072,256]{1,0:T(8,128)(2,1)S(1)} %get-tuple-element.63.toeplitz, bf16[1,64,512]{2,1,0:T(8,128)(2,1)S(1)} %sum.7.after), custom_call_target="tpu_custom_call" | custom-call | tf_op jit(solution)/shard_map/backward/pallas_call | solution.py:705
  49.7 1.5 %collective-permute-done.15 = bf16[1,64,512]{2,1,0:T(8,128)(2,1)S(1)} collective-permute-done((bf16[1,64,512]{2,1,0:T(8,128)(2,1)S(1)}, bf16[1,64,512]{2,1,0:T(8,128)(2,1)S(1)}, u32[]{:S(2)}, u32[]{:S(2)}) %collective-permute-start.15) | collective-permute-done | bytes 65568 | tf_op jit(solution)/shard_map/ppermute | solution.py:526
  51.2 0.7 %finish.1 = (f32[64,432]{1,0:T(8,128)}, f32[1,16]{1,0:T(1,128)}) custom-call(bf16[64,512]{1,0:T(8,128)(2,1)S(1)} %bitcast.13, bf16[64,512]{1,0:T(8,128)(2,1)S(1)} %bitcast.14), custom_call_target="tpu_custom_call" | custom-call | tf_op jit(solution)/shard_map/finish/pallas_call | solution.py:714
  (4 shorter events, 0.1 us)
Async XLA Ops:
  3.4 8.7 %collective-permute-start.1 = (bf16[64,512]{1,0:T(8,128)(2,1)S(1)}, bf16[64,512]{1,0:T(8,128)(2,1)S(1)}, u32[]{:S(2)}, u32[]{:S(2)}) collective-permute-start(bf16[64,512]{1,0:T(8,128)(2,1)S(1)} %get-tuple-element.37.refs_0_), channel_id=1, source_target_pairs={{0,2},{1,3},{2,0},{3,1},{4,6},{5,7},{6,4},{7,5},{8,10},{9,11},{10,... | collective-permute-start | bytes 196616 | tf_op jit(solution)/shard_map/ppermute | solution.py:516
  6.4 10.1 %collective-permute-start = (bf16[64,512]{1,0:T(8,128)(2,1)S(1)}, bf16[64,512]{1,0:T(8,128)(2,1)S(1)}, u32[]{:S(2)}, u32[]{:S(2)}) collective-permute-start(bf16[64,512]{1,0:T(8,128)(2,1)S(1)} %get-tuple-element.37.refs_0_), channel_id=1, source_target_pairs={{0,1},{1,0},{2,3},{3,2},{4,5},{5,4},{6,7},{7,6},{8,9},{9,8},{10,11... | collective-permute-start | bytes 196616 | tf_op jit(solution)/shard_map/ppermute | solution.py:516
  6.4 12.1 %collective-permute-start.3 = (bf16[384,128]{1,0:T(8,128)(2,1)S(1)}, bf16[384,128]{1,0:T(8,128)(2,1)S(1)}, u32[]{:S(2)}, u32[]{:S(2)}) collective-permute-start(bf16[384,128]{1,0:T(8,128)(2,1)S(1)} %get-tuple-element.43), channel_id=1, source_target_pairs={{4,8},{8,4},{12,16},{16,12},{20,24},{24,20},{9,17},{17,9},{13,21},... | collective-permute-start | bytes 294920 | tf_op jit(solution)/shard_map/ppermute | solution.py:526
  7.1 11.4 %collective-permute-start.4 = (bf16[384,128]{1,0:T(8,128)(2,1)S(1)}, bf16[384,128]{1,0:T(8,128)(2,1)S(1)}, u32[]{:S(2)}, u32[]{:S(2)}) collective-permute-start(bf16[384,128]{1,0:T(8,128)(2,1)S(1)} %get-tuple-element.44), channel_id=1, source_target_pairs={{8,16},{16,8},{12,20},{20,12},{5,9},{9,5},{13,17},{17,13},{21,25},... | collective-permute-start | bytes 294920 | tf_op jit(solution)/shard_map/ppermute | solution.py:526
  7.8 10.8 %collective-permute-start.5 = (bf16[384,128]{1,0:T(8,128)(2,1)S(1)}, bf16[384,128]{1,0:T(8,128)(2,1)S(1)}, u32[]{:S(2)}, u32[]{:S(2)}) collective-permute-start(bf16[384,128]{1,0:T(8,128)(2,1)S(1)} %get-tuple-element.45), channel_id=1, source_target_pairs={{0,4},{4,0},{8,12},{12,8},{16,20},{20,16},{24,28},{28,24},{1,9},{9... | collective-permute-start | bytes 294920 | tf_op jit(solution)/shard_map/ppermute | solution.py:526
  12.1 7.0 %collective-permute-start.6 = (bf16[384,128]{1,0:T(8,128)(2,1)S(1)}, bf16[384,128]{1,0:T(8,128)(2,1)S(1)}, u32[]{:S(2)}, u32[]{:S(2)}) collective-permute-start(bf16[384,128]{1,0:T(8,128)(2,1)S(1)} %get-tuple-element.46), channel_id=1, source_target_pairs={{0,8},{8,0},{4,12},{12,4},{16,24},{24,16},{20,28},{28,20},{1,5},{5... | collective-permute-start | bytes 294920 | tf_op jit(solution)/shard_map/ppermute | solution.py:526
  16.5 1.3 %collective-permute-start.2 = (bf16[64,512]{1,0:T(8,128)(2,1)S(1)}, bf16[64,512]{1,0:T(8,128)(2,1)S(1)}, u32[]{:S(2)}, u32[]{:S(2)}) collective-permute-start(bf16[64,512]{1,0:T(8,128)(2,1)S(1)} %collective-permute-done.1.refs_2_), channel_id=1, source_target_pairs={{0,1},{1,0},{2,3},{3,2},{4,5},{5,4},{6,7},{7,6},{8,9},{9,8},{10,11... | collective-permute-start | bytes 196616 | tf_op jit(solution)/shard_map/ppermute | solution.py:516
  25.1 1.4 %collective-permute-start.7 = (bf16[2,64,512]{2,1,0:T(8,128)(2,1)S(1)}, bf16[2,64,512]{2,1,0:T(8,128)(2,1)S(1)}, u32[]{:S(2)}, u32[]{:S(2)}) collective-permute-start(bf16[2,64,512]{2,1,0:T(8,128)(2,1)S(1)} %get-tuple-element.51), channel_id=1, source_target_pairs={{0,1},{1,0},{2,3},{3,2},{4,5},{5,4},{6,7},{7,6},{8,9},{9,8},{10,11... | collective-permute-start | bytes 393224 | tf_op jit(solution)/shard_map/ppermute | solution.py:516
  26.6 5.1 %collective-permute-start.9 = (bf16[384,128]{1,0:T(8,128)(2,1)S(1)}, bf16[384,128]{1,0:T(8,128)(2,1)S(1)}, u32[]{:S(2)}, u32[]{:S(2)}) collective-permute-start(bf16[384,128]{1,0:T(8,128)(2,1)S(1)} %get-tuple-element.55), channel_id=1, source_target_pairs={{0,4},{4,0},{8,12},{12,8},{16,20},{20,16},{24,28},{28,24},{1,9},{9... | collective-permute-start | bytes 294920 | tf_op jit(solution)/shard_map/ppermute | solution.py:526
  27.1 4.6 %collective-permute-start.8 = (bf16[1,64,512]{2,1,0:T(8,128)(2,1)S(1)}, bf16[1,64,512]{2,1,0:T(8,128)(2,1)S(1)}, u32[]{:S(2)}, u32[]{:S(2)}) collective-permute-start(bf16[1,64,512]{2,1,0:T(8,128)(2,1)S(1)} %get-tuple-element.54), channel_id=1, source_target_pairs={{0,2},{1,3},{2,0},{3,1},{4,6},{5,7},{6,4},{7,5},{8,10},{9,11},{10,... | collective-permute-start | bytes 196616 | tf_op jit(solution)/shard_map/ppermute | solution.py:516
  31.7 9.1 %collective-permute-start.10 = (bf16[384,128]{1,0:T(8,128)(2,1)S(1)}, bf16[384,128]{1,0:T(8,128)(2,1)S(1)}, u32[]{:S(2)}, u32[]{:S(2)}) collective-permute-start(bf16[384,128]{1,0:T(8,128)(2,1)S(1)} %get-tuple-element.59), channel_id=1, source_target_pairs={{4,8},{8,4},{12,16},{16,12},{20,24},{24,20},{9,17},{17,9},{13,21},... | collective-permute-start | bytes 294920 | tf_op jit(solution)/shard_map/ppermute | solution.py:526
  32.4 8.5 %collective-permute-start.13 = (bf16[1,64,512]{2,1,0:T(8,128)(2,1)S(1)}, bf16[1,64,512]{2,1,0:T(8,128)(2,1)S(1)}, u32[]{:S(2)}, u32[]{:S(2)}) collective-permute-start(bf16[1,64,512]{2,1,0:T(8,128)(2,1)S(1)} %get-tuple-element.62.refs_0_), channel_id=1, source_target_pairs={{0,4},{4,0},{8,12},{12,8},{16,20},{20,16},{24,28},{28,24},{1,9},{5... | collective-permute-start | bytes 196616 | tf_op jit(solution)/shard_map/ppermute | solution.py:526
  37.3 6.4 %collective-permute-start.11 = (bf16[384,128]{1,0:T(8,128)(2,1)S(1)}, bf16[384,128]{1,0:T(8,128)(2,1)S(1)}, u32[]{:S(2)}, u32[]{:S(2)}) collective-permute-start(bf16[384,128]{1,0:T(8,128)(2,1)S(1)} %get-tuple-element.60), channel_id=1, source_target_pairs={{8,16},{16,8},{12,20},{20,12},{5,9},{9,5},{13,17},{17,13},{21,25},... | collective-permute-start | bytes 294920 | tf_op jit(solution)/shard_map/ppermute | solution.py:526
  38.0 5.7 %collective-permute-start.12 = (bf16[384,128]{1,0:T(8,128)(2,1)S(1)}, bf16[384,128]{1,0:T(8,128)(2,1)S(1)}, u32[]{:S(2)}, u32[]{:S(2)}) collective-permute-start(bf16[384,128]{1,0:T(8,128)(2,1)S(1)} %get-tuple-element.61), channel_id=1, source_target_pairs={{0,8},{8,0},{4,12},{12,4},{16,24},{24,16},{20,28},{28,20},{1,5},{5... | collective-permute-start | bytes 294920 | tf_op jit(solution)/shard_map/ppermute | solution.py:526
  40.9 5.0 %collective-permute-start.14 = (bf16[1,64,512]{2,1,0:T(8,128)(2,1)S(1)}, bf16[1,64,512]{2,1,0:T(8,128)(2,1)S(1)}, u32[]{:S(2)}, u32[]{:S(2)}) collective-permute-start(bf16[1,64,512]{2,1,0:T(8,128)(2,1)S(1)} %sum.6.after.refs_0_), channel_id=1, source_target_pairs={{0,8},{4,12},{8,0},{12,4},{16,24},{20,28},{24,16},{28,20},{1,17},{... | collective-permute-start | bytes 196616 | tf_op jit(solution)/shard_map/ppermute | solution.py:526
  46.0 5.2 %collective-permute-start.15 = (bf16[1,64,512]{2,1,0:T(8,128)(2,1)S(1)}, bf16[1,64,512]{2,1,0:T(8,128)(2,1)S(1)}, u32[]{:S(2)}, u32[]{:S(2)}) collective-permute-start(bf16[1,64,512]{2,1,0:T(8,128)(2,1)S(1)} %sum.7.after), channel_id=1, source_target_pairs={{0,16},{4,20},{8,24},{12,28},{16,0},{20,4},{24,8},{28,12},{1,5},{5... | collective-permute-start | bytes 196616 | tf_op jit(solution)/shard_map/ppermute | solution.py:526

commit v12 on v10

--- a/solution.py
+++ b/solution.py
@@ -542,7 +542,7 @@
     bits = []
     while 2 ** len(bits) < lax.axis_size("space"):
         bits.append(2 ** len(bits))
-    return list(zip(bits, bits[1:] + bits[:1]))
+    return list(zip(bits[1:] + bits[:1], bits))
 
 
 def stepped(total, step):

time: 50.6 us -> 51 us (level)
  waiting for transfers between devices: 11.3 us -> 13.3 us
  starting transfers between devices: 25.3 us -> 23.7 us
    ppermute x11, waiting for transfers between devices: 5.63 us -> 7.62 us  [by_parity(): return lax.ppermute(block, ('space', 'dp'), pairs)]
    ppermute x11, starting transfers between devices: 21.6 us -> 20 us  [by_parity(): return lax.ppermute(block, ('space', 'dp'), pairs)]
  transfers between devices with their start and end apart: 16 -> 16, of which waited for: 7 -> 8; matrix products, arithmetic and copies ran while one was open for 0% -> 0% of each run, Pallas kernels for 7% -> 7%
where the time goes in v12:
time: 51 us; the launch traced here: 50.7 us
  starting transfers between devices  23.7 us (46%)
  waiting for transfers between devices  13.3 us (26%)
  Pallas kernels  12.4 us (24%)
  between operations  1.4 us (3%)
    ppermute x11, starting transfers between devices, by_parity(): return lax.ppermute(block, ('space', 'dp'), pairs)  20 us
    ppermute x11, waiting for transfers between devices, by_parity(): return lax.ppermute(block, ('space', 'dp'), pairs)  7.62 us
    pallas_call x1, Pallas kernels, body(): pl.pallas_call(functools.partial(forward_kernel, shard=shard), name='forw...  6 us
    ppermute x5, waiting for transfers between devices, swapped(): lax.ppermute(block, axis, [(i, i ^ bit) for i in range(lax.axis_size(axis...  5.64 us
    ppermute x5, starting transfers between devices, swapped(): lax.ppermute(block, axis, [(i, i ^ bit) for i in range(lax.axis_size(axis...  3.69 us
    pallas_call x1, Pallas kernels, body(): pl.pallas_call(prepare_kernel, name='prepare', out_shape=[grid_type, grid...  2.15 us
    pallas_call x1, Pallas kernels, body(): pl.pallas_call(backward_kernel, name='backward', out_shape=grid_type, in_...  1.69 us
    pallas_call x1, Pallas kernels, body(): pl.pallas_call(assemble_kernel, name='assemble', out_shape=jax.ShapeDtype...  1.07 us
  transfers between devices with their start and end apart: 16, of which 8 were waited for; matrix products, arithmetic and copies ran while one was open for 0% of the time, Pallas kernels for 7%

profile of v12, /device:TPU:0, one launch (start us, length us, event | category | flops | bytes accessed | tf_op | source)
XLA Modules:
  0.0 50.7 jit_solution(14422124884592725582)
XLA Ops:
  1.3 2.1 %prepare.1 = (bf16[4,4,2,8,512]{4,3,2,1,0:T(8,128)(2,1)S(1)}, bf16[4,4,2,8,512]{4,3,2,1,0:T(8,128)(2,1)S(1)}, s32[4,26]{1,0:T(4,128)S(1)}, s32[5,1,12]{2,1,0:T(1...) custom-call(bf16[4,4,2,8,512]{4,3,2,1,0:T(8,128)(2,1)} %bitcast.17, ...), custom_call_target="tpu_custom_call" | custom-call | tf_op jit(solution)/shard_map/prepare/pallas_call | solution.py:570
  3.4 3.0 %collective-permute-start.1 = (bf16[64,512]{1,0:T(8,128)(2,1)S(1)}, bf16[64,512]{1,0:T(8,128)(2,1)S(1)}, u32[]{:S(2)}, u32[]{:S(2)}) collective-permute-start(bf16[64,512]{1,0:T(8,128)(2,1)S(1)} %get-tuple-element.36.refs_0_), channel_id=1, source_target_pairs={{0,2},{1,3},{2,0},{3,1},{4,6},{5,7},{6,4},{7,5},{8,10},{9,11},{10,... | collective-permute-start | bytes 196616 | tf_op jit(solution)/shard_map/ppermute | solution.py:516
  6.4 0.0 collective-permute-start
  6.4 0.7 %collective-permute-start.3 = (bf16[384,128]{1,0:T(8,128)(2,1)S(1)}, bf16[384,128]{1,0:T(8,128)(2,1)S(1)}, u32[]{:S(2)}, u32[]{:S(2)}) collective-permute-start(bf16[384,128]{1,0:T(8,128)(2,1)S(1)} %get-tuple-element.42), channel_id=1, source_target_pairs={{4,8},{8,4},{12,16},{16,12},{20,24},{24,20},{9,17},{17,9},{13,21},... | collective-permute-start | bytes 294920 | tf_op jit(solution)/shard_map/ppermute | solution.py:526
  7.1 0.7 %collective-permute-start.4 = (bf16[384,128]{1,0:T(8,128)(2,1)S(1)}, bf16[384,128]{1,0:T(8,128)(2,1)S(1)}, u32[]{:S(2)}, u32[]{:S(2)}) collective-permute-start(bf16[384,128]{1,0:T(8,128)(2,1)S(1)} %get-tuple-element.43), channel_id=1, source_target_pairs={{8,16},{16,8},{12,20},{20,12},{5,9},{9,5},{13,17},{17,13},{21,25},... | collective-permute-start | bytes 294920 | tf_op jit(solution)/shard_map/ppermute | solution.py:526
  7.8 4.3 %collective-permute-start.5 = (bf16[384,128]{1,0:T(8,128)(2,1)S(1)}, bf16[384,128]{1,0:T(8,128)(2,1)S(1)}, u32[]{:S(2)}, u32[]{:S(2)}) collective-permute-start(bf16[384,128]{1,0:T(8,128)(2,1)S(1)} %get-tuple-element.44), channel_id=1, source_target_pairs={{0,4},{4,0},{8,12},{12,8},{16,20},{20,16},{24,28},{28,24},{1,9},{9... | collective-permute-start | bytes 294920 | tf_op jit(solution)/shard_map/ppermute | solution.py:526
  12.1 0.0 collective-permute-done.1.refs_2_
  12.1 4.4 %collective-permute-start.6 = (bf16[384,128]{1,0:T(8,128)(2,1)S(1)}, bf16[384,128]{1,0:T(8,128)(2,1)S(1)}, u32[]{:S(2)}, u32[]{:S(2)}) collective-permute-start(bf16[384,128]{1,0:T(8,128)(2,1)S(1)} %get-tuple-element.45), channel_id=1, source_target_pairs={{0,8},{8,0},{4,12},{12,4},{16,24},{24,16},{20,28},{28,20},{1,5},{5... | collective-permute-start | bytes 294920 | tf_op jit(solution)/shard_map/ppermute | solution.py:526
  16.5 0.0 collective-permute-done.refs_1_
  16.5 0.0 collective-permute-start.2
  16.5 1.3 %collective-permute-done.2.refs_3_ = bf16[64,512]{1,0:T(8,128)(2,1)S(1)} collective-permute-done((bf16[64,512]{1,0:T(8,128)(2,1)S(1)}, bf16[64,512]{1,0:T(8,128)(2,1)S(1)}, u32[]{:S(2)}, u32[]{:S(2)}) %collective-permute-start.2) | collective-permute-done | bytes 65568 | tf_op jit(solution)/shard_map/ppermute | solution.py:516
  17.8 0.7 %weights.1 = (bf16[3072,256]{1,0:T(8,128)(2,1)S(1)}, bf16[3072,256]{1,0:T(8,128)(2,1)S(1)}, f32[8,128]{1,0:T(8,128)S(1)}) custom-call(bf16[64,512]{1,0:T(8,128)(2,1)S(1)} %get-tuple-element.36.refs_0_, bf16[64,512]{1,0:T(8,128)(2,1)S(1)} %collective-permute-done.refs_1_, bf16[64,512]{1,0:T(8,128)(2,1)S(1)} %collective-permute-done.1.refs_2_, ...), custom_call_target="tpu_custom_call" | custom-call | tf_op jit(solution)/shard_map/weights/pallas_call | solution.py:618
  18.5 0.0 collective-permute-done.3.r1
  18.5 0.0 collective-permute-done.4.r2
  18.5 0.0 collective-permute-done.5.r3
  18.5 0.6 %collective-permute-done.6.r4 = bf16[384,128]{1,0:T(8,128)(2,1)S(1)} collective-permute-done((bf16[384,128]{1,0:T(8,128)(2,1)S(1)}, bf16[384,128]{1,0:T(8,128)(2,1)S(1)}, u32[]{:S(2)}, u32[]{:S(2)}) %collective-permute-start.6) | collective-permute-done | bytes 98336 | tf_op jit(solution)/shard_map/ppermute | solution.py:526
  19.1 6.0 %forward.1 = (bf16[4,4,2,8,512]{4,3,2,1,0:T(8,128)(2,1)}, bf16[4,4,2,8,512]{4,3,2,1,0:T(8,128)(2,1)S(1)}, bf16[2,64,512]{2,1,0:T(8,128)(2,1)S(1)}, bf16[2,64,512...) custom-call(bf16[4,4,2,8,512]{4,3,2,1,0:T(8,128)(2,1)S(1)} %get-tupl, ...), custom_call_target="tpu_custom_call" | custom-call | tf_op jit(solution)/shard_map/forward/pallas_call | solution.py:637
  25.1 0.1 collective-permute-start.8
  25.2 0.7 %collective-permute-start.7 = (bf16[384,128]{1,0:T(8,128)(2,1)S(1)}, bf16[384,128]{1,0:T(8,128)(2,1)S(1)}, u32[]{:S(2)}, u32[]{:S(2)}) collective-permute-start(bf16[384,128]{1,0:T(8,128)(2,1)S(1)} %get-tuple-element.49), channel_id=1, source_target_pairs={{4,8},{8,4},{12,16},{16,12},{20,24},{24,20},{9,17},{17,9},{13,21},... | collective-permute-start | bytes 294920 | tf_op jit(solution)/shard_map/ppermute | solution.py:526
  25.9 0.7 %collective-permute-done.8.refs_1_ = bf16[2,64,512]{2,1,0:T(8,128)(2,1)S(1)} collective-permute-done((bf16[2,64,512]{2,1,0:T(8,128)(2,1)S(1)}, bf16[2,64,512]{2,1,0:T(8,128)(2,1)S(1)}, u32[]{:S(2)}, u32[]{:S(2)}) %collective-permute-start.8) | collective-permute-done | bytes 131104 | tf_op jit(solution)/shard_map/ppermute | solution.py:516
  26.6 0.6 %collective-permute-start.10 = (bf16[1,64,512]{2,1,0:T(8,128)(2,1)S(1)}, bf16[1,64,512]{2,1,0:T(8,128)(2,1)S(1)}, u32[]{:S(2)}, u32[]{:S(2)}) collective-permute-start(bf16[1,64,512]{2,1,0:T(8,128)(2,1)S(1)} %get-tuple-element.55), channel_id=1, source_target_pairs={{0,2},{1,3},{2,0},{3,1},{4,6},{5,7},{6,4},{7,5},{8,10},{9,11},{10,... | collective-permute-start | bytes 196616 | tf_op jit(solution)/shard_map/ppermute | solution.py:516
  27.2 0.0 collective-permute-done.7.refs_2_.r1
  27.2 3.7 %collective-permute-done.10.refs_1_ = bf16[1,64,512]{2,1,0:T(8,128)(2,1)S(1)} collective-permute-done((bf16[1,64,512]{2,1,0:T(8,128)(2,1)S(1)}, bf16[1,64,512]{2,1,0:T(8,128)(2,1)S(1)}, u32[]{:S(2)}, u32[]{:S(2)}) %collective-permute-start.10) | collective-permute-done | bytes 65568 | tf_op jit(solution)/shard_map/ppermute | solution.py:516
  30.9 4.1 %collective-permute-start.11 = (bf16[384,128]{1,0:T(8,128)(2,1)S(1)}, bf16[384,128]{1,0:T(8,128)(2,1)S(1)}, u32[]{:S(2)}, u32[]{:S(2)}) collective-permute-start(bf16[384,128]{1,0:T(8,128)(2,1)S(1)} %get-tuple-element.58), channel_id=1, source_target_pairs={{0,4},{4,0},{8,12},{12,8},{16,20},{20,16},{24,28},{28,24},{1,9},{9... | collective-permute-start | bytes 294920 | tf_op jit(solution)/shard_map/ppermute | solution.py:526
  35.1 0.8 %collective-permute-start.13 = (bf16[1,64,512]{2,1,0:T(8,128)(2,1)S(1)}, bf16[1,64,512]{2,1,0:T(8,128)(2,1)S(1)}, u32[]{:S(2)}, u32[]{:S(2)}) collective-permute-start(bf16[1,64,512]{2,1,0:T(8,128)(2,1)S(1)} %get-tuple-element.60.refs_0_), channel_id=1, source_target_pairs={{0,8},{4,12},{8,0},{12,4},{16,24},{20,28},{24,16},{28,20},{1,5},{5... | collective-permute-start | bytes 196616 | tf_op jit(solution)/shard_map/ppermute | solution.py:526
  35.9 0.7 %collective-permute-start.9 = (bf16[384,128]{1,0:T(8,128)(2,1)S(1)}, bf16[384,128]{1,0:T(8,128)(2,1)S(1)}, u32[]{:S(2)}, u32[]{:S(2)}) collective-permute-start(bf16[384,128]{1,0:T(8,128)(2,1)S(1)} %get-tuple-element.53), channel_id=1, source_target_pairs={{8,16},{16,8},{12,20},{20,12},{5,9},{9,5},{13,17},{17,13},{21,25},... | collective-permute-start | bytes 294920 | tf_op jit(solution)/shard_map/ppermute | solution.py:526
  36.5 2.6 %collective-permute-start.12 = (bf16[384,128]{1,0:T(8,128)(2,1)S(1)}, bf16[384,128]{1,0:T(8,128)(2,1)S(1)}, u32[]{:S(2)}, u32[]{:S(2)}) collective-permute-start(bf16[384,128]{1,0:T(8,128)(2,1)S(1)} %get-tuple-element.59), channel_id=1, source_target_pairs={{0,8},{8,0},{4,12},{12,4},{16,24},{24,16},{20,28},{28,20},{1,5},{5... | collective-permute-start | bytes 294920 | tf_op jit(solution)/shard_map/ppermute | solution.py:526
  39.1 0.5 collective-permute-done.13.refs_1_
  39.6 0.0 collective-permute-done.11.refs_2_.r3
  39.6 1.0 %collective-permute-start.14 = (bf16[1,64,512]{2,1,0:T(8,128)(2,1)S(1)}, bf16[1,64,512]{2,1,0:T(8,128)(2,1)S(1)}, u32[]{:S(2)}, u32[]{:S(2)}) collective-permute-start(bf16[1,64,512]{2,1,0:T(8,128)(2,1)S(1)} %sum.6.after.refs_0_), channel_id=1, source_target_pairs={{0,16},{4,20},{8,24},{12,28},{16,0},{20,4},{24,8},{28,12},{1,9},{5... | collective-permute-start | bytes 196616 | tf_op jit(solution)/shard_map/ppermute | solution.py:526
  40.7 0.0 collective-permute-done.9.r2
  40.7 1.5 %collective-permute-done.12.r4 = bf16[384,128]{1,0:T(8,128)(2,1)S(1)} collective-permute-done((bf16[384,128]{1,0:T(8,128)(2,1)S(1)}, bf16[384,128]{1,0:T(8,128)(2,1)S(1)}, u32[]{:S(2)}, u32[]{:S(2)}) %collective-permute-start.12) | collective-permute-done | bytes 98336 | tf_op jit(solution)/shard_map/ppermute | solution.py:526
  42.1 1.1 %assemble.1.refs_2_.windows = bf16[3,4,2,5,2,16,256]{6,5,4,3,2,1,0:T(8,128)(2,1)S(1)} custom-call(bf16[4,4,2,8,512]{4,3,2,1,0:T(8,128)(2,1)S(1)} %get-tuple-element.47.grad, s32[4,26]{1,0:T(4,128)S(1)} %get-tuple-element.39.rows, bf16[384,128]{1,0:T(8,128)(2,1)S(1)} %get-tuple-element.48.r0, bf16[384,128]{1,0:T(8,128)(2,1)S(1)} %collective-permute-done.7.refs_2_.r1, ...), custom_call_target="tpu_custom_call" | custom-call | tf_op jit(solution)/shard_map/assemble/pallas_call | solution.py:687
  43.2 2.5 %collective-permute-done.14.refs_1_ = bf16[1,64,512]{2,1,0:T(8,128)(2,1)S(1)} collective-permute-done((bf16[1,64,512]{2,1,0:T(8,128)(2,1)S(1)}, bf16[1,64,512]{2,1,0:T(8,128)(2,1)S(1)}, u32[]{:S(2)}, u32[]{:S(2)}) %collective-permute-start.14) | collective-permute-done | bytes 65568 | tf_op jit(solution)/shard_map/ppermute | solution.py:526
  45.7 0.1 collective-permute-start.15
  45.8 1.7 %backward.1 = bf16[4,4,2,8,512]{4,3,2,1,0:T(8,128)(2,1)} custom-call(bf16[3,4,2,5,2,16,256]{6,5,4,3,2,1,0:T(8,128)(2,1)S(1)} %assemble.1.refs_2_.windows, bf16[4,4,2,8,512]{4,3,2,1,0:T(8,128)(2,1)S(1)} %get-tuple-element.35.mask, bf16[3072,256]{1,0:T(8,128)(2,1)S(1)} %get-tuple-element.61.toeplitz, bf16[1,64,512]{2,1,0:T(8,128)(2,1)S(1)} %sum.7.after), custom_call_target="tpu_custom_call" | custom-call | tf_op jit(solution)/shard_map/backward/pallas_call | solution.py:701
  47.5 2.6 %collective-permute-done.15 = bf16[1,64,512]{2,1,0:T(8,128)(2,1)S(1)} collective-permute-done((bf16[1,64,512]{2,1,0:T(8,128)(2,1)S(1)}, bf16[1,64,512]{2,1,0:T(8,128)(2,1)S(1)}, u32[]{:S(2)}, u32[]{:S(2)}) %collective-permute-start.15) | collective-permute-done | bytes 65568 | tf_op jit(solution)/shard_map/ppermute | solution.py:526
  50.0 0.7 %finish.1 = (f32[64,432]{1,0:T(8,128)}, f32[1,16]{1,0:T(1,128)}) custom-call(bf16[64,512]{1,0:T(8,128)(2,1)S(1)} %bitcast.13, bf16[64,512]{1,0:T(8,128)(2,1)S(1)} %bitcast.14), custom_call_target="tpu_custom_call" | custom-call | tf_op jit(solution)/shard_map/finish/pallas_call | solution.py:710
  (4 shorter events, 0.1 us)
Async XLA Ops:
  3.4 8.7 %collective-permute-start.1 = (bf16[64,512]{1,0:T(8,128)(2,1)S(1)}, bf16[64,512]{1,0:T(8,128)(2,1)S(1)}, u32[]{:S(2)}, u32[]{:S(2)}) collective-permute-start(bf16[64,512]{1,0:T(8,128)(2,1)S(1)} %get-tuple-element.36.refs_0_), channel_id=1, source_target_pairs={{0,2},{1,3},{2,0},{3,1},{4,6},{5,7},{6,4},{7,5},{8,10},{9,11},{10,... | collective-permute-start | bytes 196616 | tf_op jit(solution)/shard_map/ppermute | solution.py:516
  6.4 10.1 %collective-permute-start = (bf16[64,512]{1,0:T(8,128)(2,1)S(1)}, bf16[64,512]{1,0:T(8,128)(2,1)S(1)}, u32[]{:S(2)}, u32[]{:S(2)}) collective-permute-start(bf16[64,512]{1,0:T(8,128)(2,1)S(1)} %get-tuple-element.36.refs_0_), channel_id=1, source_target_pairs={{0,1},{1,0},{2,3},{3,2},{4,5},{5,4},{6,7},{7,6},{8,9},{9,8},{10,11... | collective-permute-start | bytes 196616 | tf_op jit(solution)/shard_map/ppermute | solution.py:516
  6.4 12.1 %collective-permute-start.3 = (bf16[384,128]{1,0:T(8,128)(2,1)S(1)}, bf16[384,128]{1,0:T(8,128)(2,1)S(1)}, u32[]{:S(2)}, u32[]{:S(2)}) collective-permute-start(bf16[384,128]{1,0:T(8,128)(2,1)S(1)} %get-tuple-element.42), channel_id=1, source_target_pairs={{4,8},{8,4},{12,16},{16,12},{20,24},{24,20},{9,17},{17,9},{13,21},... | collective-permute-start | bytes 294920 | tf_op jit(solution)/shard_map/ppermute | solution.py:526
  7.1 11.4 %collective-permute-start.4 = (bf16[384,128]{1,0:T(8,128)(2,1)S(1)}, bf16[384,128]{1,0:T(8,128)(2,1)S(1)}, u32[]{:S(2)}, u32[]{:S(2)}) collective-permute-start(bf16[384,128]{1,0:T(8,128)(2,1)S(1)} %get-tuple-element.43), channel_id=1, source_target_pairs={{8,16},{16,8},{12,20},{20,12},{5,9},{9,5},{13,17},{17,13},{21,25},... | collective-permute-start | bytes 294920 | tf_op jit(solution)/shard_map/ppermute | solution.py:526
  7.8 10.8 %collective-permute-start.5 = (bf16[384,128]{1,0:T(8,128)(2,1)S(1)}, bf16[384,128]{1,0:T(8,128)(2,1)S(1)}, u32[]{:S(2)}, u32[]{:S(2)}) collective-permute-start(bf16[384,128]{1,0:T(8,128)(2,1)S(1)} %get-tuple-element.44), channel_id=1, source_target_pairs={{0,4},{4,0},{8,12},{12,8},{16,20},{20,16},{24,28},{28,24},{1,9},{9... | collective-permute-start | bytes 294920 | tf_op jit(solution)/shard_map/ppermute | solution.py:526
  12.1 7.0 %collective-permute-start.6 = (bf16[384,128]{1,0:T(8,128)(2,1)S(1)}, bf16[384,128]{1,0:T(8,128)(2,1)S(1)}, u32[]{:S(2)}, u32[]{:S(2)}) collective-permute-start(bf16[384,128]{1,0:T(8,128)(2,1)S(1)} %get-tuple-element.45), channel_id=1, source_target_pairs={{0,8},{8,0},{4,12},{12,4},{16,24},{24,16},{20,28},{28,20},{1,5},{5... | collective-permute-start | bytes 294920 | tf_op jit(solution)/shard_map/ppermute | solution.py:526
  16.5 1.3 %collective-permute-start.2 = (bf16[64,512]{1,0:T(8,128)(2,1)S(1)}, bf16[64,512]{1,0:T(8,128)(2,1)S(1)}, u32[]{:S(2)}, u32[]{:S(2)}) collective-permute-start(bf16[64,512]{1,0:T(8,128)(2,1)S(1)} %collective-permute-done.1.refs_2_), channel_id=1, source_target_pairs={{0,1},{1,0},{2,3},{3,2},{4,5},{5,4},{6,7},{7,6},{8,9},{9,8},{10,11... | collective-permute-start | bytes 196616 | tf_op jit(solution)/shard_map/ppermute | solution.py:516
  25.1 1.4 %collective-permute-start.8 = (bf16[2,64,512]{2,1,0:T(8,128)(2,1)S(1)}, bf16[2,64,512]{2,1,0:T(8,128)(2,1)S(1)}, u32[]{:S(2)}, u32[]{:S(2)}) collective-permute-start(bf16[2,64,512]{2,1,0:T(8,128)(2,1)S(1)} %get-tuple-element.51), channel_id=1, source_target_pairs={{0,1},{1,0},{2,3},{3,2},{4,5},{5,4},{6,7},{7,6},{8,9},{9,8},{10,11... | collective-permute-start | bytes 393224 | tf_op jit(solution)/shard_map/ppermute | solution.py:516
  25.2 2.0 %collective-permute-start.7 = (bf16[384,128]{1,0:T(8,128)(2,1)S(1)}, bf16[384,128]{1,0:T(8,128)(2,1)S(1)}, u32[]{:S(2)}, u32[]{:S(2)}) collective-permute-start(bf16[384,128]{1,0:T(8,128)(2,1)S(1)} %get-tuple-element.49), channel_id=1, source_target_pairs={{4,8},{8,4},{12,16},{16,12},{20,24},{24,20},{9,17},{17,9},{13,21},... | collective-permute-start | bytes 294920 | tf_op jit(solution)/shard_map/ppermute | solution.py:526
  26.6 4.3 %collective-permute-start.10 = (bf16[1,64,512]{2,1,0:T(8,128)(2,1)S(1)}, bf16[1,64,512]{2,1,0:T(8,128)(2,1)S(1)}, u32[]{:S(2)}, u32[]{:S(2)}) collective-permute-start(bf16[1,64,512]{2,1,0:T(8,128)(2,1)S(1)} %get-tuple-element.55), channel_id=1, source_target_pairs={{0,2},{1,3},{2,0},{3,1},{4,6},{5,7},{6,4},{7,5},{8,10},{9,11},{10,... | collective-permute-start | bytes 196616 | tf_op jit(solution)/shard_map/ppermute | solution.py:516
  30.9 8.7 %collective-permute-start.11 = (bf16[384,128]{1,0:T(8,128)(2,1)S(1)}, bf16[384,128]{1,0:T(8,128)(2,1)S(1)}, u32[]{:S(2)}, u32[]{:S(2)}) collective-permute-start(bf16[384,128]{1,0:T(8,128)(2,1)S(1)} %get-tuple-element.58), channel_id=1, source_target_pairs={{0,4},{4,0},{8,12},{12,8},{16,20},{20,16},{24,28},{28,24},{1,9},{9... | collective-permute-start | bytes 294920 | tf_op jit(solution)/shard_map/ppermute | solution.py:526
  35.1 4.5 %collective-permute-start.13 = (bf16[1,64,512]{2,1,0:T(8,128)(2,1)S(1)}, bf16[1,64,512]{2,1,0:T(8,128)(2,1)S(1)}, u32[]{:S(2)}, u32[]{:S(2)}) collective-permute-start(bf16[1,64,512]{2,1,0:T(8,128)(2,1)S(1)} %get-tuple-element.60.refs_0_), channel_id=1, source_target_pairs={{0,8},{4,12},{8,0},{12,4},{16,24},{20,28},{24,16},{28,20},{1,5},{5... | collective-permute-start | bytes 196616 | tf_op jit(solution)/shard_map/ppermute | solution.py:526
  35.9 4.8 %collective-permute-start.9 = (bf16[384,128]{1,0:T(8,128)(2,1)S(1)}, bf16[384,128]{1,0:T(8,128)(2,1)S(1)}, u32[]{:S(2)}, u32[]{:S(2)}) collective-permute-start(bf16[384,128]{1,0:T(8,128)(2,1)S(1)} %get-tuple-element.53), channel_id=1, source_target_pairs={{8,16},{16,8},{12,20},{20,12},{5,9},{9,5},{13,17},{17,13},{21,25},... | collective-permute-start | bytes 294920 | tf_op jit(solution)/shard_map/ppermute | solution.py:526
  36.5 5.6 %collective-permute-start.12 = (bf16[384,128]{1,0:T(8,128)(2,1)S(1)}, bf16[384,128]{1,0:T(8,128)(2,1)S(1)}, u32[]{:S(2)}, u32[]{:S(2)}) collective-permute-start(bf16[384,128]{1,0:T(8,128)(2,1)S(1)} %get-tuple-element.59), channel_id=1, source_target_pairs={{0,8},{8,0},{4,12},{12,4},{16,24},{24,16},{20,28},{28,20},{1,5},{5... | collective-permute-start | bytes 294920 | tf_op jit(solution)/shard_map/ppermute | solution.py:526
  39.6 6.1 %collective-permute-start.14 = (bf16[1,64,512]{2,1,0:T(8,128)(2,1)S(1)}, bf16[1,64,512]{2,1,0:T(8,128)(2,1)S(1)}, u32[]{:S(2)}, u32[]{:S(2)}) collective-permute-start(bf16[1,64,512]{2,1,0:T(8,128)(2,1)S(1)} %sum.6.after.refs_0_), channel_id=1, source_target_pairs={{0,16},{4,20},{8,24},{12,28},{16,0},{20,4},{24,8},{28,12},{1,9},{5... | collective-permute-start | bytes 196616 | tf_op jit(solution)/shard_map/ppermute | solution.py:526
  45.7 4.3 %collective-permute-start.15 = (bf16[1,64,512]{2,1,0:T(8,128)(2,1)S(1)}, bf16[1,64,512]{2,1,0:T(8,128)(2,1)S(1)}, u32[]{:S(2)}, u32[]{:S(2)}) collective-permute-start(bf16[1,64,512]{2,1,0:T(8,128)(2,1)S(1)} %sum.7.after), channel_id=1, source_target_pairs={{0,4},{4,0},{8,12},{12,8},{16,20},{20,16},{24,28},{28,24},{1,17},{... | collective-permute-start | bytes 196616 | tf_op jit(solution)/shard_map/ppermute | solution.py:526

commit v13 on v12

--- a/solution.py
+++ b/solution.py
@@ -666,16 +666,14 @@
         *received,
     )
 
-    later = grad_units[2:]
+    later = grad_units[1:]
     bit = 1
     while 2 * bit < groups:
-        first = later[:1] if bit == 1 else []
-        (keep, give), first = sum_after(keep, swapped(give, "dp", bit), through=first, parts=2)
-        later = first + later[1:] if bit == 1 else later
+        (keep, give), _ = sum_after(keep, swapped(give, "dp", bit), parts=2)
         bit *= 2
-    grad_received = [grad_units[0], exchanged(1, grad_units[1])]
-    (total,), last = sum_after(keep, swapped(give, "dp", bit), grad_received[1:], later[1:])
-    for number, unit in enumerate([later[0], *last], 2):
+    (total,), later = sum_after(keep, swapped(give, "dp", bit), through=later)
+    grad_received = grad_units[:1]
+    for number, unit in enumerate(later, 1):
         grad_received.append(exchanged(number, unit))
 
     steps = space_steps()

time: 51 us -> 52.2 us (1.024)
  starting transfers between devices: 23.7 us -> 24.8 us
    ppermute x11, starting transfers between devices: 20 us -> 21.1 us  [by_parity(): return lax.ppermute(block, ('space', 'dp'), pairs)]
    ppermute x5, waiting for transfers between devices: 5.64 us -> 6.32 us  [swapped(): lax.ppermute(block, axis, [(i, i ^ bit) for i in range(lax.axis_size(axis...]
    ppermute x11, waiting for transfers between devices: 7.62 us -> 7.06 us  [by_parity(): return lax.ppermute(block, ('space', 'dp'), pairs)]
  transfers between devices with their start and end apart: 16 -> 16, of which waited for: 8 -> 7; matrix products, arithmetic and copies ran while one was open for 0% -> 0% of each run, Pallas kernels for 7% -> 7%
where the time goes in v13:
time: 52.2 us; the launch traced here: 52 us
  starting transfers between devices  24.8 us (48%)
  waiting for transfers between devices  13.4 us (26%)
  Pallas kernels  12.4 us (24%)
  between operations  1.41 us (3%)
    ppermute x11, starting transfers between devices, by_parity(): return lax.ppermute(block, ('space', 'dp'), pairs)  21.1 us
    ppermute x11, waiting for transfers between devices, by_parity(): return lax.ppermute(block, ('space', 'dp'), pairs)  7.06 us
    ppermute x5, waiting for transfers between devices, swapped(): lax.ppermute(block, axis, [(i, i ^ bit) for i in range(lax.axis_size(axis...  6.32 us
    pallas_call x1, Pallas kernels, body(): pl.pallas_call(functools.partial(forward_kernel, shard=shard), name='forw...  5.99 us
    ppermute x5, starting transfers between devices, swapped(): lax.ppermute(block, axis, [(i, i ^ bit) for i in range(lax.axis_size(axis...  3.69 us
    pallas_call x1, Pallas kernels, body(): pl.pallas_call(prepare_kernel, name='prepare', out_shape=[grid_type, grid...  2.15 us
    pallas_call x1, Pallas kernels, body(): pl.pallas_call(backward_kernel, name='backward', out_shape=grid_type, in_...  1.69 us
    pallas_call x1, Pallas kernels, body(): pl.pallas_call(assemble_kernel, name='assemble', out_shape=jax.ShapeDtype...  1.07 us
  transfers between devices with their start and end apart: 16, of which 7 were waited for; matrix products, arithmetic and copies ran while one was open for 0% of the time, Pallas kernels for 7%

profile of v13, /device:TPU:0, one launch (start us, length us, event | category | flops | bytes accessed | tf_op | source)
XLA Modules:
  0.0 52.0 jit_solution(1711628183119687739)
XLA Ops:
  1.3 2.1 %prepare.1 = (bf16[4,4,2,8,512]{4,3,2,1,0:T(8,128)(2,1)S(1)}, bf16[4,4,2,8,512]{4,3,2,1,0:T(8,128)(2,1)S(1)}, s32[4,26]{1,0:T(4,128)S(1)}, s32[5,1,12]{2,1,0:T(1...) custom-call(bf16[4,4,2,8,512]{4,3,2,1,0:T(8,128)(2,1)} %bitcast.17, ...), custom_call_target="tpu_custom_call" | custom-call | tf_op jit(solution)/shard_map/prepare/pallas_call | solution.py:570
  3.4 3.0 %collective-permute-start.1 = (bf16[64,512]{1,0:T(8,128)(2,1)S(1)}, bf16[64,512]{1,0:T(8,128)(2,1)S(1)}, u32[]{:S(2)}, u32[]{:S(2)}) collective-permute-start(bf16[64,512]{1,0:T(8,128)(2,1)S(1)} %get-tuple-element.37.refs_0_), channel_id=1, source_target_pairs={{0,2},{1,3},{2,0},{3,1},{4,6},{5,7},{6,4},{7,5},{8,10},{9,11},{10,... | collective-permute-start | bytes 196616 | tf_op jit(solution)/shard_map/ppermute | solution.py:516
  6.4 0.0 collective-permute-start
  6.4 0.7 %collective-permute-start.3 = (bf16[384,128]{1,0:T(8,128)(2,1)S(1)}, bf16[384,128]{1,0:T(8,128)(2,1)S(1)}, u32[]{:S(2)}, u32[]{:S(2)}) collective-permute-start(bf16[384,128]{1,0:T(8,128)(2,1)S(1)} %get-tuple-element.43), channel_id=1, source_target_pairs={{4,8},{8,4},{12,16},{16,12},{20,24},{24,20},{9,17},{17,9},{13,21},... | collective-permute-start | bytes 294920 | tf_op jit(solution)/shard_map/ppermute | solution.py:526
  7.1 0.7 %collective-permute-start.4 = (bf16[384,128]{1,0:T(8,128)(2,1)S(1)}, bf16[384,128]{1,0:T(8,128)(2,1)S(1)}, u32[]{:S(2)}, u32[]{:S(2)}) collective-permute-start(bf16[384,128]{1,0:T(8,128)(2,1)S(1)} %get-tuple-element.44), channel_id=1, source_target_pairs={{8,16},{16,8},{12,20},{20,12},{5,9},{9,5},{13,17},{17,13},{21,25},... | collective-permute-start | bytes 294920 | tf_op jit(solution)/shard_map/ppermute | solution.py:526
  7.8 4.3 %collective-permute-start.5 = (bf16[384,128]{1,0:T(8,128)(2,1)S(1)}, bf16[384,128]{1,0:T(8,128)(2,1)S(1)}, u32[]{:S(2)}, u32[]{:S(2)}) collective-permute-start(bf16[384,128]{1,0:T(8,128)(2,1)S(1)} %get-tuple-element.45), channel_id=1, source_target_pairs={{0,4},{4,0},{8,12},{12,8},{16,20},{20,16},{24,28},{28,24},{1,9},{9... | collective-permute-start | bytes 294920 | tf_op jit(solution)/shard_map/ppermute | solution.py:526
  12.1 0.0 collective-permute-done.1.refs_2_
  12.1 4.4 %collective-permute-start.6 = (bf16[384,128]{1,0:T(8,128)(2,1)S(1)}, bf16[384,128]{1,0:T(8,128)(2,1)S(1)}, u32[]{:S(2)}, u32[]{:S(2)}) collective-permute-start(bf16[384,128]{1,0:T(8,128)(2,1)S(1)} %get-tuple-element.46), channel_id=1, source_target_pairs={{0,8},{8,0},{4,12},{12,4},{16,24},{24,16},{20,28},{28,20},{1,5},{5... | collective-permute-start | bytes 294920 | tf_op jit(solution)/shard_map/ppermute | solution.py:526
  16.5 0.0 collective-permute-done.refs_1_
  16.5 0.0 collective-permute-start.2
  16.5 1.3 %collective-permute-done.2.refs_3_ = bf16[64,512]{1,0:T(8,128)(2,1)S(1)} collective-permute-done((bf16[64,512]{1,0:T(8,128)(2,1)S(1)}, bf16[64,512]{1,0:T(8,128)(2,1)S(1)}, u32[]{:S(2)}, u32[]{:S(2)}) %collective-permute-start.2) | collective-permute-done | bytes 65568 | tf_op jit(solution)/shard_map/ppermute | solution.py:516
  17.8 0.7 %weights.1 = (bf16[3072,256]{1,0:T(8,128)(2,1)S(1)}, bf16[3072,256]{1,0:T(8,128)(2,1)S(1)}, f32[8,128]{1,0:T(8,128)S(1)}) custom-call(bf16[64,512]{1,0:T(8,128)(2,1)S(1)} %get-tuple-element.37.refs_0_, bf16[64,512]{1,0:T(8,128)(2,1)S(1)} %collective-permute-done.refs_1_, bf16[64,512]{1,0:T(8,128)(2,1)S(1)} %collective-permute-done.1.refs_2_, ...), custom_call_target="tpu_custom_call" | custom-call | tf_op jit(solution)/shard_map/weights/pallas_call | solution.py:618
  18.5 0.0 collective-permute-done.3.r1
  18.5 0.0 collective-permute-done.4.r2
  18.5 0.0 collective-permute-done.5.r3
  18.5 0.6 %collective-permute-done.6.r4 = bf16[384,128]{1,0:T(8,128)(2,1)S(1)} collective-permute-done((bf16[384,128]{1,0:T(8,128)(2,1)S(1)}, bf16[384,128]{1,0:T(8,128)(2,1)S(1)}, u32[]{:S(2)}, u32[]{:S(2)}) %collective-permute-start.6) | collective-permute-done | bytes 98336 | tf_op jit(solution)/shard_map/ppermute | solution.py:526
  19.1 6.0 %forward.1 = (bf16[4,4,2,8,512]{4,3,2,1,0:T(8,128)(2,1)}, bf16[4,4,2,8,512]{4,3,2,1,0:T(8,128)(2,1)S(1)}, bf16[2,64,512]{2,1,0:T(8,128)(2,1)S(1)}, bf16[2,64,512...) custom-call(bf16[4,4,2,8,512]{4,3,2,1,0:T(8,128)(2,1)S(1)} %get-tupl, ...), custom_call_target="tpu_custom_call" | custom-call | tf_op jit(solution)/shard_map/forward/pallas_call | solution.py:637
  25.1 0.1 collective-permute-start.7
  25.2 1.3 %collective-permute-done.7.refs_1_ = bf16[2,64,512]{2,1,0:T(8,128)(2,1)S(1)} collective-permute-done((bf16[2,64,512]{2,1,0:T(8,128)(2,1)S(1)}, bf16[2,64,512]{2,1,0:T(8,128)(2,1)S(1)}, u32[]{:S(2)}, u32[]{:S(2)}) %collective-permute-start.7) | collective-permute-done | bytes 131104 | tf_op jit(solution)/shard_map/ppermute | solution.py:516
  26.6 0.6 %collective-permute-start.8 = (bf16[1,64,512]{2,1,0:T(8,128)(2,1)S(1)}, bf16[1,64,512]{2,1,0:T(8,128)(2,1)S(1)}, u32[]{:S(2)}, u32[]{:S(2)}) collective-permute-start(bf16[1,64,512]{2,1,0:T(8,128)(2,1)S(1)} %get-tuple-element.53), channel_id=1, source_target_pairs={{0,2},{1,3},{2,0},{3,1},{4,6},{5,7},{6,4},{7,5},{8,10},{9,11},{10,... | collective-permute-start | bytes 196616 | tf_op jit(solution)/shard_map/ppermute | solution.py:516
  27.2 3.7 %collective-permute-done.8.refs_1_ = bf16[1,64,512]{2,1,0:T(8,128)(2,1)S(1)} collective-permute-done((bf16[1,64,512]{2,1,0:T(8,128)(2,1)S(1)}, bf16[1,64,512]{2,1,0:T(8,128)(2,1)S(1)}, u32[]{:S(2)}, u32[]{:S(2)}) %collective-permute-start.8) | collective-permute-done | bytes 65568 | tf_op jit(solution)/shard_map/ppermute | solution.py:516
  30.9 0.5 %collective-permute-start.11 = (bf16[384,128]{1,0:T(8,128)(2,1)S(1)}, bf16[384,128]{1,0:T(8,128)(2,1)S(1)}, u32[]{:S(2)}, u32[]{:S(2)}) collective-permute-start(bf16[384,128]{1,0:T(8,128)(2,1)S(1)} %get-tuple-element.60), channel_id=1, source_target_pairs={{0,4},{4,0},{8,12},{12,8},{16,20},{20,16},{24,28},{28,24},{1,9},{9... | collective-permute-start | bytes 294920 | tf_op jit(solution)/shard_map/ppermute | solution.py:526
  31.5 2.5 %collective-permute-start.13 = (bf16[1,64,512]{2,1,0:T(8,128)(2,1)S(1)}, bf16[1,64,512]{2,1,0:T(8,128)(2,1)S(1)}, u32[]{:S(2)}, u32[]{:S(2)}) collective-permute-start(bf16[1,64,512]{2,1,0:T(8,128)(2,1)S(1)} %get-tuple-element.62.refs_0_), channel_id=1, source_target_pairs={{0,8},{4,12},{8,0},{12,4},{16,24},{20,28},{24,16},{28,20},{1,5},{5... | collective-permute-start | bytes 196616 | tf_op jit(solution)/shard_map/ppermute | solution.py:526
  33.9 0.7 %collective-permute-start.9 = (bf16[384,128]{1,0:T(8,128)(2,1)S(1)}, bf16[384,128]{1,0:T(8,128)(2,1)S(1)}, u32[]{:S(2)}, u32[]{:S(2)}) collective-permute-start(bf16[384,128]{1,0:T(8,128)(2,1)S(1)} %get-tuple-element.58), channel_id=1, source_target_pairs={{4,8},{8,4},{12,16},{16,12},{20,24},{24,20},{9,17},{17,9},{13,21},... | collective-permute-start | bytes 294920 | tf_op jit(solution)/shard_map/ppermute | solution.py:526
  34.6 0.7 %collective-permute-start.10 = (bf16[384,128]{1,0:T(8,128)(2,1)S(1)}, bf16[384,128]{1,0:T(8,128)(2,1)S(1)}, u32[]{:S(2)}, u32[]{:S(2)}) collective-permute-start(bf16[384,128]{1,0:T(8,128)(2,1)S(1)} %get-tuple-element.59), channel_id=1, source_target_pairs={{8,16},{16,8},{12,20},{20,12},{5,9},{9,5},{13,17},{17,13},{21,25},... | collective-permute-start | bytes 294920 | tf_op jit(solution)/shard_map/ppermute | solution.py:526
  35.3 5.1 %collective-permute-start.12 = (bf16[384,128]{1,0:T(8,128)(2,1)S(1)}, bf16[384,128]{1,0:T(8,128)(2,1)S(1)}, u32[]{:S(2)}, u32[]{:S(2)}) collective-permute-start(bf16[384,128]{1,0:T(8,128)(2,1)S(1)} %get-tuple-element.61), channel_id=1, source_target_pairs={{0,8},{8,0},{4,12},{12,4},{16,24},{24,16},{20,28},{28,20},{1,5},{5... | collective-permute-start | bytes 294920 | tf_op jit(solution)/shard_map/ppermute | solution.py:526
  40.4 0.0 collective-permute-done.13.refs_1_
  40.4 0.0 collective-permute-done.11.refs_2_.r3
  40.4 1.5 %collective-permute-start.14 = (bf16[1,64,512]{2,1,0:T(8,128)(2,1)S(1)}, bf16[1,64,512]{2,1,0:T(8,128)(2,1)S(1)}, u32[]{:S(2)}, u32[]{:S(2)}) collective-permute-start(bf16[1,64,512]{2,1,0:T(8,128)(2,1)S(1)} %sum.6.after.refs_0_), channel_id=1, source_target_pairs={{0,16},{4,20},{8,24},{12,28},{16,0},{20,4},{24,8},{28,12},{1,9},{5... | collective-permute-start | bytes 196616 | tf_op jit(solution)/shard_map/ppermute | solution.py:526
  42.0 0.0 collective-permute-done.9.r1
  42.0 0.0 collective-permute-done.10.r2
  42.0 1.0 %collective-permute-done.12.r4 = bf16[384,128]{1,0:T(8,128)(2,1)S(1)} collective-permute-done((bf16[384,128]{1,0:T(8,128)(2,1)S(1)}, bf16[384,128]{1,0:T(8,128)(2,1)S(1)}, u32[]{:S(2)}, u32[]{:S(2)}) %collective-permute-start.12) | collective-permute-done | bytes 98336 | tf_op jit(solution)/shard_map/ppermute | solution.py:526
  43.0 1.1 %assemble.1.refs_2_.windows = bf16[3,4,2,5,2,16,256]{6,5,4,3,2,1,0:T(8,128)(2,1)S(1)} custom-call(bf16[4,4,2,8,512]{4,3,2,1,0:T(8,128)(2,1)S(1)} %get-tuple-element.48.grad, s32[4,26]{1,0:T(4,128)S(1)} %get-tuple-element.40.rows, bf16[384,128]{1,0:T(8,128)(2,1)S(1)} %get-tuple-element.49.r0, bf16[384,128]{1,0:T(8,128)(2,1)S(1)} %collective-permute-done.9.r1, ...), custom_call_target="tpu_custom_call" | custom-call | tf_op jit(solution)/shard_map/assemble/pallas_call | solution.py:685
  44.1 2.9 %collective-permute-done.14.refs_1_ = bf16[1,64,512]{2,1,0:T(8,128)(2,1)S(1)} collective-permute-done((bf16[1,64,512]{2,1,0:T(8,128)(2,1)S(1)}, bf16[1,64,512]{2,1,0:T(8,128)(2,1)S(1)}, u32[]{:S(2)}, u32[]{:S(2)}) %collective-permute-start.14) | collective-permute-done | bytes 65568 | tf_op jit(solution)/shard_map/ppermute | solution.py:526
  47.0 0.1 collective-permute-start.15
  47.1 1.7 %backward.1 = bf16[4,4,2,8,512]{4,3,2,1,0:T(8,128)(2,1)} custom-call(bf16[3,4,2,5,2,16,256]{6,5,4,3,2,1,0:T(8,128)(2,1)S(1)} %assemble.1.refs_2_.windows, bf16[4,4,2,8,512]{4,3,2,1,0:T(8,128)(2,1)S(1)} %get-tuple-element.36.mask, bf16[3072,256]{1,0:T(8,128)(2,1)S(1)} %get-tuple-element.63.toeplitz, bf16[1,64,512]{2,1,0:T(8,128)(2,1)S(1)} %sum.7.after), custom_call_target="tpu_custom_call" | custom-call | tf_op jit(solution)/shard_map/backward/pallas_call | solution.py:699
  48.7 2.6 %collective-permute-done.15 = bf16[1,64,512]{2,1,0:T(8,128)(2,1)S(1)} collective-permute-done((bf16[1,64,512]{2,1,0:T(8,128)(2,1)S(1)}, bf16[1,64,512]{2,1,0:T(8,128)(2,1)S(1)}, u32[]{:S(2)}, u32[]{:S(2)}) %collective-permute-start.15) | collective-permute-done | bytes 65568 | tf_op jit(solution)/shard_map/ppermute | solution.py:526
  51.3 0.7 %finish.1 = (f32[64,432]{1,0:T(8,128)}, f32[1,16]{1,0:T(1,128)}) custom-call(bf16[64,512]{1,0:T(8,128)(2,1)S(1)} %bitcast.13, bf16[64,512]{1,0:T(8,128)(2,1)S(1)} %bitcast.14), custom_call_target="tpu_custom_call" | custom-call | tf_op jit(solution)/shard_map/finish/pallas_call | solution.py:708
  (4 shorter events, 0.1 us)
Async XLA Ops:
  3.4 8.7 %collective-permute-start.1 = (bf16[64,512]{1,0:T(8,128)(2,1)S(1)}, bf16[64,512]{1,0:T(8,128)(2,1)S(1)}, u32[]{:S(2)}, u32[]{:S(2)}) collective-permute-start(bf16[64,512]{1,0:T(8,128)(2,1)S(1)} %get-tuple-element.37.refs_0_), channel_id=1, source_target_pairs={{0,2},{1,3},{2,0},{3,1},{4,6},{5,7},{6,4},{7,5},{8,10},{9,11},{10,... | collective-permute-start | bytes 196616 | tf_op jit(solution)/shard_map/ppermute | solution.py:516
  6.4 10.1 %collective-permute-start = (bf16[64,512]{1,0:T(8,128)(2,1)S(1)}, bf16[64,512]{1,0:T(8,128)(2,1)S(1)}, u32[]{:S(2)}, u32[]{:S(2)}) collective-permute-start(bf16[64,512]{1,0:T(8,128)(2,1)S(1)} %get-tuple-element.37.refs_0_), channel_id=1, source_target_pairs={{0,1},{1,0},{2,3},{3,2},{4,5},{5,4},{6,7},{7,6},{8,9},{9,8},{10,11... | collective-permute-start | bytes 196616 | tf_op jit(solution)/shard_map/ppermute | solution.py:516
  6.4 12.1 %collective-permute-start.3 = (bf16[384,128]{1,0:T(8,128)(2,1)S(1)}, bf16[384,128]{1,0:T(8,128)(2,1)S(1)}, u32[]{:S(2)}, u32[]{:S(2)}) collective-permute-start(bf16[384,128]{1,0:T(8,128)(2,1)S(1)} %get-tuple-element.43), channel_id=1, source_target_pairs={{4,8},{8,4},{12,16},{16,12},{20,24},{24,20},{9,17},{17,9},{13,21},... | collective-permute-start | bytes 294920 | tf_op jit(solution)/shard_map/ppermute | solution.py:526
  7.1 11.4 %collective-permute-start.4 = (bf16[384,128]{1,0:T(8,128)(2,1)S(1)}, bf16[384,128]{1,0:T(8,128)(2,1)S(1)}, u32[]{:S(2)}, u32[]{:S(2)}) collective-permute-start(bf16[384,128]{1,0:T(8,128)(2,1)S(1)} %get-tuple-element.44), channel_id=1, source_target_pairs={{8,16},{16,8},{12,20},{20,12},{5,9},{9,5},{13,17},{17,13},{21,25},... | collective-permute-start | bytes 294920 | tf_op jit(solution)/shard_map/ppermute | solution.py:526
  7.8 10.8 %collective-permute-start.5 = (bf16[384,128]{1,0:T(8,128)(2,1)S(1)}, bf16[384,128]{1,0:T(8,128)(2,1)S(1)}, u32[]{:S(2)}, u32[]{:S(2)}) collective-permute-start(bf16[384,128]{1,0:T(8,128)(2,1)S(1)} %get-tuple-element.45), channel_id=1, source_target_pairs={{0,4},{4,0},{8,12},{12,8},{16,20},{20,16},{24,28},{28,24},{1,9},{9... | collective-permute-start | bytes 294920 | tf_op jit(solution)/shard_map/ppermute | solution.py:526
  12.1 7.0 %collective-permute-start.6 = (bf16[384,128]{1,0:T(8,128)(2,1)S(1)}, bf16[384,128]{1,0:T(8,128)(2,1)S(1)}, u32[]{:S(2)}, u32[]{:S(2)}) collective-permute-start(bf16[384,128]{1,0:T(8,128)(2,1)S(1)} %get-tuple-element.46), channel_id=1, source_target_pairs={{0,8},{8,0},{4,12},{12,4},{16,24},{24,16},{20,28},{28,20},{1,5},{5... | collective-permute-start | bytes 294920 | tf_op jit(solution)/shard_map/ppermute | solution.py:526
  16.5 1.3 %collective-permute-start.2 = (bf16[64,512]{1,0:T(8,128)(2,1)S(1)}, bf16[64,512]{1,0:T(8,128)(2,1)S(1)}, u32[]{:S(2)}, u32[]{:S(2)}) collective-permute-start(bf16[64,512]{1,0:T(8,128)(2,1)S(1)} %collective-permute-done.1.refs_2_), channel_id=1, source_target_pairs={{0,1},{1,0},{2,3},{3,2},{4,5},{5,4},{6,7},{7,6},{8,9},{9,8},{10,11... | collective-permute-start | bytes 196616 | tf_op jit(solution)/shard_map/ppermute | solution.py:516
  25.1 1.4 %collective-permute-start.7 = (bf16[2,64,512]{2,1,0:T(8,128)(2,1)S(1)}, bf16[2,64,512]{2,1,0:T(8,128)(2,1)S(1)}, u32[]{:S(2)}, u32[]{:S(2)}) collective-permute-start(bf16[2,64,512]{2,1,0:T(8,128)(2,1)S(1)} %get-tuple-element.51), channel_id=1, source_target_pairs={{0,1},{1,0},{2,3},{3,2},{4,5},{5,4},{6,7},{7,6},{8,9},{9,8},{10,11... | collective-permute-start | bytes 393224 | tf_op jit(solution)/shard_map/ppermute | solution.py:516
  26.6 4.3 %collective-permute-start.8 = (bf16[1,64,512]{2,1,0:T(8,128)(2,1)S(1)}, bf16[1,64,512]{2,1,0:T(8,128)(2,1)S(1)}, u32[]{:S(2)}, u32[]{:S(2)}) collective-permute-start(bf16[1,64,512]{2,1,0:T(8,128)(2,1)S(1)} %get-tuple-element.53), channel_id=1, source_target_pairs={{0,2},{1,3},{2,0},{3,1},{4,6},{5,7},{6,4},{7,5},{8,10},{9,11},{10,... | collective-permute-start | bytes 196616 | tf_op jit(solution)/shard_map/ppermute | solution.py:516
  30.9 9.5 %collective-permute-start.11 = (bf16[384,128]{1,0:T(8,128)(2,1)S(1)}, bf16[384,128]{1,0:T(8,128)(2,1)S(1)}, u32[]{:S(2)}, u32[]{:S(2)}) collective-permute-start(bf16[384,128]{1,0:T(8,128)(2,1)S(1)} %get-tuple-element.60), channel_id=1, source_target_pairs={{0,4},{4,0},{8,12},{12,8},{16,20},{20,16},{24,28},{28,24},{1,9},{9... | collective-permute-start | bytes 294920 | tf_op jit(solution)/shard_map/ppermute | solution.py:526
  31.5 8.9 %collective-permute-start.13 = (bf16[1,64,512]{2,1,0:T(8,128)(2,1)S(1)}, bf16[1,64,512]{2,1,0:T(8,128)(2,1)S(1)}, u32[]{:S(2)}, u32[]{:S(2)}) collective-permute-start(bf16[1,64,512]{2,1,0:T(8,128)(2,1)S(1)} %get-tuple-element.62.refs_0_), channel_id=1, source_target_pairs={{0,8},{4,12},{8,0},{12,4},{16,24},{20,28},{24,16},{28,20},{1,5},{5... | collective-permute-start | bytes 196616 | tf_op jit(solution)/shard_map/ppermute | solution.py:526
  33.9 8.1 %collective-permute-start.9 = (bf16[384,128]{1,0:T(8,128)(2,1)S(1)}, bf16[384,128]{1,0:T(8,128)(2,1)S(1)}, u32[]{:S(2)}, u32[]{:S(2)}) collective-permute-start(bf16[384,128]{1,0:T(8,128)(2,1)S(1)} %get-tuple-element.58), channel_id=1, source_target_pairs={{4,8},{8,4},{12,16},{16,12},{20,24},{24,20},{9,17},{17,9},{13,21},... | collective-permute-start | bytes 294920 | tf_op jit(solution)/shard_map/ppermute | solution.py:526
  34.6 7.4 %collective-permute-start.10 = (bf16[384,128]{1,0:T(8,128)(2,1)S(1)}, bf16[384,128]{1,0:T(8,128)(2,1)S(1)}, u32[]{:S(2)}, u32[]{:S(2)}) collective-permute-start(bf16[384,128]{1,0:T(8,128)(2,1)S(1)} %get-tuple-element.59), channel_id=1, source_target_pairs={{8,16},{16,8},{12,20},{20,12},{5,9},{9,5},{13,17},{17,13},{21,25},... | collective-permute-start | bytes 294920 | tf_op jit(solution)/shard_map/ppermute | solution.py:526
  35.3 7.7 %collective-permute-start.12 = (bf16[384,128]{1,0:T(8,128)(2,1)S(1)}, bf16[384,128]{1,0:T(8,128)(2,1)S(1)}, u32[]{:S(2)}, u32[]{:S(2)}) collective-permute-start(bf16[384,128]{1,0:T(8,128)(2,1)S(1)} %get-tuple-element.61), channel_id=1, source_target_pairs={{0,8},{8,0},{4,12},{12,4},{16,24},{24,16},{20,28},{28,20},{1,5},{5... | collective-permute-start | bytes 294920 | tf_op jit(solution)/shard_map/ppermute | solution.py:526
  40.4 6.5 %collective-permute-start.14 = (bf16[1,64,512]{2,1,0:T(8,128)(2,1)S(1)}, bf16[1,64,512]{2,1,0:T(8,128)(2,1)S(1)}, u32[]{:S(2)}, u32[]{:S(2)}) collective-permute-start(bf16[1,64,512]{2,1,0:T(8,128)(2,1)S(1)} %sum.6.after.refs_0_), channel_id=1, source_target_pairs={{0,16},{4,20},{8,24},{12,28},{16,0},{20,4},{24,8},{28,12},{1,9},{5... | collective-permute-start | bytes 196616 | tf_op jit(solution)/shard_map/ppermute | solution.py:526
  47.0 4.3 %collective-permute-start.15 = (bf16[1,64,512]{2,1,0:T(8,128)(2,1)S(1)}, bf16[1,64,512]{2,1,0:T(8,128)(2,1)S(1)}, u32[]{:S(2)}, u32[]{:S(2)}) collective-permute-start(bf16[1,64,512]{2,1,0:T(8,128)(2,1)S(1)} %sum.7.after), channel_id=1, source_target_pairs={{0,4},{4,0},{8,12},{12,8},{16,20},{20,16},{24,28},{28,24},{1,17},{... | collective-permute-start | bytes 196616 | tf_op jit(solution)/shard_map/ppermute | solution.py:526

commit v14 on v10

--- a/solution.py
+++ b/solution.py
@@ -388,7 +388,8 @@
 def forward_kernel(
     masked, mask, cotangent_hbm, toeplitz, bias, rows, send, r0, r1, r2, r3, r4,
     block_out, grad_out, keep_out, give_out, u0, u1, u2, u3, u4,
-    table, windows, sides, walls, flat, shifted, values, flipped, cotangent, sem, *, shard,
+    table, windows, sides, walls, flat, shifted, values, flipped, cotangent, product, sem,
+    *, shard,
 ):
     fetch = pltpu.make_async_copy(cotangent_hbm, cotangent, sem)
     fetch.start()
@@ -404,27 +405,51 @@
     values[:, bricks * 64 :, :] = jnp.zeros((4, 64, LANES), F32)
 
     bias_row = jnp.concatenate([bias_row, bias_row], axis=1)
-    total = jnp.dot(all_taps(windows), toeplitz[...], preferred_element_type=F32)
-    rows_of_chunk = total.shape[0] // 4
-    bias_sum = jnp.zeros((8, 256), F32)
-    for q in range(4):
-        p = total[q * rows_of_chunk : (q + 1) * rows_of_chunk] + bias_row
-        active = chunk_of(mask, q)
-        sig = jax.nn.sigmoid(p)
-        put_chunk(block_out, q, p * sig * active)
-        grad = (chunk_of(cotangent, q) * sig * (1.0 + p * (1.0 - sig)) * active).astype(BF16)
-        wide = grad.astype(F32)
-        put_chunk(grad_out, q, wide)
-        for n, (brick, i) in enumerate(chunk_places(bricks)):
-            for x in range(2):
-                at = brick * 64 + (2 * i + x) * 8
-                values[q, at : at + 8, :] = wide[
-                    8 * n : 8 * n + 8, x * LANES : (x + 1) * LANES
-                ]
-        flipped[:, q * rows_of_chunk : (q + 1) * rows_of_chunk] = jnp.transpose(wide).astype(BF16)
-        bias_sum += jnp.sum(wide.reshape(-1, 8, 256), axis=0)
+    product[...] = jnp.dot(all_taps(windows), toeplitz[...], preferred_element_type=F32)
+    rows_of_chunk = product.shape[0] // 4
+
+    def one_chunk(q, bias_sum):
+        lanes = pl.ds(pl.multiple_of(q * LANES, LANES), LANES)
+        for pair in range(pairs):
+            for i in range(4):
+                at = pl.multiple_of(q * rows_of_chunk + (pair * 4 + i) * 16, 16)
+                p = product[pl.ds(at, 16), :] + bias_row
+
+                def both(ref, i=i, pair=pair):
+                    return jnp.concatenate(
+                        [
+                            jnp.concatenate(
+                                [ref[2 * pair + b, i, x, :, lanes].astype(F32) for b in range(2)],
+                                axis=0,
+                            )
+                            for x in range(2)
+                        ],
+                        axis=1,
+                    )
+
+                active = both(mask)
+                sig = jax.nn.sigmoid(p)
+                out = p * sig * active
+                grad = both(cotangent) * sig * (1.0 + p * (1.0 - sig)) * active
+                wide = grad.astype(BF16).astype(F32)
+                product[pl.ds(at, 16), :] = wide
+                bias_sum += wide[0:8] + wide[8:16]
+                for b in range(2):
+                    brick = 2 * pair + b
+                    for x in range(2):
+                        rows_, half = slice(8 * b, 8 * b + 8), slice(x * LANES, (x + 1) * LANES)
+                        block_out[brick, i, x, :, lanes] = out[rows_, half].astype(BF16)
+                        grad_out[brick, i, x, :, lanes] = wide[rows_, half].astype(BF16)
+                        to = brick * 64 + (2 * i + x) * 8
+                        values[q, to : to + 8, :] = wide[rows_, half]
+        return bias_sum
+
+    bias_sum = lax.fori_loop(0, 4, one_chunk, jnp.zeros((8, 256), F32))
     bias_sum = bias_sum[:, 0:LANES] + bias_sum[:, LANES:]
     pack_units(values, send, (u0, u1, u2, u3, u4))
+    for q in range(4):
+        rows_of_q = slice(q * rows_of_chunk, (q + 1) * rows_of_chunk)
+        flipped[:, rows_of_q] = jnp.transpose(product[rows_of_q, :]).astype(BF16)
 
     for ae in range(9):
         a, e = ae // 3, ae % 3
@@ -652,6 +677,7 @@
             pltpu.VMEM((4, (bricks + 1) * 64, LANES), F32),
             pltpu.VMEM((256, bricks * LANES), BF16),
             pltpu.VMEM(grid_shape, BF16),
+            pltpu.VMEM((bricks * LANES, 256), F32),
             pltpu.SemaphoreType.DMA,
         ],
         compiler_params=params,

time: 50.6 us -> 50.9 us (level)
  no operation moved by 1% of the time
where the time goes in v14:
time: 50.9 us; the launch traced here: 50.7 us
  starting transfers between devices  25.3 us (50%)
  Pallas kernels  12.7 us (25%)
  waiting for transfers between devices  11.3 us (22%)
  between operations  1.4 us (3%)
    ppermute x11, starting transfers between devices, by_parity(): return lax.ppermute(block, ('space', 'dp'), pairs)  21.6 us
    pallas_call x1, Pallas kernels, body(): pl.pallas_call(functools.partial(forward_kernel, shard=shard), name='forw...  6.34 us
    ppermute x5, waiting for transfers between devices, swapped(): lax.ppermute(block, axis, [(i, i ^ bit) for i in range(lax.axis_size(axis...  5.64 us
    ppermute x11, waiting for transfers between devices, by_parity(): return lax.ppermute(block, ('space', 'dp'), pairs)  5.62 us
    ppermute x5, starting transfers between devices, swapped(): lax.ppermute(block, axis, [(i, i ^ bit) for i in range(lax.axis_size(axis...  3.69 us
    pallas_call x1, Pallas kernels, body(): pl.pallas_call(prepare_kernel, name='prepare', out_shape=[grid_type, grid...  2.15 us
    pallas_call x1, Pallas kernels, body(): pl.pallas_call(backward_kernel, name='backward', out_shape=grid_type, in_...  1.68 us
    pallas_call x1, Pallas kernels, body(): pl.pallas_call(assemble_kernel, name='assemble', out_shape=jax.ShapeDtype...  1.07 us
  transfers between devices with their start and end apart: 16, of which 7 were waited for; matrix products, arithmetic and copies ran while one was open for 0% of the time, Pallas kernels for 7%

profile of v14, /device:TPU:0, one launch (start us, length us, event | category | flops | bytes accessed | tf_op | source)
XLA Modules:
  0.0 50.7 jit_solution(2796581615488153006)
XLA Ops:
  1.3 2.1 %prepare.1 = (bf16[4,4,2,8,512]{4,3,2,1,0:T(8,128)(2,1)S(1)}, bf16[4,4,2,8,512]{4,3,2,1,0:T(8,128)(2,1)S(1)}, s32[4,26]{1,0:T(4,128)S(1)}, s32[5,1,12]{2,1,0:T(1...) custom-call(bf16[4,4,2,8,512]{4,3,2,1,0:T(8,128)(2,1)} %bitcast.17, ...), custom_call_target="tpu_custom_call" | custom-call | tf_op jit(solution)/shard_map/prepare/pallas_call | solution.py:595
  3.4 3.0 %collective-permute-start.1 = (bf16[64,512]{1,0:T(8,128)(2,1)S(1)}, bf16[64,512]{1,0:T(8,128)(2,1)S(1)}, u32[]{:S(2)}, u32[]{:S(2)}) collective-permute-start(bf16[64,512]{1,0:T(8,128)(2,1)S(1)} %get-tuple-element.36.refs_0_), channel_id=1, source_target_pairs={{0,2},{1,3},{2,0},{3,1},{4,6},{5,7},{6,4},{7,5},{8,10},{9,11},{10,... | collective-permute-start | bytes 196616 | tf_op jit(solution)/shard_map/ppermute | solution.py:541
  6.4 0.0 collective-permute-start
  6.4 0.7 %collective-permute-start.3 = (bf16[384,128]{1,0:T(8,128)(2,1)S(1)}, bf16[384,128]{1,0:T(8,128)(2,1)S(1)}, u32[]{:S(2)}, u32[]{:S(2)}) collective-permute-start(bf16[384,128]{1,0:T(8,128)(2,1)S(1)} %get-tuple-element.42), channel_id=1, source_target_pairs={{4,8},{8,4},{12,16},{16,12},{20,24},{24,20},{9,17},{17,9},{13,21},... | collective-permute-start | bytes 294920 | tf_op jit(solution)/shard_map/ppermute | solution.py:551
  7.1 0.7 %collective-permute-start.4 = (bf16[384,128]{1,0:T(8,128)(2,1)S(1)}, bf16[384,128]{1,0:T(8,128)(2,1)S(1)}, u32[]{:S(2)}, u32[]{:S(2)}) collective-permute-start(bf16[384,128]{1,0:T(8,128)(2,1)S(1)} %get-tuple-element.43), channel_id=1, source_target_pairs={{8,16},{16,8},{12,20},{20,12},{5,9},{9,5},{13,17},{17,13},{21,25},... | collective-permute-start | bytes 294920 | tf_op jit(solution)/shard_map/ppermute | solution.py:551
  7.8 4.3 %collective-permute-start.5 = (bf16[384,128]{1,0:T(8,128)(2,1)S(1)}, bf16[384,128]{1,0:T(8,128)(2,1)S(1)}, u32[]{:S(2)}, u32[]{:S(2)}) collective-permute-start(bf16[384,128]{1,0:T(8,128)(2,1)S(1)} %get-tuple-element.44), channel_id=1, source_target_pairs={{0,4},{4,0},{8,12},{12,8},{16,20},{20,16},{24,28},{28,24},{1,9},{9... | collective-permute-start | bytes 294920 | tf_op jit(solution)/shard_map/ppermute | solution.py:551
  12.1 0.0 collective-permute-done.1.refs_2_
  12.1 4.4 %collective-permute-start.6 = (bf16[384,128]{1,0:T(8,128)(2,1)S(1)}, bf16[384,128]{1,0:T(8,128)(2,1)S(1)}, u32[]{:S(2)}, u32[]{:S(2)}) collective-permute-start(bf16[384,128]{1,0:T(8,128)(2,1)S(1)} %get-tuple-element.45), channel_id=1, source_target_pairs={{0,8},{8,0},{4,12},{12,4},{16,24},{24,16},{20,28},{28,20},{1,5},{5... | collective-permute-start | bytes 294920 | tf_op jit(solution)/shard_map/ppermute | solution.py:551
  16.5 0.0 collective-permute-done.refs_1_
  16.5 0.0 collective-permute-start.2
  16.5 1.3 %collective-permute-done.2.refs_3_ = bf16[64,512]{1,0:T(8,128)(2,1)S(1)} collective-permute-done((bf16[64,512]{1,0:T(8,128)(2,1)S(1)}, bf16[64,512]{1,0:T(8,128)(2,1)S(1)}, u32[]{:S(2)}, u32[]{:S(2)}) %collective-permute-start.2) | collective-permute-done | bytes 65568 | tf_op jit(solution)/shard_map/ppermute | solution.py:541
  17.8 0.7 %weights.1 = (bf16[3072,256]{1,0:T(8,128)(2,1)S(1)}, bf16[3072,256]{1,0:T(8,128)(2,1)S(1)}, f32[8,128]{1,0:T(8,128)S(1)}) custom-call(bf16[64,512]{1,0:T(8,128)(2,1)S(1)} %get-tuple-element.36.refs_0_, bf16[64,512]{1,0:T(8,128)(2,1)S(1)} %collective-permute-done.refs_1_, bf16[64,512]{1,0:T(8,128)(2,1)S(1)} %collective-permute-done.1.refs_2_, ...), custom_call_target="tpu_custom_call" | custom-call | tf_op jit(solution)/shard_map/weights/pallas_call | solution.py:643
  18.5 0.0 collective-permute-done.3.r1
  18.5 0.0 collective-permute-done.4.r2
  18.5 0.0 collective-permute-done.5.r3
  18.5 0.6 %collective-permute-done.6.r4 = bf16[384,128]{1,0:T(8,128)(2,1)S(1)} collective-permute-done((bf16[384,128]{1,0:T(8,128)(2,1)S(1)}, bf16[384,128]{1,0:T(8,128)(2,1)S(1)}, u32[]{:S(2)}, u32[]{:S(2)}) %collective-permute-start.6) | collective-permute-done | bytes 98336 | tf_op jit(solution)/shard_map/ppermute | solution.py:551
  19.1 6.3 %forward.1 = (bf16[4,4,2,8,512]{4,3,2,1,0:T(8,128)(2,1)}, bf16[4,4,2,8,512]{4,3,2,1,0:T(8,128)(2,1)S(1)}, bf16[2,64,512]{2,1,0:T(8,128)(2,1)S(1)}, bf16[2,64,512...) custom-call(bf16[4,4,2,8,512]{4,3,2,1,0:T(8,128)(2,1)S(1)} %get-tupl, ...), custom_call_target="tpu_custom_call" | custom-call | tf_op jit(solution)/shard_map/forward/pallas_call | solution.py:662
  25.5 0.1 collective-permute-start.8
  25.5 0.7 %collective-permute-start.7 = (bf16[384,128]{1,0:T(8,128)(2,1)S(1)}, bf16[384,128]{1,0:T(8,128)(2,1)S(1)}, u32[]{:S(2)}, u32[]{:S(2)}) collective-permute-start(bf16[384,128]{1,0:T(8,128)(2,1)S(1)} %get-tuple-element.49), channel_id=1, source_target_pairs={{4,8},{8,4},{12,16},{16,12},{20,24},{24,20},{9,17},{17,9},{13,21},... | collective-permute-start | bytes 294920 | tf_op jit(solution)/shard_map/ppermute | solution.py:551
  26.2 0.7 %collective-permute-done.8.refs_1_ = bf16[2,64,512]{2,1,0:T(8,128)(2,1)S(1)} collective-permute-done((bf16[2,64,512]{2,1,0:T(8,128)(2,1)S(1)}, bf16[2,64,512]{2,1,0:T(8,128)(2,1)S(1)}, u32[]{:S(2)}, u32[]{:S(2)}) %collective-permute-start.8) | collective-permute-done | bytes 131104 | tf_op jit(solution)/shard_map/ppermute | solution.py:541
  26.9 0.6 %collective-permute-start.10 = (bf16[1,64,512]{2,1,0:T(8,128)(2,1)S(1)}, bf16[1,64,512]{2,1,0:T(8,128)(2,1)S(1)}, u32[]{:S(2)}, u32[]{:S(2)}) collective-permute-start(bf16[1,64,512]{2,1,0:T(8,128)(2,1)S(1)} %get-tuple-element.55), channel_id=1, source_target_pairs={{0,2},{1,3},{2,0},{3,1},{4,6},{5,7},{6,4},{7,5},{8,10},{9,11},{10,... | collective-permute-start | bytes 196616 | tf_op jit(solution)/shard_map/ppermute | solution.py:541
  27.5 0.0 collective-permute-done.7.refs_2_.r1
  27.5 3.7 %collective-permute-done.10.refs_1_ = bf16[1,64,512]{2,1,0:T(8,128)(2,1)S(1)} collective-permute-done((bf16[1,64,512]{2,1,0:T(8,128)(2,1)S(1)}, bf16[1,64,512]{2,1,0:T(8,128)(2,1)S(1)}, u32[]{:S(2)}, u32[]{:S(2)}) %collective-permute-start.10) | collective-permute-done | bytes 65568 | tf_op jit(solution)/shard_map/ppermute | solution.py:541
  31.3 4.1 %collective-permute-start.11 = (bf16[384,128]{1,0:T(8,128)(2,1)S(1)}, bf16[384,128]{1,0:T(8,128)(2,1)S(1)}, u32[]{:S(2)}, u32[]{:S(2)}) collective-permute-start(bf16[384,128]{1,0:T(8,128)(2,1)S(1)} %get-tuple-element.58), channel_id=1, source_target_pairs={{0,4},{4,0},{8,12},{12,8},{16,20},{20,16},{24,28},{28,24},{1,9},{9... | collective-permute-start | bytes 294920 | tf_op jit(solution)/shard_map/ppermute | solution.py:551
  35.4 0.1 collective-permute-start.13
  35.5 0.7 %collective-permute-start.9 = (bf16[384,128]{1,0:T(8,128)(2,1)S(1)}, bf16[384,128]{1,0:T(8,128)(2,1)S(1)}, u32[]{:S(2)}, u32[]{:S(2)}) collective-permute-start(bf16[384,128]{1,0:T(8,128)(2,1)S(1)} %get-tuple-element.53), channel_id=1, source_target_pairs={{8,16},{16,8},{12,20},{20,12},{5,9},{9,5},{13,17},{17,13},{21,25},... | collective-permute-start | bytes 294920 | tf_op jit(solution)/shard_map/ppermute | solution.py:551
  36.2 4.2 %collective-permute-start.12 = (bf16[384,128]{1,0:T(8,128)(2,1)S(1)}, bf16[384,128]{1,0:T(8,128)(2,1)S(1)}, u32[]{:S(2)}, u32[]{:S(2)}) collective-permute-start(bf16[384,128]{1,0:T(8,128)(2,1)S(1)} %get-tuple-element.59), channel_id=1, source_target_pairs={{0,8},{8,0},{4,12},{12,4},{16,24},{24,16},{20,28},{28,20},{1,5},{5... | collective-permute-start | bytes 294920 | tf_op jit(solution)/shard_map/ppermute | solution.py:551
  40.3 0.0 collective-permute-done.13.refs_1_
  40.3 0.0 collective-permute-done.11.refs_2_.r3
  40.3 0.2 collective-permute-start.14
  40.6 0.0 collective-permute-done.9.r2
  40.6 2.7 %collective-permute-done.12.r4 = bf16[384,128]{1,0:T(8,128)(2,1)S(1)} collective-permute-done((bf16[384,128]{1,0:T(8,128)(2,1)S(1)}, bf16[384,128]{1,0:T(8,128)(2,1)S(1)}, u32[]{:S(2)}, u32[]{:S(2)}) %collective-permute-start.12) | collective-permute-done | bytes 98336 | tf_op jit(solution)/shard_map/ppermute | solution.py:551
  43.3 1.1 %assemble.1.refs_2_.windows = bf16[3,4,2,5,2,16,256]{6,5,4,3,2,1,0:T(8,128)(2,1)S(1)} custom-call(bf16[4,4,2,8,512]{4,3,2,1,0:T(8,128)(2,1)S(1)} %get-tuple-element.47.grad, s32[4,26]{1,0:T(4,128)S(1)} %get-tuple-element.39.rows, bf16[384,128]{1,0:T(8,128)(2,1)S(1)} %get-tuple-element.48.r0, bf16[384,128]{1,0:T(8,128)(2,1)S(1)} %collective-permute-done.7.refs_2_.r1, ...), custom_call_target="tpu_custom_call" | custom-call | tf_op jit(solution)/shard_map/assemble/pallas_call | solution.py:713
  44.4 0.4 collective-permute-done.14.refs_1_
  44.8 1.7 %collective-permute-start.15 = (bf16[1,64,512]{2,1,0:T(8,128)(2,1)S(1)}, bf16[1,64,512]{2,1,0:T(8,128)(2,1)S(1)}, u32[]{:S(2)}, u32[]{:S(2)}) collective-permute-start(bf16[1,64,512]{2,1,0:T(8,128)(2,1)S(1)} %sum.7.after), channel_id=1, source_target_pairs={{0,16},{4,20},{8,24},{12,28},{16,0},{20,4},{24,8},{28,12},{1,5},{5... | collective-permute-start | bytes 196616 | tf_op jit(solution)/shard_map/ppermute | solution.py:551
  46.5 1.7 %backward.1 = bf16[4,4,2,8,512]{4,3,2,1,0:T(8,128)(2,1)} custom-call(bf16[3,4,2,5,2,16,256]{6,5,4,3,2,1,0:T(8,128)(2,1)S(1)} %assemble.1.refs_2_.windows, bf16[4,4,2,8,512]{4,3,2,1,0:T(8,128)(2,1)S(1)} %get-tuple-element.35.mask, bf16[3072,256]{1,0:T(8,128)(2,1)S(1)} %get-tuple-element.61.toeplitz, bf16[1,64,512]{2,1,0:T(8,128)(2,1)S(1)} %sum.7.after), custom_call_target="tpu_custom_call" | custom-call | tf_op jit(solution)/shard_map/backward/pallas_call | solution.py:727
  48.1 1.9 %collective-permute-done.15 = bf16[1,64,512]{2,1,0:T(8,128)(2,1)S(1)} collective-permute-done((bf16[1,64,512]{2,1,0:T(8,128)(2,1)S(1)}, bf16[1,64,512]{2,1,0:T(8,128)(2,1)S(1)}, u32[]{:S(2)}, u32[]{:S(2)}) %collective-permute-start.15) | collective-permute-done | bytes 65568 | tf_op jit(solution)/shard_map/ppermute | solution.py:551
  50.0 0.7 %finish.1 = (f32[64,432]{1,0:T(8,128)}, f32[1,16]{1,0:T(1,128)}) custom-call(bf16[64,512]{1,0:T(8,128)(2,1)S(1)} %bitcast.13, bf16[64,512]{1,0:T(8,128)(2,1)S(1)} %bitcast.14), custom_call_target="tpu_custom_call" | custom-call | tf_op jit(solution)/shard_map/finish/pallas_call | solution.py:736
  (4 shorter events, 0.1 us)
Async XLA Ops:
  3.4 8.7 %collective-permute-start.1 = (bf16[64,512]{1,0:T(8,128)(2,1)S(1)}, bf16[64,512]{1,0:T(8,128)(2,1)S(1)}, u32[]{:S(2)}, u32[]{:S(2)}) collective-permute-start(bf16[64,512]{1,0:T(8,128)(2,1)S(1)} %get-tuple-element.36.refs_0_), channel_id=1, source_target_pairs={{0,2},{1,3},{2,0},{3,1},{4,6},{5,7},{6,4},{7,5},{8,10},{9,11},{10,... | collective-permute-start | bytes 196616 | tf_op jit(solution)/shard_map/ppermute | solution.py:541
  6.4 10.1 %collective-permute-start = (bf16[64,512]{1,0:T(8,128)(2,1)S(1)}, bf16[64,512]{1,0:T(8,128)(2,1)S(1)}, u32[]{:S(2)}, u32[]{:S(2)}) collective-permute-start(bf16[64,512]{1,0:T(8,128)(2,1)S(1)} %get-tuple-element.36.refs_0_), channel_id=1, source_target_pairs={{0,1},{1,0},{2,3},{3,2},{4,5},{5,4},{6,7},{7,6},{8,9},{9,8},{10,11... | collective-permute-start | bytes 196616 | tf_op jit(solution)/shard_map/ppermute | solution.py:541
  6.4 12.1 %collective-permute-start.3 = (bf16[384,128]{1,0:T(8,128)(2,1)S(1)}, bf16[384,128]{1,0:T(8,128)(2,1)S(1)}, u32[]{:S(2)}, u32[]{:S(2)}) collective-permute-start(bf16[384,128]{1,0:T(8,128)(2,1)S(1)} %get-tuple-element.42), channel_id=1, source_target_pairs={{4,8},{8,4},{12,16},{16,12},{20,24},{24,20},{9,17},{17,9},{13,21},... | collective-permute-start | bytes 294920 | tf_op jit(solution)/shard_map/ppermute | solution.py:551
  7.1 11.4 %collective-permute-start.4 = (bf16[384,128]{1,0:T(8,128)(2,1)S(1)}, bf16[384,128]{1,0:T(8,128)(2,1)S(1)}, u32[]{:S(2)}, u32[]{:S(2)}) collective-permute-start(bf16[384,128]{1,0:T(8,128)(2,1)S(1)} %get-tuple-element.43), channel_id=1, source_target_pairs={{8,16},{16,8},{12,20},{20,12},{5,9},{9,5},{13,17},{17,13},{21,25},... | collective-permute-start | bytes 294920 | tf_op jit(solution)/shard_map/ppermute | solution.py:551
  7.8 10.8 %collective-permute-start.5 = (bf16[384,128]{1,0:T(8,128)(2,1)S(1)}, bf16[384,128]{1,0:T(8,128)(2,1)S(1)}, u32[]{:S(2)}, u32[]{:S(2)}) collective-permute-start(bf16[384,128]{1,0:T(8,128)(2,1)S(1)} %get-tuple-element.44), channel_id=1, source_target_pairs={{0,4},{4,0},{8,12},{12,8},{16,20},{20,16},{24,28},{28,24},{1,9},{9... | collective-permute-start | bytes 294920 | tf_op jit(solution)/shard_map/ppermute | solution.py:551
  12.1 7.0 %collective-permute-start.6 = (bf16[384,128]{1,0:T(8,128)(2,1)S(1)}, bf16[384,128]{1,0:T(8,128)(2,1)S(1)}, u32[]{:S(2)}, u32[]{:S(2)}) collective-permute-start(bf16[384,128]{1,0:T(8,128)(2,1)S(1)} %get-tuple-element.45), channel_id=1, source_target_pairs={{0,8},{8,0},{4,12},{12,4},{16,24},{24,16},{20,28},{28,20},{1,5},{5... | collective-permute-start | bytes 294920 | tf_op jit(solution)/shard_map/ppermute | solution.py:551
  16.5 1.3 %collective-permute-start.2 = (bf16[64,512]{1,0:T(8,128)(2,1)S(1)}, bf16[64,512]{1,0:T(8,128)(2,1)S(1)}, u32[]{:S(2)}, u32[]{:S(2)}) collective-permute-start(bf16[64,512]{1,0:T(8,128)(2,1)S(1)} %collective-permute-done.1.refs_2_), channel_id=1, source_target_pairs={{0,1},{1,0},{2,3},{3,2},{4,5},{5,4},{6,7},{7,6},{8,9},{9,8},{10,11... | collective-permute-start | bytes 196616 | tf_op jit(solution)/shard_map/ppermute | solution.py:541
  25.5 1.4 %collective-permute-start.8 = (bf16[2,64,512]{2,1,0:T(8,128)(2,1)S(1)}, bf16[2,64,512]{2,1,0:T(8,128)(2,1)S(1)}, u32[]{:S(2)}, u32[]{:S(2)}) collective-permute-start(bf16[2,64,512]{2,1,0:T(8,128)(2,1)S(1)} %get-tuple-element.51), channel_id=1, source_target_pairs={{0,1},{1,0},{2,3},{3,2},{4,5},{5,4},{6,7},{7,6},{8,9},{9,8},{10,11... | collective-permute-start | bytes 393224 | tf_op jit(solution)/shard_map/ppermute | solution.py:541
  25.5 2.0 %collective-permute-start.7 = (bf16[384,128]{1,0:T(8,128)(2,1)S(1)}, bf16[384,128]{1,0:T(8,128)(2,1)S(1)}, u32[]{:S(2)}, u32[]{:S(2)}) collective-permute-start(bf16[384,128]{1,0:T(8,128)(2,1)S(1)} %get-tuple-element.49), channel_id=1, source_target_pairs={{4,8},{8,4},{12,16},{16,12},{20,24},{24,20},{9,17},{17,9},{13,21},... | collective-permute-start | bytes 294920 | tf_op jit(solution)/shard_map/ppermute | solution.py:551
  26.9 4.3 %collective-permute-start.10 = (bf16[1,64,512]{2,1,0:T(8,128)(2,1)S(1)}, bf16[1,64,512]{2,1,0:T(8,128)(2,1)S(1)}, u32[]{:S(2)}, u32[]{:S(2)}) collective-permute-start(bf16[1,64,512]{2,1,0:T(8,128)(2,1)S(1)} %get-tuple-element.55), channel_id=1, source_target_pairs={{0,2},{1,3},{2,0},{3,1},{4,6},{5,7},{6,4},{7,5},{8,10},{9,11},{10,... | collective-permute-start | bytes 196616 | tf_op jit(solution)/shard_map/ppermute | solution.py:541
  31.3 9.1 %collective-permute-start.11 = (bf16[384,128]{1,0:T(8,128)(2,1)S(1)}, bf16[384,128]{1,0:T(8,128)(2,1)S(1)}, u32[]{:S(2)}, u32[]{:S(2)}) collective-permute-start(bf16[384,128]{1,0:T(8,128)(2,1)S(1)} %get-tuple-element.58), channel_id=1, source_target_pairs={{0,4},{4,0},{8,12},{12,8},{16,20},{20,16},{24,28},{28,24},{1,9},{9... | collective-permute-start | bytes 294920 | tf_op jit(solution)/shard_map/ppermute | solution.py:551
  35.4 4.9 %collective-permute-start.13 = (bf16[1,64,512]{2,1,0:T(8,128)(2,1)S(1)}, bf16[1,64,512]{2,1,0:T(8,128)(2,1)S(1)}, u32[]{:S(2)}, u32[]{:S(2)}) collective-permute-start(bf16[1,64,512]{2,1,0:T(8,128)(2,1)S(1)} %get-tuple-element.60.refs_0_), channel_id=1, source_target_pairs={{0,4},{4,0},{8,12},{12,8},{16,20},{20,16},{24,28},{28,24},{1,9},{5... | collective-permute-start | bytes 196616 | tf_op jit(solution)/shard_map/ppermute | solution.py:551
  35.5 5.1 %collective-permute-start.9 = (bf16[384,128]{1,0:T(8,128)(2,1)S(1)}, bf16[384,128]{1,0:T(8,128)(2,1)S(1)}, u32[]{:S(2)}, u32[]{:S(2)}) collective-permute-start(bf16[384,128]{1,0:T(8,128)(2,1)S(1)} %get-tuple-element.53), channel_id=1, source_target_pairs={{8,16},{16,8},{12,20},{20,12},{5,9},{9,5},{13,17},{17,13},{21,25},... | collective-permute-start | bytes 294920 | tf_op jit(solution)/shard_map/ppermute | solution.py:551
  36.2 7.1 %collective-permute-start.12 = (bf16[384,128]{1,0:T(8,128)(2,1)S(1)}, bf16[384,128]{1,0:T(8,128)(2,1)S(1)}, u32[]{:S(2)}, u32[]{:S(2)}) collective-permute-start(bf16[384,128]{1,0:T(8,128)(2,1)S(1)} %get-tuple-element.59), channel_id=1, source_target_pairs={{0,8},{8,0},{4,12},{12,4},{16,24},{24,16},{20,28},{28,20},{1,5},{5... | collective-permute-start | bytes 294920 | tf_op jit(solution)/shard_map/ppermute | solution.py:551
  40.3 4.4 %collective-permute-start.14 = (bf16[1,64,512]{2,1,0:T(8,128)(2,1)S(1)}, bf16[1,64,512]{2,1,0:T(8,128)(2,1)S(1)}, u32[]{:S(2)}, u32[]{:S(2)}) collective-permute-start(bf16[1,64,512]{2,1,0:T(8,128)(2,1)S(1)} %sum.6.after.refs_0_), channel_id=1, source_target_pairs={{0,8},{4,12},{8,0},{12,4},{16,24},{20,28},{24,16},{28,20},{1,17},{... | collective-permute-start | bytes 196616 | tf_op jit(solution)/shard_map/ppermute | solution.py:551
  44.8 5.2 %collective-permute-start.15 = (bf16[1,64,512]{2,1,0:T(8,128)(2,1)S(1)}, bf16[1,64,512]{2,1,0:T(8,128)(2,1)S(1)}, u32[]{:S(2)}, u32[]{:S(2)}) collective-permute-start(bf16[1,64,512]{2,1,0:T(8,128)(2,1)S(1)} %sum.7.after), channel_id=1, source_target_pairs={{0,16},{4,20},{8,24},{12,28},{16,0},{20,4},{24,8},{28,12},{1,5},{5... | collective-permute-start | bytes 196616 | tf_op jit(solution)/shard_map/ppermute | solution.py:551

commit v15 on v12

--- a/solution.py
+++ b/solution.py
@@ -542,7 +542,7 @@
     bits = []
     while 2 ** len(bits) < lax.axis_size("space"):
         bits.append(2 ** len(bits))
-    return list(zip(bits[1:] + bits[:1], bits))
+    return [(bit, bit) for bit in bits[1:] + bits[:1]]
 
 
 def stepped(total, step):

time: 51 us -> 51 us (level)
  waiting for transfers between devices: 13.3 us -> 12.7 us
    ppermute x11, starting transfers between devices: 20 us -> 20.5 us  [by_parity(): return lax.ppermute(block, ('space', 'dp'), pairs)]
    ppermute x11, waiting for transfers between devices: 7.62 us -> 7.1 us  [by_parity(): return lax.ppermute(block, ('space', 'dp'), pairs)]
where the time goes in v15:
time: 51 us; the launch traced here: 50.7 us
  starting transfers between devices  24.2 us (47%)
  waiting for transfers between devices  12.7 us (25%)
  Pallas kernels  12.4 us (24%)
  between operations  1.4 us (3%)
    ppermute x11, starting transfers between devices, by_parity(): return lax.ppermute(block, ('space', 'dp'), pairs)  20.5 us
    ppermute x11, waiting for transfers between devices, by_parity(): return lax.ppermute(block, ('space', 'dp'), pairs)  7.1 us
    pallas_call x1, Pallas kernels, body(): pl.pallas_call(functools.partial(forward_kernel, shard=shard), name='forw...  5.99 us
    ppermute x5, waiting for transfers between devices, swapped(): lax.ppermute(block, axis, [(i, i ^ bit) for i in range(lax.axis_size(axis...  5.64 us
    ppermute x5, starting transfers between devices, swapped(): lax.ppermute(block, axis, [(i, i ^ bit) for i in range(lax.axis_size(axis...  3.69 us
    pallas_call x1, Pallas kernels, body(): pl.pallas_call(prepare_kernel, name='prepare', out_shape=[grid_type, grid...  2.15 us
    pallas_call x1, Pallas kernels, body(): pl.pallas_call(backward_kernel, name='backward', out_shape=grid_type, in_...  1.68 us
    pallas_call x1, Pallas kernels, body(): pl.pallas_call(assemble_kernel, name='assemble', out_shape=jax.ShapeDtype...  1.07 us
  transfers between devices with their start and end apart: 16, of which 8 were waited for; matrix products, arithmetic and copies ran while one was open for 0% of the time, Pallas kernels for 7%

profile of v15, /device:TPU:0, one launch (start us, length us, event | category | flops | bytes accessed | tf_op | source)
XLA Modules:
  0.0 50.7 jit_solution(15505128943636805043)
XLA Ops:
  1.3 2.1 %prepare.1 = (bf16[4,4,2,8,512]{4,3,2,1,0:T(8,128)(2,1)S(1)}, bf16[4,4,2,8,512]{4,3,2,1,0:T(8,128)(2,1)S(1)}, s32[4,26]{1,0:T(4,128)S(1)}, s32[5,1,12]{2,1,0:T(1...) custom-call(bf16[4,4,2,8,512]{4,3,2,1,0:T(8,128)(2,1)} %bitcast.17, ...), custom_call_target="tpu_custom_call" | custom-call | tf_op jit(solution)/shard_map/prepare/pallas_call | solution.py:570
  3.4 3.0 %collective-permute-start.1 = (bf16[64,512]{1,0:T(8,128)(2,1)S(1)}, bf16[64,512]{1,0:T(8,128)(2,1)S(1)}, u32[]{:S(2)}, u32[]{:S(2)}) collective-permute-start(bf16[64,512]{1,0:T(8,128)(2,1)S(1)} %get-tuple-element.36.refs_0_), channel_id=1, source_target_pairs={{0,2},{1,3},{2,0},{3,1},{4,6},{5,7},{6,4},{7,5},{8,10},{9,11},{10,... | collective-permute-start | bytes 196616 | tf_op jit(solution)/shard_map/ppermute | solution.py:516
  6.4 0.0 collective-permute-start
  6.4 0.7 %collective-permute-start.3 = (bf16[384,128]{1,0:T(8,128)(2,1)S(1)}, bf16[384,128]{1,0:T(8,128)(2,1)S(1)}, u32[]{:S(2)}, u32[]{:S(2)}) collective-permute-start(bf16[384,128]{1,0:T(8,128)(2,1)S(1)} %get-tuple-element.42), channel_id=1, source_target_pairs={{4,8},{8,4},{12,16},{16,12},{20,24},{24,20},{9,17},{17,9},{13,21},... | collective-permute-start | bytes 294920 | tf_op jit(solution)/shard_map/ppermute | solution.py:526
  7.1 0.7 %collective-permute-start.4 = (bf16[384,128]{1,0:T(8,128)(2,1)S(1)}, bf16[384,128]{1,0:T(8,128)(2,1)S(1)}, u32[]{:S(2)}, u32[]{:S(2)}) collective-permute-start(bf16[384,128]{1,0:T(8,128)(2,1)S(1)} %get-tuple-element.43), channel_id=1, source_target_pairs={{8,16},{16,8},{12,20},{20,12},{5,9},{9,5},{13,17},{17,13},{21,25},... | collective-permute-start | bytes 294920 | tf_op jit(solution)/shard_map/ppermute | solution.py:526
  7.8 4.3 %collective-permute-start.5 = (bf16[384,128]{1,0:T(8,128)(2,1)S(1)}, bf16[384,128]{1,0:T(8,128)(2,1)S(1)}, u32[]{:S(2)}, u32[]{:S(2)}) collective-permute-start(bf16[384,128]{1,0:T(8,128)(2,1)S(1)} %get-tuple-element.44), channel_id=1, source_target_pairs={{0,4},{4,0},{8,12},{12,8},{16,20},{20,16},{24,28},{28,24},{1,9},{9... | collective-permute-start | bytes 294920 | tf_op jit(solution)/shard_map/ppermute | solution.py:526
  12.1 0.0 collective-permute-done.1.refs_2_
  12.1 4.4 %collective-permute-start.6 = (bf16[384,128]{1,0:T(8,128)(2,1)S(1)}, bf16[384,128]{1,0:T(8,128)(2,1)S(1)}, u32[]{:S(2)}, u32[]{:S(2)}) collective-permute-start(bf16[384,128]{1,0:T(8,128)(2,1)S(1)} %get-tuple-element.45), channel_id=1, source_target_pairs={{0,8},{8,0},{4,12},{12,4},{16,24},{24,16},{20,28},{28,20},{1,5},{5... | collective-permute-start | bytes 294920 | tf_op jit(solution)/shard_map/ppermute | solution.py:526
  16.5 0.0 collective-permute-done.refs_1_
  16.5 0.0 collective-permute-start.2
  16.5 1.3 %collective-permute-done.2.refs_3_ = bf16[64,512]{1,0:T(8,128)(2,1)S(1)} collective-permute-done((bf16[64,512]{1,0:T(8,128)(2,1)S(1)}, bf16[64,512]{1,0:T(8,128)(2,1)S(1)}, u32[]{:S(2)}, u32[]{:S(2)}) %collective-permute-start.2) | collective-permute-done | bytes 65568 | tf_op jit(solution)/shard_map/ppermute | solution.py:516
  17.8 0.7 %weights.1 = (bf16[3072,256]{1,0:T(8,128)(2,1)S(1)}, bf16[3072,256]{1,0:T(8,128)(2,1)S(1)}, f32[8,128]{1,0:T(8,128)S(1)}) custom-call(bf16[64,512]{1,0:T(8,128)(2,1)S(1)} %get-tuple-element.36.refs_0_, bf16[64,512]{1,0:T(8,128)(2,1)S(1)} %collective-permute-done.refs_1_, bf16[64,512]{1,0:T(8,128)(2,1)S(1)} %collective-permute-done.1.refs_2_, ...), custom_call_target="tpu_custom_call" | custom-call | tf_op jit(solution)/shard_map/weights/pallas_call | solution.py:618
  18.5 0.0 collective-permute-done.3.r1
  18.5 0.0 collective-permute-done.4.r2
  18.5 0.0 collective-permute-done.5.r3
  18.5 0.6 %collective-permute-done.6.r4 = bf16[384,128]{1,0:T(8,128)(2,1)S(1)} collective-permute-done((bf16[384,128]{1,0:T(8,128)(2,1)S(1)}, bf16[384,128]{1,0:T(8,128)(2,1)S(1)}, u32[]{:S(2)}, u32[]{:S(2)}) %collective-permute-start.6) | collective-permute-done | bytes 98336 | tf_op jit(solution)/shard_map/ppermute | solution.py:526
  19.1 6.0 %forward.1 = (bf16[4,4,2,8,512]{4,3,2,1,0:T(8,128)(2,1)}, bf16[4,4,2,8,512]{4,3,2,1,0:T(8,128)(2,1)S(1)}, bf16[2,64,512]{2,1,0:T(8,128)(2,1)S(1)}, bf16[2,64,512...) custom-call(bf16[4,4,2,8,512]{4,3,2,1,0:T(8,128)(2,1)S(1)} %get-tupl, ...), custom_call_target="tpu_custom_call" | custom-call | tf_op jit(solution)/shard_map/forward/pallas_call | solution.py:637
  25.1 0.1 collective-permute-start.8
  25.2 0.7 %collective-permute-start.7 = (bf16[384,128]{1,0:T(8,128)(2,1)S(1)}, bf16[384,128]{1,0:T(8,128)(2,1)S(1)}, u32[]{:S(2)}, u32[]{:S(2)}) collective-permute-start(bf16[384,128]{1,0:T(8,128)(2,1)S(1)} %get-tuple-element.49), channel_id=1, source_target_pairs={{4,8},{8,4},{12,16},{16,12},{20,24},{24,20},{9,17},{17,9},{13,21},... | collective-permute-start | bytes 294920 | tf_op jit(solution)/shard_map/ppermute | solution.py:526
  25.9 0.7 %collective-permute-done.8.refs_1_ = bf16[2,64,512]{2,1,0:T(8,128)(2,1)S(1)} collective-permute-done((bf16[2,64,512]{2,1,0:T(8,128)(2,1)S(1)}, bf16[2,64,512]{2,1,0:T(8,128)(2,1)S(1)}, u32[]{:S(2)}, u32[]{:S(2)}) %collective-permute-start.8) | collective-permute-done | bytes 131104 | tf_op jit(solution)/shard_map/ppermute | solution.py:516
  26.6 0.6 %collective-permute-start.10 = (bf16[1,64,512]{2,1,0:T(8,128)(2,1)S(1)}, bf16[1,64,512]{2,1,0:T(8,128)(2,1)S(1)}, u32[]{:S(2)}, u32[]{:S(2)}) collective-permute-start(bf16[1,64,512]{2,1,0:T(8,128)(2,1)S(1)} %get-tuple-element.55), channel_id=1, source_target_pairs={{0,2},{1,3},{2,0},{3,1},{4,6},{5,7},{6,4},{7,5},{8,10},{9,11},{10,... | collective-permute-start | bytes 196616 | tf_op jit(solution)/shard_map/ppermute | solution.py:516
  27.2 0.0 collective-permute-done.7.refs_2_.r1
  27.2 3.7 %collective-permute-done.10.refs_1_ = bf16[1,64,512]{2,1,0:T(8,128)(2,1)S(1)} collective-permute-done((bf16[1,64,512]{2,1,0:T(8,128)(2,1)S(1)}, bf16[1,64,512]{2,1,0:T(8,128)(2,1)S(1)}, u32[]{:S(2)}, u32[]{:S(2)}) %collective-permute-start.10) | collective-permute-done | bytes 65568 | tf_op jit(solution)/shard_map/ppermute | solution.py:516
  30.9 4.1 %collective-permute-start.11 = (bf16[384,128]{1,0:T(8,128)(2,1)S(1)}, bf16[384,128]{1,0:T(8,128)(2,1)S(1)}, u32[]{:S(2)}, u32[]{:S(2)}) collective-permute-start(bf16[384,128]{1,0:T(8,128)(2,1)S(1)} %get-tuple-element.58), channel_id=1, source_target_pairs={{0,4},{4,0},{8,12},{12,8},{16,20},{20,16},{24,28},{28,24},{1,9},{9... | collective-permute-start | bytes 294920 | tf_op jit(solution)/shard_map/ppermute | solution.py:526
  35.1 0.8 %collective-permute-start.13 = (bf16[1,64,512]{2,1,0:T(8,128)(2,1)S(1)}, bf16[1,64,512]{2,1,0:T(8,128)(2,1)S(1)}, u32[]{:S(2)}, u32[]{:S(2)}) collective-permute-start(bf16[1,64,512]{2,1,0:T(8,128)(2,1)S(1)} %get-tuple-element.60.refs_0_), channel_id=1, source_target_pairs={{0,8},{4,12},{8,0},{12,4},{16,24},{20,28},{24,16},{28,20},{1,9},{5... | collective-permute-start | bytes 196616 | tf_op jit(solution)/shard_map/ppermute | solution.py:526
  35.9 0.7 %collective-permute-start.9 = (bf16[384,128]{1,0:T(8,128)(2,1)S(1)}, bf16[384,128]{1,0:T(8,128)(2,1)S(1)}, u32[]{:S(2)}, u32[]{:S(2)}) collective-permute-start(bf16[384,128]{1,0:T(8,128)(2,1)S(1)} %get-tuple-element.53), channel_id=1, source_target_pairs={{8,16},{16,8},{12,20},{20,12},{5,9},{9,5},{13,17},{17,13},{21,25},... | collective-permute-start | bytes 294920 | tf_op jit(solution)/shard_map/ppermute | solution.py:526
  36.5 2.6 %collective-permute-start.12 = (bf16[384,128]{1,0:T(8,128)(2,1)S(1)}, bf16[384,128]{1,0:T(8,128)(2,1)S(1)}, u32[]{:S(2)}, u32[]{:S(2)}) collective-permute-start(bf16[384,128]{1,0:T(8,128)(2,1)S(1)} %get-tuple-element.59), channel_id=1, source_target_pairs={{0,8},{8,0},{4,12},{12,4},{16,24},{24,16},{20,28},{28,20},{1,5},{5... | collective-permute-start | bytes 294920 | tf_op jit(solution)/shard_map/ppermute | solution.py:526
  39.1 0.7 %collective-permute-done.13.refs_1_ = bf16[1,64,512]{2,1,0:T(8,128)(2,1)S(1)} collective-permute-done((bf16[1,64,512]{2,1,0:T(8,128)(2,1)S(1)}, bf16[1,64,512]{2,1,0:T(8,128)(2,1)S(1)}, u32[]{:S(2)}, u32[]{:S(2)}) %collective-permute-start.13) | collective-permute-done | bytes 65568 | tf_op jit(solution)/shard_map/ppermute | solution.py:526
  39.7 0.0 collective-permute-done.11.refs_2_.r3
  39.8 0.9 %collective-permute-start.14 = (bf16[1,64,512]{2,1,0:T(8,128)(2,1)S(1)}, bf16[1,64,512]{2,1,0:T(8,128)(2,1)S(1)}, u32[]{:S(2)}, u32[]{:S(2)}) collective-permute-start(bf16[1,64,512]{2,1,0:T(8,128)(2,1)S(1)} %sum.6.after.refs_0_), channel_id=1, source_target_pairs={{0,16},{4,20},{8,24},{12,28},{16,0},{20,4},{24,8},{28,12},{1,17},{... | collective-permute-start | bytes 196616 | tf_op jit(solution)/shard_map/ppermute | solution.py:526
  40.7 0.0 collective-permute-done.9.r2
  40.7 1.0 %collective-permute-done.12.r4 = bf16[384,128]{1,0:T(8,128)(2,1)S(1)} collective-permute-done((bf16[384,128]{1,0:T(8,128)(2,1)S(1)}, bf16[384,128]{1,0:T(8,128)(2,1)S(1)}, u32[]{:S(2)}, u32[]{:S(2)}) %collective-permute-start.12) | collective-permute-done | bytes 98336 | tf_op jit(solution)/shard_map/ppermute | solution.py:526
  41.7 1.1 %assemble.1.refs_2_.windows = bf16[3,4,2,5,2,16,256]{6,5,4,3,2,1,0:T(8,128)(2,1)S(1)} custom-call(bf16[4,4,2,8,512]{4,3,2,1,0:T(8,128)(2,1)S(1)} %get-tuple-element.47.grad, s32[4,26]{1,0:T(4,128)S(1)} %get-tuple-element.39.rows, bf16[384,128]{1,0:T(8,128)(2,1)S(1)} %get-tuple-element.48.r0, bf16[384,128]{1,0:T(8,128)(2,1)S(1)} %collective-permute-done.7.refs_2_.r1, ...), custom_call_target="tpu_custom_call" | custom-call | tf_op jit(solution)/shard_map/assemble/pallas_call | solution.py:687
  42.7 3.0 %collective-permute-done.14.refs_1_ = bf16[1,64,512]{2,1,0:T(8,128)(2,1)S(1)} collective-permute-done((bf16[1,64,512]{2,1,0:T(8,128)(2,1)S(1)}, bf16[1,64,512]{2,1,0:T(8,128)(2,1)S(1)}, u32[]{:S(2)}, u32[]{:S(2)}) %collective-permute-start.14) | collective-permute-done | bytes 65568 | tf_op jit(solution)/shard_map/ppermute | solution.py:526
  45.7 0.8 %collective-permute-start.15 = (bf16[1,64,512]{2,1,0:T(8,128)(2,1)S(1)}, bf16[1,64,512]{2,1,0:T(8,128)(2,1)S(1)}, u32[]{:S(2)}, u32[]{:S(2)}) collective-permute-start(bf16[1,64,512]{2,1,0:T(8,128)(2,1)S(1)} %sum.7.after), channel_id=1, source_target_pairs={{0,4},{4,0},{8,12},{12,8},{16,20},{20,16},{24,28},{28,24},{1,5},{5... | collective-permute-start | bytes 196616 | tf_op jit(solution)/shard_map/ppermute | solution.py:526
  46.5 1.7 %backward.1 = bf16[4,4,2,8,512]{4,3,2,1,0:T(8,128)(2,1)} custom-call(bf16[3,4,2,5,2,16,256]{6,5,4,3,2,1,0:T(8,128)(2,1)S(1)} %assemble.1.refs_2_.windows, bf16[4,4,2,8,512]{4,3,2,1,0:T(8,128)(2,1)S(1)} %get-tuple-element.35.mask, bf16[3072,256]{1,0:T(8,128)(2,1)S(1)} %get-tuple-element.61.toeplitz, bf16[1,64,512]{2,1,0:T(8,128)(2,1)S(1)} %sum.7.after), custom_call_target="tpu_custom_call" | custom-call | tf_op jit(solution)/shard_map/backward/pallas_call | solution.py:701
  48.2 1.9 %collective-permute-done.15 = bf16[1,64,512]{2,1,0:T(8,128)(2,1)S(1)} collective-permute-done((bf16[1,64,512]{2,1,0:T(8,128)(2,1)S(1)}, bf16[1,64,512]{2,1,0:T(8,128)(2,1)S(1)}, u32[]{:S(2)}, u32[]{:S(2)}) %collective-permute-start.15) | collective-permute-done | bytes 65568 | tf_op jit(solution)/shard_map/ppermute | solution.py:526
  50.1 0.7 %finish.1 = (f32[64,432]{1,0:T(8,128)}, f32[1,16]{1,0:T(1,128)}) custom-call(bf16[64,512]{1,0:T(8,128)(2,1)S(1)} %bitcast.13, bf16[64,512]{1,0:T(8,128)(2,1)S(1)} %bitcast.14), custom_call_target="tpu_custom_call" | custom-call | tf_op jit(solution)/shard_map/finish/pallas_call | solution.py:710
  (4 shorter events, 0.1 us)
Async XLA Ops:
  3.4 8.7 %collective-permute-start.1 = (bf16[64,512]{1,0:T(8,128)(2,1)S(1)}, bf16[64,512]{1,0:T(8,128)(2,1)S(1)}, u32[]{:S(2)}, u32[]{:S(2)}) collective-permute-start(bf16[64,512]{1,0:T(8,128)(2,1)S(1)} %get-tuple-element.36.refs_0_), channel_id=1, source_target_pairs={{0,2},{1,3},{2,0},{3,1},{4,6},{5,7},{6,4},{7,5},{8,10},{9,11},{10,... | collective-permute-start | bytes 196616 | tf_op jit(solution)/shard_map/ppermute | solution.py:516
  6.4 10.1 %collective-permute-start = (bf16[64,512]{1,0:T(8,128)(2,1)S(1)}, bf16[64,512]{1,0:T(8,128)(2,1)S(1)}, u32[]{:S(2)}, u32[]{:S(2)}) collective-permute-start(bf16[64,512]{1,0:T(8,128)(2,1)S(1)} %get-tuple-element.36.refs_0_), channel_id=1, source_target_pairs={{0,1},{1,0},{2,3},{3,2},{4,5},{5,4},{6,7},{7,6},{8,9},{9,8},{10,11... | collective-permute-start | bytes 196616 | tf_op jit(solution)/shard_map/ppermute | solution.py:516
  6.4 12.1 %collective-permute-start.3 = (bf16[384,128]{1,0:T(8,128)(2,1)S(1)}, bf16[384,128]{1,0:T(8,128)(2,1)S(1)}, u32[]{:S(2)}, u32[]{:S(2)}) collective-permute-start(bf16[384,128]{1,0:T(8,128)(2,1)S(1)} %get-tuple-element.42), channel_id=1, source_target_pairs={{4,8},{8,4},{12,16},{16,12},{20,24},{24,20},{9,17},{17,9},{13,21},... | collective-permute-start | bytes 294920 | tf_op jit(solution)/shard_map/ppermute | solution.py:526
  7.1 11.4 %collective-permute-start.4 = (bf16[384,128]{1,0:T(8,128)(2,1)S(1)}, bf16[384,128]{1,0:T(8,128)(2,1)S(1)}, u32[]{:S(2)}, u32[]{:S(2)}) collective-permute-start(bf16[384,128]{1,0:T(8,128)(2,1)S(1)} %get-tuple-element.43), channel_id=1, source_target_pairs={{8,16},{16,8},{12,20},{20,12},{5,9},{9,5},{13,17},{17,13},{21,25},... | collective-permute-start | bytes 294920 | tf_op jit(solution)/shard_map/ppermute | solution.py:526
  7.8 10.8 %collective-permute-start.5 = (bf16[384,128]{1,0:T(8,128)(2,1)S(1)}, bf16[384,128]{1,0:T(8,128)(2,1)S(1)}, u32[]{:S(2)}, u32[]{:S(2)}) collective-permute-start(bf16[384,128]{1,0:T(8,128)(2,1)S(1)} %get-tuple-element.44), channel_id=1, source_target_pairs={{0,4},{4,0},{8,12},{12,8},{16,20},{20,16},{24,28},{28,24},{1,9},{9... | collective-permute-start | bytes 294920 | tf_op jit(solution)/shard_map/ppermute | solution.py:526
  12.1 7.0 %collective-permute-start.6 = (bf16[384,128]{1,0:T(8,128)(2,1)S(1)}, bf16[384,128]{1,0:T(8,128)(2,1)S(1)}, u32[]{:S(2)}, u32[]{:S(2)}) collective-permute-start(bf16[384,128]{1,0:T(8,128)(2,1)S(1)} %get-tuple-element.45), channel_id=1, source_target_pairs={{0,8},{8,0},{4,12},{12,4},{16,24},{24,16},{20,28},{28,20},{1,5},{5... | collective-permute-start | bytes 294920 | tf_op jit(solution)/shard_map/ppermute | solution.py:526
  16.5 1.3 %collective-permute-start.2 = (bf16[64,512]{1,0:T(8,128)(2,1)S(1)}, bf16[64,512]{1,0:T(8,128)(2,1)S(1)}, u32[]{:S(2)}, u32[]{:S(2)}) collective-permute-start(bf16[64,512]{1,0:T(8,128)(2,1)S(1)} %collective-permute-done.1.refs_2_), channel_id=1, source_target_pairs={{0,1},{1,0},{2,3},{3,2},{4,5},{5,4},{6,7},{7,6},{8,9},{9,8},{10,11... | collective-permute-start | bytes 196616 | tf_op jit(solution)/shard_map/ppermute | solution.py:516
  25.1 1.4 %collective-permute-start.8 = (bf16[2,64,512]{2,1,0:T(8,128)(2,1)S(1)}, bf16[2,64,512]{2,1,0:T(8,128)(2,1)S(1)}, u32[]{:S(2)}, u32[]{:S(2)}) collective-permute-start(bf16[2,64,512]{2,1,0:T(8,128)(2,1)S(1)} %get-tuple-element.51), channel_id=1, source_target_pairs={{0,1},{1,0},{2,3},{3,2},{4,5},{5,4},{6,7},{7,6},{8,9},{9,8},{10,11... | collective-permute-start | bytes 393224 | tf_op jit(solution)/shard_map/ppermute | solution.py:516
  25.2 2.0 %collective-permute-start.7 = (bf16[384,128]{1,0:T(8,128)(2,1)S(1)}, bf16[384,128]{1,0:T(8,128)(2,1)S(1)}, u32[]{:S(2)}, u32[]{:S(2)}) collective-permute-start(bf16[384,128]{1,0:T(8,128)(2,1)S(1)} %get-tuple-element.49), channel_id=1, source_target_pairs={{4,8},{8,4},{12,16},{16,12},{20,24},{24,20},{9,17},{17,9},{13,21},... | collective-permute-start | bytes 294920 | tf_op jit(solution)/shard_map/ppermute | solution.py:526
  26.6 4.3 %collective-permute-start.10 = (bf16[1,64,512]{2,1,0:T(8,128)(2,1)S(1)}, bf16[1,64,512]{2,1,0:T(8,128)(2,1)S(1)}, u32[]{:S(2)}, u32[]{:S(2)}) collective-permute-start(bf16[1,64,512]{2,1,0:T(8,128)(2,1)S(1)} %get-tuple-element.55), channel_id=1, source_target_pairs={{0,2},{1,3},{2,0},{3,1},{4,6},{5,7},{6,4},{7,5},{8,10},{9,11},{10,... | collective-permute-start | bytes 196616 | tf_op jit(solution)/shard_map/ppermute | solution.py:516
  30.9 8.8 %collective-permute-start.11 = (bf16[384,128]{1,0:T(8,128)(2,1)S(1)}, bf16[384,128]{1,0:T(8,128)(2,1)S(1)}, u32[]{:S(2)}, u32[]{:S(2)}) collective-permute-start(bf16[384,128]{1,0:T(8,128)(2,1)S(1)} %get-tuple-element.58), channel_id=1, source_target_pairs={{0,4},{4,0},{8,12},{12,8},{16,20},{20,16},{24,28},{28,24},{1,9},{9... | collective-permute-start | bytes 294920 | tf_op jit(solution)/shard_map/ppermute | solution.py:526
  35.1 4.7 %collective-permute-start.13 = (bf16[1,64,512]{2,1,0:T(8,128)(2,1)S(1)}, bf16[1,64,512]{2,1,0:T(8,128)(2,1)S(1)}, u32[]{:S(2)}, u32[]{:S(2)}) collective-permute-start(bf16[1,64,512]{2,1,0:T(8,128)(2,1)S(1)} %get-tuple-element.60.refs_0_), channel_id=1, source_target_pairs={{0,8},{4,12},{8,0},{12,4},{16,24},{20,28},{24,16},{28,20},{1,9},{5... | collective-permute-start | bytes 196616 | tf_op jit(solution)/shard_map/ppermute | solution.py:526
  35.9 4.8 %collective-permute-start.9 = (bf16[384,128]{1,0:T(8,128)(2,1)S(1)}, bf16[384,128]{1,0:T(8,128)(2,1)S(1)}, u32[]{:S(2)}, u32[]{:S(2)}) collective-permute-start(bf16[384,128]{1,0:T(8,128)(2,1)S(1)} %get-tuple-element.53), channel_id=1, source_target_pairs={{8,16},{16,8},{12,20},{20,12},{5,9},{9,5},{13,17},{17,13},{21,25},... | collective-permute-start | bytes 294920 | tf_op jit(solution)/shard_map/ppermute | solution.py:526
  36.5 5.2 %collective-permute-start.12 = (bf16[384,128]{1,0:T(8,128)(2,1)S(1)}, bf16[384,128]{1,0:T(8,128)(2,1)S(1)}, u32[]{:S(2)}, u32[]{:S(2)}) collective-permute-start(bf16[384,128]{1,0:T(8,128)(2,1)S(1)} %get-tuple-element.59), channel_id=1, source_target_pairs={{0,8},{8,0},{4,12},{12,4},{16,24},{24,16},{20,28},{28,20},{1,5},{5... | collective-permute-start | bytes 294920 | tf_op jit(solution)/shard_map/ppermute | solution.py:526
  39.8 5.9 %collective-permute-start.14 = (bf16[1,64,512]{2,1,0:T(8,128)(2,1)S(1)}, bf16[1,64,512]{2,1,0:T(8,128)(2,1)S(1)}, u32[]{:S(2)}, u32[]{:S(2)}) collective-permute-start(bf16[1,64,512]{2,1,0:T(8,128)(2,1)S(1)} %sum.6.after.refs_0_), channel_id=1, source_target_pairs={{0,16},{4,20},{8,24},{12,28},{16,0},{20,4},{24,8},{28,12},{1,17},{... | collective-permute-start | bytes 196616 | tf_op jit(solution)/shard_map/ppermute | solution.py:526
  45.7 4.3 %collective-permute-start.15 = (bf16[1,64,512]{2,1,0:T(8,128)(2,1)S(1)}, bf16[1,64,512]{2,1,0:T(8,128)(2,1)S(1)}, u32[]{:S(2)}, u32[]{:S(2)}) collective-permute-start(bf16[1,64,512]{2,1,0:T(8,128)(2,1)S(1)} %sum.7.after), channel_id=1, source_target_pairs={{0,4},{4,0},{8,12},{12,8},{16,20},{20,16},{24,28},{28,24},{1,5},{5... | collective-permute-start | bytes 196616 | tf_op jit(solution)/shard_map/ppermute | solution.py:526
